TPU v7x, 512 devices: a whole 4x4x16 slice. The times are simulated.
512 devices in a mesh: dp: 64 (over z, y), seq: 8 (over x, core).
Axes of the slice: x: 4, y: 4, z: 16, core: 2. Of those that a mesh axis runs over, the one named last changes fastest.
Arguments:
- queries: bfloat16 [98304, 4096], P(('dp', 'seq')), may hold values from -10 to 10
- key_value: bfloat16 [98304, 8, 2, 128], P(('dp', 'seq')), may hold values from -10 to 10
- route_group: int32 [98304], P(('dp', 'seq')), may hold values from 0 to 63, as said below
- arrive_slot: int32 [98304], P(('dp', 'seq')), may hold values from 0 to 383, as said below
- segment_ids: int32 [64, 1536], P('dp', 'seq'), may hold values from 0 to 7, never falling along the last dimension, each value on 1 to 384 neighbouring positions
Outputs:
- attended: bfloat16 [98304, 4096], P(('dp', 'seq'))
Inputs may be any that keep to these rules, and one draw needn't show every extreme that they name: Rows keep their index along seq: the row of device (g, s) goes to device (route_group, s). Each device sends 6 rows to one group, 3 rows to most others and none to one; every device receives 192 rows. For one index s along seq, how many rows device g sends to group (g + k) modulo the number of groups depends on k only. `arrive_slot`: equals src * 6 + r, where src is the sending group and r the place of the row among that group's rows sent to this device, in row order; with route_group it maps rows one to one.
All inputs are finite; a program needn't handle non-finite values.
Results may differ from a plain program's by a relative error of at most 0.0046.
Values may be sent and summed in bfloat16 or wider, within the bound.
No kernel may reach another device: no remote copies, remote signals or barrier semaphores. Data moves between devices by JAX's collectives and lax.ppermute only.
A program may use at most 64 MiB of HBM per device.

v0:
```python
import jax
import jax.numpy as jnp
from jax import lax
from jax.sharding import PartitionSpec as P


def attend(queries, key_value, segment, start):
    q_rows = queries.shape[0]
    total_len = key_value.shape[0]
    kv_heads = key_value.shape[1]
    head_dim = key_value.shape[3]
    grouped = queries.shape[1] // (kv_heads * head_dim)
    scaling = head_dim ** (-0.5)
    longest = total_len // 4
    block_rows = min(512, q_rows)
    blocks = q_rows // block_rows
    width = longest + block_rows
    shaped = queries.reshape(blocks, block_rows, kv_heads, grouped, head_dim)
    padded_kv = jnp.concatenate(
        [jnp.zeros((longest, kv_heads, 2, head_dim), key_value.dtype), key_value], axis=0
    )
    padded_seg = jnp.concatenate([jnp.full((longest,), -1, jnp.int32), segment], axis=0)

    def per_head(head_idx):
        kv_head = lax.dynamic_index_in_dim(padded_kv, head_idx, 1, False)

        def per_block(block_idx):
            q_block = lax.dynamic_index_in_dim(shaped, block_idx, 0, False)
            q_block = lax.dynamic_index_in_dim(q_block, head_idx, 1, False)
            first = start + block_idx * block_rows
            window = lax.dynamic_slice_in_dim(kv_head, first, width, 0)
            seg_win = lax.dynamic_slice_in_dim(padded_seg, first, width, 0)
            q_seg = lax.dynamic_slice_in_dim(segment, first, block_rows, 0)
            q_pos = first + jnp.arange(block_rows, dtype=jnp.int32)
            k_pos = first - longest + jnp.arange(width, dtype=jnp.int32)
            visible = (q_pos[:, None] >= k_pos[None, :]) & (q_seg[:, None] == seg_win[None, :])
            scores = (
                jnp.einsum("qgd,sd->gqs", q_block, window[:, 0], preferred_element_type=jnp.float32)
                * scaling
            )
            scores = jnp.where(visible[None], scores, -jnp.inf)
            top_score = jnp.max(scores, axis=2, keepdims=True)
            powers = jnp.exp(scores - top_score)
            weights = (powers / jnp.sum(powers, axis=2, keepdims=True)).astype(jnp.bfloat16)
            mixed = jnp.einsum(
                "gqs,sd->qgd", weights, window[:, 1], preferred_element_type=jnp.float32
            )
            return mixed.astype(jnp.bfloat16)

        return lax.map(per_block, jnp.arange(blocks, dtype=jnp.int32))

    outs = lax.map(per_head, jnp.arange(kv_heads, dtype=jnp.int32))
    return outs.transpose(1, 2, 0, 3, 4).reshape(q_rows, -1)


def on_device(queries, key_value, route_group, arrive_slot, segment_ids):
    tok_rows = queries.shape[0]
    q_width = queries.shape[1]
    kv_heads = key_value.shape[1]
    head_dim = key_value.shape[3]
    groups = lax.axis_size("dp")
    seq_ways = lax.axis_size("seq")
    capacity = 2 * tok_rows // groups
    lane_ids = jnp.arange(groups, dtype=jnp.int32)
    onehot = (route_group[:, None] == lane_ids[None, :]).astype(jnp.int32)
    before = jnp.cumsum(onehot, axis=0) - onehot
    order_rank = jnp.sum(before * onehot, axis=1)
    slot_index = route_group * capacity + order_rank
    send_q = jnp.zeros((groups * capacity, q_width), queries.dtype).at[slot_index].set(queries)
    send_kv = (
        jnp.zeros((groups * capacity, kv_heads, 2, head_dim), key_value.dtype)
        .at[slot_index]
        .set(key_value)
    )
    recv_q, recv_kv = (
        lax.all_to_all(
            send_q.reshape(groups, capacity, q_width), "dp", split_axis=0, concat_axis=0, tiled=True
        ),
        lax.all_to_all(
            send_kv.reshape(groups, capacity, kv_heads, 2, head_dim),
            "dp",
            split_axis=0,
            concat_axis=0,
            tiled=True,
        ),
    )
    packed_q = recv_q.reshape(groups * capacity, q_width)[arrive_slot]
    packed_kv = recv_kv.reshape(groups * capacity, kv_heads, 2, head_dim)[arrive_slot]
    segment = lax.all_gather(segment_ids, "seq", axis=1, tiled=True)[0]
    head_q, head_kv = (
        lax.all_to_all(
            packed_q.reshape(tok_rows, seq_ways, q_width // seq_ways),
            "seq",
            split_axis=1,
            concat_axis=0,
            tiled=True,
        ),
        lax.all_to_all(
            packed_kv.reshape(tok_rows, seq_ways, kv_heads // seq_ways, 2, head_dim),
            "seq",
            split_axis=1,
            concat_axis=0,
            tiled=True,
        ),
    )
    total_len = tok_rows * seq_ways
    local_out = attend(
        head_q.reshape(total_len, q_width // seq_ways),
        head_kv.reshape(total_len, kv_heads // seq_ways, 2, head_dim),
        segment,
        0,
    )
    returned = lax.all_to_all(
        local_out.reshape(seq_ways, tok_rows, 1, q_width // seq_ways),
        "seq",
        split_axis=0,
        concat_axis=2,
        tiled=True,
    )
    return returned.reshape(tok_rows, q_width)


def solution(mesh):
    return jax.shard_map(
        on_device,
        mesh=mesh,
        in_specs=(
            P(("dp", "seq"), None),
            P(("dp", "seq"), None, None, None),
            P(("dp", "seq")),
            P(("dp", "seq")),
            P("dp", "seq"),
        ),
        out_specs=P(("dp", "seq"), None),
        check_vma=False,
    )
```

profile of v0, /device:TPU:1, one launch (start us, length us, event | category | flops | bytes accessed | tf_op | source)
XLA Modules:
  0.0 442.5 jit_solution(18226214635791926)
XLA Ops:
  5.6 19.5 %scatter_fusion = bf16[384,8,2,128]{3,1,2,0:T(8,128)(2,1)} fusion(bf16[384,8,2,128]{3,1,2,0:T(8,128)(2,1)} %broadcast_in_dim.59, s32[192]{0:T(256)S(1)} %compare_select_fusion.1, bf16[192,8,2,128]{3,1,2,0:T(8,128)(2,1)S(1)} %copy.31), kind=kCustom, calls=%fused_computation.2 | custom fusion | bytes 2360064 | tf_op jit(solution)/shard_map/scatter | solution.py:73
  25.1 19.5 %all-to-all-start = ((bf16[64,6,8,2,128]{4,2,3,1,0:T(8,128)(2,1)}), bf16[64,6,8,2,128]{4,2,3,1,0:T(8,128)(2,1)}, u32[]{:S(2)}, u32[]{:S(2)}) async-start(bf16[64,6,8,2,128]{4,2,3,1,0:T(8,128)(2,1)} %bitcast.10), calls=%async_computation | async-start | bytes 3145728 | tf_op jit(solution)/shard_map/all_to_all | solution.py:79
  44.6 4.7 %scatter_custom_fusion.1 = bf16[384,4096]{1,0:T(8,128)(2,1)S(1)} fusion(s32[192]{0:T(256)S(1)} %compare_select_fusion.1, bf16[192,4096]{1,0:T(8,128)(2,1)} %param.7, bf16[]{:T(256)} %constant.105.clone.1), kind=kCustom, calls=%fused_computation.31 | custom fusion | bytes 3146240 | tf_op jit(solution)/shard_map/scatter | solution.py:69
  49.3 2.9 reshape.116
  52.2 65.7 %all-to-all-done = bf16[64,6,8,2,128]{4,2,3,1,0:T(8,128)(2,1)} async-done(((bf16[64,6,8,2,128]{4,2,3,1,0:T(8,128)(2,1)}), bf16[64,6,8,2,128]{4,2,3,1,0:T(8,128)(2,1)}, u32[]{:S(2)}, u32[]{:S(2)}) %all-to-all-start) | async-done | bytes 1572896 | tf_op jit(solution)/shard_map/all_to_all | solution.py:79
  117.8 10.0 %all-to-all-start.2 = ((bf16[64,6,4096]{2,1,0:T(8,128)(2,1)}), bf16[64,6,4096]{2,1,0:T(8,128)(2,1)}, u32[]{:S(2)}, u32[]{:S(2)}) async-start(bf16[64,6,4096]{2,1,0:T(8,128)(2,1)} %reshape.116), calls=%async_computation.2 | async-start | bytes 8388608 | tf_op jit(solution)/shard_map/all_to_all | solution.py:76
  127.9 2.2 gather_fusion
  131.6 179.9 %all-to-all-done.2 = bf16[64,6,4096]{2,1,0:T(8,128)(2,1)} async-done(((bf16[64,6,4096]{2,1,0:T(8,128)(2,1)}), bf16[64,6,4096]{2,1,0:T(8,128)(2,1)}, u32[]{:S(2)}, u32[]{:S(2)}) %all-to-all-start.2) | async-done | bytes 3145760 | tf_op jit(solution)/shard_map/all_to_all | solution.py:76
  311.5 11.6 %all-to-all-start.1 = ((bf16[192,8,1,2,128]{4,3,0,2,1:T(2,128)(2,1)}), bf16[192,8,1,2,128]{4,3,0,2,1:T(2,128)(2,1)}, u32[]{:S(2)}, u32[]{:S(2)}) async-start(bf16[192,8,1,2,128]{4,3,0,2,1:T(2,128)(2,1)} %copy.32), calls=%async_computation.1 | async-start | bytes 1572864 | tf_op jit(solution)/shard_map/all_to_all | solution.py:98
  323.0 4.2 reshape.117
  327.2 2.7 gather_fusion.1
  329.9 2.7 copy.65
  332.6 2.9 all-to-all-done.1
  335.4 4.4 all-to-all-start.3
  342.0 20.6 %all-reduce.3 = s32[1536]{0:T(1024)S(1)} all-reduce(s32[1536]{0:T(1024)S(1)} %dynamic-update-slice), channel_id=1, replica_groups=mesh['dp'=64,'seq'=8] {'seq'}, use_global_device_ids=true, to_apply=%add.3 | all-reduce | flops 1536 | bytes 12288 | tf_op jit(solution)/shard_map/squeeze | solution.py:89
  365.3 48.3 %while.20 = (s32[]{:T(128)}, bf16[3,512,4,128]{3,2,1,0:T(4,128)(2,1)}, s32[3]{0:T(128)S(1)}, bf16[1920,2,128]{2,0,1:T(8,128)(2,1)}, s32[1536]{0:T(1024)S(1)}, /*...) while((s32[]{:T(128)}, ...), condition=%wide.region_8.9_spmd, body=%wide.region_5.8_spmd.sunk | while | flops 952174848 | bytes 20295992 | solution.py:50
  369.6 6.6 %fusion.25 = (f32[4,512]{1,0:T(4,128)S(1)}, f32[4,512,896]{1,2,0:T(8,128)}) fusion(pred[512,896]{0,1:T(8,128)(4,1)S(1)} %compare_and_fusion.2, bf16[1,512,1,4,128]{4,3,1,0,2:T(4,128)(2,1)S(1)} %constant_dynamic-slice_fusion.2, bf16[1920,2,128]{2,0,1:T(8,128)(2,1)} %get-tuple-element.248, s32[]{:T(128)S(6)} %select_n.64), kind=kOutput, calls=%fused_computation.47.clone.1 | convolution fusion | flops 477102976 | bytes 8560644 | tf_op jit(solution)/shard_map/while/body/eval_jaxpr/while/body/eval_jaxpr/sub | solution.py:43
  376.2 4.0 fusion.26
  385.7 6.6 %fusion.25 = (f32[4,512]{1,0:T(4,128)S(1)}, f32[4,512,896]{1,2,0:T(8,128)}) fusion(pred[512,896]{0,1:T(8,128)(4,1)S(1)} %compare_and_fusion.2, bf16[1,512,1,4,128]{4,3,1,0,2:T(4,128)(2,1)S(1)} %constant_dynamic-slice_fusion.2, bf16[1920,2,128]{2,0,1:T(8,128)(2,1)} %get-tuple-element.248, s32[]{:T(128)S(6)} %select_n.64), kind=kOutput, calls=%fused_computation.47.clone.1 | convolution fusion | flops 477102976 | bytes 8560644 | tf_op jit(solution)/shard_map/while/body/eval_jaxpr/while/body/eval_jaxpr/sub | solution.py:43
  392.3 4.0 fusion.26
  401.8 6.6 %fusion.25 = (f32[4,512]{1,0:T(4,128)S(1)}, f32[4,512,896]{1,2,0:T(8,128)}) fusion(pred[512,896]{0,1:T(8,128)(4,1)S(1)} %compare_and_fusion.2, bf16[1,512,1,4,128]{4,3,1,0,2:T(4,128)(2,1)S(1)} %constant_dynamic-slice_fusion.2, bf16[1920,2,128]{2,0,1:T(8,128)(2,1)} %get-tuple-element.248, s32[]{:T(128)S(6)} %select_n.64), kind=kOutput, calls=%fused_computation.47.clone.1 | convolution fusion | flops 477102976 | bytes 8560644 | tf_op jit(solution)/shard_map/while/body/eval_jaxpr/while/body/eval_jaxpr/sub | solution.py:43
  408.4 4.0 fusion.26
  413.6 2.5 reshape_reshape_transpose.3
  416.2 25.0 %all_to_all.55 = bf16[8,192,1,512]{3,1,2,0:T(8,128)(2,1)S(1)} all-to-all(bf16[8,192,1,512]{3,1,2,0:T(8,128)(2,1)S(1)} %bitcast.103), channel_id=1, replica_groups=mesh['dp'=64,'seq'=8] {'seq'}, dimensions={0} | all-to-all | bytes 3145728 | tf_op jit(solution)/shard_map/all_to_all | solution.py:113
  (56 shorter events, 21.0 us)
Async XLA Ops:
  25.1 92.7 %all-to-all-start = ((bf16[64,6,8,2,128]{4,2,3,1,0:T(8,128)(2,1)}), bf16[64,6,8,2,128]{4,2,3,1,0:T(8,128)(2,1)}, u32[]{:S(2)}, u32[]{:S(2)}) async-start(bf16[64,6,8,2,128]{4,2,3,1,0:T(8,128)(2,1)} %bitcast.10), calls=%async_computation | async-start | bytes 3145728 | tf_op jit(solution)/shard_map/all_to_all | solution.py:79
  52.2 75.7 %copy-start = (s32[192]{0:T(256)S(1)}, s32[192]{0:T(256)}, u32[]{:S(2)}) copy-start(s32[192]{0:T(256)} %param.10) | copy-start | bytes 2308
  117.8 193.7 %all-to-all-start.2 = ((bf16[64,6,4096]{2,1,0:T(8,128)(2,1)}), bf16[64,6,4096]{2,1,0:T(8,128)(2,1)}, u32[]{:S(2)}, u32[]{:S(2)}) async-start(bf16[64,6,4096]{2,1,0:T(8,128)(2,1)} %reshape.116), calls=%async_computation.2 | async-start | bytes 8388608 | tf_op jit(solution)/shard_map/all_to_all | solution.py:76
  311.5 23.9 %all-to-all-start.1 = ((bf16[192,8,1,2,128]{4,3,0,2,1:T(2,128)(2,1)}), bf16[192,8,1,2,128]{4,3,0,2,1:T(2,128)(2,1)}, u32[]{:S(2)}, u32[]{:S(2)}) async-start(bf16[192,8,1,2,128]{4,3,0,2,1:T(2,128)(2,1)} %copy.32), calls=%async_computation.1 | async-start | bytes 1572864 | tf_op jit(solution)/shard_map/all_to_all | solution.py:98
  332.6 9.1 %copy-start.1 = (s32[1,192]{1,0:T(1,128)S(1)}, s32[1,192]{1,0:T(1,128)}, u32[]{:S(2)}) copy-start(s32[1,192]{1,0:T(1,128)} %param.11) | copy-start | bytes 2308
  335.4 29.4 %all-to-all-start.3 = ((bf16[192,8,512]{2,0,1:T(8,128)(2,1)}), bf16[192,8,512]{2,0,1:T(8,128)(2,1)S(1)}, u32[]{:S(2)}, u32[]{:S(2)}) async-start(bf16[192,8,512]{2,0,1:T(8,128)(2,1)} %bitcast.88), calls=%async_computation.3 | async-start | bytes 3145728 | tf_op jit(solution)/shard_map/all_to_all | solution.py:91
where the time goes:
time: 444 us; the launch traced here: 442 us
  waiting for transfers between devices  248 us (56%)
  local copies, waits for them, and re-layouts  58 us (13%)
  blocking collectives  45.6 us (10%)
  starting transfers between devices  45.4 us (10%)
  matrix products  31.7 us (7%)
  loops' own time  8.43 us (2%)
    all_to_all x1, waiting for transfers between devices, on_device(): lax.all_to_all(send_q.reshape(groups, capacity, q_width), 'dp', split_axi...  180 us
    all_to_all x1, waiting for transfers between devices, on_device(): lax.all_to_all(send_kv.reshape(groups, capacity, kv_heads, 2, head_dim),...  65.7 us
    all_to_all x1, blocking collectives, on_device(): lax.all_to_all(local_out.reshape(seq_ways, tok_rows, 1, q_width // seq_wa...  25 us
    squeeze x1, blocking collectives, on_device(): segment = lax.all_gather(segment_ids, 'seq', axis=1, tiled=True)[0]  20.6 us
    sub x3, matrix products, per_block(): powers = jnp.exp(scores - top_score)  19.8 us
    all_to_all x1, starting transfers between devices, on_device(): lax.all_to_all(send_kv.reshape(groups, capacity, kv_heads, 2, head_dim),...  19.5 us
    scatter x1, local copies, waits for them, and re-layouts, on_device(): send_kv = jnp.zeros((groups * capacity, kv_heads, 2, head_dim), key_value...  19.5 us
    dot_general x3, matrix products, per_block(): jnp.einsum('gqs,sd->qgd', weights, window[:, 1], preferred_element_type=j...  11.9 us
  transfers between devices with their start and end apart: 4, of which 3 were waited for; matrix products, arithmetic and copies ran while one was open for 6% of the time, Pallas kernels for 0%

commit v1 on v0

v1 whole, which is shorter than its diff:
```python
import functools

import jax
import jax.numpy as jnp
from jax import lax
from jax.experimental import pallas as pl
from jax.experimental.pallas import tpu as pltpu
from jax.sharding import Mesh, PartitionSpec as P

ROWS = 192
NZ, NY, NS = 16, 4, 8
PER = 3
TILE = 16
HD = 128
EXT = 9
BF = jnp.bfloat16
VMEM_LIMIT = 48 * 1024 * 1024

VM = pl.BlockSpec(memory_space=pltpu.VMEM)
SM = pl.BlockSpec(memory_space=pltpu.SMEM)
ANY = pl.BlockSpec(memory_space=pl.ANY)


def params(**kw):
    return pltpu.CompilerParams(vmem_limit_bytes=VMEM_LIMIT, **kw)


def pack_kv_kernel(me_ref, rg_ref, kv_ref, q_ref, out_ref, slot_ref, meta_ref, cnt, xrow, qs, sem):
    y = me_ref[0]
    out_ref[...] = jnp.zeros_like(out_ref)
    for i in range(NZ * NY):
        cnt[i] = 0
    for e in range(4):
        xrow[e] = 0
    for e in range(8):
        meta_ref[e] = 0

    def step(i, carry):
        d = rg_ref[i]
        r = cnt[d]
        cnt[d] = r + 1
        over = r >= PER
        gy, gz = d & (NY - 1), d >> 2
        tile = jnp.where(over, NZ * PER + (r - PER) * 3, gz * PER + r)
        out_ref[gy, tile] = kv_ref[i]
        slot_ref[i] = jnp.where(over, ROWS + r - PER, (((gy - y) & (NY - 1)) * NZ + gz) * PER + r)

        @pl.when(over)
        def _():
            xrow[r - PER] = i
            meta_ref[0] = d

        return carry

    lax.fori_loop(0, ROWS, step, 0, unroll=8)
    copies = []
    for e in range(3):
        first = pl.multiple_of((xrow[e] >> 4) << 4, 16)
        cp = pltpu.make_async_copy(q_ref.at[pl.ds(first, 16)], qs.at[e], sem.at[e])
        cp.start()
        copies.append(cp)
    gy = meta_ref[0] & (NY - 1)
    row = lax.broadcasted_iota(jnp.int32, (16, 2 * TILE * HD), 0)
    for e in range(3):
        copies[e].wait()
        block = qs[e].astype(jnp.float32)
        one = jnp.sum(jnp.where(row == (xrow[e] & 15), block, 0.0), axis=0, keepdims=True)
        for t in range(2):
            parts = [one[:, (t * TILE + c) * HD:(t * TILE + c + 1) * HD] for c in range(TILE)]
            out_ref[gy, NZ * PER + e * 3 + 1 + t] = jnp.concatenate(parts, axis=0).astype(BF)


def pack_kv(me, rg, kv, q):
    return pl.pallas_call(
        pack_kv_kernel,
        out_shape=(
            jax.ShapeDtypeStruct((NY, NZ * PER + EXT, TILE, HD), BF),
            jax.ShapeDtypeStruct((ROWS,), jnp.int32),
            jax.ShapeDtypeStruct((8,), jnp.int32),
        ),
        in_specs=[SM, SM, VM, ANY],
        out_specs=(VM, SM, SM),
        scratch_shapes=[
            pltpu.SMEM((NZ * NY,), jnp.int32),
            pltpu.SMEM((4,), jnp.int32),
            pltpu.VMEM((3, 16, 2 * TILE * HD), BF),
            pltpu.SemaphoreType.DMA((3,)),
        ],
        compiler_params=params(),
        name="pack_kv",
    )(me, rg, kv, q)


def assemble_kv_kernel(sc_ref, yr_ref, out_ref):
    ysrc = sc_ref[0]
    for z in range(NZ):
        for y in range(NY):
            out_ref[z, y * PER:(y + 1) * PER] = yr_ref[y, z * PER:(z + 1) * PER]
        if z < EXT:
            out_ref[z, NY * PER] = yr_ref[ysrc, NZ * PER + z]
        else:
            out_ref[z, NY * PER] = jnp.zeros((TILE, HD), BF)


def assemble_kv(sc, yr):
    return pl.pallas_call(
        assemble_kv_kernel,
        out_shape=jax.ShapeDtypeStruct((NZ, NY * PER + 1, TILE, HD), BF),
        in_specs=[SM, VM],
        out_specs=VM,
        compiler_params=params(),
        name="assemble_kv",
    )(sc, yr)


def pack_q_kernel(slot_ref, q_ref, a_ref, b_ref):
    a_ref[...] = jnp.zeros_like(a_ref)
    b_ref[...] = jnp.zeros_like(b_ref)

    def step(i, carry):
        s = slot_ref[i]

        @pl.when(s < ROWS)
        def _():
            a_ref[s] = q_ref[i, 0:TILE]
            b_ref[s] = q_ref[i, TILE:2 * TILE]

        return carry

    lax.fori_loop(0, ROWS, step, 0, unroll=8)


def pack_q(slot, q3):
    shape = jax.ShapeDtypeStruct((ROWS, TILE, HD), BF)
    return pl.pallas_call(
        pack_q_kernel,
        out_shape=(shape, shape),
        in_specs=[SM, VM],
        out_specs=(VM, VM),
        compiler_params=params(),
        name="pack_q",
    )(slot, q3)


def assemble_q_hop_kernel(sc_ref, b0, b1, b2, b3, hop_ref, out_ref):
    dz = sc_ref[1]
    for z in range(NZ):
        for k, b in enumerate((b0, b1, b2, b3)):
            out_ref[z, k * PER:(k + 1) * PER] = b[z * PER:(z + 1) * PER]
        out_ref[z, NY * PER] = hop_ref[(z - dz) & (NZ - 1), 0]


def assemble_q_hop(sc, blocks, zr1):
    whole = lambda n: pl.BlockSpec((n, TILE, HD), lambda i: (0, 0, 0))
    return pl.pallas_call(
        assemble_q_hop_kernel,
        grid=(1,),
        out_shape=jax.ShapeDtypeStruct((NZ, NY * PER + 1, TILE, HD), BF),
        in_specs=[SM] + [whole(NZ * PER)] * NY
        + [pl.BlockSpec((NZ, 1, TILE, HD), lambda i: (0, NY * PER, 0, 0))],
        out_specs=pl.BlockSpec((NZ, NY * PER + 1, TILE, HD), lambda i: (0, 0, 0, 0)),
        compiler_params=params(),
        name="assemble_q_hop",
    )(sc, *blocks, zr1)


def unpack_kernel(part, limit, idx_ref, src_ref, hop_ref, out_ref):
    def step(p, carry):
        i = idx_ref[p]
        over = i >= limit
        base = src_ref[jnp.where(over, 0, i)]
        ext = hop_ref[jnp.where(over, (i - limit) * 3 + part, 0), 0]
        out_ref[p] = jnp.where(over, ext, base)
        return carry

    lax.fori_loop(0, ROWS, step, 0, unroll=8)


def unpack(part, idx, zr, zr2):
    limit = zr.shape[0] * zr.shape[1]
    return pl.pallas_call(
        functools.partial(unpack_kernel, part, limit),
        grid=(1,),
        out_shape=jax.ShapeDtypeStruct((ROWS, TILE, HD), BF),
        in_specs=[
            SM,
            pl.BlockSpec((limit, TILE, HD), lambda i: (0, 0, 0)),
            pl.BlockSpec((NZ, 1, TILE, HD), lambda i: (0, NY * PER, 0, 0)),
        ],
        out_specs=pl.BlockSpec((ROWS, TILE, HD), lambda i: (0, 0, 0)),
        compiler_params=params(),
        name="unpack",
    )(idx, zr.reshape(limit, TILE, HD), zr2)


def attend_kernel(scale, q_ref, kv_ref, segq_ref, segk_ref, *rest):
    out_ref = rest[-1]
    half = ROWS // 2
    for b in range(2):
        lo, width = b * half, ROWS * 2 + half
        segq = segq_ref[lo:lo + half, :]
        segk = segk_ref[:, lo:lo + width]
        i = lax.broadcasted_iota(jnp.int32, (half, width), 0)
        j = lax.broadcasted_iota(jnp.int32, (half, width), 1)
        seen = (segq == segk) & (j <= i + 2 * ROWS)
        keys = kv_ref[0, lo:lo + width, :]
        values = kv_ref[1, lo:lo + width, :]
        for g in range(4):
            q = q_ref[g, lo:lo + half, :]
            s = lax.dot_general(q, keys, (((1,), (1,)), ((), ())), preferred_element_type=jnp.float32)
            s = jnp.where(seen, s * scale, -jnp.inf)
            w = jnp.exp(s - jnp.max(s, axis=1, keepdims=True))
            total = jnp.sum(w, axis=1, keepdims=True)
            o = jnp.dot(w.astype(BF), values, preferred_element_type=jnp.float32)
            out_ref[lo:lo + half, g * HD:(g + 1) * HD] = (o / total).astype(BF)


def attend(part, qt, kvt, segq, segk, prior=None):
    heads = TILE // 4
    in_specs = [
        pl.BlockSpec((4, ROWS, HD), lambda h: (h, 0, 0)),
        pl.BlockSpec((2, 3 * ROWS, HD), lambda h: (h + part * heads, 0, 0)),
        pl.BlockSpec((ROWS, 1), lambda h: (0, 0)),
        pl.BlockSpec((1, 3 * ROWS), lambda h: (0, 0)),
    ]
    args = [qt, kvt, segq, segk]
    alias = {}
    if prior is not None:
        in_specs.append(ANY)
        args.append(prior)
        alias = {4: 0}
    return pl.pallas_call(
        functools.partial(attend_kernel, HD ** -0.5),
        grid=(heads,),
        out_shape=jax.ShapeDtypeStruct((ROWS, 2 * TILE * HD), BF),
        in_specs=in_specs,
        out_specs=pl.BlockSpec((ROWS, 4 * HD), lambda h: (0, h + part * heads)),
        input_output_aliases=alias,
        compiler_params=params(),
        cost_estimate=pl.CostEstimate(
            flops=4 * ROWS * 480 * TILE * HD, bytes_accessed=4 << 20, transcendentals=ROWS * 480 * TILE
        ),
        name="attend",
    )(*args)


def on_device(queries, key_value, route_group, arrive_slot, segment_ids):
    z, y, s = lax.axis_index("z"), lax.axis_index("y"), lax.axis_index("seq")
    kv = key_value.reshape(ROWS, TILE, HD)
    up = lambda a, n: lax.ppermute(a, "seq", [(i, i + n) for i in range(NS - n)])

    seg = segment_ids.reshape(ROWS)
    seg1 = jnp.where(s >= 1, up(seg, 1), -1)
    seg2 = jnp.where(s >= 2, up(seg, 2), -1)
    segk = jnp.concatenate([seg2, seg1, seg])[None]
    segq = seg[:, None]

    src, rank = arrive_slot // 6, arrive_slot % 6
    sy, sz = src & (NY - 1), src >> 2
    over = rank >= PER
    dy = (y - sy) & (NY - 1)
    idx1 = jnp.where(over, NZ * 13 + rank - PER, sz * 13 + sy * PER + rank)
    idx2 = jnp.where(over, NZ * 13 + rank - PER, sz * 13 + dy * PER + rank)
    idx3 = jnp.where(over, NZ * 12 + rank - PER, sz * 12 + dy * PER + rank)

    yb, slot, meta = pack_kv(y.reshape(1), route_group, kv, queries)
    k6 = (meta[0] - (z * NY + y)) & (NZ * NY - 1)
    ysrc = (y - k6) & (NY - 1)
    dz = ((ysrc + k6) >> 2) & (NZ - 1)
    sc = jnp.stack([ysrc, dz]).astype(jnp.int32)

    yr = lax.all_to_all(yb, "y", 0, 0, tiled=True)
    zs1 = assemble_kv(sc, yr)
    zr1 = lax.all_to_all(zs1, "z", 0, 0, tiled=True)

    qa, qb = pack_q(slot, queries.reshape(ROWS, 2 * TILE, HD))

    def along_y(a):
        a = a.reshape(NY, NZ * PER, TILE, HD)
        return [a[0]] + [
            lax.ppermute(a[k], "y", [(i, (i + k) % NY) for i in range(NY)]) for k in range(1, NY)
        ]

    za, zb = along_y(qa), along_y(qb)
    zs3 = jnp.stack([b.reshape(NZ, PER, TILE, HD) for b in zb], axis=1).reshape(NZ, NY * PER, TILE, HD)

    zs2 = assemble_q_hop(sc, za, zr1)
    zr2 = lax.all_to_all(zs2, "z", 0, 0, tiled=True)
    zr3 = lax.all_to_all(zs3, "z", 0, 0, tiled=True)

    own = unpack(0, idx1, zr1, zr2)
    window = jnp.concatenate([up(own, 2), up(own, 1), own], axis=0)
    kvt = window.transpose(1, 0, 2)
    out = attend(0, unpack(1, idx2, zr2, zr2).transpose(1, 0, 2), kvt, segq, segk)
    return attend(1, unpack(2, idx3, zr3, zr2).transpose(1, 0, 2), kvt, segq, segk, out)


def solution(mesh):
    fine = Mesh(mesh.devices.reshape(NZ, NY, NS), ("z", "y", "seq"))
    rows = ("z", "y", "seq")
    return jax.shard_map(
        on_device,
        mesh=fine,
        in_specs=(
            P(rows, None),
            P(rows, None, None, None),
            P(rows),
            P(rows),
            P(("z", "y"), "seq"),
        ),
        out_specs=P(rows, None),
        check_vma=False,
    )
```

time: 444 us -> 215 us (0.48)
  the two profiles are of different devices: /device:TPU:1 before, /device:TPU:34 now
where the time goes in v1:
time: 215 us
  waiting for transfers between devices  102 us (47%)
  starting transfers between devices  62.8 us (29%)
  Pallas kernels  40.6 us (19%)
  local copies, waits for them, and re-layouts  7.43 us (3%)
    pallas_call x2, Pallas kernels, attend(): pl.pallas_call(functools.partial(attend_kernel, HD ** (-0.5)), grid=(head...  28.1 us
    all_to_all x1, waiting for transfers between devices, on_device(): zr2 = lax.all_to_all(zs2, 'z', 0, 0, tiled=True)  23.8 us
    all_to_all x1, waiting for transfers between devices, on_device(): zr1 = lax.all_to_all(zs1, 'z', 0, 0, tiled=True)  21.4 us
    ppermute x4, waiting for transfers between devices, on_device(): lax.ppermute(a, 'seq', [(i, i + n) for i in range(NS - n)])  19.6 us
    ppermute x6, starting transfers between devices, along_y(): lax.ppermute(a[k], 'y', [(i, (i + k) % NY) for i in range(NY)])  16.7 us
    ppermute x6, waiting for transfers between devices, along_y(): lax.ppermute(a[k], 'y', [(i, (i + k) % NY) for i in range(NY)])  15.6 us
    all_to_all x1, starting transfers between devices, on_device(): zr1 = lax.all_to_all(zs1, 'z', 0, 0, tiled=True)  15.2 us
    all_to_all x1, waiting for transfers between devices, on_device(): yr = lax.all_to_all(yb, 'y', 0, 0, tiled=True)  13.7 us
  transfers between devices with their start and end apart: 14, of which 11 were waited for; matrix products, arithmetic and copies ran while one was open for 1% of the time, Pallas kernels for 3%

profile of v1, /device:TPU:34, one launch (start us, length us, event | category | flops | bytes accessed | tf_op | source)
XLA Modules:
  0.0 214.6 jit_solution(535986384110973382)
XLA Ops:
  3.2 3.9 %pack_kv.1 = (bf16[4,57,16,128]{3,2,1,0:T(8,128)(2,1)S(1)}, s32[192]{0:T(256)S(1)}, s32[8]{0:T(128)S(1)}) custom-call(s32[1]{0:T(128)} %bitcast.me_ref, s32[192]{0:T(256)S(1)} %copy-done.5, bf16[192,16,128]{2,1,0:T(8,128)(2,1)S(1)} %bitcast.33, bf16[192,4096]{1,0:T(8,128)(2,1)S(1)} %copy-done), custom_call_target="tpu_custom_call" | custom-call | tf_op jit(solution)/shard_map/pack_kv/pallas_call | solution.py:74
  8.1 4.6 %all-to-all-start.1 = ((bf16[4,57,16,128]{3,2,1,0:T(8,128)(2,1)}), bf16[4,57,16,128]{3,2,1,0:T(8,128)(2,1)S(1)}, u32[]{:S(2)}, u32[]{:S(2)}) async-start(bf16[4,57,16,128]{3,2,1,0:T(8,128)(2,1)} %copy-done.3), calls=%async_computation.1 | async-start | bytes 1867776 | tf_op jit(solution)/shard_map/all_to_all | solution.py:272
  12.8 13.7 %all-to-all-done.1.yr_ref = bf16[4,57,16,128]{3,2,1,0:T(8,128)(2,1)S(1)} async-done(((bf16[4,57,16,128]{3,2,1,0:T(8,128)(2,1)}), bf16[4,57,16,128]{3,2,1,0:T(8,128)(2,1)S(1)}, u32[]{:S(2)}, u32[]{:S(2)}) %all-to-all-start.1) | async-done | bytes 933920 | tf_op jit(solution)/shard_map/all_to_all | solution.py:272
  28.1 15.2 %all-to-all-start.2 = ((bf16[16,13,16,128]{3,2,1,0:T(8,128)(2,1)}), bf16[16,13,16,128]{3,2,1,0:T(8,128)(2,1)S(1)}, u32[]{:S(2)}, u32[]{:S(2)}) async-start(bf16[16,13,16,128]{3,2,1,0:T(8,128)(2,1)} %copy-done.2), calls=%async_computation.2 | async-start | bytes 1703936 | tf_op jit(solution)/shard_map/all_to_all | solution.py:274
  43.6 2.3 %pack_q.1 = (bf16[192,16,128]{2,1,0:T(8,128)(2,1)S(1)}, bf16[192,16,128]{2,1,0:T(8,128)(2,1)S(1)}) custom-call(s32[192]{0:T(256)S(1)} %get-tuple-element.10.slot_ref, bf16[192,32,128]{2,1,0:T(8,128)(2,1)S(1)} %bitcast.29), custom_call_target="tpu_custom_call" | custom-call | tf_op jit(solution)/shard_map/pack_q/pallas_call | solution.py:135
  46.1 3.1 %collective-permute-start.5 = (bf16[48,16,128]{2,1,0:T(8,128)(2,1)S(1)}, bf16[48,16,128]{2,1,0:T(8,128)(2,1)S(1)}, u32[]{:S(2)}, u32[]{:S(2)}) collective-permute-start(bf16[48,16,128]{2,1,0:T(8,128)(2,1)S(1)} %get-tuple-element.17), channel_id=1, source_target_pairs={{0,24},{8,0},{16,8},{24,16},{1,25},{9,1},{17,9},{25,17},{2,26},{10... | collective-permute-start | bytes 589832 | tf_op jit(solution)/shard_map/ppermute | solution.py:281
  49.2 3.4 %collective-permute-start.4 = (bf16[48,16,128]{2,1,0:T(8,128)(2,1)S(1)}, bf16[48,16,128]{2,1,0:T(8,128)(2,1)S(1)}, u32[]{:S(2)}, u32[]{:S(2)}) collective-permute-start(bf16[48,16,128]{2,1,0:T(8,128)(2,1)S(1)} %get-tuple-element.18), channel_id=1, source_target_pairs={{0,16},{8,24},{16,0},{24,8},{1,17},{9,25},{17,1},{25,9},{2,18},{10... | collective-permute-start | bytes 589832 | tf_op jit(solution)/shard_map/ppermute | solution.py:281
  55.0 5.4 %collective-permute-done.4.b2 = bf16[48,16,128]{2,1,0:T(8,128)(2,1)S(1)} collective-permute-done((bf16[48,16,128]{2,1,0:T(8,128)(2,1)S(1)}, bf16[48,16,128]{2,1,0:T(8,128)(2,1)S(1)}, u32[]{:S(2)}, u32[]{:S(2)}) %collective-permute-start.4) | collective-permute-done | bytes 196640 | tf_op jit(solution)/shard_map/ppermute | solution.py:281
  62.1 21.4 %all-to-all-done.2.hop_ref = bf16[16,13,16,128]{3,2,1,0:T(8,128)(2,1)S(1)} async-done(((bf16[16,13,16,128]{3,2,1,0:T(8,128)(2,1)}), bf16[16,13,16,128]{3,2,1,0:T(8,128)(2,1)S(1)}, u32[]{:S(2)}, u32[]{:S(2)}) %all-to-all-start.2) | async-done | bytes 852000 | tf_op jit(solution)/shard_map/all_to_all | solution.py:274
  85.0 8.1 %all-to-all-start.3 = ((bf16[16,13,16,128]{3,2,1,0:T(8,128)(2,1)}), bf16[16,13,16,128]{3,2,1,0:T(8,128)(2,1)S(1)}, u32[]{:S(2)}, u32[]{:S(2)}) async-start(bf16[16,13,16,128]{3,2,1,0:T(8,128)(2,1)} %assemble_q_hop.1), calls=%async_computation.3 | async-start | bytes 1703936 | tf_op jit(solution)/shard_map/all_to_all | solution.py:288
  93.2 3.1 %collective-permute-start.2 = (bf16[48,16,128]{2,1,0:T(8,128)(2,1)S(1)}, bf16[48,16,128]{2,1,0:T(8,128)(2,1)S(1)}, u32[]{:S(2)}, u32[]{:S(2)}) collective-permute-start(bf16[48,16,128]{2,1,0:T(8,128)(2,1)S(1)} %get-tuple-element.22), channel_id=1, source_target_pairs={{0,24},{8,0},{16,8},{24,16},{1,25},{9,1},{17,9},{25,17},{2,26},{10... | collective-permute-start | bytes 589832 | tf_op jit(solution)/shard_map/ppermute | solution.py:281
  96.3 3.4 %collective-permute-start.1 = (bf16[48,16,128]{2,1,0:T(8,128)(2,1)S(1)}, bf16[48,16,128]{2,1,0:T(8,128)(2,1)S(1)}, u32[]{:S(2)}, u32[]{:S(2)}) collective-permute-start(bf16[48,16,128]{2,1,0:T(8,128)(2,1)S(1)} %get-tuple-element.23), channel_id=1, source_target_pairs={{0,16},{8,24},{16,0},{24,8},{1,17},{9,25},{17,1},{25,9},{2,18},{10... | collective-permute-start | bytes 589832 | tf_op jit(solution)/shard_map/ppermute | solution.py:281
  102.9 3.6 %collective-permute-done.1 = bf16[48,16,128]{2,1,0:T(8,128)(2,1)S(1)} collective-permute-done((bf16[48,16,128]{2,1,0:T(8,128)(2,1)S(1)}, bf16[48,16,128]{2,1,0:T(8,128)(2,1)S(1)}, u32[]{:S(2)}, u32[]{:S(2)}) %collective-permute-start.1) | collective-permute-done | bytes 196640 | tf_op jit(solution)/shard_map/ppermute | solution.py:281
  106.5 3.0 %collective-permute-done = bf16[48,16,128]{2,1,0:T(8,128)(2,1)S(1)} collective-permute-done((bf16[48,16,128]{2,1,0:T(8,128)(2,1)S(1)}, bf16[48,16,128]{2,1,0:T(8,128)(2,1)S(1)}, u32[]{:S(2)}, u32[]{:S(2)}) %collective-permute-start) | collective-permute-done | bytes 196640 | tf_op jit(solution)/shard_map/ppermute | solution.py:281
  110.7 23.8 %all-to-all-done.3.hop_ref = bf16[16,13,16,128]{3,2,1,0:T(8,128)(2,1)S(1)} async-done(((bf16[16,13,16,128]{3,2,1,0:T(8,128)(2,1)}), bf16[16,13,16,128]{3,2,1,0:T(8,128)(2,1)S(1)}, u32[]{:S(2)}, u32[]{:S(2)}) %all-to-all-start.3) | async-done | bytes 852000 | tf_op jit(solution)/shard_map/all_to_all | solution.py:288
  134.5 7.8 %all-to-all-start = ((bf16[16,12,16,128]{3,2,1,0:T(8,128)(2,1)}), bf16[16,12,16,128]{3,2,1,0:T(8,128)(2,1)S(1)}, u32[]{:S(2)}, u32[]{:S(2)}) async-start(bf16[16,12,16,128]{3,2,1,0:T(8,128)(2,1)} %bitcast.6), calls=%async_computation | async-start | bytes 1572864 | tf_op jit(solution)/shard_map/all_to_all | solution.py:289
  144.0 1.9 collective-permute-start.7
  145.9 3.4 %collective-permute-start.6 = (bf16[192,16,128]{2,0,1:T(8,128)(2,1)S(1)}, bf16[192,16,128]{2,0,1:T(8,128)(2,1)}, u32[]{:S(2)}, u32[]{:S(2)}) collective-permute-start(bf16[192,16,128]{2,0,1:T(8,128)(2,1)S(1)} %copy.15), channel_id=1, source_target_pairs={{0,2},{1,3},{2,4},{3,5},{4,6},{5,7},{8,10},{9,11},{10,12},{11,13},... | collective-permute-start | bytes 2359304 | tf_op jit(solution)/shard_map/ppermute | solution.py:250
  149.3 2.9 %collective-permute-start.9 = (s32[192]{0:T(256)S(1)}, s32[192]{0:T(256)S(1)}, u32[]{:S(2)}, u32[]{:S(2)}) collective-permute-start(s32[192]{0:T(256)S(1)} %bitcast.39), channel_id=1, source_target_pairs={{0,1},{1,2},{2,3},{3,4},{4,5},{5,6},{6,7},{8,9},{9,10},{10,11},{11... | collective-permute-start | bytes 2312 | tf_op jit(solution)/shard_map/ppermute | solution.py:250
  152.2 2.2 %collective-permute-start.8 = (s32[192]{0:T(256)S(1)}, s32[192]{0:T(256)S(1)}, u32[]{:S(2)}, u32[]{:S(2)}) collective-permute-start(s32[192]{0:T(256)S(1)} %bitcast.40), channel_id=1, source_target_pairs={{0,2},{1,3},{2,4},{3,5},{4,6},{5,7},{8,10},{9,11},{10,12},{11,13},... | collective-permute-start | bytes 2312 | tf_op jit(solution)/shard_map/ppermute | solution.py:250
  154.6 19.6 %collective-permute-done.9 = s32[192]{0:T(256)S(1)} collective-permute-done((s32[192]{0:T(256)S(1)}, s32[192]{0:T(256)S(1)}, u32[]{:S(2)}, u32[]{:S(2)}) %collective-permute-start.9) | collective-permute-done | bytes 800 | tf_op jit(solution)/shard_map/ppermute | solution.py:250
  174.2 7.4 %all-to-all-done = bf16[16,12,16,128]{3,2,1,0:T(8,128)(2,1)S(1)} async-done(((bf16[16,12,16,128]{3,2,1,0:T(8,128)(2,1)}), bf16[16,12,16,128]{3,2,1,0:T(8,128)(2,1)S(1)}, u32[]{:S(2)}, u32[]{:S(2)}) %all-to-all-start) | async-done | bytes 786464 | tf_op jit(solution)/shard_map/all_to_all | solution.py:289
  186.5 14.1 %attend.2.rest_0_ = bf16[192,4096]{1,0:T(8,128)(2,1)} custom-call(bf16[16,192,128]{2,1,0:T(8,128)(2,1)S(1)} %bitcast.31, bf16[16,576,128]{2,1,0:T(8,128)(2,1)S(1)} %maximum_bitcast_fusion.kv_ref, s32[192,1]{1,0:T(8,128)S(1)} %copy.20.segq_ref, s32[1,576]{1,0:T(1,128)S(1)} %broadcast_in_dim.6.segk_ref), custom_call_target="tpu_custom_call" | custom-call | flops 754974720 | bytes 4194304 | tf_op jit(solution)/shard_map/attend/pallas_call | solution.py:232
  200.6 14.0 %attend.3 = bf16[192,4096]{1,0:T(8,128)(2,1)} custom-call(bf16[16,192,128]{2,1,0:T(8,128)(2,1)S(1)} %bitcast.30, bf16[16,576,128]{2,1,0:T(8,128)(2,1)S(1)} %maximum_bitcast_fusion.kv_ref, s32[192,1]{1,0:T(8,128)S(1)} %copy.20.segq_ref, s32[1,576]{1,0:T(1,128)S(1)} %broadcast_in_dim.6.segk_ref, ...), custom_call_target="tpu_custom_call", output_to_operand_aliasing={{}: (4, {})} | custom-call | flops 754974720 | bytes 4194304 | tf_op jit(solution)/shard_map/attend/pallas_call | solution.py:232
  (46 shorter events, 23.0 us)
Async XLA Ops:
  0.0 1.4 copy-start
  1.4 1.1 copy-start.4
  2.5 0.7 copy-start.5
  7.2 0.9 copy-start.3
  8.1 35.2 %copy-start.1 = (bf16[192,4096]{1,0:T(8,128)(2,1)S(1)}, bf16[192,4096]{1,0:T(8,128)(2,1)}, u32[]{:S(2)}) copy-start(bf16[192,4096]{1,0:T(8,128)(2,1)} %q_ref.1) | copy-start | bytes 4718596
  8.1 18.5 %all-to-all-start.1 = ((bf16[4,57,16,128]{3,2,1,0:T(8,128)(2,1)}), bf16[4,57,16,128]{3,2,1,0:T(8,128)(2,1)S(1)}, u32[]{:S(2)}, u32[]{:S(2)}) async-start(bf16[4,57,16,128]{3,2,1,0:T(8,128)(2,1)} %copy-done.3), calls=%async_computation.1 | async-start | bytes 1867776 | tf_op jit(solution)/shard_map/all_to_all | solution.py:272
  27.2 0.9 copy-start.2
  28.1 55.4 %all-to-all-start.2 = ((bf16[16,13,16,128]{3,2,1,0:T(8,128)(2,1)}), bf16[16,13,16,128]{3,2,1,0:T(8,128)(2,1)S(1)}, u32[]{:S(2)}, u32[]{:S(2)}) async-start(bf16[16,13,16,128]{3,2,1,0:T(8,128)(2,1)} %copy-done.2), calls=%async_computation.2 | async-start | bytes 1703936 | tf_op jit(solution)/shard_map/all_to_all | solution.py:274
  46.1 8.9 %collective-permute-start.5 = (bf16[48,16,128]{2,1,0:T(8,128)(2,1)S(1)}, bf16[48,16,128]{2,1,0:T(8,128)(2,1)S(1)}, u32[]{:S(2)}, u32[]{:S(2)}) collective-permute-start(bf16[48,16,128]{2,1,0:T(8,128)(2,1)S(1)} %get-tuple-element.17), channel_id=1, source_target_pairs={{0,24},{8,0},{16,8},{24,16},{1,25},{9,1},{17,9},{25,17},{2,26},{10... | collective-permute-start | bytes 589832 | tf_op jit(solution)/shard_map/ppermute | solution.py:281
  49.2 11.2 %collective-permute-start.4 = (bf16[48,16,128]{2,1,0:T(8,128)(2,1)S(1)}, bf16[48,16,128]{2,1,0:T(8,128)(2,1)S(1)}, u32[]{:S(2)}, u32[]{:S(2)}) collective-permute-start(bf16[48,16,128]{2,1,0:T(8,128)(2,1)S(1)} %get-tuple-element.18), channel_id=1, source_target_pairs={{0,16},{8,24},{16,0},{24,8},{1,17},{9,25},{17,1},{25,9},{2,18},{10... | collective-permute-start | bytes 589832 | tf_op jit(solution)/shard_map/ppermute | solution.py:281
  52.5 9.5 %collective-permute-start.3 = (bf16[48,16,128]{2,1,0:T(8,128)(2,1)S(1)}, bf16[48,16,128]{2,1,0:T(8,128)(2,1)S(1)}, u32[]{:S(2)}, u32[]{:S(2)}) collective-permute-start(bf16[48,16,128]{2,1,0:T(8,128)(2,1)S(1)} %get-tuple-element.19), channel_id=1, source_target_pairs={{0,8},{8,16},{16,24},{24,0},{1,9},{9,17},{17,25},{25,1},{2,10},{10... | collective-permute-start | bytes 589832 | tf_op jit(solution)/shard_map/ppermute | solution.py:281
  85.0 49.5 %all-to-all-start.3 = ((bf16[16,13,16,128]{3,2,1,0:T(8,128)(2,1)}), bf16[16,13,16,128]{3,2,1,0:T(8,128)(2,1)S(1)}, u32[]{:S(2)}, u32[]{:S(2)}) async-start(bf16[16,13,16,128]{3,2,1,0:T(8,128)(2,1)} %assemble_q_hop.1), calls=%async_computation.3 | async-start | bytes 1703936 | tf_op jit(solution)/shard_map/all_to_all | solution.py:288
  93.2 9.7 %collective-permute-start.2 = (bf16[48,16,128]{2,1,0:T(8,128)(2,1)S(1)}, bf16[48,16,128]{2,1,0:T(8,128)(2,1)S(1)}, u32[]{:S(2)}, u32[]{:S(2)}) collective-permute-start(bf16[48,16,128]{2,1,0:T(8,128)(2,1)S(1)} %get-tuple-element.22), channel_id=1, source_target_pairs={{0,24},{8,0},{16,8},{24,16},{1,25},{9,1},{17,9},{25,17},{2,26},{10... | collective-permute-start | bytes 589832 | tf_op jit(solution)/shard_map/ppermute | solution.py:281
  96.3 10.2 %collective-permute-start.1 = (bf16[48,16,128]{2,1,0:T(8,128)(2,1)S(1)}, bf16[48,16,128]{2,1,0:T(8,128)(2,1)S(1)}, u32[]{:S(2)}, u32[]{:S(2)}) collective-permute-start(bf16[48,16,128]{2,1,0:T(8,128)(2,1)S(1)} %get-tuple-element.23), channel_id=1, source_target_pairs={{0,16},{8,24},{16,0},{24,8},{1,17},{9,25},{17,1},{25,9},{2,18},{10... | collective-permute-start | bytes 589832 | tf_op jit(solution)/shard_map/ppermute | solution.py:281
  99.6 9.9 %collective-permute-start = (bf16[48,16,128]{2,1,0:T(8,128)(2,1)S(1)}, bf16[48,16,128]{2,1,0:T(8,128)(2,1)S(1)}, u32[]{:S(2)}, u32[]{:S(2)}) collective-permute-start(bf16[48,16,128]{2,1,0:T(8,128)(2,1)S(1)} %get-tuple-element.24), channel_id=1, source_target_pairs={{0,8},{8,16},{16,24},{24,0},{1,9},{9,17},{17,25},{25,1},{2,10},{10... | collective-permute-start | bytes 589832 | tf_op jit(solution)/shard_map/ppermute | solution.py:281
  109.5 32.8 %copy-start.7 = (s32[192]{0:T(256)S(1)}, s32[192]{0:T(256)}, u32[]{:S(2)}) copy-start(s32[192]{0:T(256)} %param.8) | copy-start | bytes 2308
  134.5 47.1 %all-to-all-start = ((bf16[16,12,16,128]{3,2,1,0:T(8,128)(2,1)}), bf16[16,12,16,128]{3,2,1,0:T(8,128)(2,1)S(1)}, u32[]{:S(2)}, u32[]{:S(2)}) async-start(bf16[16,12,16,128]{3,2,1,0:T(8,128)(2,1)} %bitcast.6), calls=%async_computation | async-start | bytes 1572864 | tf_op jit(solution)/shard_map/all_to_all | solution.py:289
  142.3 7.0 %copy-start.6 = (s32[1,192]{1,0:T(1,128)S(1)}, s32[1,192]{1,0:T(1,128)}, u32[]{:S(2)}) copy-start(s32[1,192]{1,0:T(1,128)} %param.9) | copy-start | bytes 2308
  144.0 41.0 %collective-permute-start.7 = (bf16[192,16,128]{2,0,1:T(8,128)(2,1)S(1)}, bf16[192,16,128]{2,0,1:T(8,128)(2,1)}, u32[]{:S(2)}, u32[]{:S(2)}) collective-permute-start(bf16[192,16,128]{2,0,1:T(8,128)(2,1)S(1)} %copy.15), channel_id=1, source_target_pairs={{0,1},{1,2},{2,3},{3,4},{4,5},{5,6},{6,7},{8,9},{9,10},{10,11},{11... | collective-permute-start | bytes 2359304 | tf_op jit(solution)/shard_map/ppermute | solution.py:250
  145.9 39.1 %collective-permute-start.6 = (bf16[192,16,128]{2,0,1:T(8,128)(2,1)S(1)}, bf16[192,16,128]{2,0,1:T(8,128)(2,1)}, u32[]{:S(2)}, u32[]{:S(2)}) collective-permute-start(bf16[192,16,128]{2,0,1:T(8,128)(2,1)S(1)} %copy.15), channel_id=1, source_target_pairs={{0,2},{1,3},{2,4},{3,5},{4,6},{5,7},{8,10},{9,11},{10,12},{11,13},... | collective-permute-start | bytes 2359304 | tf_op jit(solution)/shard_map/ppermute | solution.py:250
  149.3 24.8 %collective-permute-start.9 = (s32[192]{0:T(256)S(1)}, s32[192]{0:T(256)S(1)}, u32[]{:S(2)}, u32[]{:S(2)}) collective-permute-start(s32[192]{0:T(256)S(1)} %bitcast.39), channel_id=1, source_target_pairs={{0,1},{1,2},{2,3},{3,4},{4,5},{5,6},{6,7},{8,9},{9,10},{10,11},{11... | collective-permute-start | bytes 2312 | tf_op jit(solution)/shard_map/ppermute | solution.py:250
  152.2 21.9 %collective-permute-start.8 = (s32[192]{0:T(256)S(1)}, s32[192]{0:T(256)S(1)}, u32[]{:S(2)}, u32[]{:S(2)}) collective-permute-start(s32[192]{0:T(256)S(1)} %bitcast.40), channel_id=1, source_target_pairs={{0,2},{1,3},{2,4},{3,5},{4,6},{5,7},{8,10},{9,11},{10,12},{11,13},... | collective-permute-start | bytes 2312 | tf_op jit(solution)/shard_map/ppermute | solution.py:250

commit v2 on v1

v2 whole, which is shorter than its diff:
```python
import functools
import math

import jax
import jax.numpy as jnp
from jax import lax
from jax.experimental import pallas as pl
from jax.experimental.pallas import tpu as pltpu
from jax.sharding import Mesh, PartitionSpec as P

ROWS = 192
NZ, NY, NS = 16, 4, 8
PER = 3
TILE = 16
HD = 128
SLOT = NY * PER + 1
EXT = 9
BF = jnp.bfloat16
VMEM_LIMIT = 48 * 1024 * 1024

VM = pl.BlockSpec(memory_space=pltpu.VMEM)
SM = pl.BlockSpec(memory_space=pltpu.SMEM)
ANY = pl.BlockSpec(memory_space=pl.ANY)


def params(**kw):
    return pltpu.CompilerParams(vmem_limit_bytes=VMEM_LIMIT, **kw)


def pack_kv_kernel(me_ref, rg_ref, kv_ref, q_ref, out_ref, slot_ref, meta_ref, cnt, tile, xrow, kvs, qs, sem):
    load = pltpu.make_async_copy(kv_ref, kvs, sem.at[3])
    load.start()
    y = me_ref[0]
    for i in range(NZ * NY):
        cnt[i] = 0
    for e in range(4):
        xrow[e] = 0
    for e in range(8):
        meta_ref[e] = 0
    out_ref[...] = jnp.zeros_like(out_ref)

    def step(i, carry):
        d = rg_ref[i]
        r = cnt[d]
        cnt[d] = r + 1
        over = r >= PER
        dy, gz = ((d & (NY - 1)) - y) & (NY - 1), d >> 2
        tile[i] = jnp.where(over, (r - PER) * 3 * SLOT + SLOT - 1, gz * SLOT + dy * PER + r)
        slot_ref[i] = jnp.where(over, ROWS + r - PER, (dy * NZ + gz) * PER + r)

        @pl.when(over)
        def _():
            xrow[r - PER] = i
            meta_ref[0] = d

        return carry

    lax.fori_loop(0, ROWS, step, 0, unroll=8)
    copies = []
    for e in range(3):
        first = pl.multiple_of((xrow[e] >> 4) << 4, 16)
        cp = pltpu.make_async_copy(q_ref.at[pl.ds(first, 16)], qs.at[e], sem.at[e])
        cp.start()
        copies.append(cp)
    load.wait()

    def move(i, carry):
        out_ref[tile[i]] = kvs[i]
        return carry

    lax.fori_loop(0, ROWS, move, 0, unroll=8)
    row = lax.broadcasted_iota(jnp.int32, (16, 2 * TILE * HD), 0)
    for e in range(3):
        copies[e].wait()
        block = qs[e].astype(jnp.float32)
        one = jnp.sum(jnp.where(row == (xrow[e] & 15), block, 0.0), axis=0, keepdims=True)
        for t in range(2):
            parts = [one[:, (t * TILE + c) * HD:(t * TILE + c + 1) * HD] for c in range(TILE)]
            out_ref[(e * 3 + 1 + t) * SLOT + SLOT - 1] = jnp.concatenate(parts, axis=0).astype(BF)


def pack_kv(me, rg, kv, q):
    return pl.pallas_call(
        pack_kv_kernel,
        out_shape=(
            jax.ShapeDtypeStruct((NZ * SLOT, TILE, HD), BF),
            jax.ShapeDtypeStruct((ROWS,), jnp.int32),
            jax.ShapeDtypeStruct((8,), jnp.int32),
        ),
        in_specs=[SM, SM, ANY, ANY],
        out_specs=(VM, SM, SM),
        scratch_shapes=[
            pltpu.SMEM((NZ * NY,), jnp.int32),
            pltpu.SMEM((ROWS,), jnp.int32),
            pltpu.SMEM((4,), jnp.int32),
            pltpu.VMEM((ROWS, TILE, HD), BF),
            pltpu.VMEM((3, 16, 2 * TILE * HD), BF),
            pltpu.SemaphoreType.DMA((4,)),
        ],
        compiler_params=params(),
        name="pack_kv",
    )(me, rg, kv, q)


def pack_q_kernel(slot_ref, q_ref, a_ref, b_ref):
    a_ref[...] = jnp.zeros_like(a_ref)
    b_ref[...] = jnp.zeros_like(b_ref)

    def step(i, carry):
        s = slot_ref[i]

        @pl.when(s < ROWS)
        def _():
            a_ref[s] = q_ref[i, 0:TILE]
            b_ref[s] = q_ref[i, TILE:2 * TILE]

        return carry

    lax.fori_loop(0, ROWS, step, 0, unroll=8)


def pack_q(slot, q3):
    shape = jax.ShapeDtypeStruct((ROWS, TILE, HD), BF)
    return pl.pallas_call(
        pack_q_kernel,
        out_shape=(shape, shape),
        in_specs=[SM, VM],
        out_specs=(VM, VM),
        compiler_params=params(),
        name="pack_q",
    )(slot, q3)


def assemble_q_hop_kernel(sc_ref, b0, b1, b2, b3, hop_ref, out_ref):
    dz = sc_ref[0]
    for z in range(NZ):
        for k, b in enumerate((b0, b1, b2, b3)):
            out_ref[z, k * PER:(k + 1) * PER] = b[z * PER:(z + 1) * PER]
        out_ref[z, NY * PER] = hop_ref[(z - dz) & (NZ - 1), 0]


def assemble_q_hop(sc, blocks, zr1):
    whole = lambda n: pl.BlockSpec((n, TILE, HD), lambda i: (0, 0, 0))
    return pl.pallas_call(
        assemble_q_hop_kernel,
        grid=(1,),
        out_shape=jax.ShapeDtypeStruct((NZ, NY * PER + 1, TILE, HD), BF),
        in_specs=[SM] + [whole(NZ * PER)] * NY
        + [pl.BlockSpec((NZ, 1, TILE, HD), lambda i: (0, NY * PER, 0, 0))],
        out_specs=pl.BlockSpec((NZ, NY * PER + 1, TILE, HD), lambda i: (0, 0, 0, 0)),
        compiler_params=params(),
        name="assemble_q_hop",
    )(sc, *blocks, zr1)


def unpack_kv_kernel(idx_ref, b0, b1, b2, b3, out_ref, held):
    for k, b in enumerate((b0, b1, b2, b3)):
        held[k * NZ * PER:(k + 1) * NZ * PER] = b[...]

    def step(p, carry):
        out_ref[p] = held[idx_ref[p]]
        return carry

    lax.fori_loop(0, ROWS, step, 0, unroll=8)


def unpack_kv(idx, blocks):
    return pl.pallas_call(
        unpack_kv_kernel,
        out_shape=jax.ShapeDtypeStruct((ROWS, TILE, HD), BF),
        in_specs=[SM] + [VM] * NY,
        out_specs=VM,
        scratch_shapes=[pltpu.VMEM((ROWS, TILE, HD), BF)],
        compiler_params=params(),
        name="unpack_kv",
    )(idx, *blocks)


def window_kernel(pos_ref, h2, h1, h0, e2, e1, e0, out_ref):
    for k, (h, e) in enumerate(((h2, e2), (h1, e1), (h0, e0))):
        out_ref[k * ROWS:(k + 1) * ROWS] = h[...]
        for i in range(3):
            out_ref[k * ROWS + pos_ref[k * 3 + i]] = e[i]


def window(pos, rows, extra):
    return pl.pallas_call(
        window_kernel,
        out_shape=jax.ShapeDtypeStruct((3 * ROWS, TILE, HD), BF),
        in_specs=[SM] + [VM] * 6,
        out_specs=VM,
        compiler_params=params(),
        name="window",
    )(pos, *rows, *extra)


def unpack_q_kernel(part, limit, idx_ref, src_ref, ext_ref, *rest):
    out_ref = rest[-1]

    def step(p, carry):
        i = idx_ref[p]
        over = i >= limit
        base = src_ref[jnp.where(over, 0, i)]
        ext = ext_ref[jnp.where(over, (i - limit) * 3 + part, 0)]
        out_ref[p] = jnp.where(over, ext, base)
        return carry

    lax.fori_loop(0, ROWS, step, 0, unroll=8)


def unpack_q(part, idx, zr, ext, *after):
    limit = zr.shape[0] * zr.shape[1]
    return pl.pallas_call(
        functools.partial(unpack_q_kernel, part, limit),
        out_shape=jax.ShapeDtypeStruct((ROWS, TILE, HD), BF),
        in_specs=[SM, VM, VM] + [ANY] * len(after),
        out_specs=VM,
        compiler_params=params(),
        name="unpack_q",
    )(idx, zr.reshape(limit, TILE, HD), ext, *after)


def attend_kernel(scale, q_ref, kv_ref, segq_ref, segk_ref, *rest):
    out_ref = rest[-1]
    span = 3 * ROWS
    i = lax.broadcasted_iota(jnp.int32, (ROWS, span), 0)
    j = lax.broadcasted_iota(jnp.int32, (ROWS, span), 1)
    seen = (segq_ref[...] == segk_ref[...]) & (j <= i + 2 * ROWS)
    q = q_ref[...].reshape(4 * ROWS, HD)
    s = lax.dot_general(q, kv_ref[0], (((1,), (1,)), ((), ())), preferred_element_type=jnp.float32)
    s = jnp.where(seen[None], s.reshape(4, ROWS, span), -jnp.inf).reshape(4 * ROWS, span)
    w = jnp.exp2((s - jnp.max(s, axis=1, keepdims=True)) * (scale * math.log2(math.e)))
    total = jnp.sum(w, axis=1, keepdims=True)
    o = jnp.dot(w.astype(BF), kv_ref[1], preferred_element_type=jnp.float32)
    o = (o / total).astype(BF)
    for g in range(4):
        out_ref[:, g * HD:(g + 1) * HD] = o[g * ROWS:(g + 1) * ROWS]


def attend(part, qt, kvt, segq, segk, prior=None):
    heads = TILE // 4
    in_specs = [
        pl.BlockSpec((4, ROWS, HD), lambda h: (h, 0, 0)),
        pl.BlockSpec((2, 3 * ROWS, HD), lambda h: (h + part * heads, 0, 0)),
        pl.BlockSpec((ROWS, 1), lambda h: (0, 0)),
        pl.BlockSpec((1, 3 * ROWS), lambda h: (0, 0)),
    ]
    args = [qt, kvt, segq, segk]
    alias = {}
    if prior is not None:
        in_specs.append(ANY)
        args.append(prior)
        alias = {4: 0}
    return pl.pallas_call(
        functools.partial(attend_kernel, HD ** -0.5),
        grid=(heads,),
        out_shape=jax.ShapeDtypeStruct((ROWS, 2 * TILE * HD), BF),
        in_specs=in_specs,
        out_specs=pl.BlockSpec((ROWS, 4 * HD), lambda h: (0, h + part * heads)),
        input_output_aliases=alias,
        compiler_params=params(),
        cost_estimate=pl.CostEstimate(
            flops=4 * ROWS * 576 * TILE * HD, bytes_accessed=4 << 20, transcendentals=ROWS * 576 * TILE
        ),
        name="attend",
    )(*args)


def on_device(queries, key_value, route_group, arrive_slot, segment_ids):
    z, y, s = lax.axis_index("z"), lax.axis_index("y"), lax.axis_index("seq")
    kv = key_value.reshape(ROWS, TILE, HD)
    up = lambda a, n: lax.ppermute(a, "seq", [(i, i + n) for i in range(NS - n)])
    side = lambda a, n: lax.ppermute(a, "y", [(i, (i + n) % NY) for i in range(NY)])

    src, rank = arrive_slot // 6, arrive_slot % 6
    sy, sz = src & (NY - 1), src >> 2
    over = rank >= PER
    dy = (y - sy) & (NY - 1)
    idx1 = jnp.where(over, 0, (dy * NZ + sz) * PER + rank)
    idx2 = jnp.where(over, NZ * SLOT + rank - PER, sz * SLOT + dy * PER + rank)
    idx3 = jnp.where(over, NZ * NY * PER + rank - PER, (sz * NY + dy) * PER + rank)

    place = jnp.arange(ROWS, dtype=jnp.int32)
    pos = jnp.stack([jnp.sum(jnp.where(rank == PER + e, place, 0)) for e in range(3)])
    note = jnp.concatenate([segment_ids.reshape(ROWS), pos])
    note1, note2 = up(note, 1), up(note, 2)
    seg = note[:ROWS]
    segk = jnp.concatenate(
        [jnp.where(s >= 2, note2[:ROWS], -1), jnp.where(s >= 1, note1[:ROWS], -1), seg]
    )[None]
    segq = seg[:, None]
    poses = jnp.concatenate([note2[ROWS:], note1[ROWS:], pos])

    zs1, slot, meta = pack_kv(y.reshape(1), route_group, kv, queries)
    k6 = (meta[0] - (z * NY + y)) & (NZ * NY - 1)
    dz = (((y + k6) >> 2) & (NZ - 1)).reshape(1)
    zr1 = lax.all_to_all(zs1.reshape(NZ, SLOT, TILE, HD), "z", 0, 0, tiled=True)

    qa, qb = pack_q(slot, queries.reshape(ROWS, 2 * TILE, HD))

    def along_y(a):
        a = a.reshape(NY, NZ * PER, TILE, HD)
        return [a[0]] + [side(a[k], k) for k in range(1, NY)]

    za, zb = along_y(qa), along_y(qb)
    za, zb = lax.optimization_barrier((za, zb))
    zs2 = assemble_q_hop(dz, za, zr1)
    zs3 = jnp.stack([b.reshape(NZ, PER, TILE, HD) for b in zb], axis=1).reshape(NZ, NY * PER, TILE, HD)
    zr2 = lax.all_to_all(zs2, "z", 0, 0, tiled=True)

    part = [zr1[:, k * PER:(k + 1) * PER].reshape(NZ * PER, TILE, HD) for k in range(NY)]
    own = unpack_kv(idx1, [part[0]] + [side(part[k], k) for k in range(1, NY)])
    own1, own2 = up(own, 1), up(own, 2)
    zs3, own1, own2 = lax.optimization_barrier((zs3, own1, own2))
    zr3 = lax.all_to_all(zs3, "z", 0, 0, tiled=True)

    came = zr2[:EXT, SLOT - 1]
    ext = jnp.stack([came] + [side(came, k) for k in range(1, NY)])
    ext = lax.dynamic_index_in_dim(ext, k6 & (NY - 1), 0, False)
    ext0 = ext.reshape(3, 3, TILE, HD)[:, 0]
    kvt = window(poses, (own2, own1, own), (up(ext0, 2), up(ext0, 1), ext0)).transpose(1, 0, 2)
    out = attend(0, unpack_q(1, idx2, zr2, ext).transpose(1, 0, 2), kvt, segq, segk)
    return attend(1, unpack_q(2, idx3, zr3, ext, out[:8, :HD]).transpose(1, 0, 2), kvt, segq, segk, out)


def solution(mesh):
    fine = Mesh(mesh.devices.reshape(NZ, NY, NS), ("z", "y", "seq"))
    rows = ("z", "y", "seq")
    return jax.shard_map(
        on_device,
        mesh=fine,
        in_specs=(
            P(rows, None),
            P(rows, None, None, None),
            P(rows),
            P(rows),
            P(("z", "y"), "seq"),
        ),
        out_specs=P(rows, None),
        check_vma=False,
    )
```

time: 215 us -> 183 us (0.85)
  the two profiles are of different devices: /device:TPU:34 before, /device:TPU:1 now
where the time goes in v2:
time: 183 us; the launch traced here: 182 us
  starting transfers between devices  103 us (56%)
  waiting for transfers between devices  41.2 us (23%)
  Pallas kernels  23.8 us (13%)
  local copies, waits for them, and re-layouts  10.7 us (6%)
  other arithmetic  2.87 us (2%)
    ppermute x12, starting transfers between devices, on_device(): lax.ppermute(a, 'y', [(i, (i + n) % NY) for i in range(NY)])  40.6 us
    ppermute x6, starting transfers between devices, on_device(): lax.ppermute(a, 'seq', [(i, i + n) for i in range(NS - n)])  22.2 us
    ppermute x6, waiting for transfers between devices, on_device(): lax.ppermute(a, 'seq', [(i, i + n) for i in range(NS - n)])  20.5 us
    all_to_all x1, starting transfers between devices, on_device(): zr1 = lax.all_to_all(zs1.reshape(NZ, SLOT, TILE, HD), 'z', 0, 0, tiled=True)  15.8 us
    all_to_all x1, starting transfers between devices, on_device(): zr2 = lax.all_to_all(zs2, 'z', 0, 0, tiled=True)  12.8 us
    ppermute x12, waiting for transfers between devices, on_device(): lax.ppermute(a, 'y', [(i, (i + n) % NY) for i in range(NY)])  11.7 us
    pallas_call x2, Pallas kernels, attend(): pl.pallas_call(functools.partial(attend_kernel, HD ** (-0.5)), grid=(head...  11.5 us
    all_to_all x1, starting transfers between devices, on_device(): zr3 = lax.all_to_all(zs3, 'z', 0, 0, tiled=True)  11.5 us
  transfers between devices with their start and end apart: 21, of which 8 were waited for; matrix products, arithmetic and copies ran while one was open for 5% of the time, Pallas kernels for 6%

profile of v2, /device:TPU:1, one launch (start us, length us, event | category | flops | bytes accessed | tf_op | source)
XLA Modules:
  0.0 181.9 jit_solution(18168560707385584318)
XLA Ops:
  3.2 4.6 %pack_kv.1 = (bf16[208,16,128]{2,1,0:T(8,128)(2,1)}, s32[192]{0:T(256)S(1)}, s32[8]{0:T(128)S(1)}) custom-call(s32[1]{0:T(128)} %bitcast.me_ref, s32[192]{0:T(256)S(1)} %copy-done.7, bf16[192,16,128]{2,1,0:T(8,128)(2,1)S(1)} %bitcast.54, bf16[192,4096]{1,0:T(8,128)(2,1)S(1)} %copy-done), custom_call_target="tpu_custom_call" | custom-call | tf_op jit(solution)/shard_map/pack_kv/pallas_call | solution.py:83
  7.8 15.8 %all-to-all-start = ((bf16[16,13,16,128]{3,2,1,0:T(8,128)(2,1)}), bf16[16,13,16,128]{3,2,1,0:T(8,128)(2,1)S(1)}, u32[]{:S(2)}, u32[]{:S(2)}) async-start(bf16[16,13,16,128]{3,2,1,0:T(8,128)(2,1)} %bitcast.7), calls=%async_computation | async-start | bytes 1703936 | tf_op jit(solution)/shard_map/all_to_all | solution.py:297
  26.3 3.2 %collective-permute-start = (bf16[48,16,128]{2,1,0:T(8,128)(2,1)S(1)}, bf16[48,16,128]{2,1,0:T(8,128)(2,1)S(1)}, u32[]{:S(2)}, u32[]{:S(2)}) collective-permute-start(bf16[48,16,128]{2,1,0:T(8,128)(2,1)S(1)} %get-tuple-element.55), channel_id=1, source_target_pairs={{0,8},{8,16},{16,24},{24,0},{1,9},{9,17},{17,25},{25,1},{2,10},{10... | collective-permute-start | bytes 589832 | tf_op jit(solution)/shard_map/ppermute | solution.py:273
  29.6 4.5 %collective-permute-start.1 = (bf16[48,16,128]{2,1,0:T(8,128)(2,1)S(1)}, bf16[48,16,128]{2,1,0:T(8,128)(2,1)S(1)}, u32[]{:S(2)}, u32[]{:S(2)}) collective-permute-start(bf16[48,16,128]{2,1,0:T(8,128)(2,1)S(1)} %get-tuple-element.54), channel_id=1, source_target_pairs={{0,16},{8,24},{16,0},{24,8},{1,17},{9,25},{17,1},{25,9},{2,18},{10... | collective-permute-start | bytes 589832 | tf_op jit(solution)/shard_map/ppermute | solution.py:273
  42.3 3.5 %collective-permute-start.5 = (bf16[48,16,128]{2,1,0:T(8,128)(2,1)S(1)}, bf16[48,16,128]{2,1,0:T(8,128)(2,1)S(1)}, u32[]{:S(2)}, u32[]{:S(2)}) collective-permute-start(bf16[48,16,128]{2,1,0:T(8,128)(2,1)S(1)} %get-tuple-element.49), channel_id=1, source_target_pairs={{0,24},{8,0},{16,8},{24,16},{1,25},{9,1},{17,9},{25,17},{2,26},{10... | collective-permute-start | bytes 589832 | tf_op jit(solution)/shard_map/ppermute | solution.py:273
  48.2 3.2 %collective-permute-done.5 = bf16[48,16,128]{2,1,0:T(8,128)(2,1)S(1)} collective-permute-done((bf16[48,16,128]{2,1,0:T(8,128)(2,1)S(1)}, bf16[48,16,128]{2,1,0:T(8,128)(2,1)S(1)}, u32[]{:S(2)}, u32[]{:S(2)}) %collective-permute-start.5) | collective-permute-done | bytes 196640 | tf_op jit(solution)/shard_map/ppermute | solution.py:273
  51.4 9.0 %all-to-all-done.hop_ref = bf16[16,13,16,128]{3,2,1,0:T(8,128)(2,1)S(1)} async-done(((bf16[16,13,16,128]{3,2,1,0:T(8,128)(2,1)}), bf16[16,13,16,128]{3,2,1,0:T(8,128)(2,1)S(1)}, u32[]{:S(2)}, u32[]{:S(2)}) %all-to-all-start) | async-done | bytes 852000 | tf_op jit(solution)/shard_map/all_to_all | solution.py:297
  61.3 12.8 %all-to-all-start.2 = ((bf16[16,13,16,128]{3,2,1,0:T(8,128)(2,1)}), bf16[16,13,16,128]{3,2,1,0:T(8,128)(2,1)S(1)}, u32[]{:S(2)}, u32[]{:S(2)}) async-start(bf16[16,13,16,128]{3,2,1,0:T(8,128)(2,1)} %assemble_q_hop.1), calls=%async_computation.2 | async-start | bytes 1703936 | tf_op jit(solution)/shard_map/all_to_all | solution.py:309
  75.0 3.2 %collective-permute-start.6 = (bf16[48,16,128]{2,1,0:T(8,128)(2,1)S(1)}, bf16[48,16,128]{2,1,0:T(8,128)(2,1)S(1)}, u32[]{:S(2)}, u32[]{:S(2)}) collective-permute-start(bf16[48,16,128]{2,1,0:T(8,128)(2,1)S(1)} %bitcast.67), channel_id=1, source_target_pairs={{0,8},{8,16},{16,24},{24,0},{1,9},{9,17},{17,25},{25,1},{2,10},{10... | collective-permute-start | bytes 589832 | tf_op jit(solution)/shard_map/ppermute | solution.py:273
  78.2 4.5 %collective-permute-start.7 = (bf16[48,16,128]{2,1,0:T(8,128)(2,1)S(1)}, bf16[48,16,128]{2,1,0:T(8,128)(2,1)S(1)}, u32[]{:S(2)}, u32[]{:S(2)}) collective-permute-start(bf16[48,16,128]{2,1,0:T(8,128)(2,1)S(1)} %bitcast.66), channel_id=1, source_target_pairs={{0,16},{8,24},{16,0},{24,8},{1,17},{9,25},{17,1},{25,9},{2,18},{10... | collective-permute-start | bytes 589832 | tf_op jit(solution)/shard_map/ppermute | solution.py:273
  85.7 3.4 %collective-permute-done.7.b2 = bf16[48,16,128]{2,1,0:T(8,128)(2,1)S(1)} collective-permute-done((bf16[48,16,128]{2,1,0:T(8,128)(2,1)S(1)}, bf16[48,16,128]{2,1,0:T(8,128)(2,1)S(1)}, u32[]{:S(2)}, u32[]{:S(2)}) %collective-permute-start.7) | collective-permute-done | bytes 196640 | tf_op jit(solution)/shard_map/ppermute | solution.py:273
  91.1 5.0 %collective-permute-start.9 = (bf16[192,16,128]{2,1,0:T(8,128)(2,1)S(1)}, bf16[192,16,128]{2,1,0:T(8,128)(2,1)S(1)}, u32[]{:S(2)}, u32[]{:S(2)}) collective-permute-start(bf16[192,16,128]{2,1,0:T(8,128)(2,1)S(1)} %unpack_kv.1.h0), channel_id=1, source_target_pairs={{0,1},{1,2},{2,3},{3,4},{4,5},{5,6},{6,7},{8,9},{9,10},{10,11},{11... | collective-permute-start | bytes 2359304 | tf_op jit(solution)/shard_map/ppermute | solution.py:272
  96.1 3.2 %collective-permute-start.10 = (bf16[192,16,128]{2,1,0:T(8,128)(2,1)S(1)}, bf16[192,16,128]{2,1,0:T(8,128)(2,1)S(1)}, u32[]{:S(2)}, u32[]{:S(2)}) collective-permute-start(bf16[192,16,128]{2,1,0:T(8,128)(2,1)S(1)} %unpack_kv.1.h0), channel_id=1, source_target_pairs={{0,2},{1,3},{2,4},{3,5},{4,6},{5,7},{8,10},{9,11},{10,12},{11,13},... | collective-permute-start | bytes 2359304 | tf_op jit(solution)/shard_map/ppermute | solution.py:272
  100.4 10.4 %collective-permute-done.9.h1 = bf16[192,16,128]{2,1,0:T(8,128)(2,1)S(1)} collective-permute-done((bf16[192,16,128]{2,1,0:T(8,128)(2,1)S(1)}, bf16[192,16,128]{2,1,0:T(8,128)(2,1)S(1)}, u32[]{:S(2)}, u32[]{:S(2)}) %collective-permute-start.9) | collective-permute-done | bytes 786464 | tf_op jit(solution)/shard_map/ppermute | solution.py:272
  111.8 10.1 %collective-permute-done.10.h2 = bf16[192,16,128]{2,1,0:T(8,128)(2,1)S(1)} collective-permute-done((bf16[192,16,128]{2,1,0:T(8,128)(2,1)S(1)}, bf16[192,16,128]{2,1,0:T(8,128)(2,1)S(1)}, u32[]{:S(2)}, u32[]{:S(2)}) %collective-permute-start.10) | collective-permute-done | bytes 786464 | tf_op jit(solution)/shard_map/ppermute | solution.py:272
  122.8 11.5 %all-to-all-start.1 = ((bf16[16,12,16,128]{3,2,1,0:T(8,128)(2,1)}), bf16[16,12,16,128]{3,2,1,0:T(8,128)(2,1)S(1)}, u32[]{:S(2)}, u32[]{:S(2)}) async-start(bf16[16,12,16,128]{3,2,1,0:T(8,128)(2,1)} %bitcast.60), calls=%async_computation.1 | async-start | bytes 1572864 | tf_op jit(solution)/shard_map/all_to_all | solution.py:315
  138.1 3.8 %collective-permute-start.14 = (s32[195]{0:T(256)S(1)}, s32[195]{0:T(256)S(1)}, u32[]{:S(2)}, u32[]{:S(2)}) collective-permute-start(s32[195]{0:T(256)S(1)} %pad_add_fusion.1), channel_id=1, source_target_pairs={{0,2},{1,3},{2,4},{3,5},{4,6},{5,7},{8,10},{9,11},{10,12},{11,13},... | collective-permute-start | bytes 2348 | tf_op jit(solution)/shard_map/ppermute | solution.py:272
  142.1 4.1 %collective-permute-start.11 = (bf16[9,16,128]{2,1,0:T(8,128)(2,1)S(1)}, bf16[9,16,128]{2,1,0:T(8,128)(2,1)S(1)}, u32[]{:S(2)}, u32[]{:S(2)}) collective-permute-start(bf16[9,16,128]{2,1,0:T(8,128)(2,1)S(1)} %get-tuple-element.43), channel_id=1, source_target_pairs={{0,8},{8,16},{16,24},{24,0},{1,9},{9,17},{17,25},{25,1},{2,10},{10... | collective-permute-start | bytes 110600 | tf_op jit(solution)/shard_map/ppermute | solution.py:273
  146.2 3.2 %collective-permute-start.12 = (bf16[9,16,128]{2,1,0:T(8,128)(2,1)S(1)}, bf16[9,16,128]{2,1,0:T(8,128)(2,1)S(1)}, u32[]{:S(2)}, u32[]{:S(2)}) collective-permute-start(bf16[9,16,128]{2,1,0:T(8,128)(2,1)S(1)} %get-tuple-element.43), channel_id=1, source_target_pairs={{0,16},{8,24},{16,0},{24,8},{1,17},{9,25},{17,1},{25,9},{2,18},{10... | collective-permute-start | bytes 110600 | tf_op jit(solution)/shard_map/ppermute | solution.py:273
  149.5 3.2 %collective-permute-start.13 = (bf16[9,16,128]{2,1,0:T(8,128)(2,1)S(1)}, bf16[9,16,128]{2,1,0:T(8,128)(2,1)S(1)}, u32[]{:S(2)}, u32[]{:S(2)}) collective-permute-start(bf16[9,16,128]{2,1,0:T(8,128)(2,1)S(1)} %get-tuple-element.43), channel_id=1, source_target_pairs={{0,24},{8,0},{16,8},{24,16},{1,25},{9,1},{17,9},{25,17},{2,26},{10... | collective-permute-start | bytes 110600 | tf_op jit(solution)/shard_map/ppermute | solution.py:273
  154.5 3.1 %collective-permute-start.16 = (bf16[3,16,128]{2,1,0:T(8,128)(2,1)S(1)}, bf16[3,16,128]{2,1,0:T(8,128)(2,1)S(1)}, u32[]{:S(2)}, u32[]{:S(2)}) collective-permute-start(bf16[3,16,128]{2,1,0:T(8,128)(2,1)S(1)} %slice_bitcast_fusion.2.e0), channel_id=1, source_target_pairs={{0,2},{1,3},{2,4},{3,5},{4,6},{5,7},{8,10},{9,11},{10,12},{11,13},... | collective-permute-start | bytes 36872 | tf_op jit(solution)/shard_map/ppermute | solution.py:272
  157.7 5.2 %collective-permute-start.17 = (bf16[3,16,128]{2,1,0:T(8,128)(2,1)S(1)}, bf16[3,16,128]{2,1,0:T(8,128)(2,1)S(1)}, u32[]{:S(2)}, u32[]{:S(2)}) collective-permute-start(bf16[3,16,128]{2,1,0:T(8,128)(2,1)S(1)} %slice_bitcast_fusion.2.e0), channel_id=1, source_target_pairs={{0,1},{1,2},{2,3},{3,4},{4,5},{5,6},{6,7},{8,9},{9,10},{10,11},{11... | collective-permute-start | bytes 36872 | tf_op jit(solution)/shard_map/ppermute | solution.py:272
  168.0 5.8 %attend.2.rest_0_ = bf16[192,4096]{1,0:T(8,128)(2,1)} custom-call(bf16[16,192,128]{2,1,0:T(8,128)(2,1)S(1)} %bitcast.51, bf16[16,576,128]{2,1,0:T(8,128)(2,1)S(1)} %bitcast.46, s32[192,1]{1,0:T(8,128)S(1)} %copy.15.segq_ref, s32[1,576]{1,0:T(1,128)S(1)} %broadcast_in_dim.12.segk_ref), custom_call_target="tpu_custom_call" | custom-call | flops 905969664 | bytes 4194304 | tf_op jit(solution)/shard_map/attend/pallas_call | solution.py:254
  176.1 5.8 %attend.3 = bf16[192,4096]{1,0:T(8,128)(2,1)} custom-call(bf16[16,192,128]{2,1,0:T(8,128)(2,1)S(1)} %bitcast.52, bf16[16,576,128]{2,1,0:T(8,128)(2,1)S(1)} %bitcast.47, s32[192,1]{1,0:T(8,128)S(1)} %copy.15.segq_ref, s32[1,576]{1,0:T(1,128)S(1)} %broadcast_in_dim.12.segk_ref, bf16[192,4096]{1,0:T(8,128)(2,1)} %attend.2.rest_0_), custom_call_target="tpu_custom_call", output_to_operand_aliasing={{}: (4, {})} | custom-call | flops 905969664 | bytes 4194304 | tf_op jit(solution)/shard_map/attend/pallas_call | solution.py:254
  (72 shorter events, 39.2 us)
Async XLA Ops:
  3.2 20.3 %copy-start.1 = (bf16[192,4096]{1,0:T(8,128)(2,1)S(1)}, bf16[192,4096]{1,0:T(8,128)(2,1)}, u32[]{:S(2)}) copy-start(bf16[192,4096]{1,0:T(8,128)(2,1)} %q_ref.1) | copy-start | bytes 4718596
  7.8 52.6 %all-to-all-start = ((bf16[16,13,16,128]{3,2,1,0:T(8,128)(2,1)}), bf16[16,13,16,128]{3,2,1,0:T(8,128)(2,1)S(1)}, u32[]{:S(2)}, u32[]{:S(2)}) async-start(bf16[16,13,16,128]{3,2,1,0:T(8,128)(2,1)} %bitcast.7), calls=%async_computation | async-start | bytes 1703936 | tf_op jit(solution)/shard_map/all_to_all | solution.py:297
  26.3 15.9 %collective-permute-start = (bf16[48,16,128]{2,1,0:T(8,128)(2,1)S(1)}, bf16[48,16,128]{2,1,0:T(8,128)(2,1)S(1)}, u32[]{:S(2)}, u32[]{:S(2)}) collective-permute-start(bf16[48,16,128]{2,1,0:T(8,128)(2,1)S(1)} %get-tuple-element.55), channel_id=1, source_target_pairs={{0,8},{8,16},{16,24},{24,0},{1,9},{9,17},{17,25},{25,1},{2,10},{10... | collective-permute-start | bytes 589832 | tf_op jit(solution)/shard_map/ppermute | solution.py:273
  29.6 16.3 %collective-permute-start.1 = (bf16[48,16,128]{2,1,0:T(8,128)(2,1)S(1)}, bf16[48,16,128]{2,1,0:T(8,128)(2,1)S(1)}, u32[]{:S(2)}, u32[]{:S(2)}) collective-permute-start(bf16[48,16,128]{2,1,0:T(8,128)(2,1)S(1)} %get-tuple-element.54), channel_id=1, source_target_pairs={{0,16},{8,24},{16,0},{24,8},{1,17},{9,25},{17,1},{25,9},{2,18},{10... | collective-permute-start | bytes 589832 | tf_op jit(solution)/shard_map/ppermute | solution.py:273
  34.1 11.8 %collective-permute-start.2 = (bf16[48,16,128]{2,1,0:T(8,128)(2,1)S(1)}, bf16[48,16,128]{2,1,0:T(8,128)(2,1)S(1)}, u32[]{:S(2)}, u32[]{:S(2)}) collective-permute-start(bf16[48,16,128]{2,1,0:T(8,128)(2,1)S(1)} %get-tuple-element.53), channel_id=1, source_target_pairs={{0,24},{8,0},{16,8},{24,16},{1,25},{9,1},{17,9},{25,17},{2,26},{10... | collective-permute-start | bytes 589832 | tf_op jit(solution)/shard_map/ppermute | solution.py:273
  37.2 8.6 %collective-permute-start.3 = (bf16[48,16,128]{2,1,0:T(8,128)(2,1)S(1)}, bf16[48,16,128]{2,1,0:T(8,128)(2,1)S(1)}, u32[]{:S(2)}, u32[]{:S(2)}) collective-permute-start(bf16[48,16,128]{2,1,0:T(8,128)(2,1)S(1)} %get-tuple-element.51), channel_id=1, source_target_pairs={{0,8},{8,16},{16,24},{24,0},{1,9},{9,17},{17,25},{25,1},{2,10},{10... | collective-permute-start | bytes 589832 | tf_op jit(solution)/shard_map/ppermute | solution.py:273
  39.5 8.7 %collective-permute-start.4 = (bf16[48,16,128]{2,1,0:T(8,128)(2,1)S(1)}, bf16[48,16,128]{2,1,0:T(8,128)(2,1)S(1)}, u32[]{:S(2)}, u32[]{:S(2)}) collective-permute-start(bf16[48,16,128]{2,1,0:T(8,128)(2,1)S(1)} %get-tuple-element.50), channel_id=1, source_target_pairs={{0,16},{8,24},{16,0},{24,8},{1,17},{9,25},{17,1},{25,9},{2,18},{10... | collective-permute-start | bytes 589832 | tf_op jit(solution)/shard_map/ppermute | solution.py:273
  42.3 9.1 %collective-permute-start.5 = (bf16[48,16,128]{2,1,0:T(8,128)(2,1)S(1)}, bf16[48,16,128]{2,1,0:T(8,128)(2,1)S(1)}, u32[]{:S(2)}, u32[]{:S(2)}) collective-permute-start(bf16[48,16,128]{2,1,0:T(8,128)(2,1)S(1)} %get-tuple-element.49), channel_id=1, source_target_pairs={{0,24},{8,0},{16,8},{24,16},{1,25},{9,1},{17,9},{25,17},{2,26},{10... | collective-permute-start | bytes 589832 | tf_op jit(solution)/shard_map/ppermute | solution.py:273
  60.3 13.8 %copy-start.9 = (s32[192]{0:T(256)S(1)}, s32[192]{0:T(256)}, u32[]{:S(2)}) copy-start(s32[192]{0:T(256)} %param.8) | copy-start | bytes 2308
  61.3 61.5 %all-to-all-start.2 = ((bf16[16,13,16,128]{3,2,1,0:T(8,128)(2,1)}), bf16[16,13,16,128]{3,2,1,0:T(8,128)(2,1)S(1)}, u32[]{:S(2)}, u32[]{:S(2)}) async-start(bf16[16,13,16,128]{3,2,1,0:T(8,128)(2,1)} %assemble_q_hop.1), calls=%async_computation.2 | async-start | bytes 1703936 | tf_op jit(solution)/shard_map/all_to_all | solution.py:309
  75.0 10.8 %collective-permute-start.6 = (bf16[48,16,128]{2,1,0:T(8,128)(2,1)S(1)}, bf16[48,16,128]{2,1,0:T(8,128)(2,1)S(1)}, u32[]{:S(2)}, u32[]{:S(2)}) collective-permute-start(bf16[48,16,128]{2,1,0:T(8,128)(2,1)S(1)} %bitcast.67), channel_id=1, source_target_pairs={{0,8},{8,16},{16,24},{24,0},{1,9},{9,17},{17,25},{25,1},{2,10},{10... | collective-permute-start | bytes 589832 | tf_op jit(solution)/shard_map/ppermute | solution.py:273
  78.2 11.0 %collective-permute-start.7 = (bf16[48,16,128]{2,1,0:T(8,128)(2,1)S(1)}, bf16[48,16,128]{2,1,0:T(8,128)(2,1)S(1)}, u32[]{:S(2)}, u32[]{:S(2)}) collective-permute-start(bf16[48,16,128]{2,1,0:T(8,128)(2,1)S(1)} %bitcast.66), channel_id=1, source_target_pairs={{0,16},{8,24},{16,0},{24,8},{1,17},{9,25},{17,1},{25,9},{2,18},{10... | collective-permute-start | bytes 589832 | tf_op jit(solution)/shard_map/ppermute | solution.py:273
  82.7 7.4 %collective-permute-start.8 = (bf16[48,16,128]{2,1,0:T(8,128)(2,1)S(1)}, bf16[48,16,128]{2,1,0:T(8,128)(2,1)S(1)}, u32[]{:S(2)}, u32[]{:S(2)}) collective-permute-start(bf16[48,16,128]{2,1,0:T(8,128)(2,1)S(1)} %bitcast.65), channel_id=1, source_target_pairs={{0,24},{8,0},{16,8},{24,16},{1,25},{9,1},{17,9},{25,17},{2,26},{10... | collective-permute-start | bytes 589832 | tf_op jit(solution)/shard_map/ppermute | solution.py:273
  91.1 19.8 %collective-permute-start.9 = (bf16[192,16,128]{2,1,0:T(8,128)(2,1)S(1)}, bf16[192,16,128]{2,1,0:T(8,128)(2,1)S(1)}, u32[]{:S(2)}, u32[]{:S(2)}) collective-permute-start(bf16[192,16,128]{2,1,0:T(8,128)(2,1)S(1)} %unpack_kv.1.h0), channel_id=1, source_target_pairs={{0,1},{1,2},{2,3},{3,4},{4,5},{5,6},{6,7},{8,9},{9,10},{10,11},{11... | collective-permute-start | bytes 2359304 | tf_op jit(solution)/shard_map/ppermute | solution.py:272
  96.1 25.8 %collective-permute-start.10 = (bf16[192,16,128]{2,1,0:T(8,128)(2,1)S(1)}, bf16[192,16,128]{2,1,0:T(8,128)(2,1)S(1)}, u32[]{:S(2)}, u32[]{:S(2)}) collective-permute-start(bf16[192,16,128]{2,1,0:T(8,128)(2,1)S(1)} %unpack_kv.1.h0), channel_id=1, source_target_pairs={{0,2},{1,3},{2,4},{3,5},{4,6},{5,7},{8,10},{9,11},{10,12},{11,13},... | collective-permute-start | bytes 2359304 | tf_op jit(solution)/shard_map/ppermute | solution.py:272
  99.4 34.9 %copy-start.8 = (s32[1,192]{1,0:T(1,128)S(1)}, s32[1,192]{1,0:T(1,128)}, u32[]{:S(2)}) copy-start(s32[1,192]{1,0:T(1,128)} %param.9) | copy-start | bytes 2308
  122.8 51.7 %all-to-all-start.1 = ((bf16[16,12,16,128]{3,2,1,0:T(8,128)(2,1)}), bf16[16,12,16,128]{3,2,1,0:T(8,128)(2,1)S(1)}, u32[]{:S(2)}, u32[]{:S(2)}) async-start(bf16[16,12,16,128]{3,2,1,0:T(8,128)(2,1)} %bitcast.60), calls=%async_computation.1 | async-start | bytes 1572864 | tf_op jit(solution)/shard_map/all_to_all | solution.py:315
  136.2 5.9 %collective-permute-start.15 = (s32[195]{0:T(256)S(1)}, s32[195]{0:T(256)S(1)}, u32[]{:S(2)}, u32[]{:S(2)}) collective-permute-start(s32[195]{0:T(256)S(1)} %pad_add_fusion.1), channel_id=1, source_target_pairs={{0,1},{1,2},{2,3},{3,4},{4,5},{5,6},{6,7},{8,9},{9,10},{10,11},{11... | collective-permute-start | bytes 2348 | tf_op jit(solution)/shard_map/ppermute | solution.py:272
  138.1 14.7 %collective-permute-start.14 = (s32[195]{0:T(256)S(1)}, s32[195]{0:T(256)S(1)}, u32[]{:S(2)}, u32[]{:S(2)}) collective-permute-start(s32[195]{0:T(256)S(1)} %pad_add_fusion.1), channel_id=1, source_target_pairs={{0,2},{1,3},{2,4},{3,5},{4,6},{5,7},{8,10},{9,11},{10,12},{11,13},... | collective-permute-start | bytes 2348 | tf_op jit(solution)/shard_map/ppermute | solution.py:272
  142.1 10.7 %collective-permute-start.11 = (bf16[9,16,128]{2,1,0:T(8,128)(2,1)S(1)}, bf16[9,16,128]{2,1,0:T(8,128)(2,1)S(1)}, u32[]{:S(2)}, u32[]{:S(2)}) collective-permute-start(bf16[9,16,128]{2,1,0:T(8,128)(2,1)S(1)} %get-tuple-element.43), channel_id=1, source_target_pairs={{0,8},{8,16},{16,24},{24,0},{1,9},{9,17},{17,25},{25,1},{2,10},{10... | collective-permute-start | bytes 110600 | tf_op jit(solution)/shard_map/ppermute | solution.py:273
  146.2 6.5 %collective-permute-start.12 = (bf16[9,16,128]{2,1,0:T(8,128)(2,1)S(1)}, bf16[9,16,128]{2,1,0:T(8,128)(2,1)S(1)}, u32[]{:S(2)}, u32[]{:S(2)}) collective-permute-start(bf16[9,16,128]{2,1,0:T(8,128)(2,1)S(1)} %get-tuple-element.43), channel_id=1, source_target_pairs={{0,16},{8,24},{16,0},{24,8},{1,17},{9,25},{17,1},{25,9},{2,18},{10... | collective-permute-start | bytes 110600 | tf_op jit(solution)/shard_map/ppermute | solution.py:273
  149.5 5.0 %collective-permute-start.13 = (bf16[9,16,128]{2,1,0:T(8,128)(2,1)S(1)}, bf16[9,16,128]{2,1,0:T(8,128)(2,1)S(1)}, u32[]{:S(2)}, u32[]{:S(2)}) collective-permute-start(bf16[9,16,128]{2,1,0:T(8,128)(2,1)S(1)} %get-tuple-element.43), channel_id=1, source_target_pairs={{0,24},{8,0},{16,8},{24,16},{1,25},{9,1},{17,9},{25,17},{2,26},{10... | collective-permute-start | bytes 110600 | tf_op jit(solution)/shard_map/ppermute | solution.py:273
  154.5 12.1 %collective-permute-start.16 = (bf16[3,16,128]{2,1,0:T(8,128)(2,1)S(1)}, bf16[3,16,128]{2,1,0:T(8,128)(2,1)S(1)}, u32[]{:S(2)}, u32[]{:S(2)}) collective-permute-start(bf16[3,16,128]{2,1,0:T(8,128)(2,1)S(1)} %slice_bitcast_fusion.2.e0), channel_id=1, source_target_pairs={{0,2},{1,3},{2,4},{3,5},{4,6},{5,7},{8,10},{9,11},{10,12},{11,13},... | collective-permute-start | bytes 36872 | tf_op jit(solution)/shard_map/ppermute | solution.py:272
  157.7 9.0 %collective-permute-start.17 = (bf16[3,16,128]{2,1,0:T(8,128)(2,1)S(1)}, bf16[3,16,128]{2,1,0:T(8,128)(2,1)S(1)}, u32[]{:S(2)}, u32[]{:S(2)}) collective-permute-start(bf16[3,16,128]{2,1,0:T(8,128)(2,1)S(1)} %slice_bitcast_fusion.2.e0), channel_id=1, source_target_pairs={{0,1},{1,2},{2,3},{3,4},{4,5},{5,6},{6,7},{8,9},{9,10},{10,11},{11... | collective-permute-start | bytes 36872 | tf_op jit(solution)/shard_map/ppermute | solution.py:272
  (7 other events, 8.4 us)

commit v3 on v2

v3 whole, which is shorter than its diff:
```python
import functools
import math

import jax
import jax.numpy as jnp
from jax import lax
from jax.experimental import pallas as pl
from jax.experimental.pallas import tpu as pltpu
from jax.sharding import Mesh, PartitionSpec as P

ROWS = 192
NZ, NY, NS = 16, 4, 8
PER = 3
TILE = 16
HD = 128
SLOT = NY * PER + 1
EXT = 9
BF = jnp.bfloat16
MIB = 1024 * 1024

VM = pl.BlockSpec(memory_space=pltpu.VMEM)
SM = pl.BlockSpec(memory_space=pltpu.SMEM)
HB = pl.BlockSpec(memory_space=pltpu.HBM)


def params(mib=16):
    return pltpu.CompilerParams(vmem_limit_bytes=mib * MIB)


def pack_kv_kernel(me_ref, rg_hbm, kv_hbm, q_hbm, out_ref, slot_ref, meta_ref, rg, cnt, tile, xrow, kvs, qs, sem, rsem):
    plan = pltpu.make_async_copy(rg_hbm, rg, rsem)
    plan.start()
    load = pltpu.make_async_copy(kv_hbm, kvs, sem.at[3])
    load.start()
    y = me_ref[0]
    for i in range(NZ * NY):
        cnt[i] = 0
    for e in range(4):
        xrow[e] = 0
    out_ref[...] = jnp.zeros_like(out_ref)
    plan.wait()

    def step(i, far):
        d = rg[i]
        r = cnt[d]
        cnt[d] = r + 1
        over = r >= PER
        dy, gz = ((d & (NY - 1)) - y) & (NY - 1), d >> 2
        tile[i] = jnp.where(over, (r - PER) * 3 * SLOT + SLOT - 1, gz * SLOT + dy * PER + r)
        slot_ref[i] = jnp.where(over, ROWS, (dy * NZ + gz) * PER + r)
        xrow[jnp.where(over, r - PER, 3)] = i
        return jnp.where(over, d, far)

    meta_ref[0] = lax.fori_loop(0, ROWS, step, 0, unroll=16)
    copies = []
    for e in range(3):
        first = pl.multiple_of((xrow[e] >> 4) << 4, 16)
        cp = pltpu.make_async_copy(q_hbm.at[pl.ds(first, 16)], qs.at[e], sem.at[e])
        cp.start()
        copies.append(cp)
    load.wait()

    def move(i, carry):
        out_ref[tile[i]] = kvs[i]
        return carry

    lax.fori_loop(0, ROWS, move, 0, unroll=16)
    row = lax.broadcasted_iota(jnp.int32, (16, 2 * TILE * HD), 0)
    for e in range(3):
        copies[e].wait()
        block = qs[e].astype(jnp.float32)
        one = jnp.sum(jnp.where(row == (xrow[e] & 15), block, 0.0), axis=0, keepdims=True)
        for t in range(2):
            parts = [one[:, (t * TILE + c) * HD:(t * TILE + c + 1) * HD] for c in range(TILE)]
            out_ref[(e * 3 + 1 + t) * SLOT + SLOT - 1] = jnp.concatenate(parts, axis=0).astype(BF)


def pack_kv(me, rg, kv, q):
    return pl.pallas_call(
        pack_kv_kernel,
        out_shape=(
            jax.ShapeDtypeStruct((NZ * SLOT, TILE, HD), BF),
            jax.ShapeDtypeStruct((ROWS,), jnp.int32),
            jax.ShapeDtypeStruct((1,), jnp.int32),
        ),
        in_specs=[SM, HB, HB, HB],
        out_specs=(VM, SM, SM),
        scratch_shapes=[
            pltpu.SMEM((ROWS,), jnp.int32),
            pltpu.SMEM((NZ * NY,), jnp.int32),
            pltpu.SMEM((ROWS,), jnp.int32),
            pltpu.SMEM((4,), jnp.int32),
            pltpu.VMEM((ROWS, TILE, HD), BF),
            pltpu.VMEM((3, 16, 2 * TILE * HD), BF),
            pltpu.SemaphoreType.DMA((4,)),
            pltpu.SemaphoreType.DMA,
        ],
        compiler_params=params(),
        name="pack_kv",
    )(me, rg, kv, q)


def pack_q_kernel(slot_ref, q_ref, a_ref, b_ref):
    a_ref[...] = jnp.zeros_like(a_ref)
    b_ref[...] = jnp.zeros_like(b_ref)

    def step(i, carry):
        s = slot_ref[i]

        @pl.when(s < ROWS)
        def _():
            a_ref[s] = q_ref[i, 0:TILE]
            b_ref[s] = q_ref[i, TILE:2 * TILE]

        return carry

    lax.fori_loop(0, ROWS, step, 0, unroll=8)


def pack_q(slot, q3):
    shape = jax.ShapeDtypeStruct((ROWS, TILE, HD), BF)
    return pl.pallas_call(
        pack_q_kernel,
        out_shape=(shape, shape),
        in_specs=[SM, VM],
        out_specs=(VM, VM),
        compiler_params=params(),
        name="pack_q",
    )(slot, q3)


def assemble_q_hop_kernel(sc_ref, b0, b1, b2, b3, hop_ref, out_ref):
    dz = sc_ref[0]
    for z in range(NZ):
        for k, b in enumerate((b0, b1, b2, b3)):
            out_ref[z, k * PER:(k + 1) * PER] = b[z * PER:(z + 1) * PER]
        out_ref[z, NY * PER] = hop_ref[(z - dz) & (NZ - 1), 0]


def assemble_q_hop(sc, blocks, zr1):
    whole = lambda n: pl.BlockSpec((n, TILE, HD), lambda i: (0, 0, 0))
    return pl.pallas_call(
        assemble_q_hop_kernel,
        grid=(1,),
        out_shape=jax.ShapeDtypeStruct((NZ, NY * PER + 1, TILE, HD), BF),
        in_specs=[SM] + [whole(NZ * PER)] * NY
        + [pl.BlockSpec((NZ, 1, TILE, HD), lambda i: (0, NY * PER, 0, 0))],
        out_specs=pl.BlockSpec((NZ, NY * PER + 1, TILE, HD), lambda i: (0, 0, 0, 0)),
        compiler_params=params(),
        name="assemble_q_hop",
    )(sc, *blocks, zr1)


def unpack_kv_kernel(idx_ref, b0, b1, b2, b3, out_ref, held):
    for k, b in enumerate((b0, b1, b2, b3)):
        held[k * NZ * PER:(k + 1) * NZ * PER] = b[...]

    def step(p, carry):
        out_ref[p] = held[idx_ref[p]]
        return carry

    lax.fori_loop(0, ROWS, step, 0, unroll=8)


def unpack_kv(idx, blocks):
    return pl.pallas_call(
        unpack_kv_kernel,
        out_shape=jax.ShapeDtypeStruct((ROWS, TILE, HD), BF),
        in_specs=[SM] + [VM] * NY,
        out_specs=VM,
        scratch_shapes=[pltpu.VMEM((ROWS, TILE, HD), BF)],
        compiler_params=params(),
        name="unpack_kv",
    )(idx, *blocks)


def window_kernel(pos_ref, h2, h1, h0, e2, e1, e0, out_ref):
    for k, (h, e) in enumerate(((h2, e2), (h1, e1), (h0, e0))):
        out_ref[k * ROWS:(k + 1) * ROWS] = h[...]
        for i in range(3):
            out_ref[k * ROWS + pos_ref[k * 3 + i]] = e[i]


def window(pos, rows, extra):
    return pl.pallas_call(
        window_kernel,
        out_shape=jax.ShapeDtypeStruct((3 * ROWS, TILE, HD), BF),
        in_specs=[SM] + [VM] * 6,
        out_specs=VM,
        compiler_params=params(),
        name="window",
    )(pos, *rows, *extra)


def unpack_q_kernel(part, idx_ref, pos_ref, src_ref, ext_ref, *rest):
    out_ref = rest[-1]

    def step(p, carry):
        out_ref[p] = src_ref[idx_ref[p]]
        return carry

    lax.fori_loop(0, ROWS, step, 0, unroll=16)
    for e in range(3):
        out_ref[pos_ref[e]] = ext_ref[e * 3 + part]


def unpack_q(part, idx, pos, zr, ext, *after):
    return pl.pallas_call(
        functools.partial(unpack_q_kernel, part),
        out_shape=jax.ShapeDtypeStruct((ROWS, TILE, HD), BF),
        in_specs=[SM, SM, VM, VM] + [VM] * len(after),
        out_specs=VM,
        compiler_params=params(),
        name="unpack_q",
    )(idx, pos, zr.reshape(-1, TILE, HD), ext, *after)


def attend_kernel(part, scale, q_ref, kv_ref, segq_ref, segk_ref, *rest):
    out_hbm, held, sem = rest[-3:]
    heads = TILE // 4
    blocks = []
    for lo, rows in ((0, 128), (128, 64)):
        span = min(rows + 2 * ROWS, 3 * ROWS - lo)
        i = lax.broadcasted_iota(jnp.int32, (rows, span), 0)
        j = lax.broadcasted_iota(jnp.int32, (rows, span), 1)
        seen = (segq_ref[lo:lo + rows, :] == segk_ref[:, lo:lo + span]) & (j <= i + 2 * ROWS)
        blocks.append((lo, rows, span, seen))
    copies = []
    for h in range(heads):
        k = 2 * (part * heads + h)
        for lo, rows, span, seen in blocks:
            q = q_ref[4 * h:4 * h + 4, lo:lo + rows].reshape(4 * rows, HD)
            s = lax.dot_general(
                q, kv_ref[k, lo:lo + span], (((1,), (1,)), ((), ())), preferred_element_type=jnp.float32
            )
            s = jnp.where(seen[None], s.reshape(4, rows, span), -jnp.inf).reshape(4 * rows, span)
            w = jnp.exp2((s - jnp.max(s, axis=1, keepdims=True)) * (scale * math.log2(math.e)))
            total = jnp.sum(w, axis=1, keepdims=True)
            o = jnp.dot(w.astype(BF), kv_ref[k + 1, lo:lo + span], preferred_element_type=jnp.float32)
            o = (o / total).astype(BF)
            for g in range(4):
                held[h, lo:lo + rows, g * HD:(g + 1) * HD] = o[g * rows:(g + 1) * rows]
        first = (part * heads + h) * 4 * HD
        cp = pltpu.make_async_copy(held.at[h], out_hbm.at[:, first:first + 4 * HD], sem.at[h])
        cp.start()
        copies.append(cp)
    for cp in copies:
        cp.wait()


def attend(part, qt, kvt, segq, segk, *prior):
    heads = TILE // 4
    return pl.pallas_call(
        functools.partial(attend_kernel, part, HD ** -0.5),
        out_shape=jax.ShapeDtypeStruct((ROWS, 2 * TILE * HD), BF),
        in_specs=[VM] * 4 + [HB] * len(prior),
        out_specs=HB,
        scratch_shapes=[pltpu.VMEM((heads, ROWS, 4 * HD), BF), pltpu.SemaphoreType.DMA((heads,))],
        input_output_aliases={4: 0} if prior else {},
        compiler_params=params(32),
        cost_estimate=pl.CostEstimate(
            flops=4 * ROWS * 576 * TILE * HD, bytes_accessed=4 << 20, transcendentals=ROWS * 576 * TILE
        ),
        name="attend",
    )(qt, kvt, segq, segk, *prior)


def on_device(queries, key_value, route_group, arrive_slot, segment_ids):
    z, y, s = lax.axis_index("z"), lax.axis_index("y"), lax.axis_index("seq")
    kv = key_value.reshape(ROWS, TILE, HD)
    up = lambda a, n: lax.ppermute(a, "seq", [(i, i + n) for i in range(NS - n)])
    side = lambda a, n: lax.ppermute(a, "y", [(i, (i + n) % NY) for i in range(NY)])

    src, rank = arrive_slot // 6, arrive_slot % 6
    sy, sz = src & (NY - 1), src >> 2
    over = rank >= PER
    dy = (y - sy) & (NY - 1)
    idx1 = jnp.where(over, 0, (dy * NZ + sz) * PER + rank)
    idx2 = jnp.where(over, 0, sz * SLOT + dy * PER + rank)
    idx3 = jnp.where(over, 0, (sz * NY + dy) * PER + rank)

    place = jnp.arange(ROWS, dtype=jnp.int32)
    pos = jnp.stack([jnp.sum(jnp.where(rank == PER + e, place, 0)) for e in range(3)])
    note = jnp.concatenate([segment_ids.reshape(ROWS), pos])
    note1, note2 = up(note, 1), up(note, 2)

    zs1, slot, meta = pack_kv(y.reshape(1), route_group, kv, queries)
    k6 = (meta[0] - (z * NY + y)) & (NZ * NY - 1)
    dz = (((y + k6) >> 2) & (NZ - 1)).reshape(1)
    zr1 = lax.all_to_all(zs1.reshape(NZ, SLOT, TILE, HD), "z", 0, 0, tiled=True)

    qa, qb = pack_q(slot, queries.reshape(ROWS, 2 * TILE, HD))

    def along_y(a):
        a = a.reshape(NY, NZ * PER, TILE, HD)
        return [a[0]] + [side(a[k], k) for k in range(1, NY)]

    za, zb = along_y(qa), along_y(qb)
    za, zb, note1, note2 = lax.optimization_barrier((za, zb, note1, note2))
    seg = note[:ROWS]
    segk = jnp.concatenate(
        [jnp.where(s >= 2, note2[:ROWS], -1), jnp.where(s >= 1, note1[:ROWS], -1), seg]
    )[None]
    segq = seg[:, None]
    poses = jnp.concatenate([note2[ROWS:], note1[ROWS:], pos])

    zs2 = assemble_q_hop(dz, za, zr1)
    zs3 = jnp.stack([b.reshape(NZ, PER, TILE, HD) for b in zb], axis=1).reshape(NZ, NY * PER, TILE, HD)
    zr2 = lax.all_to_all(zs2, "z", 0, 0, tiled=True)

    part = [zr1[:, k * PER:(k + 1) * PER].reshape(NZ * PER, TILE, HD) for k in range(NY)]
    own = unpack_kv(idx1, [part[0]] + [side(part[k], k) for k in range(1, NY)])
    own2 = up(own, 2)
    zs3, own2 = lax.optimization_barrier((zs3, own2))
    own1 = lax.ppermute(jnp.where(s % 2 == 0, own, own2), "seq", [(i, i ^ 1) for i in range(NS)])
    zr3 = lax.all_to_all(zs3, "z", 0, 0, tiled=True)

    came = zr2[:EXT, SLOT - 1]
    ext = jnp.stack([came] + [side(came, k) for k in range(1, NY)])
    ext = lax.dynamic_index_in_dim(ext, k6 & (NY - 1), 0, False)
    ext0 = ext.reshape(3, 3, TILE, HD)[:, 0]
    kvt = window(poses, (own2, own1, own), (up(ext0, 2), up(ext0, 1), ext0)).transpose(1, 0, 2)
    out = attend(0, unpack_q(1, idx2, pos, zr2, ext).transpose(1, 0, 2), kvt, segq, segk)
    return attend(1, unpack_q(2, idx3, pos, zr3, ext, out[:8, :HD]).transpose(1, 0, 2), kvt, segq, segk, out)


def solution(mesh):
    fine = Mesh(mesh.devices.reshape(NZ, NY, NS), ("z", "y", "seq"))
    rows = ("z", "y", "seq")
    return jax.shard_map(
        on_device,
        mesh=fine,
        in_specs=(
            P(rows, None),
            P(rows, None, None, None),
            P(rows),
            P(rows),
            P(("z", "y"), "seq"),
        ),
        out_specs=P(rows, None),
        check_vma=False,
    )
```

time: 183 us -> 170 us (0.929)
  the two profiles are of different devices: /device:TPU:1 before, /device:TPU:56 now
where the time goes in v3:
time: 170 us; the launch traced here: 169 us
  starting transfers between devices  82.5 us (49%)
  waiting for transfers between devices  51.8 us (30%)
  Pallas kernels  18.8 us (11%)
  local copies, waits for them, and re-layouts  8.86 us (5%)
  other arithmetic  5.75 us (3%)
    ppermute x12, starting transfers between devices, on_device(): lax.ppermute(a, 'y', [(i, (i + n) % NY) for i in range(NY)])  34.6 us
    ppermute x12, waiting for transfers between devices, on_device(): lax.ppermute(a, 'y', [(i, (i + n) % NY) for i in range(NY)])  21.1 us
    all_to_all x1, starting transfers between devices, on_device(): zr1 = lax.all_to_all(zs1.reshape(NZ, SLOT, TILE, HD), 'z', 0, 0, tiled=True)  15.2 us
    ppermute x5, waiting for transfers between devices, on_device(): lax.ppermute(a, 'seq', [(i, i + n) for i in range(NS - n)])  14.5 us
    ppermute x5, starting transfers between devices, on_device(): lax.ppermute(a, 'seq', [(i, i + n) for i in range(NS - n)])  13.8 us
    all_to_all x1, starting transfers between devices, on_device(): zr2 = lax.all_to_all(zs2, 'z', 0, 0, tiled=True)  9.25 us
    all_to_all x1, waiting for transfers between devices, on_device(): zr3 = lax.all_to_all(zs3, 'z', 0, 0, tiled=True)  7.49 us
    pallas_call x2, Pallas kernels, attend(): pl.pallas_call(functools.partial(attend_kernel, part, HD ** (-0.5)), out_...  7.29 us
  transfers between devices with their start and end apart: 21, of which 12 were waited for; matrix products, arithmetic and copies ran while one was open for 7% of the time, Pallas kernels for 5%

profile of v3, /device:TPU:56, one launch (start us, length us, event | category | flops | bytes accessed | tf_op | source)
XLA Modules:
  0.0 168.8 jit_solution(14685962258181301639)
XLA Ops:
  3.2 4.2 %pack_kv.1 = (bf16[208,16,128]{2,1,0:T(8,128)(2,1)}, s32[192]{0:T(256)S(1)}, s32[1]{0:T(128)}) custom-call(s32[1]{0:T(128)} %bitcast.3.me_ref, s32[192]{0:T(256)S(1)} %copy-done.3, bf16[192,16,128]{2,1,0:T(8,128)(2,1)S(1)} %bitcast.53, bf16[192,4096]{1,0:T(8,128)(2,1)S(1)} %copy-done), custom_call_target="tpu_custom_call" | custom-call | tf_op jit(solution)/shard_map/pack_kv/pallas_call | solution.py:79
  7.4 15.2 %all-to-all-start = ((bf16[16,13,16,128]{3,2,1,0:T(8,128)(2,1)}), bf16[16,13,16,128]{3,2,1,0:T(8,128)(2,1)S(1)}, u32[]{:S(2)}, u32[]{:S(2)}) async-start(bf16[16,13,16,128]{3,2,1,0:T(8,128)(2,1)} %bitcast.11), calls=%async_computation | async-start | bytes 1703936 | tf_op jit(solution)/shard_map/all_to_all | solution.py:290
  26.6 4.0 %collective-permute-start.7 = (s32[195]{0:T(256)S(1)}, s32[195]{0:T(256)S(1)}, u32[]{:S(2)}, u32[]{:S(2)}) collective-permute-start(s32[195]{0:T(256)S(1)} %pad_add_fusion.1), channel_id=1, source_target_pairs={{0,2},{1,3},{2,4},{3,5},{4,6},{5,7},{8,10},{9,11},{10,12},{11,13},... | collective-permute-start | bytes 2348 | tf_op jit(solution)/shard_map/ppermute | solution.py:271
  35.5 4.5 %collective-permute-start.1 = (bf16[48,16,128]{2,1,0:T(8,128)(2,1)S(1)}, bf16[48,16,128]{2,1,0:T(8,128)(2,1)S(1)}, u32[]{:S(2)}, u32[]{:S(2)}) collective-permute-start(bf16[48,16,128]{2,1,0:T(8,128)(2,1)S(1)} %get-tuple-element.56), channel_id=1, source_target_pairs={{0,16},{8,24},{16,0},{24,8},{1,17},{9,25},{17,1},{25,9},{2,18},{10... | collective-permute-start | bytes 589832 | tf_op jit(solution)/shard_map/ppermute | solution.py:272
  42.1 5.1 %collective-permute-start.3 = (bf16[48,16,128]{2,1,0:T(8,128)(2,1)S(1)}, bf16[48,16,128]{2,1,0:T(8,128)(2,1)S(1)}, u32[]{:S(2)}, u32[]{:S(2)}) collective-permute-start(bf16[48,16,128]{2,1,0:T(8,128)(2,1)S(1)} %get-tuple-element.53), channel_id=1, source_target_pairs={{0,8},{8,16},{16,24},{24,0},{1,9},{9,17},{17,25},{25,1},{2,10},{10... | collective-permute-start | bytes 589832 | tf_op jit(solution)/shard_map/ppermute | solution.py:272
  49.3 3.3 %collective-permute-start.5 = (bf16[48,16,128]{2,1,0:T(8,128)(2,1)S(1)}, bf16[48,16,128]{2,1,0:T(8,128)(2,1)S(1)}, u32[]{:S(2)}, u32[]{:S(2)}) collective-permute-start(bf16[48,16,128]{2,1,0:T(8,128)(2,1)S(1)} %get-tuple-element.51), channel_id=1, source_target_pairs={{0,24},{8,0},{16,8},{24,16},{1,25},{9,1},{17,9},{25,17},{2,26},{10... | collective-permute-start | bytes 589832 | tf_op jit(solution)/shard_map/ppermute | solution.py:272
  53.4 2.9 %collective-permute-done.3 = bf16[48,16,128]{2,1,0:T(8,128)(2,1)S(1)} collective-permute-done((bf16[48,16,128]{2,1,0:T(8,128)(2,1)S(1)}, bf16[48,16,128]{2,1,0:T(8,128)(2,1)S(1)}, u32[]{:S(2)}, u32[]{:S(2)}) %collective-permute-start.3) | collective-permute-done | bytes 196640 | tf_op jit(solution)/shard_map/ppermute | solution.py:272
  58.4 3.4 %collective-permute-done.5 = bf16[48,16,128]{2,1,0:T(8,128)(2,1)S(1)} collective-permute-done((bf16[48,16,128]{2,1,0:T(8,128)(2,1)S(1)}, bf16[48,16,128]{2,1,0:T(8,128)(2,1)S(1)}, u32[]{:S(2)}, u32[]{:S(2)}) %collective-permute-start.5) | collective-permute-done | bytes 196640 | tf_op jit(solution)/shard_map/ppermute | solution.py:272
  61.9 2.8 %all-to-all-done.hop_ref = bf16[16,13,16,128]{3,2,1,0:T(8,128)(2,1)S(1)} async-done(((bf16[16,13,16,128]{3,2,1,0:T(8,128)(2,1)}), bf16[16,13,16,128]{3,2,1,0:T(8,128)(2,1)S(1)}, u32[]{:S(2)}, u32[]{:S(2)}) %all-to-all-start) | async-done | bytes 852000 | tf_op jit(solution)/shard_map/all_to_all | solution.py:290
  65.6 9.2 %all-to-all-start.2 = ((bf16[16,13,16,128]{3,2,1,0:T(8,128)(2,1)}), bf16[16,13,16,128]{3,2,1,0:T(8,128)(2,1)S(1)}, u32[]{:S(2)}, u32[]{:S(2)}) async-start(bf16[16,13,16,128]{3,2,1,0:T(8,128)(2,1)} %assemble_q_hop.1), calls=%async_computation.2 | async-start | bytes 1703936 | tf_op jit(solution)/shard_map/all_to_all | solution.py:309
  75.0 2.5 %collective-permute-start.8 = (bf16[48,16,128]{2,1,0:T(8,128)(2,1)S(1)}, bf16[48,16,128]{2,1,0:T(8,128)(2,1)S(1)}, u32[]{:S(2)}, u32[]{:S(2)}) collective-permute-start(bf16[48,16,128]{2,1,0:T(8,128)(2,1)S(1)} %bitcast.65), channel_id=1, source_target_pairs={{0,8},{8,16},{16,24},{24,0},{1,9},{9,17},{17,25},{25,1},{2,10},{10... | collective-permute-start | bytes 589832 | tf_op jit(solution)/shard_map/ppermute | solution.py:272
  79.8 3.0 %collective-permute-start.10 = (bf16[48,16,128]{2,1,0:T(8,128)(2,1)S(1)}, bf16[48,16,128]{2,1,0:T(8,128)(2,1)S(1)}, u32[]{:S(2)}, u32[]{:S(2)}) collective-permute-start(bf16[48,16,128]{2,1,0:T(8,128)(2,1)S(1)} %bitcast.63), channel_id=1, source_target_pairs={{0,24},{8,0},{16,8},{24,16},{1,25},{9,1},{17,9},{25,17},{2,26},{10... | collective-permute-start | bytes 589832 | tf_op jit(solution)/shard_map/ppermute | solution.py:272
  86.7 4.0 %collective-permute-done.10.b3 = bf16[48,16,128]{2,1,0:T(8,128)(2,1)S(1)} collective-permute-done((bf16[48,16,128]{2,1,0:T(8,128)(2,1)S(1)}, bf16[48,16,128]{2,1,0:T(8,128)(2,1)S(1)}, u32[]{:S(2)}, u32[]{:S(2)}) %collective-permute-start.10) | collective-permute-done | bytes 196640 | tf_op jit(solution)/shard_map/ppermute | solution.py:272
  91.7 4.0 %collective-permute-start.11 = (bf16[192,16,128]{2,1,0:T(8,128)(2,1)S(1)}, bf16[192,16,128]{2,1,0:T(8,128)(2,1)}, u32[]{:S(2)}, u32[]{:S(2)}) collective-permute-start(bf16[192,16,128]{2,1,0:T(8,128)(2,1)S(1)} %unpack_kv.1.h0), channel_id=1, source_target_pairs={{0,2},{1,3},{2,4},{3,5},{4,6},{5,7},{8,10},{9,11},{10,12},{11,13},... | collective-permute-start | bytes 2359304 | tf_op jit(solution)/shard_map/ppermute | solution.py:271
  96.9 14.5 %collective-permute-done.11.h2 = bf16[192,16,128]{2,1,0:T(8,128)(2,1)} collective-permute-done((bf16[192,16,128]{2,1,0:T(8,128)(2,1)S(1)}, bf16[192,16,128]{2,1,0:T(8,128)(2,1)}, u32[]{:S(2)}, u32[]{:S(2)}) %collective-permute-start.11) | collective-permute-done | bytes 786464 | tf_op jit(solution)/shard_map/ppermute | solution.py:271
  111.4 5.9 %all-to-all-done.2 = bf16[16,13,16,128]{3,2,1,0:T(8,128)(2,1)S(1)} async-done(((bf16[16,13,16,128]{3,2,1,0:T(8,128)(2,1)}), bf16[16,13,16,128]{3,2,1,0:T(8,128)(2,1)S(1)}, u32[]{:S(2)}, u32[]{:S(2)}) %all-to-all-start.2) | async-done | bytes 852000 | tf_op jit(solution)/shard_map/all_to_all | solution.py:309
  117.3 7.2 %all-to-all-start.1 = ((bf16[16,12,16,128]{3,2,1,0:T(8,128)(2,1)}), bf16[16,12,16,128]{3,2,1,0:T(8,128)(2,1)S(1)}, u32[]{:S(2)}, u32[]{:S(2)}) async-start(bf16[16,12,16,128]{3,2,1,0:T(8,128)(2,1)} %bitcast.58), calls=%async_computation.1 | async-start | bytes 1572864 | tf_op jit(solution)/shard_map/all_to_all | solution.py:316
  132.0 2.8 %collective-permute-start.13 = (bf16[9,16,128]{2,1,0:T(8,128)(2,1)S(1)}, bf16[9,16,128]{2,1,0:T(8,128)(2,1)S(1)}, u32[]{:S(2)}, u32[]{:S(2)}) collective-permute-start(bf16[9,16,128]{2,1,0:T(8,128)(2,1)S(1)} %get-tuple-element.45), channel_id=1, source_target_pairs={{0,16},{8,24},{16,0},{24,8},{1,17},{9,25},{17,1},{25,9},{2,18},{10... | collective-permute-start | bytes 110600 | tf_op jit(solution)/shard_map/ppermute | solution.py:272
  134.8 3.0 %collective-permute-start.14 = (bf16[9,16,128]{2,1,0:T(8,128)(2,1)S(1)}, bf16[9,16,128]{2,1,0:T(8,128)(2,1)S(1)}, u32[]{:S(2)}, u32[]{:S(2)}) collective-permute-start(bf16[9,16,128]{2,1,0:T(8,128)(2,1)S(1)} %get-tuple-element.45), channel_id=1, source_target_pairs={{0,24},{8,0},{16,8},{24,16},{1,25},{9,1},{17,9},{25,17},{2,26},{10... | collective-permute-start | bytes 110600 | tf_op jit(solution)/shard_map/ppermute | solution.py:272
  139.3 3.1 %collective-permute-done.14 = bf16[9,16,128]{2,1,0:T(8,128)(2,1)S(1)} collective-permute-done((bf16[9,16,128]{2,1,0:T(8,128)(2,1)S(1)}, bf16[9,16,128]{2,1,0:T(8,128)(2,1)S(1)}, u32[]{:S(2)}, u32[]{:S(2)}) %collective-permute-start.14) | collective-permute-done | bytes 36896 | tf_op jit(solution)/shard_map/ppermute | solution.py:272
  142.5 3.2 %collective-permute-start.16 = (bf16[3,16,128]{2,1,0:T(8,128)(2,1)S(1)}, bf16[3,16,128]{2,1,0:T(8,128)(2,1)S(1)}, u32[]{:S(2)}, u32[]{:S(2)}) collective-permute-start(bf16[3,16,128]{2,1,0:T(8,128)(2,1)S(1)} %slice_bitcast_fusion.2.e0), channel_id=1, source_target_pairs={{0,2},{1,3},{2,4},{3,5},{4,6},{5,7},{8,10},{9,11},{10,12},{11,13},... | collective-permute-start | bytes 36872 | tf_op jit(solution)/shard_map/ppermute | solution.py:271
  152.3 3.6 %attend.2.rest_0_ = bf16[192,4096]{1,0:T(8,128)(2,1)} custom-call(bf16[16,192,128]{2,1,0:T(8,128)(2,1)S(1)} %bitcast.50, bf16[16,576,128]{2,1,0:T(8,128)(2,1)S(1)} %bitcast.45, s32[192,1]{1,0:T(8,128)S(1)} %copy.15.segq_ref, s32[1,576]{1,0:T(1,128)S(1)} %broadcast_in_dim.14.segk_ref), custom_call_target="tpu_custom_call" | custom-call | flops 905969664 | bytes 4194304 | tf_op jit(solution)/shard_map/attend/pallas_call | solution.py:253
  156.7 7.5 %all-to-all-done.1 = bf16[16,12,16,128]{3,2,1,0:T(8,128)(2,1)S(1)} async-done(((bf16[16,12,16,128]{3,2,1,0:T(8,128)(2,1)}), bf16[16,12,16,128]{3,2,1,0:T(8,128)(2,1)S(1)}, u32[]{:S(2)}, u32[]{:S(2)}) %all-to-all-start.1) | async-done | bytes 786464 | tf_op jit(solution)/shard_map/all_to_all | solution.py:316
  165.2 3.6 %attend.3 = bf16[192,4096]{1,0:T(8,128)(2,1)} custom-call(bf16[16,192,128]{2,1,0:T(8,128)(2,1)S(1)} %bitcast.51, bf16[16,576,128]{2,1,0:T(8,128)(2,1)S(1)} %bitcast.46, s32[192,1]{1,0:T(8,128)S(1)} %copy.15.segq_ref, s32[1,576]{1,0:T(1,128)S(1)} %broadcast_in_dim.14.segk_ref, bf16[192,4096]{1,0:T(8,128)(2,1)} %attend.2.rest_0_), custom_call_target="tpu_custom_call", output_to_operand_aliasing={{}: (4, {})} | custom-call | flops 905969664 | bytes 4194304 | tf_op jit(solution)/shard_map/attend/pallas_call | solution.py:253
  (64 shorter events, 45.0 us)
Async XLA Ops:
  3.2 19.4 %copy-start.5 = (s32[192]{0:T(256)S(1)}, s32[192]{0:T(256)}, u32[]{:S(2)}) copy-start(s32[192]{0:T(256)} %param.8) | copy-start | bytes 2308
  3.2 20.1 %copy-start.4 = (s32[1,192]{1,0:T(1,128)S(1)}, s32[1,192]{1,0:T(1,128)}, u32[]{:S(2)}) copy-start(s32[1,192]{1,0:T(1,128)} %param.9) | copy-start | bytes 2308
  3.2 27.4 %copy-start.1 = (bf16[192,4096]{1,0:T(8,128)(2,1)S(1)}, bf16[192,4096]{1,0:T(8,128)(2,1)}, u32[]{:S(2)}) copy-start(bf16[192,4096]{1,0:T(8,128)(2,1)} %q_hbm.1) | copy-start | bytes 4718596
  7.4 57.3 %all-to-all-start = ((bf16[16,13,16,128]{3,2,1,0:T(8,128)(2,1)}), bf16[16,13,16,128]{3,2,1,0:T(8,128)(2,1)S(1)}, u32[]{:S(2)}, u32[]{:S(2)}) async-start(bf16[16,13,16,128]{3,2,1,0:T(8,128)(2,1)} %bitcast.11), calls=%async_computation | async-start | bytes 1703936 | tf_op jit(solution)/shard_map/all_to_all | solution.py:290
  25.3 16.8 %collective-permute-start.6 = (s32[195]{0:T(256)S(1)}, s32[195]{0:T(256)S(1)}, u32[]{:S(2)}, u32[]{:S(2)}) collective-permute-start(s32[195]{0:T(256)S(1)} %pad_add_fusion.1), channel_id=1, source_target_pairs={{0,1},{1,2},{2,3},{3,4},{4,5},{5,6},{6,7},{8,9},{9,10},{10,11},{11... | collective-permute-start | bytes 2348 | tf_op jit(solution)/shard_map/ppermute | solution.py:271
  26.6 20.7 %collective-permute-start.7 = (s32[195]{0:T(256)S(1)}, s32[195]{0:T(256)S(1)}, u32[]{:S(2)}, u32[]{:S(2)}) collective-permute-start(s32[195]{0:T(256)S(1)} %pad_add_fusion.1), channel_id=1, source_target_pairs={{0,2},{1,3},{2,4},{3,5},{4,6},{5,7},{8,10},{9,11},{10,12},{11,13},... | collective-permute-start | bytes 2348 | tf_op jit(solution)/shard_map/ppermute | solution.py:271
  33.4 15.9 %collective-permute-start = (bf16[48,16,128]{2,1,0:T(8,128)(2,1)S(1)}, bf16[48,16,128]{2,1,0:T(8,128)(2,1)S(1)}, u32[]{:S(2)}, u32[]{:S(2)}) collective-permute-start(bf16[48,16,128]{2,1,0:T(8,128)(2,1)S(1)} %get-tuple-element.57), channel_id=1, source_target_pairs={{0,8},{8,16},{16,24},{24,0},{1,9},{9,17},{17,25},{25,1},{2,10},{10... | collective-permute-start | bytes 589832 | tf_op jit(solution)/shard_map/ppermute | solution.py:272
  35.5 17.8 %collective-permute-start.1 = (bf16[48,16,128]{2,1,0:T(8,128)(2,1)S(1)}, bf16[48,16,128]{2,1,0:T(8,128)(2,1)S(1)}, u32[]{:S(2)}, u32[]{:S(2)}) collective-permute-start(bf16[48,16,128]{2,1,0:T(8,128)(2,1)S(1)} %get-tuple-element.56), channel_id=1, source_target_pairs={{0,16},{8,24},{16,0},{24,8},{1,17},{9,25},{17,1},{25,9},{2,18},{10... | collective-permute-start | bytes 589832 | tf_op jit(solution)/shard_map/ppermute | solution.py:272
  40.0 13.3 %collective-permute-start.2 = (bf16[48,16,128]{2,1,0:T(8,128)(2,1)S(1)}, bf16[48,16,128]{2,1,0:T(8,128)(2,1)S(1)}, u32[]{:S(2)}, u32[]{:S(2)}) collective-permute-start(bf16[48,16,128]{2,1,0:T(8,128)(2,1)S(1)} %get-tuple-element.55), channel_id=1, source_target_pairs={{0,24},{8,0},{16,8},{24,16},{1,25},{9,1},{17,9},{25,17},{2,26},{10... | collective-permute-start | bytes 589832 | tf_op jit(solution)/shard_map/ppermute | solution.py:272
  42.1 14.1 %collective-permute-start.3 = (bf16[48,16,128]{2,1,0:T(8,128)(2,1)S(1)}, bf16[48,16,128]{2,1,0:T(8,128)(2,1)S(1)}, u32[]{:S(2)}, u32[]{:S(2)}) collective-permute-start(bf16[48,16,128]{2,1,0:T(8,128)(2,1)S(1)} %get-tuple-element.53), channel_id=1, source_target_pairs={{0,8},{8,16},{16,24},{24,0},{1,9},{9,17},{17,25},{25,1},{2,10},{10... | collective-permute-start | bytes 589832 | tf_op jit(solution)/shard_map/ppermute | solution.py:272
  47.3 11.2 %collective-permute-start.4 = (bf16[48,16,128]{2,1,0:T(8,128)(2,1)S(1)}, bf16[48,16,128]{2,1,0:T(8,128)(2,1)S(1)}, u32[]{:S(2)}, u32[]{:S(2)}) collective-permute-start(bf16[48,16,128]{2,1,0:T(8,128)(2,1)S(1)} %get-tuple-element.52), channel_id=1, source_target_pairs={{0,16},{8,24},{16,0},{24,8},{1,17},{9,25},{17,1},{25,9},{2,18},{10... | collective-permute-start | bytes 589832 | tf_op jit(solution)/shard_map/ppermute | solution.py:272
  49.3 12.6 %collective-permute-start.5 = (bf16[48,16,128]{2,1,0:T(8,128)(2,1)S(1)}, bf16[48,16,128]{2,1,0:T(8,128)(2,1)S(1)}, u32[]{:S(2)}, u32[]{:S(2)}) collective-permute-start(bf16[48,16,128]{2,1,0:T(8,128)(2,1)S(1)} %get-tuple-element.51), channel_id=1, source_target_pairs={{0,24},{8,0},{16,8},{24,16},{1,25},{9,1},{17,9},{25,17},{2,26},{10... | collective-permute-start | bytes 589832 | tf_op jit(solution)/shard_map/ppermute | solution.py:272
  65.6 51.7 %all-to-all-start.2 = ((bf16[16,13,16,128]{3,2,1,0:T(8,128)(2,1)}), bf16[16,13,16,128]{3,2,1,0:T(8,128)(2,1)S(1)}, u32[]{:S(2)}, u32[]{:S(2)}) async-start(bf16[16,13,16,128]{3,2,1,0:T(8,128)(2,1)} %assemble_q_hop.1), calls=%async_computation.2 | async-start | bytes 1703936 | tf_op jit(solution)/shard_map/all_to_all | solution.py:309
  75.0 9.7 %collective-permute-start.8 = (bf16[48,16,128]{2,1,0:T(8,128)(2,1)S(1)}, bf16[48,16,128]{2,1,0:T(8,128)(2,1)S(1)}, u32[]{:S(2)}, u32[]{:S(2)}) collective-permute-start(bf16[48,16,128]{2,1,0:T(8,128)(2,1)S(1)} %bitcast.65), channel_id=1, source_target_pairs={{0,8},{8,16},{16,24},{24,0},{1,9},{9,17},{17,25},{25,1},{2,10},{10... | collective-permute-start | bytes 589832 | tf_op jit(solution)/shard_map/ppermute | solution.py:272
  77.5 9.3 %collective-permute-start.9 = (bf16[48,16,128]{2,1,0:T(8,128)(2,1)S(1)}, bf16[48,16,128]{2,1,0:T(8,128)(2,1)S(1)}, u32[]{:S(2)}, u32[]{:S(2)}) collective-permute-start(bf16[48,16,128]{2,1,0:T(8,128)(2,1)S(1)} %bitcast.64), channel_id=1, source_target_pairs={{0,16},{8,24},{16,0},{24,8},{1,17},{9,25},{17,1},{25,9},{2,18},{10... | collective-permute-start | bytes 589832 | tf_op jit(solution)/shard_map/ppermute | solution.py:272
  79.8 11.0 %collective-permute-start.10 = (bf16[48,16,128]{2,1,0:T(8,128)(2,1)S(1)}, bf16[48,16,128]{2,1,0:T(8,128)(2,1)S(1)}, u32[]{:S(2)}, u32[]{:S(2)}) collective-permute-start(bf16[48,16,128]{2,1,0:T(8,128)(2,1)S(1)} %bitcast.63), channel_id=1, source_target_pairs={{0,24},{8,0},{16,8},{24,16},{1,25},{9,1},{17,9},{25,17},{2,26},{10... | collective-permute-start | bytes 589832 | tf_op jit(solution)/shard_map/ppermute | solution.py:272
  91.7 19.7 %collective-permute-start.11 = (bf16[192,16,128]{2,1,0:T(8,128)(2,1)S(1)}, bf16[192,16,128]{2,1,0:T(8,128)(2,1)}, u32[]{:S(2)}, u32[]{:S(2)}) collective-permute-start(bf16[192,16,128]{2,1,0:T(8,128)(2,1)S(1)} %unpack_kv.1.h0), channel_id=1, source_target_pairs={{0,2},{1,3},{2,4},{3,5},{4,6},{5,7},{8,10},{9,11},{10,12},{11,13},... | collective-permute-start | bytes 2359304 | tf_op jit(solution)/shard_map/ppermute | solution.py:271
  117.3 46.9 %all-to-all-start.1 = ((bf16[16,12,16,128]{3,2,1,0:T(8,128)(2,1)}), bf16[16,12,16,128]{3,2,1,0:T(8,128)(2,1)S(1)}, u32[]{:S(2)}, u32[]{:S(2)}) async-start(bf16[16,12,16,128]{3,2,1,0:T(8,128)(2,1)} %bitcast.58), calls=%async_computation.1 | async-start | bytes 1572864 | tf_op jit(solution)/shard_map/all_to_all | solution.py:316
  127.5 22.6 %collective-permute-start.15 = (bf16[192,16,128]{2,1,0:T(8,128)(2,1)}, bf16[192,16,128]{2,1,0:T(8,128)(2,1)}, u32[]{:S(2)}, u32[]{:S(2)}) collective-permute-start(bf16[192,16,128]{2,1,0:T(8,128)(2,1)} %broadcast_select_fusion), channel_id=1, source_target_pairs={{0,1},{1,0},{2,3},{3,2},{4,5},{5,4},{6,7},{7,6},{8,9},{9,8},{10,11... | collective-permute-start | bytes 2359304 | tf_op jit(solution)/shard_map/ppermute | solution.py:315
  130.0 7.8 %collective-permute-start.12 = (bf16[9,16,128]{2,1,0:T(8,128)(2,1)S(1)}, bf16[9,16,128]{2,1,0:T(8,128)(2,1)S(1)}, u32[]{:S(2)}, u32[]{:S(2)}) collective-permute-start(bf16[9,16,128]{2,1,0:T(8,128)(2,1)S(1)} %get-tuple-element.45), channel_id=1, source_target_pairs={{0,8},{8,16},{16,24},{24,0},{1,9},{9,17},{17,25},{25,1},{2,10},{10... | collective-permute-start | bytes 110600 | tf_op jit(solution)/shard_map/ppermute | solution.py:272
  132.0 7.4 %collective-permute-start.13 = (bf16[9,16,128]{2,1,0:T(8,128)(2,1)S(1)}, bf16[9,16,128]{2,1,0:T(8,128)(2,1)S(1)}, u32[]{:S(2)}, u32[]{:S(2)}) collective-permute-start(bf16[9,16,128]{2,1,0:T(8,128)(2,1)S(1)} %get-tuple-element.45), channel_id=1, source_target_pairs={{0,16},{8,24},{16,0},{24,8},{1,17},{9,25},{17,1},{25,9},{2,18},{10... | collective-permute-start | bytes 110600 | tf_op jit(solution)/shard_map/ppermute | solution.py:272
  134.8 7.6 %collective-permute-start.14 = (bf16[9,16,128]{2,1,0:T(8,128)(2,1)S(1)}, bf16[9,16,128]{2,1,0:T(8,128)(2,1)S(1)}, u32[]{:S(2)}, u32[]{:S(2)}) collective-permute-start(bf16[9,16,128]{2,1,0:T(8,128)(2,1)S(1)} %get-tuple-element.45), channel_id=1, source_target_pairs={{0,24},{8,0},{16,8},{24,16},{1,25},{9,1},{17,9},{25,17},{2,26},{10... | collective-permute-start | bytes 110600 | tf_op jit(solution)/shard_map/ppermute | solution.py:272
  142.5 7.7 %collective-permute-start.16 = (bf16[3,16,128]{2,1,0:T(8,128)(2,1)S(1)}, bf16[3,16,128]{2,1,0:T(8,128)(2,1)S(1)}, u32[]{:S(2)}, u32[]{:S(2)}) collective-permute-start(bf16[3,16,128]{2,1,0:T(8,128)(2,1)S(1)} %slice_bitcast_fusion.2.e0), channel_id=1, source_target_pairs={{0,2},{1,3},{2,4},{3,5},{4,6},{5,7},{8,10},{9,11},{10,12},{11,13},... | collective-permute-start | bytes 36872 | tf_op jit(solution)/shard_map/ppermute | solution.py:271
  145.7 4.5 %collective-permute-start.17 = (bf16[3,16,128]{2,1,0:T(8,128)(2,1)S(1)}, bf16[3,16,128]{2,1,0:T(8,128)(2,1)S(1)}, u32[]{:S(2)}, u32[]{:S(2)}) collective-permute-start(bf16[3,16,128]{2,1,0:T(8,128)(2,1)S(1)} %slice_bitcast_fusion.2.e0), channel_id=1, source_target_pairs={{0,1},{1,2},{2,3},{3,4},{4,5},{5,6},{6,7},{8,9},{9,10},{10,11},{11... | collective-permute-start | bytes 36872 | tf_op jit(solution)/shard_map/ppermute | solution.py:271
  (3 other events, 3.2 us)

commit v4 on v3

--- a/solution.py
+++ b/solution.py
@@ -95,7 +95,7 @@
             pltpu.SemaphoreType.DMA((4,)),
             pltpu.SemaphoreType.DMA,
         ],
-        compiler_params=params(),
+        compiler_params=params(60),
         name="pack_kv",
     )(me, rg, kv, q)
 
@@ -106,19 +106,15 @@
 
     def step(i, carry):
         s = slot_ref[i]
-
-        @pl.when(s < ROWS)
-        def _():
-            a_ref[s] = q_ref[i, 0:TILE]
-            b_ref[s] = q_ref[i, TILE:2 * TILE]
-
+        a_ref[s] = q_ref[i, 0:TILE]
+        b_ref[s] = q_ref[i, TILE:2 * TILE]
         return carry
 
-    lax.fori_loop(0, ROWS, step, 0, unroll=8)
+    lax.fori_loop(0, ROWS, step, 0, unroll=16)
 
 
 def pack_q(slot, q3):
-    shape = jax.ShapeDtypeStruct((ROWS, TILE, HD), BF)
+    shape = jax.ShapeDtypeStruct((ROWS + 1, TILE, HD), BF)
     return pl.pallas_call(
         pack_q_kernel,
         out_shape=(shape, shape),
@@ -174,9 +170,11 @@
     )(idx, *blocks)
 
 
-def window_kernel(pos_ref, h2, h1, h0, e2, e1, e0, out_ref):
-    for k, (h, e) in enumerate(((h2, e2), (h1, e1), (h0, e0))):
-        out_ref[k * ROWS:(k + 1) * ROWS] = h[...]
+def window_kernel(pos_ref, h2, h1a, h1b, h0, e2, e1, e0, out_ref):
+    out_ref[:ROWS] = h2[...]
+    out_ref[ROWS:2 * ROWS] = h1a[...] + h1b[...]
+    out_ref[2 * ROWS:] = h0[...]
+    for k, e in enumerate((e2, e1, e0)):
         for i in range(3):
             out_ref[k * ROWS + pos_ref[k * 3 + i]] = e[i]
 
@@ -185,7 +183,7 @@
     return pl.pallas_call(
         window_kernel,
         out_shape=jax.ShapeDtypeStruct((3 * ROWS, TILE, HD), BF),
-        in_specs=[SM] + [VM] * 6,
+        in_specs=[SM] + [VM] * 7,
         out_specs=VM,
         compiler_params=params(),
         name="window",
@@ -216,7 +214,8 @@
 
 
 def attend_kernel(part, scale, q_ref, kv_ref, segq_ref, segk_ref, *rest):
-    out_hbm, held, sem = rest[-3:]
+    out_hbm, done_ref, held, sem = rest[-4:]
+    done_ref[...] = jnp.zeros_like(done_ref)
     heads = TILE // 4
     blocks = []
     for lo, rows in ((0, 128), (128, 64)):
@@ -252,9 +251,12 @@
     heads = TILE // 4
     return pl.pallas_call(
         functools.partial(attend_kernel, part, HD ** -0.5),
-        out_shape=jax.ShapeDtypeStruct((ROWS, 2 * TILE * HD), BF),
+        out_shape=(
+            jax.ShapeDtypeStruct((ROWS, 2 * TILE * HD), BF),
+            jax.ShapeDtypeStruct((8, HD), jnp.float32),
+        ),
         in_specs=[VM] * 4 + [HB] * len(prior),
-        out_specs=HB,
+        out_specs=(HB, VM),
         scratch_shapes=[pltpu.VMEM((heads, ROWS, 4 * HD), BF), pltpu.SemaphoreType.DMA((heads,))],
         input_output_aliases={4: 0} if prior else {},
         compiler_params=params(32),
@@ -289,20 +291,23 @@
     dz = (((y + k6) >> 2) & (NZ - 1)).reshape(1)
     zr1 = lax.all_to_all(zs1.reshape(NZ, SLOT, TILE, HD), "z", 0, 0, tiled=True)
 
+    slot, queries = lax.optimization_barrier((slot, queries))
     qa, qb = pack_q(slot, queries.reshape(ROWS, 2 * TILE, HD))
 
     def along_y(a):
-        a = a.reshape(NY, NZ * PER, TILE, HD)
-        return [a[0]] + [side(a[k], k) for k in range(1, NY)]
+        n = NZ * PER
+        return [a[:n]] + [side(a[k * n:(k + 1) * n], k) for k in range(1, NY)]
 
     za, zb = along_y(qa), along_y(qb)
-    za, zb, note1, note2 = lax.optimization_barrier((za, zb, note1, note2))
     seg = note[:ROWS]
     segk = jnp.concatenate(
         [jnp.where(s >= 2, note2[:ROWS], -1), jnp.where(s >= 1, note1[:ROWS], -1), seg]
     )[None]
     segq = seg[:, None]
     poses = jnp.concatenate([note2[ROWS:], note1[ROWS:], pos])
+    small = (segk, segq, poses, pos, idx1, idx2, idx3, k6, dz)
+    za, zb, small = lax.optimization_barrier((za, zb, small))
+    segk, segq, poses, pos, idx1, idx2, idx3, k6, dz = small
 
     zs2 = assemble_q_hop(dz, za, zr1)
     zs3 = jnp.stack([b.reshape(NZ, PER, TILE, HD) for b in zb], axis=1).reshape(NZ, NY * PER, TILE, HD)
@@ -311,17 +316,18 @@
     part = [zr1[:, k * PER:(k + 1) * PER].reshape(NZ * PER, TILE, HD) for k in range(NY)]
     own = unpack_kv(idx1, [part[0]] + [side(part[k], k) for k in range(1, NY)])
     own2 = up(own, 2)
-    zs3, own2 = lax.optimization_barrier((zs3, own2))
-    own1 = lax.ppermute(jnp.where(s % 2 == 0, own, own2), "seq", [(i, i ^ 1) for i in range(NS)])
+    own1a = lax.ppermute(own, "seq", [(i, i + 1) for i in range(0, NS, 2)])
+    zs3, own2, own1a = lax.optimization_barrier((zs3, own2, own1a))
+    own1b = lax.ppermute(own2, "seq", [(i + 1, i) for i in range(0, NS, 2)])
     zr3 = lax.all_to_all(zs3, "z", 0, 0, tiled=True)
 
     came = zr2[:EXT, SLOT - 1]
     ext = jnp.stack([came] + [side(came, k) for k in range(1, NY)])
     ext = lax.dynamic_index_in_dim(ext, k6 & (NY - 1), 0, False)
     ext0 = ext.reshape(3, 3, TILE, HD)[:, 0]
-    kvt = window(poses, (own2, own1, own), (up(ext0, 2), up(ext0, 1), ext0)).transpose(1, 0, 2)
-    out = attend(0, unpack_q(1, idx2, pos, zr2, ext).transpose(1, 0, 2), kvt, segq, segk)
-    return attend(1, unpack_q(2, idx3, pos, zr3, ext, out[:8, :HD]).transpose(1, 0, 2), kvt, segq, segk, out)
+    kvt = window(poses, (own2, own1a, own1b, own), (up(ext0, 2), up(ext0, 1), ext0)).transpose(1, 0, 2)
+    out, done = attend(0, unpack_q(1, idx2, pos, zr2, ext).transpose(1, 0, 2), kvt, segq, segk)
+    return attend(1, unpack_q(2, idx3, pos, zr3, ext, done).transpose(1, 0, 2), kvt, segq, segk, out)[0]
 
 
 def solution(mesh):

time: 170 us -> 171 us (level)
  starting transfers between devices: 82.5 us -> 87.8 us
  waiting for transfers between devices: 51.8 us -> 49.9 us
    all_to_all x1, waiting for transfers between devices: 7.49 us -> 11.9 us  [on_device(): zr3 = lax.all_to_all(zs3, 'z', 0, 0, tiled=True)]
    all_to_all x1, waiting for transfers between devices: 2.78 us -> 0.01 us  [on_device(): zr1 = lax.all_to_all(zs1.reshape(NZ, SLOT, TILE, HD), 'z', 0, 0, tiled=True)]
    all_to_all x1, starting transfers between devices: 9.25 us -> 12 us  [on_device(): zr2 = lax.all_to_all(zs2, 'z', 0, 0, tiled=True)]
    ppermute x5, starting transfers between devices: 13.8 us -> 16.2 us  [on_device(): lax.ppermute(a, 'seq', [(i, i + n) for i in range(NS - n)])]
    unnamed x13, local copies, waits for them, and re-layouts: 3.56 us -> 1.58 us
  transfers between devices with their start and end apart: 21 -> 22, of which waited for: 12 -> 11; matrix products, arithmetic and copies ran while one was open for 7% -> 6% of each run, Pallas kernels for 5% -> 5%
where the time goes in v4:
time: 171 us; the launch traced here: 170 us
  starting transfers between devices  87.8 us (51%)
  waiting for transfers between devices  49.9 us (29%)
  Pallas kernels  18.7 us (11%)
  local copies, waits for them, and re-layouts  7.63 us (4%)
  other arithmetic  4.87 us (3%)
    ppermute x12, starting transfers between devices, on_device(): lax.ppermute(a, 'y', [(i, (i + n) % NY) for i in range(NY)])  34.5 us
    ppermute x12, waiting for transfers between devices, on_device(): lax.ppermute(a, 'y', [(i, (i + n) % NY) for i in range(NY)])  19.8 us
    ppermute x5, starting transfers between devices, on_device(): lax.ppermute(a, 'seq', [(i, i + n) for i in range(NS - n)])  16.2 us
    all_to_all x1, starting transfers between devices, on_device(): zr1 = lax.all_to_all(zs1.reshape(NZ, SLOT, TILE, HD), 'z', 0, 0, tiled=True)  15.2 us
    ppermute x5, waiting for transfers between devices, on_device(): lax.ppermute(a, 'seq', [(i, i + n) for i in range(NS - n)])  13.2 us
    all_to_all x1, starting transfers between devices, on_device(): zr2 = lax.all_to_all(zs2, 'z', 0, 0, tiled=True)  12 us
    all_to_all x1, waiting for transfers between devices, on_device(): zr3 = lax.all_to_all(zs3, 'z', 0, 0, tiled=True)  11.9 us
    pallas_call x2, Pallas kernels, attend(): pl.pallas_call(functools.partial(attend_kernel, part, HD ** (-0.5)), out_...  7.9 us
  transfers between devices with their start and end apart: 22, of which 11 were waited for; matrix products, arithmetic and copies ran while one was open for 6% of the time, Pallas kernels for 5%

profile of v4, /device:TPU:56, one launch (start us, length us, event | category | flops | bytes accessed | tf_op | source)
XLA Modules:
  0.0 170.0 jit_solution(16022898247465010754)
XLA Ops:
  0.0 4.6 %pack_kv.1 = (bf16[208,16,128]{2,1,0:T(8,128)(2,1)}, s32[192]{0:T(256)}, s32[1]{0:T(128)}) custom-call(s32[1]{0:T(128)} %bitcast.me_ref, s32[192]{0:T(256)} %rg_hbm.1, bf16[192,16,128]{2,1,0:T(8,128)(2,1)} %bitcast.60, bf16[192,4096]{1,0:T(8,128)(2,1)} %q_hbm.1), custom_call_target="tpu_custom_call" | custom-call | tf_op jit(solution)/shard_map/pack_kv/pallas_call | solution.py:79
  4.6 15.2 %all-to-all-start = ((bf16[16,13,16,128]{3,2,1,0:T(8,128)(2,1)}), bf16[16,13,16,128]{3,2,1,0:T(8,128)(2,1)S(1)}, u32[]{:S(2)}, u32[]{:S(2)}) async-start(bf16[16,13,16,128]{3,2,1,0:T(8,128)(2,1)} %bitcast.58), calls=%async_computation | async-start | bytes 1703936 | tf_op jit(solution)/shard_map/all_to_all | solution.py:292
  23.8 4.0 %collective-permute-start.6 = (s32[195]{0:T(256)S(1)}, s32[195]{0:T(256)S(1)}, u32[]{:S(2)}, u32[]{:S(2)}) collective-permute-start(s32[195]{0:T(256)S(1)} %pad_add_fusion.1), channel_id=1, source_target_pairs={{0,2},{1,3},{2,4},{3,5},{4,6},{5,7},{8,10},{9,11},{10,12},{11,13},... | collective-permute-start | bytes 2348 | tf_op jit(solution)/shard_map/ppermute | solution.py:273
  32.5 4.5 %collective-permute-start.1 = (bf16[48,16,128]{2,1,0:T(8,128)(2,1)}, bf16[48,16,128]{2,1,0:T(8,128)(2,1)S(1)}, u32[]{:S(2)}, u32[]{:S(2)}) collective-permute-start(bf16[48,16,128]{2,1,0:T(8,128)(2,1)} %get-tuple-element.82), channel_id=1, source_target_pairs={{0,16},{8,24},{16,0},{24,8},{1,17},{9,25},{17,1},{25,9},{2,18},{10... | collective-permute-start | bytes 589832 | tf_op jit(solution)/shard_map/ppermute | solution.py:274
  42.5 5.1 %collective-permute-start.3 = (bf16[48,16,128]{2,1,0:T(8,128)(2,1)}, bf16[48,16,128]{2,1,0:T(8,128)(2,1)S(1)}, u32[]{:S(2)}, u32[]{:S(2)}) collective-permute-start(bf16[48,16,128]{2,1,0:T(8,128)(2,1)} %get-tuple-element.79), channel_id=1, source_target_pairs={{0,8},{8,16},{16,24},{24,0},{1,9},{9,17},{17,25},{25,1},{2,10},{10... | collective-permute-start | bytes 589832 | tf_op jit(solution)/shard_map/ppermute | solution.py:274
  49.7 3.3 %collective-permute-start.5 = (bf16[48,16,128]{2,1,0:T(8,128)(2,1)}, bf16[48,16,128]{2,1,0:T(8,128)(2,1)S(1)}, u32[]{:S(2)}, u32[]{:S(2)}) collective-permute-start(bf16[48,16,128]{2,1,0:T(8,128)(2,1)} %get-tuple-element.77), channel_id=1, source_target_pairs={{0,24},{8,0},{16,8},{24,16},{1,25},{9,1},{17,9},{25,17},{2,26},{10... | collective-permute-start | bytes 589832 | tf_op jit(solution)/shard_map/ppermute | solution.py:274
  59.0 3.4 %collective-permute-done.5 = bf16[48,16,128]{2,1,0:T(8,128)(2,1)S(1)} collective-permute-done((bf16[48,16,128]{2,1,0:T(8,128)(2,1)}, bf16[48,16,128]{2,1,0:T(8,128)(2,1)S(1)}, u32[]{:S(2)}, u32[]{:S(2)}) %collective-permute-start.5) | collective-permute-done | bytes 196640 | tf_op jit(solution)/shard_map/ppermute | solution.py:274
  63.4 12.0 %all-to-all-start.2 = ((bf16[16,13,16,128]{3,2,1,0:T(8,128)(2,1)}), bf16[16,13,16,128]{3,2,1,0:T(8,128)(2,1)S(1)}, u32[]{:S(2)}, u32[]{:S(2)}) async-start(bf16[16,13,16,128]{3,2,1,0:T(8,128)(2,1)} %assemble_q_hop.1), calls=%async_computation.2 | async-start | bytes 1703936 | tf_op jit(solution)/shard_map/all_to_all | solution.py:314
  75.5 2.5 %collective-permute-start.8 = (bf16[48,16,128]{2,1,0:T(8,128)(2,1)S(1)}, bf16[48,16,128]{2,1,0:T(8,128)(2,1)S(1)}, u32[]{:S(2)}, u32[]{:S(2)}) collective-permute-start(bf16[48,16,128]{2,1,0:T(8,128)(2,1)S(1)} %bitcast.66), channel_id=1, source_target_pairs={{0,8},{8,16},{16,24},{24,0},{1,9},{9,17},{17,25},{25,1},{2,10},{10... | collective-permute-start | bytes 589832 | tf_op jit(solution)/shard_map/ppermute | solution.py:274
  78.0 2.3 %collective-permute-start.9 = (bf16[48,16,128]{2,1,0:T(8,128)(2,1)S(1)}, bf16[48,16,128]{2,1,0:T(8,128)(2,1)S(1)}, u32[]{:S(2)}, u32[]{:S(2)}) collective-permute-start(bf16[48,16,128]{2,1,0:T(8,128)(2,1)S(1)} %bitcast.65), channel_id=1, source_target_pairs={{0,16},{8,24},{16,0},{24,8},{1,17},{9,25},{17,1},{25,9},{2,18},{10... | collective-permute-start | bytes 589832 | tf_op jit(solution)/shard_map/ppermute | solution.py:274
  80.3 3.0 %collective-permute-start.10 = (bf16[48,16,128]{2,1,0:T(8,128)(2,1)S(1)}, bf16[48,16,128]{2,1,0:T(8,128)(2,1)S(1)}, u32[]{:S(2)}, u32[]{:S(2)}) collective-permute-start(bf16[48,16,128]{2,1,0:T(8,128)(2,1)S(1)} %bitcast.64), channel_id=1, source_target_pairs={{0,24},{8,0},{16,8},{24,16},{1,25},{9,1},{17,9},{25,17},{2,26},{10... | collective-permute-start | bytes 589832 | tf_op jit(solution)/shard_map/ppermute | solution.py:274
  87.3 4.0 %collective-permute-done.10.b3 = bf16[48,16,128]{2,1,0:T(8,128)(2,1)S(1)} collective-permute-done((bf16[48,16,128]{2,1,0:T(8,128)(2,1)S(1)}, bf16[48,16,128]{2,1,0:T(8,128)(2,1)S(1)}, u32[]{:S(2)}, u32[]{:S(2)}) %collective-permute-start.10) | collective-permute-done | bytes 196640 | tf_op jit(solution)/shard_map/ppermute | solution.py:274
  92.3 4.0 %collective-permute-start.11 = (bf16[192,16,128]{2,1,0:T(8,128)(2,1)S(1)}, bf16[192,16,128]{2,1,0:T(8,128)(2,1)}, u32[]{:S(2)}, u32[]{:S(2)}) collective-permute-start(bf16[192,16,128]{2,1,0:T(8,128)(2,1)S(1)} %unpack_kv.1.h0), channel_id=1, source_target_pairs={{0,2},{1,3},{2,4},{3,5},{4,6},{5,7},{8,10},{9,11},{10,12},{11,13},... | collective-permute-start | bytes 2359304 | tf_op jit(solution)/shard_map/ppermute | solution.py:273
  98.8 13.2 %collective-permute-done.11.h2 = bf16[192,16,128]{2,1,0:T(8,128)(2,1)} collective-permute-done((bf16[192,16,128]{2,1,0:T(8,128)(2,1)S(1)}, bf16[192,16,128]{2,1,0:T(8,128)(2,1)}, u32[]{:S(2)}, u32[]{:S(2)}) %collective-permute-start.11) | collective-permute-done | bytes 786464 | tf_op jit(solution)/shard_map/ppermute | solution.py:273
  112.9 5.0 %all-to-all-done.2 = bf16[16,13,16,128]{3,2,1,0:T(8,128)(2,1)S(1)} async-done(((bf16[16,13,16,128]{3,2,1,0:T(8,128)(2,1)}), bf16[16,13,16,128]{3,2,1,0:T(8,128)(2,1)S(1)}, u32[]{:S(2)}, u32[]{:S(2)}) %all-to-all-start.2) | async-done | bytes 852000 | tf_op jit(solution)/shard_map/all_to_all | solution.py:314
  117.9 7.2 %all-to-all-start.1 = ((bf16[16,12,16,128]{3,2,1,0:T(8,128)(2,1)}), bf16[16,12,16,128]{3,2,1,0:T(8,128)(2,1)S(1)}, u32[]{:S(2)}, u32[]{:S(2)}) async-start(bf16[16,12,16,128]{3,2,1,0:T(8,128)(2,1)} %bitcast.57), calls=%async_computation.1 | async-start | bytes 1572864 | tf_op jit(solution)/shard_map/all_to_all | solution.py:322
  128.3 2.5 %collective-permute-start.14 = (bf16[9,16,128]{2,1,0:T(8,128)(2,1)S(1)}, bf16[9,16,128]{2,1,0:T(8,128)(2,1)S(1)}, u32[]{:S(2)}, u32[]{:S(2)}) collective-permute-start(bf16[9,16,128]{2,1,0:T(8,128)(2,1)S(1)} %get-tuple-element.71), channel_id=1, source_target_pairs={{0,16},{8,24},{16,0},{24,8},{1,17},{9,25},{17,1},{25,9},{2,18},{10... | collective-permute-start | bytes 110600 | tf_op jit(solution)/shard_map/ppermute | solution.py:274
  130.8 3.3 %collective-permute-start.15 = (bf16[9,16,128]{2,1,0:T(8,128)(2,1)S(1)}, bf16[9,16,128]{2,1,0:T(8,128)(2,1)S(1)}, u32[]{:S(2)}, u32[]{:S(2)}) collective-permute-start(bf16[9,16,128]{2,1,0:T(8,128)(2,1)S(1)} %get-tuple-element.71), channel_id=1, source_target_pairs={{0,24},{8,0},{16,8},{24,16},{1,25},{9,1},{17,9},{25,17},{2,26},{10... | collective-permute-start | bytes 110600 | tf_op jit(solution)/shard_map/ppermute | solution.py:274
  135.7 3.1 %collective-permute-done.15 = bf16[9,16,128]{2,1,0:T(8,128)(2,1)S(1)} collective-permute-done((bf16[9,16,128]{2,1,0:T(8,128)(2,1)S(1)}, bf16[9,16,128]{2,1,0:T(8,128)(2,1)S(1)}, u32[]{:S(2)}, u32[]{:S(2)}) %collective-permute-start.15) | collective-permute-done | bytes 36896 | tf_op jit(solution)/shard_map/ppermute | solution.py:274
  138.8 4.3 %collective-permute-start.17 = (bf16[3,16,128]{2,1,0:T(8,128)(2,1)S(1)}, bf16[3,16,128]{2,1,0:T(8,128)(2,1)S(1)}, u32[]{:S(2)}, u32[]{:S(2)}) collective-permute-start(bf16[3,16,128]{2,1,0:T(8,128)(2,1)S(1)} %slice_bitcast_fusion.2.e0), channel_id=1, source_target_pairs={{0,2},{1,3},{2,4},{3,5},{4,6},{5,7},{8,10},{9,11},{10,12},{11,13},... | collective-permute-start | bytes 36872 | tf_op jit(solution)/shard_map/ppermute | solution.py:273
  143.1 2.5 %collective-permute-start.18 = (bf16[3,16,128]{2,1,0:T(8,128)(2,1)S(1)}, bf16[3,16,128]{2,1,0:T(8,128)(2,1)S(1)}, u32[]{:S(2)}, u32[]{:S(2)}) collective-permute-start(bf16[3,16,128]{2,1,0:T(8,128)(2,1)S(1)} %slice_bitcast_fusion.2.e0), channel_id=1, source_target_pairs={{0,1},{1,2},{2,3},{3,4},{4,5},{5,6},{6,7},{8,9},{9,10},{10,11},{11... | collective-permute-start | bytes 36872 | tf_op jit(solution)/shard_map/ppermute | solution.py:273
  149.2 3.6 %attend.2 = (bf16[192,4096]{1,0:T(8,128)(2,1)}, f32[8,128]{1,0:T(8,128)S(1)}) custom-call(bf16[16,192,128]{2,1,0:T(8,128)(2,1)S(1)} %bitcast.51, bf16[16,576,128]{2,1,0:T(8,128)(2,1)S(1)} %bitcast.45, s32[192,1]{1,0:T(8,128)S(1)} %copy.15.segq_ref, s32[1,576]{1,0:T(1,128)S(1)} %broadcast_in_dim.17.segk_ref), custom_call_target="tpu_custom_call" | custom-call | flops 905969664 | bytes 4194304 | tf_op jit(solution)/shard_map/attend/pallas_call | solution.py:252
  152.9 11.9 %all-to-all-done.1 = bf16[16,12,16,128]{3,2,1,0:T(8,128)(2,1)S(1)} async-done(((bf16[16,12,16,128]{3,2,1,0:T(8,128)(2,1)}), bf16[16,12,16,128]{3,2,1,0:T(8,128)(2,1)S(1)}, u32[]{:S(2)}, u32[]{:S(2)}) %all-to-all-start.1) | async-done | bytes 786464 | tf_op jit(solution)/shard_map/all_to_all | solution.py:322
  165.8 4.3 %attend.3 = (bf16[192,4096]{1,0:T(8,128)(2,1)}, f32[8,128]{1,0:T(8,128)}) custom-call(bf16[16,192,128]{2,1,0:T(8,128)(2,1)S(1)} %bitcast.49, bf16[16,576,128]{2,1,0:T(8,128)(2,1)S(1)} %bitcast.46, s32[192,1]{1,0:T(8,128)S(1)} %copy.15.segq_ref, s32[1,576]{1,0:T(1,128)S(1)} %broadcast_in_dim.17.segk_ref, ...), custom_call_target="tpu_custom_call", output_to_operand_aliasing={{0}: (4, {})} | custom-call | flops 905969664 | bytes 4194304 | tf_op jit(solution)/shard_map/attend/pallas_call | solution.py:252
  (65 shorter events, 39.9 us)
Async XLA Ops:
  0.0 20.6 %copy-start.4 = (s32[1,192]{1,0:T(1,128)S(1)}, s32[1,192]{1,0:T(1,128)}, u32[]{:S(2)}) copy-start(s32[1,192]{1,0:T(1,128)} %param.9) | copy-start | bytes 2308
  0.0 27.9 %copy-start.3 = (bf16[192,4096]{1,0:T(8,128)(2,1)S(1)}, bf16[192,4096]{1,0:T(8,128)(2,1)}, u32[]{:S(2)}) copy-start(bf16[192,4096]{1,0:T(8,128)(2,1)} %q_hbm.1) | copy-start | bytes 4718596
  4.6 57.8 %all-to-all-start = ((bf16[16,13,16,128]{3,2,1,0:T(8,128)(2,1)}), bf16[16,13,16,128]{3,2,1,0:T(8,128)(2,1)S(1)}, u32[]{:S(2)}, u32[]{:S(2)}) async-start(bf16[16,13,16,128]{3,2,1,0:T(8,128)(2,1)} %bitcast.58), calls=%async_computation | async-start | bytes 1703936 | tf_op jit(solution)/shard_map/all_to_all | solution.py:292
  22.5 19.9 %collective-permute-start.7 = (s32[195]{0:T(256)S(1)}, s32[195]{0:T(256)S(1)}, u32[]{:S(2)}, u32[]{:S(2)}) collective-permute-start(s32[195]{0:T(256)S(1)} %pad_add_fusion.1), channel_id=1, source_target_pairs={{0,1},{1,2},{2,3},{3,4},{4,5},{5,6},{6,7},{8,9},{9,10},{10,11},{11... | collective-permute-start | bytes 2348 | tf_op jit(solution)/shard_map/ppermute | solution.py:273
  23.8 23.8 %collective-permute-start.6 = (s32[195]{0:T(256)S(1)}, s32[195]{0:T(256)S(1)}, u32[]{:S(2)}, u32[]{:S(2)}) collective-permute-start(s32[195]{0:T(256)S(1)} %pad_add_fusion.1), channel_id=1, source_target_pairs={{0,2},{1,3},{2,4},{3,5},{4,6},{5,7},{8,10},{9,11},{10,12},{11,13},... | collective-permute-start | bytes 2348 | tf_op jit(solution)/shard_map/ppermute | solution.py:273
  30.4 19.3 %collective-permute-start = (bf16[48,16,128]{2,1,0:T(8,128)(2,1)S(1)}, bf16[48,16,128]{2,1,0:T(8,128)(2,1)S(1)}, u32[]{:S(2)}, u32[]{:S(2)}) collective-permute-start(bf16[48,16,128]{2,1,0:T(8,128)(2,1)S(1)} %get-tuple-element.83), channel_id=1, source_target_pairs={{0,8},{8,16},{16,24},{24,0},{1,9},{9,17},{17,25},{25,1},{2,10},{10... | collective-permute-start | bytes 589832 | tf_op jit(solution)/shard_map/ppermute | solution.py:274
  32.5 22.7 %collective-permute-start.1 = (bf16[48,16,128]{2,1,0:T(8,128)(2,1)}, bf16[48,16,128]{2,1,0:T(8,128)(2,1)S(1)}, u32[]{:S(2)}, u32[]{:S(2)}) collective-permute-start(bf16[48,16,128]{2,1,0:T(8,128)(2,1)} %get-tuple-element.82), channel_id=1, source_target_pairs={{0,16},{8,24},{16,0},{24,8},{1,17},{9,25},{17,1},{25,9},{2,18},{10... | collective-permute-start | bytes 589832 | tf_op jit(solution)/shard_map/ppermute | solution.py:274
  37.0 18.2 %collective-permute-start.2 = (bf16[48,16,128]{2,1,0:T(8,128)(2,1)S(1)}, bf16[48,16,128]{2,1,0:T(8,128)(2,1)S(1)}, u32[]{:S(2)}, u32[]{:S(2)}) collective-permute-start(bf16[48,16,128]{2,1,0:T(8,128)(2,1)S(1)} %get-tuple-element.81), channel_id=1, source_target_pairs={{0,24},{8,0},{16,8},{24,16},{1,25},{9,1},{17,9},{25,17},{2,26},{10... | collective-permute-start | bytes 589832 | tf_op jit(solution)/shard_map/ppermute | solution.py:274
  42.5 14.4 %collective-permute-start.3 = (bf16[48,16,128]{2,1,0:T(8,128)(2,1)}, bf16[48,16,128]{2,1,0:T(8,128)(2,1)S(1)}, u32[]{:S(2)}, u32[]{:S(2)}) collective-permute-start(bf16[48,16,128]{2,1,0:T(8,128)(2,1)} %get-tuple-element.79), channel_id=1, source_target_pairs={{0,8},{8,16},{16,24},{24,0},{1,9},{9,17},{17,25},{25,1},{2,10},{10... | collective-permute-start | bytes 589832 | tf_op jit(solution)/shard_map/ppermute | solution.py:274
  47.6 11.4 %collective-permute-start.4 = (bf16[48,16,128]{2,1,0:T(8,128)(2,1)}, bf16[48,16,128]{2,1,0:T(8,128)(2,1)S(1)}, u32[]{:S(2)}, u32[]{:S(2)}) collective-permute-start(bf16[48,16,128]{2,1,0:T(8,128)(2,1)} %get-tuple-element.78), channel_id=1, source_target_pairs={{0,16},{8,24},{16,0},{24,8},{1,17},{9,25},{17,1},{25,9},{2,18},{10... | collective-permute-start | bytes 589832 | tf_op jit(solution)/shard_map/ppermute | solution.py:274
  49.7 12.8 %collective-permute-start.5 = (bf16[48,16,128]{2,1,0:T(8,128)(2,1)}, bf16[48,16,128]{2,1,0:T(8,128)(2,1)S(1)}, u32[]{:S(2)}, u32[]{:S(2)}) collective-permute-start(bf16[48,16,128]{2,1,0:T(8,128)(2,1)} %get-tuple-element.77), channel_id=1, source_target_pairs={{0,24},{8,0},{16,8},{24,16},{1,25},{9,1},{17,9},{25,17},{2,26},{10... | collective-permute-start | bytes 589832 | tf_op jit(solution)/shard_map/ppermute | solution.py:274
  63.4 54.5 %all-to-all-start.2 = ((bf16[16,13,16,128]{3,2,1,0:T(8,128)(2,1)}), bf16[16,13,16,128]{3,2,1,0:T(8,128)(2,1)S(1)}, u32[]{:S(2)}, u32[]{:S(2)}) async-start(bf16[16,13,16,128]{3,2,1,0:T(8,128)(2,1)} %assemble_q_hop.1), calls=%async_computation.2 | async-start | bytes 1703936 | tf_op jit(solution)/shard_map/all_to_all | solution.py:314
  75.5 9.7 %collective-permute-start.8 = (bf16[48,16,128]{2,1,0:T(8,128)(2,1)S(1)}, bf16[48,16,128]{2,1,0:T(8,128)(2,1)S(1)}, u32[]{:S(2)}, u32[]{:S(2)}) collective-permute-start(bf16[48,16,128]{2,1,0:T(8,128)(2,1)S(1)} %bitcast.66), channel_id=1, source_target_pairs={{0,8},{8,16},{16,24},{24,0},{1,9},{9,17},{17,25},{25,1},{2,10},{10... | collective-permute-start | bytes 589832 | tf_op jit(solution)/shard_map/ppermute | solution.py:274
  78.0 9.3 %collective-permute-start.9 = (bf16[48,16,128]{2,1,0:T(8,128)(2,1)S(1)}, bf16[48,16,128]{2,1,0:T(8,128)(2,1)S(1)}, u32[]{:S(2)}, u32[]{:S(2)}) collective-permute-start(bf16[48,16,128]{2,1,0:T(8,128)(2,1)S(1)} %bitcast.65), channel_id=1, source_target_pairs={{0,16},{8,24},{16,0},{24,8},{1,17},{9,25},{17,1},{25,9},{2,18},{10... | collective-permute-start | bytes 589832 | tf_op jit(solution)/shard_map/ppermute | solution.py:274
  80.3 11.0 %collective-permute-start.10 = (bf16[48,16,128]{2,1,0:T(8,128)(2,1)S(1)}, bf16[48,16,128]{2,1,0:T(8,128)(2,1)S(1)}, u32[]{:S(2)}, u32[]{:S(2)}) collective-permute-start(bf16[48,16,128]{2,1,0:T(8,128)(2,1)S(1)} %bitcast.64), channel_id=1, source_target_pairs={{0,24},{8,0},{16,8},{24,16},{1,25},{9,1},{17,9},{25,17},{2,26},{10... | collective-permute-start | bytes 589832 | tf_op jit(solution)/shard_map/ppermute | solution.py:274
  92.3 19.7 %collective-permute-start.11 = (bf16[192,16,128]{2,1,0:T(8,128)(2,1)S(1)}, bf16[192,16,128]{2,1,0:T(8,128)(2,1)}, u32[]{:S(2)}, u32[]{:S(2)}) collective-permute-start(bf16[192,16,128]{2,1,0:T(8,128)(2,1)S(1)} %unpack_kv.1.h0), channel_id=1, source_target_pairs={{0,2},{1,3},{2,4},{3,5},{4,6},{5,7},{8,10},{9,11},{10,12},{11,13},... | collective-permute-start | bytes 2359304 | tf_op jit(solution)/shard_map/ppermute | solution.py:273
  96.3 15.7 %collective-permute-start.12 = (bf16[192,16,128]{2,1,0:T(8,128)(2,1)S(1)}, bf16[192,16,128]{2,1,0:T(8,128)(2,1)S(1)}, u32[]{:S(2)}, u32[]{:S(2)}) collective-permute-start(bf16[192,16,128]{2,1,0:T(8,128)(2,1)S(1)} %unpack_kv.1.h0), channel_id=1, source_target_pairs={{0,1},{2,3},{4,5},{6,7},{8,9},{10,11},{12,13},{14,15},{16,17},{18,... | collective-permute-start | bytes 2359304 | tf_op jit(solution)/shard_map/ppermute | solution.py:319
  117.9 46.8 %all-to-all-start.1 = ((bf16[16,12,16,128]{3,2,1,0:T(8,128)(2,1)}), bf16[16,12,16,128]{3,2,1,0:T(8,128)(2,1)S(1)}, u32[]{:S(2)}, u32[]{:S(2)}) async-start(bf16[16,12,16,128]{3,2,1,0:T(8,128)(2,1)} %bitcast.57), calls=%async_computation.1 | async-start | bytes 1572864 | tf_op jit(solution)/shard_map/all_to_all | solution.py:322
  125.1 21.8 %collective-permute-start.16 = (bf16[192,16,128]{2,1,0:T(8,128)(2,1)}, bf16[192,16,128]{2,1,0:T(8,128)(2,1)}, u32[]{:S(2)}, u32[]{:S(2)}) collective-permute-start(bf16[192,16,128]{2,1,0:T(8,128)(2,1)} %collective-permute-done.11.h2), channel_id=1, source_target_pairs={{1,0},{3,2},{5,4},{7,6},{9,8},{11,10},{13,12},{15,14},{17,16},{19,... | collective-permute-start | bytes 2359304 | tf_op jit(solution)/shard_map/ppermute | solution.py:321
  126.4 7.8 %collective-permute-start.13 = (bf16[9,16,128]{2,1,0:T(8,128)(2,1)S(1)}, bf16[9,16,128]{2,1,0:T(8,128)(2,1)S(1)}, u32[]{:S(2)}, u32[]{:S(2)}) collective-permute-start(bf16[9,16,128]{2,1,0:T(8,128)(2,1)S(1)} %get-tuple-element.71), channel_id=1, source_target_pairs={{0,8},{8,16},{16,24},{24,0},{1,9},{9,17},{17,25},{25,1},{2,10},{10... | collective-permute-start | bytes 110600 | tf_op jit(solution)/shard_map/ppermute | solution.py:274
  128.3 7.4 %collective-permute-start.14 = (bf16[9,16,128]{2,1,0:T(8,128)(2,1)S(1)}, bf16[9,16,128]{2,1,0:T(8,128)(2,1)S(1)}, u32[]{:S(2)}, u32[]{:S(2)}) collective-permute-start(bf16[9,16,128]{2,1,0:T(8,128)(2,1)S(1)} %get-tuple-element.71), channel_id=1, source_target_pairs={{0,16},{8,24},{16,0},{24,8},{1,17},{9,25},{17,1},{25,9},{2,18},{10... | collective-permute-start | bytes 110600 | tf_op jit(solution)/shard_map/ppermute | solution.py:274
  130.8 7.9 %collective-permute-start.15 = (bf16[9,16,128]{2,1,0:T(8,128)(2,1)S(1)}, bf16[9,16,128]{2,1,0:T(8,128)(2,1)S(1)}, u32[]{:S(2)}, u32[]{:S(2)}) collective-permute-start(bf16[9,16,128]{2,1,0:T(8,128)(2,1)S(1)} %get-tuple-element.71), channel_id=1, source_target_pairs={{0,24},{8,0},{16,8},{24,16},{1,25},{9,1},{17,9},{25,17},{2,26},{10... | collective-permute-start | bytes 110600 | tf_op jit(solution)/shard_map/ppermute | solution.py:274
  138.8 8.0 %collective-permute-start.17 = (bf16[3,16,128]{2,1,0:T(8,128)(2,1)S(1)}, bf16[3,16,128]{2,1,0:T(8,128)(2,1)S(1)}, u32[]{:S(2)}, u32[]{:S(2)}) collective-permute-start(bf16[3,16,128]{2,1,0:T(8,128)(2,1)S(1)} %slice_bitcast_fusion.2.e0), channel_id=1, source_target_pairs={{0,2},{1,3},{2,4},{3,5},{4,6},{5,7},{8,10},{9,11},{10,12},{11,13},... | collective-permute-start | bytes 36872 | tf_op jit(solution)/shard_map/ppermute | solution.py:273
  143.1 3.7 %collective-permute-start.18 = (bf16[3,16,128]{2,1,0:T(8,128)(2,1)S(1)}, bf16[3,16,128]{2,1,0:T(8,128)(2,1)S(1)}, u32[]{:S(2)}, u32[]{:S(2)}) collective-permute-start(bf16[3,16,128]{2,1,0:T(8,128)(2,1)S(1)} %slice_bitcast_fusion.2.e0), channel_id=1, source_target_pairs={{0,1},{1,2},{2,3},{3,4},{4,5},{5,6},{6,7},{8,9},{9,10},{10,11},{11... | collective-permute-start | bytes 36872 | tf_op jit(solution)/shard_map/ppermute | solution.py:273
  (4 other events, 22.5 us)

commit v5 on v4

v5 whole, which is shorter than its diff:
```python
import functools
import math

import jax
import jax.numpy as jnp
from jax import lax
from jax.experimental import pallas as pl
from jax.experimental.pallas import tpu as pltpu
from jax.sharding import Mesh, PartitionSpec as P

ROWS = 192
NZ, NY, NS = 16, 4, 8
PER = 3
TILE = 16
HD = 128
SLOT = NY * PER + 1
EXT = 9
BF = jnp.bfloat16
MIB = 1024 * 1024

VM = pl.BlockSpec(memory_space=pltpu.VMEM)
SM = pl.BlockSpec(memory_space=pltpu.SMEM)
HB = pl.BlockSpec(memory_space=pltpu.HBM)


def params(mib=16):
    return pltpu.CompilerParams(vmem_limit_bytes=mib * MIB)


def pack_kv_kernel(me_ref, rg_hbm, kv_hbm, q_hbm, out_ref, tile_ref, meta_ref, rg, nxt, xrow, kvs, qs, sem):
    plan = pltpu.make_async_copy(rg_hbm, rg, sem.at[0])
    plan.start()
    load = pltpu.make_async_copy(kv_hbm, kvs, sem.at[1])
    load.start()
    load_q = pltpu.make_async_copy(q_hbm, qs, sem.at[2])
    load_q.start()
    y = me_ref[0]
    for d in range(NZ * NY):
        nxt[d] = (d // NY * SLOT + ((d % NY - y) & (NY - 1)) * PER) * 8
    for e in range(4):
        xrow[e] = 0
    out_ref[...] = jnp.zeros_like(out_ref)
    plan.wait()

    def step(i, far):
        d = rg[i]
        n = nxt[d]
        r = n & 7
        nxt[d] = n + 9
        over = r >= PER
        tile_ref[i] = jnp.where(over, (r - PER) * 3 * SLOT + SLOT - 1, n >> 3)
        xrow[jnp.where(over, r - PER, 3)] = i
        return jnp.where(over, d, far)

    meta_ref[0] = lax.fori_loop(0, ROWS, step, 0, unroll=16)
    load.wait()

    def move(i, carry):
        out_ref[tile_ref[i]] = kvs[i]
        return carry

    lax.fori_loop(0, ROWS, move, 0, unroll=16)
    load_q.wait()
    row = lax.broadcasted_iota(jnp.int32, (16, 2 * TILE * HD), 0)
    for e in range(3):
        first = pl.multiple_of((xrow[e] >> 4) << 4, 16)
        block = qs[pl.ds(first, 16), :].astype(jnp.float32)
        one = jnp.sum(jnp.where(row == (xrow[e] & 15), block, 0.0), axis=0, keepdims=True)
        for t in range(2):
            parts = [one[:, (t * TILE + c) * HD:(t * TILE + c + 1) * HD] for c in range(TILE)]
            out_ref[(e * 3 + 1 + t) * SLOT + SLOT - 1] = jnp.concatenate(parts, axis=0).astype(BF)


def pack_kv(me, rg, kv, q):
    return pl.pallas_call(
        pack_kv_kernel,
        out_shape=(
            jax.ShapeDtypeStruct((NZ * SLOT, TILE, HD), BF),
            jax.ShapeDtypeStruct((ROWS,), jnp.int32),
            jax.ShapeDtypeStruct((1,), jnp.int32),
        ),
        in_specs=[SM, HB, HB, HB],
        out_specs=(VM, SM, SM),
        scratch_shapes=[
            pltpu.SMEM((ROWS,), jnp.int32),
            pltpu.SMEM((NZ * NY,), jnp.int32),
            pltpu.SMEM((4,), jnp.int32),
            pltpu.VMEM((ROWS, TILE, HD), BF),
            pltpu.VMEM((ROWS, 2 * TILE * HD), BF),
            pltpu.SemaphoreType.DMA((3,)),
        ],
        compiler_params=params(60),
        name="pack_kv",
    )(me, rg, kv, q)


def pack_q_kernel(tile_ref, q_ref, out_ref):
    out_ref[...] = jnp.zeros_like(out_ref)

    def step(i, carry):
        t = tile_ref[i]
        gz = (t * 79) >> 10
        k = t - gz * SLOT
        dy = (k * 11) >> 5
        out_ref[jnp.where(k == SLOT - 1, ROWS, (dy * NZ + gz) * PER + k - dy * PER)] = q_ref[i]
        return carry

    lax.fori_loop(0, ROWS, step, 0, unroll=16)


def pack_q(tile, q3):
    return pl.pallas_call(
        pack_q_kernel,
        out_shape=jax.ShapeDtypeStruct((ROWS + 1, 2 * TILE, HD), BF),
        in_specs=[SM, VM],
        out_specs=VM,
        compiler_params=params(),
        name="pack_q",
    )(tile, q3)


def assemble_a_kernel(dz_ref, b0, b1, b2, b3, hop_ref, out_ref):
    dz = dz_ref[0]
    for z in range(NZ):
        for k, b in enumerate((b0, b1, b2, b3)):
            out_ref[z, k * PER:(k + 1) * PER] = b[z * PER:(z + 1) * PER, :TILE]
        out_ref[z, NY * PER] = hop_ref[(z - dz) & (NZ - 1), 0]


def assemble_a(dz, blocks, zr1):
    whole = pl.BlockSpec((NZ * PER, 2 * TILE, HD), lambda i: (0, 0, 0))
    return pl.pallas_call(
        assemble_a_kernel,
        grid=(1,),
        out_shape=jax.ShapeDtypeStruct((NZ, SLOT, TILE, HD), BF),
        in_specs=[SM] + [whole] * NY + [pl.BlockSpec((NZ, 1, TILE, HD), lambda i: (0, SLOT - 1, 0, 0))],
        out_specs=pl.BlockSpec((NZ, SLOT, TILE, HD), lambda i: (0, 0, 0, 0)),
        compiler_params=params(),
        name="assemble_a",
    )(dz, *blocks, zr1)


def assemble_b_kernel(b0, b1, b2, b3, out_ref):
    for z in range(NZ):
        for k, b in enumerate((b0, b1, b2, b3)):
            out_ref[z, k * PER:(k + 1) * PER] = b[z * PER:(z + 1) * PER, TILE:]


def assemble_b(blocks):
    return pl.pallas_call(
        assemble_b_kernel,
        out_shape=jax.ShapeDtypeStruct((NZ, NY * PER, TILE, HD), BF),
        in_specs=[VM] * NY,
        out_specs=VM,
        compiler_params=params(),
        name="assemble_b",
    )(*blocks)


def unpack_kv_kernel(idx_ref, b0, b1, b2, b3, out_ref, held):
    for k, b in enumerate((b0, b1, b2, b3)):
        held[k * NZ * PER:(k + 1) * NZ * PER] = b[...]

    def step(p, carry):
        out_ref[p] = held[idx_ref[p]]
        return carry

    lax.fori_loop(0, ROWS, step, 0, unroll=8)


def unpack_kv(idx, blocks):
    return pl.pallas_call(
        unpack_kv_kernel,
        out_shape=jax.ShapeDtypeStruct((ROWS, TILE, HD), BF),
        in_specs=[SM] + [VM] * NY,
        out_specs=VM,
        scratch_shapes=[pltpu.VMEM((ROWS, TILE, HD), BF)],
        compiler_params=params(),
        name="unpack_kv",
    )(idx, *blocks)


def window_kernel(at_ref, n2, n1, n0, m2, m1, m0, h2, h1a, h1b, h0, e2, e1, e0, out_ref, seg_ref):
    out_ref[:ROWS] = h2[...]
    out_ref[ROWS:2 * ROWS] = h1a[...] + h1b[...]
    out_ref[2 * ROWS:] = h0[...]
    for k, (n, e) in enumerate(((n2, e2), (n1, e1), (n0, e0))):
        for i in range(3):
            out_ref[k * ROWS + n[ROWS + i]] = e[i]
    at = at_ref[0]
    seg_ref[:, :ROWS] = jnp.where(at >= 2, m2[:, :ROWS], -1)
    seg_ref[:, ROWS:2 * ROWS] = jnp.where(at >= 1, m1[:, :ROWS], -1)
    seg_ref[:, 2 * ROWS:] = m0[:, :ROWS]


def window(at, notes, rows, extra):
    return pl.pallas_call(
        window_kernel,
        out_shape=(
            jax.ShapeDtypeStruct((3 * ROWS, TILE, HD), BF),
            jax.ShapeDtypeStruct((1, 3 * ROWS), jnp.int32),
        ),
        in_specs=[SM] * 4 + [VM] * 10,
        out_specs=(VM, VM),
        compiler_params=params(),
        name="window",
    )(at, *notes, *[n[None] for n in notes], *rows, *extra)


def unpack_q_kernel(part, idx_ref, note_ref, src_ref, ext_ref, *rest):
    out_ref = rest[-1]

    def step(p, carry):
        out_ref[p] = src_ref[idx_ref[p]]
        return carry

    lax.fori_loop(0, ROWS, step, 0, unroll=16)
    for e in range(3):
        out_ref[note_ref[ROWS + e]] = ext_ref[e * 3 + part]


def unpack_q(part, idx, note, zr, ext, *after):
    return pl.pallas_call(
        functools.partial(unpack_q_kernel, part),
        out_shape=jax.ShapeDtypeStruct((ROWS, TILE, HD), BF),
        in_specs=[SM, SM, VM, VM] + [VM] * len(after),
        out_specs=VM,
        compiler_params=params(),
        name="unpack_q",
    )(idx, note, zr.reshape(-1, TILE, HD), ext, *after)


def attend_kernel(part, scale, q_ref, kv_ref, segq_ref, segk_ref, *rest):
    if part == 0:
        out_hbm, done_ref, held, sem = rest
        done_ref[...] = jnp.zeros_like(done_ref)
    else:
        _, out_hbm, held, sem = rest
    heads = TILE // 4
    blocks = []
    for lo, rows in ((0, 128), (128, 64)):
        span = min(rows + 2 * ROWS, 3 * ROWS - lo)
        i = lax.broadcasted_iota(jnp.int32, (rows, span), 0)
        j = lax.broadcasted_iota(jnp.int32, (rows, span), 1)
        seen = (segq_ref[lo:lo + rows, :] == segk_ref[:, lo:lo + span]) & (j <= i + 2 * ROWS)
        blocks.append((lo, rows, span, seen))
    copies = []
    for h in range(heads):
        k = 2 * (part * heads + h)
        for lo, rows, span, seen in blocks:
            q = q_ref[4 * h:4 * h + 4, lo:lo + rows].reshape(4 * rows, HD)
            s = lax.dot_general(
                q, kv_ref[k, lo:lo + span], (((1,), (1,)), ((), ())), preferred_element_type=jnp.float32
            )
            s = jnp.where(seen[None], s.reshape(4, rows, span), -jnp.inf).reshape(4 * rows, span)
            w = jnp.exp2((s - jnp.max(s, axis=1, keepdims=True)) * (scale * math.log2(math.e)))
            total = jnp.sum(w, axis=1, keepdims=True)
            o = jnp.dot(w.astype(BF), kv_ref[k + 1, lo:lo + span], preferred_element_type=jnp.float32)
            o = (o / total).astype(BF)
            for g in range(4):
                held[h, lo:lo + rows, g * HD:(g + 1) * HD] = o[g * rows:(g + 1) * rows]
        first = (part * heads + h) * 4 * HD
        cp = pltpu.make_async_copy(held.at[h], out_hbm.at[:, first:first + 4 * HD], sem.at[h])
        cp.start()
        copies.append(cp)
    for cp in copies:
        cp.wait()


def attend(part, qt, kvt, segq, segk, *prior):
    heads = TILE // 4
    whole = jax.ShapeDtypeStruct((ROWS, 2 * TILE * HD), BF)
    return pl.pallas_call(
        functools.partial(attend_kernel, part, HD ** -0.5),
        out_shape=(whole, jax.ShapeDtypeStruct((8, HD), jnp.float32)) if part == 0 else whole,
        in_specs=[VM] * 4 + [HB] * len(prior),
        out_specs=(HB, VM) if part == 0 else HB,
        scratch_shapes=[pltpu.VMEM((heads, ROWS, 4 * HD), BF), pltpu.SemaphoreType.DMA((heads,))],
        input_output_aliases={4: 0} if prior else {},
        compiler_params=params(32),
        cost_estimate=pl.CostEstimate(
            flops=4 * ROWS * 576 * TILE * HD, bytes_accessed=4 << 20, transcendentals=ROWS * 576 * TILE
        ),
        name="attend",
    )(qt, kvt, segq, segk, *prior)


def on_device(queries, key_value, route_group, arrive_slot, segment_ids):
    z, y, s = lax.axis_index("z"), lax.axis_index("y"), lax.axis_index("seq")
    kv = key_value.reshape(ROWS, TILE, HD)
    up = lambda a, n: lax.ppermute(a, "seq", [(i, i + n) for i in range(NS - n)])
    side = lambda a, n: lax.ppermute(a, "y", [(i, (i + n) % NY) for i in range(NY)])

    src, rank = arrive_slot // 6, arrive_slot % 6
    sy, sz = src & (NY - 1), src >> 2
    over = rank >= PER
    dy = (y - sy) & (NY - 1)
    idx1 = jnp.where(over, 0, (dy * NZ + sz) * PER + rank)
    idx2 = jnp.where(over, 0, sz * SLOT + dy * PER + rank)
    idx3 = jnp.where(over, 0, (sz * NY + dy) * PER + rank)

    place = jnp.arange(ROWS, dtype=jnp.int32)
    pos = jnp.stack([jnp.sum(jnp.where(rank == PER + e, place, 0)) for e in range(3)])
    note = jnp.concatenate([segment_ids.reshape(ROWS), pos])
    note1, note2 = up(note, 1), up(note, 2)

    zs1, tile, meta = pack_kv(y.reshape(1), route_group, kv, queries)
    k6 = (meta[0] - (z * NY + y)) & (NZ * NY - 1)
    dz = (((y + k6) >> 2) & (NZ - 1)).reshape(1)
    zr1 = lax.all_to_all(zs1.reshape(NZ, SLOT, TILE, HD), "z", 0, 0, tiled=True)

    tile, queries = lax.optimization_barrier((tile, queries))
    qy = pack_q(tile, queries.reshape(ROWS, 2 * TILE, HD))
    n = NZ * PER
    qy = [qy[:n]] + [side(qy[k * n:(k + 1) * n], k) for k in range(1, NY)]
    qy, note1, note2 = lax.optimization_barrier((qy, note1, note2))

    zr2 = lax.all_to_all(assemble_a(dz, qy, zr1), "z", 0, 0, tiled=True)
    zs3 = assemble_b(qy)

    part = [zr1[:, k * PER:(k + 1) * PER].reshape(NZ * PER, TILE, HD) for k in range(NY)]
    own = unpack_kv(idx1, [part[0]] + [side(part[k], k) for k in range(1, NY)])
    own2 = up(own, 2)
    own1a = lax.ppermute(own, "seq", [(i, i + 1) for i in range(0, NS, 2)])
    zs3, own2, own1a = lax.optimization_barrier((zs3, own2, own1a))
    own1b = lax.ppermute(own2, "seq", [(i + 1, i) for i in range(0, NS, 2)])
    zr3 = lax.all_to_all(zs3, "z", 0, 0, tiled=True)

    came = zr2[:EXT, SLOT - 1]
    ext = jnp.stack([came] + [side(came, k) for k in range(1, NY)])
    ext = lax.dynamic_index_in_dim(ext, k6 & (NY - 1), 0, False)
    ext0 = ext.reshape(3, 3, TILE, HD)[:, 0]
    rows, segk = window(
        s.reshape(1), (note2, note1, note), (own2, own1a, own1b, own), (up(ext0, 2), up(ext0, 1), ext0)
    )
    kvt, segq = rows.transpose(1, 0, 2), segment_ids.reshape(ROWS, 1)
    out, done = attend(0, unpack_q(1, idx2, note, zr2, ext).transpose(1, 0, 2), kvt, segq, segk)
    return attend(1, unpack_q(2, idx3, note, zr3, ext, done).transpose(1, 0, 2), kvt, segq, segk, out)


def solution(mesh):
    fine = Mesh(mesh.devices.reshape(NZ, NY, NS), ("z", "y", "seq"))
    rows = ("z", "y", "seq")
    return jax.shard_map(
        on_device,
        mesh=fine,
        in_specs=(
            P(rows, None),
            P(rows, None, None, None),
            P(rows),
            P(rows),
            P(("z", "y"), "seq"),
        ),
        out_specs=P(rows, None),
        check_vma=False,
    )
```

time: 171 us -> 164 us (0.959)
  the two profiles are of different devices: /device:TPU:56 before, /device:TPU:44 now
where the time goes in v5:
time: 164 us; the launch traced here: 163 us
  starting transfers between devices  78.1 us (48%)
  waiting for transfers between devices  58.9 us (36%)
  Pallas kernels  18.7 us (11%)
  local copies, waits for them, and re-layouts  3.86 us (2%)
  other arithmetic  2.67 us (2%)
    ppermute x9, starting transfers between devices, on_device(): lax.ppermute(a, 'y', [(i, (i + n) % NY) for i in range(NY)])  29.4 us
    ppermute x5, waiting for transfers between devices, on_device(): lax.ppermute(a, 'seq', [(i, i + n) for i in range(NS - n)])  18.7 us
    all_to_all x1, starting transfers between devices, on_device(): zr1 = lax.all_to_all(zs1.reshape(NZ, SLOT, TILE, HD), 'z', 0, 0, tiled=True)  15.2 us
    ppermute x9, waiting for transfers between devices, on_device(): lax.ppermute(a, 'y', [(i, (i + n) % NY) for i in range(NY)])  14 us
    ppermute x5, starting transfers between devices, on_device(): lax.ppermute(a, 'seq', [(i, i + n) for i in range(NS - n)])  13.7 us
    all_to_all x1, waiting for transfers between devices, on_device(): zr1 = lax.all_to_all(zs1.reshape(NZ, SLOT, TILE, HD), 'z', 0, 0, tiled=True)  13.1 us
    all_to_all x1, waiting for transfers between devices, on_device(): zr3 = lax.all_to_all(zs3, 'z', 0, 0, tiled=True)  10.7 us
    all_to_all x1, starting transfers between devices, on_device(): zr3 = lax.all_to_all(zs3, 'z', 0, 0, tiled=True)  9.76 us
  transfers between devices with their start and end apart: 19, of which 11 were waited for; matrix products, arithmetic and copies ran while one was open for 3% of the time, Pallas kernels for 6%

profile of v5, /device:TPU:44, one launch (start us, length us, event | category | flops | bytes accessed | tf_op | source)
XLA Modules:
  0.0 163.2 jit_solution(15157158116051858762)
XLA Ops:
  0.0 3.2 %pack_kv.1 = (bf16[208,16,128]{2,1,0:T(8,128)(2,1)}, s32[192]{0:T(256)}, s32[1]{0:T(128)}) custom-call(s32[1]{0:T(128)} %bitcast.4.me_ref, s32[192]{0:T(256)} %rg_hbm.1, bf16[192,16,128]{2,1,0:T(8,128)(2,1)} %bitcast.60, bf16[192,4096]{1,0:T(8,128)(2,1)} %q_hbm.1), custom_call_target="tpu_custom_call" | custom-call | tf_op jit(solution)/shard_map/pack_kv/pallas_call | solution.py:75
  3.2 15.2 %all-to-all-start = ((bf16[16,13,16,128]{3,2,1,0:T(8,128)(2,1)}), bf16[16,13,16,128]{3,2,1,0:T(8,128)(2,1)S(1)}, u32[]{:S(2)}, u32[]{:S(2)}) async-start(bf16[16,13,16,128]{3,2,1,0:T(8,128)(2,1)} %bitcast.59), calls=%async_computation | async-start | bytes 1703936 | tf_op jit(solution)/shard_map/all_to_all | solution.py:310
  22.0 3.5 %collective-permute-start = (bf16[48,32,128]{2,1,0:T(8,128)(2,1)}, bf16[48,32,128]{2,1,0:T(8,128)(2,1)S(1)}, u32[]{:S(2)}, u32[]{:S(2)}) collective-permute-start(bf16[48,32,128]{2,1,0:T(8,128)(2,1)} %get-tuple-element.49), channel_id=1, source_target_pairs={{0,8},{8,16},{16,24},{24,0},{1,9},{9,17},{17,25},{25,1},{2,10},{10... | collective-permute-start | bytes 1179656 | tf_op jit(solution)/shard_map/ppermute | solution.py:292
  25.5 2.8 %collective-permute-start.1 = (bf16[48,32,128]{2,1,0:T(8,128)(2,1)S(1)}, bf16[48,32,128]{2,1,0:T(8,128)(2,1)S(1)}, u32[]{:S(2)}, u32[]{:S(2)}) collective-permute-start(bf16[48,32,128]{2,1,0:T(8,128)(2,1)S(1)} %get-tuple-element.48), channel_id=1, source_target_pairs={{0,16},{8,24},{16,0},{24,8},{1,17},{9,25},{17,1},{25,9},{2,18},{10... | collective-permute-start | bytes 1179656 | tf_op jit(solution)/shard_map/ppermute | solution.py:292
  28.4 4.3 %collective-permute-start.2 = (bf16[48,32,128]{2,1,0:T(8,128)(2,1)S(1)}, bf16[48,32,128]{2,1,0:T(8,128)(2,1)S(1)}, u32[]{:S(2)}, u32[]{:S(2)}) collective-permute-start(bf16[48,32,128]{2,1,0:T(8,128)(2,1)S(1)} %get-tuple-element.47), channel_id=1, source_target_pairs={{0,24},{8,0},{16,8},{24,16},{1,25},{9,1},{17,9},{25,17},{2,26},{10... | collective-permute-start | bytes 1179656 | tf_op jit(solution)/shard_map/ppermute | solution.py:292
  37.3 3.1 %collective-permute-start.4 = (s32[195]{0:T(256)S(1)}, s32[195]{0:T(256)S(1)}, u32[]{:S(2)}, u32[]{:S(2)}) collective-permute-start(s32[195]{0:T(256)S(1)} %pad_add_fusion.note_ref.n0), channel_id=1, source_target_pairs={{0,2},{1,3},{2,4},{3,5},{4,6},{5,7},{8,10},{9,11},{10,12},{11,13},... | collective-permute-start | bytes 2348 | tf_op jit(solution)/shard_map/ppermute | solution.py:291
  42.7 4.6 %collective-permute-done.2.b3 = bf16[48,32,128]{2,1,0:T(8,128)(2,1)S(1)} collective-permute-done((bf16[48,32,128]{2,1,0:T(8,128)(2,1)S(1)}, bf16[48,32,128]{2,1,0:T(8,128)(2,1)S(1)}, u32[]{:S(2)}, u32[]{:S(2)}) %collective-permute-start.2) | collective-permute-done | bytes 393248 | tf_op jit(solution)/shard_map/ppermute | solution.py:292
  47.4 13.1 %all-to-all-done.hop_ref = bf16[16,13,16,128]{3,2,1,0:T(8,128)(2,1)S(1)} async-done(((bf16[16,13,16,128]{3,2,1,0:T(8,128)(2,1)}), bf16[16,13,16,128]{3,2,1,0:T(8,128)(2,1)S(1)}, u32[]{:S(2)}, u32[]{:S(2)}) %all-to-all-start) | async-done | bytes 852000 | tf_op jit(solution)/shard_map/all_to_all | solution.py:310
  61.5 7.4 %all-to-all-start.2 = ((bf16[16,13,16,128]{3,2,1,0:T(8,128)(2,1)}), bf16[16,13,16,128]{3,2,1,0:T(8,128)(2,1)S(1)}, u32[]{:S(2)}, u32[]{:S(2)}) async-start(bf16[16,13,16,128]{3,2,1,0:T(8,128)(2,1)} %assemble_a.1), calls=%async_computation.2 | async-start | bytes 1703936 | tf_op jit(solution)/shard_map/all_to_all | solution.py:318
  69.0 3.5 %collective-permute-start.5 = (bf16[48,16,128]{2,1,0:T(8,128)(2,1)S(1)}, bf16[48,16,128]{2,1,0:T(8,128)(2,1)S(1)}, u32[]{:S(2)}, u32[]{:S(2)}) collective-permute-start(bf16[48,16,128]{2,1,0:T(8,128)(2,1)S(1)} %bitcast.63), channel_id=1, source_target_pairs={{0,8},{8,16},{16,24},{24,0},{1,9},{9,17},{17,25},{25,1},{2,10},{10... | collective-permute-start | bytes 589832 | tf_op jit(solution)/shard_map/ppermute | solution.py:292
  72.4 2.9 %collective-permute-start.6 = (bf16[48,16,128]{2,1,0:T(8,128)(2,1)S(1)}, bf16[48,16,128]{2,1,0:T(8,128)(2,1)S(1)}, u32[]{:S(2)}, u32[]{:S(2)}) collective-permute-start(bf16[48,16,128]{2,1,0:T(8,128)(2,1)S(1)} %bitcast.62), channel_id=1, source_target_pairs={{0,16},{8,24},{16,0},{24,8},{1,17},{9,25},{17,1},{25,9},{2,18},{10... | collective-permute-start | bytes 589832 | tf_op jit(solution)/shard_map/ppermute | solution.py:292
  75.3 4.3 %collective-permute-start.7 = (bf16[48,16,128]{2,1,0:T(8,128)(2,1)S(1)}, bf16[48,16,128]{2,1,0:T(8,128)(2,1)S(1)}, u32[]{:S(2)}, u32[]{:S(2)}) collective-permute-start(bf16[48,16,128]{2,1,0:T(8,128)(2,1)S(1)} %bitcast.61), channel_id=1, source_target_pairs={{0,24},{8,0},{16,8},{24,16},{1,25},{9,1},{17,9},{25,17},{2,26},{10... | collective-permute-start | bytes 589832 | tf_op jit(solution)/shard_map/ppermute | solution.py:292
  79.6 4.0 %collective-permute-done.6.b2 = bf16[48,16,128]{2,1,0:T(8,128)(2,1)S(1)} collective-permute-done((bf16[48,16,128]{2,1,0:T(8,128)(2,1)S(1)}, bf16[48,16,128]{2,1,0:T(8,128)(2,1)S(1)}, u32[]{:S(2)}, u32[]{:S(2)}) %collective-permute-start.6) | collective-permute-done | bytes 196640 | tf_op jit(solution)/shard_map/ppermute | solution.py:292
  83.7 2.4 %collective-permute-done.7.b3 = bf16[48,16,128]{2,1,0:T(8,128)(2,1)S(1)} collective-permute-done((bf16[48,16,128]{2,1,0:T(8,128)(2,1)S(1)}, bf16[48,16,128]{2,1,0:T(8,128)(2,1)S(1)}, u32[]{:S(2)}, u32[]{:S(2)}) %collective-permute-start.7) | collective-permute-done | bytes 196640 | tf_op jit(solution)/shard_map/ppermute | solution.py:292
  87.0 3.1 %collective-permute-start.8 = (bf16[192,16,128]{2,1,0:T(8,128)(2,1)S(1)}, bf16[192,16,128]{2,1,0:T(8,128)(2,1)}, u32[]{:S(2)}, u32[]{:S(2)}) collective-permute-start(bf16[192,16,128]{2,1,0:T(8,128)(2,1)S(1)} %unpack_kv.1.h0), channel_id=1, source_target_pairs={{0,2},{1,3},{2,4},{3,5},{4,6},{5,7},{8,10},{9,11},{10,12},{11,13},... | collective-permute-start | bytes 2359304 | tf_op jit(solution)/shard_map/ppermute | solution.py:291
  92.4 15.7 %collective-permute-done.8.h2 = bf16[192,16,128]{2,1,0:T(8,128)(2,1)} collective-permute-done((bf16[192,16,128]{2,1,0:T(8,128)(2,1)S(1)}, bf16[192,16,128]{2,1,0:T(8,128)(2,1)}, u32[]{:S(2)}, u32[]{:S(2)}) %collective-permute-start.8) | collective-permute-done | bytes 786464 | tf_op jit(solution)/shard_map/ppermute | solution.py:291
  109.0 2.3 %all-to-all-done.2 = bf16[16,13,16,128]{3,2,1,0:T(8,128)(2,1)S(1)} async-done(((bf16[16,13,16,128]{3,2,1,0:T(8,128)(2,1)}), bf16[16,13,16,128]{3,2,1,0:T(8,128)(2,1)S(1)}, u32[]{:S(2)}, u32[]{:S(2)}) %all-to-all-start.2) | async-done | bytes 852000 | tf_op jit(solution)/shard_map/all_to_all | solution.py:318
  111.3 9.8 %all-to-all-start.1 = ((bf16[16,12,16,128]{3,2,1,0:T(8,128)(2,1)}), bf16[16,12,16,128]{3,2,1,0:T(8,128)(2,1)S(1)}, u32[]{:S(2)}, u32[]{:S(2)}) async-start(bf16[16,12,16,128]{3,2,1,0:T(8,128)(2,1)} %assemble_b.1), calls=%async_computation.1 | async-start | bytes 1572864 | tf_op jit(solution)/shard_map/all_to_all | solution.py:327
  126.3 4.2 %collective-permute-start.12 = (bf16[9,16,128]{2,1,0:T(8,128)(2,1)S(1)}, bf16[9,16,128]{2,1,0:T(8,128)(2,1)S(1)}, u32[]{:S(2)}, u32[]{:S(2)}) collective-permute-start(bf16[9,16,128]{2,1,0:T(8,128)(2,1)S(1)} %get-tuple-element.51), channel_id=1, source_target_pairs={{0,24},{8,0},{16,8},{24,16},{1,25},{9,1},{17,9},{25,17},{2,26},{10... | collective-permute-start | bytes 110600 | tf_op jit(solution)/shard_map/ppermute | solution.py:292
  133.5 3.1 %collective-permute-start.14 = (bf16[3,16,128]{2,1,0:T(8,128)(2,1)S(1)}, bf16[3,16,128]{2,1,0:T(8,128)(2,1)S(1)}, u32[]{:S(2)}, u32[]{:S(2)}) collective-permute-start(bf16[3,16,128]{2,1,0:T(8,128)(2,1)S(1)} %slice_bitcast_fusion.2.e0), channel_id=1, source_target_pairs={{0,2},{1,3},{2,4},{3,5},{4,6},{5,7},{8,10},{9,11},{10,12},{11,13},... | collective-permute-start | bytes 36872 | tf_op jit(solution)/shard_map/ppermute | solution.py:291
  136.6 2.5 %collective-permute-start.15 = (bf16[3,16,128]{2,1,0:T(8,128)(2,1)S(1)}, bf16[3,16,128]{2,1,0:T(8,128)(2,1)S(1)}, u32[]{:S(2)}, u32[]{:S(2)}) collective-permute-start(bf16[3,16,128]{2,1,0:T(8,128)(2,1)S(1)} %slice_bitcast_fusion.2.e0), channel_id=1, source_target_pairs={{0,1},{1,2},{2,3},{3,4},{4,5},{5,6},{6,7},{8,9},{9,10},{10,11},{11... | collective-permute-start | bytes 36872 | tf_op jit(solution)/shard_map/ppermute | solution.py:291
  144.1 3.7 %attend.2 = (bf16[192,4096]{1,0:T(8,128)(2,1)}, f32[8,128]{1,0:T(8,128)S(1)}) custom-call(bf16[16,192,128]{2,1,0:T(8,128)(2,1)S(1)} %bitcast.50, bf16[16,576,128]{2,1,0:T(8,128)(2,1)S(1)} %bitcast.44, s32[192,1]{1,0:T(8,128)S(1)} %copy.13.segq_ref, s32[1,576]{1,0:T(1,128)S(1)} %get-tuple-element.38.segk_ref), custom_call_target="tpu_custom_call" | custom-call | flops 905969664 | bytes 4194304 | tf_op jit(solution)/shard_map/attend/pallas_call | solution.py:273
  147.8 10.7 %all-to-all-done.1 = bf16[16,12,16,128]{3,2,1,0:T(8,128)(2,1)S(1)} async-done(((bf16[16,12,16,128]{3,2,1,0:T(8,128)(2,1)}), bf16[16,12,16,128]{3,2,1,0:T(8,128)(2,1)S(1)}, u32[]{:S(2)}, u32[]{:S(2)}) %all-to-all-start.1) | async-done | bytes 786464 | tf_op jit(solution)/shard_map/all_to_all | solution.py:327
  159.6 3.7 %attend.3 = bf16[192,4096]{1,0:T(8,128)(2,1)} custom-call(bf16[16,192,128]{2,1,0:T(8,128)(2,1)S(1)} %bitcast.48, bf16[16,576,128]{2,1,0:T(8,128)(2,1)S(1)} %bitcast.45, s32[192,1]{1,0:T(8,128)S(1)} %copy.13.segq_ref, s32[1,576]{1,0:T(1,128)S(1)} %get-tuple-element.38.segk_ref, ...), custom_call_target="tpu_custom_call", output_to_operand_aliasing={{}: (4, {})} | custom-call | flops 905969664 | bytes 4194304 | tf_op jit(solution)/shard_map/attend/pallas_call | solution.py:273
  (49 shorter events, 29.1 us)
Async XLA Ops:
  0.0 18.5 %copy-start.3 = (bf16[192,4096]{1,0:T(8,128)(2,1)S(1)}, bf16[192,4096]{1,0:T(8,128)(2,1)}, u32[]{:S(2)}) copy-start(bf16[192,4096]{1,0:T(8,128)(2,1)} %q_hbm.1) | copy-start | bytes 4718596
  3.2 57.3 %all-to-all-start = ((bf16[16,13,16,128]{3,2,1,0:T(8,128)(2,1)}), bf16[16,13,16,128]{3,2,1,0:T(8,128)(2,1)S(1)}, u32[]{:S(2)}, u32[]{:S(2)}) async-start(bf16[16,13,16,128]{3,2,1,0:T(8,128)(2,1)} %bitcast.59), calls=%async_computation | async-start | bytes 1703936 | tf_op jit(solution)/shard_map/all_to_all | solution.py:310
  21.0 11.7 %copy-start.5 = (s32[192]{0:T(256)S(1)}, s32[192]{0:T(256)}, u32[]{:S(2)}) copy-start(s32[192]{0:T(256)} %param.8) | copy-start | bytes 2308
  21.0 12.5 %copy-start.4 = (s32[1,192]{1,0:T(1,128)S(1)}, s32[1,192]{1,0:T(1,128)}, u32[]{:S(2)}) copy-start(s32[1,192]{1,0:T(1,128)} %param.9) | copy-start | bytes 2308
  22.0 20.7 %collective-permute-start = (bf16[48,32,128]{2,1,0:T(8,128)(2,1)}, bf16[48,32,128]{2,1,0:T(8,128)(2,1)S(1)}, u32[]{:S(2)}, u32[]{:S(2)}) collective-permute-start(bf16[48,32,128]{2,1,0:T(8,128)(2,1)} %get-tuple-element.49), channel_id=1, source_target_pairs={{0,8},{8,16},{16,24},{24,0},{1,9},{9,17},{17,25},{25,1},{2,10},{10... | collective-permute-start | bytes 1179656 | tf_op jit(solution)/shard_map/ppermute | solution.py:292
  25.5 17.2 %collective-permute-start.1 = (bf16[48,32,128]{2,1,0:T(8,128)(2,1)S(1)}, bf16[48,32,128]{2,1,0:T(8,128)(2,1)S(1)}, u32[]{:S(2)}, u32[]{:S(2)}) collective-permute-start(bf16[48,32,128]{2,1,0:T(8,128)(2,1)S(1)} %get-tuple-element.48), channel_id=1, source_target_pairs={{0,16},{8,24},{16,0},{24,8},{1,17},{9,25},{17,1},{25,9},{2,18},{10... | collective-permute-start | bytes 1179656 | tf_op jit(solution)/shard_map/ppermute | solution.py:292
  28.4 19.0 %collective-permute-start.2 = (bf16[48,32,128]{2,1,0:T(8,128)(2,1)S(1)}, bf16[48,32,128]{2,1,0:T(8,128)(2,1)S(1)}, u32[]{:S(2)}, u32[]{:S(2)}) collective-permute-start(bf16[48,32,128]{2,1,0:T(8,128)(2,1)S(1)} %get-tuple-element.47), channel_id=1, source_target_pairs={{0,24},{8,0},{16,8},{24,16},{1,25},{9,1},{17,9},{25,17},{2,26},{10... | collective-permute-start | bytes 1179656 | tf_op jit(solution)/shard_map/ppermute | solution.py:292
  35.4 5.7 %collective-permute-start.3 = (s32[195]{0:T(256)S(1)}, s32[195]{0:T(256)S(1)}, u32[]{:S(2)}, u32[]{:S(2)}) collective-permute-start(s32[195]{0:T(256)S(1)} %pad_add_fusion.note_ref.n0), channel_id=1, source_target_pairs={{0,1},{1,2},{2,3},{3,4},{4,5},{5,6},{6,7},{8,9},{9,10},{10,11},{11... | collective-permute-start | bytes 2348 | tf_op jit(solution)/shard_map/ppermute | solution.py:291
  37.3 5.5 %collective-permute-start.4 = (s32[195]{0:T(256)S(1)}, s32[195]{0:T(256)S(1)}, u32[]{:S(2)}, u32[]{:S(2)}) collective-permute-start(s32[195]{0:T(256)S(1)} %pad_add_fusion.note_ref.n0), channel_id=1, source_target_pairs={{0,2},{1,3},{2,4},{3,5},{4,6},{5,7},{8,10},{9,11},{10,12},{11,13},... | collective-permute-start | bytes 2348 | tf_op jit(solution)/shard_map/ppermute | solution.py:291
  61.5 49.8 %all-to-all-start.2 = ((bf16[16,13,16,128]{3,2,1,0:T(8,128)(2,1)}), bf16[16,13,16,128]{3,2,1,0:T(8,128)(2,1)S(1)}, u32[]{:S(2)}, u32[]{:S(2)}) async-start(bf16[16,13,16,128]{3,2,1,0:T(8,128)(2,1)} %assemble_a.1), calls=%async_computation.2 | async-start | bytes 1703936 | tf_op jit(solution)/shard_map/all_to_all | solution.py:318
  69.0 10.7 %collective-permute-start.5 = (bf16[48,16,128]{2,1,0:T(8,128)(2,1)S(1)}, bf16[48,16,128]{2,1,0:T(8,128)(2,1)S(1)}, u32[]{:S(2)}, u32[]{:S(2)}) collective-permute-start(bf16[48,16,128]{2,1,0:T(8,128)(2,1)S(1)} %bitcast.63), channel_id=1, source_target_pairs={{0,8},{8,16},{16,24},{24,0},{1,9},{9,17},{17,25},{25,1},{2,10},{10... | collective-permute-start | bytes 589832 | tf_op jit(solution)/shard_map/ppermute | solution.py:292
  72.4 11.2 %collective-permute-start.6 = (bf16[48,16,128]{2,1,0:T(8,128)(2,1)S(1)}, bf16[48,16,128]{2,1,0:T(8,128)(2,1)S(1)}, u32[]{:S(2)}, u32[]{:S(2)}) collective-permute-start(bf16[48,16,128]{2,1,0:T(8,128)(2,1)S(1)} %bitcast.62), channel_id=1, source_target_pairs={{0,16},{8,24},{16,0},{24,8},{1,17},{9,25},{17,1},{25,9},{2,18},{10... | collective-permute-start | bytes 589832 | tf_op jit(solution)/shard_map/ppermute | solution.py:292
  75.3 10.7 %collective-permute-start.7 = (bf16[48,16,128]{2,1,0:T(8,128)(2,1)S(1)}, bf16[48,16,128]{2,1,0:T(8,128)(2,1)S(1)}, u32[]{:S(2)}, u32[]{:S(2)}) collective-permute-start(bf16[48,16,128]{2,1,0:T(8,128)(2,1)S(1)} %bitcast.61), channel_id=1, source_target_pairs={{0,24},{8,0},{16,8},{24,16},{1,25},{9,1},{17,9},{25,17},{2,26},{10... | collective-permute-start | bytes 589832 | tf_op jit(solution)/shard_map/ppermute | solution.py:292
  87.0 21.1 %collective-permute-start.8 = (bf16[192,16,128]{2,1,0:T(8,128)(2,1)S(1)}, bf16[192,16,128]{2,1,0:T(8,128)(2,1)}, u32[]{:S(2)}, u32[]{:S(2)}) collective-permute-start(bf16[192,16,128]{2,1,0:T(8,128)(2,1)S(1)} %unpack_kv.1.h0), channel_id=1, source_target_pairs={{0,2},{1,3},{2,4},{3,5},{4,6},{5,7},{8,10},{9,11},{10,12},{11,13},... | collective-permute-start | bytes 2359304 | tf_op jit(solution)/shard_map/ppermute | solution.py:291
  90.1 18.0 %collective-permute-start.9 = (bf16[192,16,128]{2,1,0:T(8,128)(2,1)S(1)}, bf16[192,16,128]{2,1,0:T(8,128)(2,1)S(1)}, u32[]{:S(2)}, u32[]{:S(2)}) collective-permute-start(bf16[192,16,128]{2,1,0:T(8,128)(2,1)S(1)} %unpack_kv.1.h0), channel_id=1, source_target_pairs={{0,1},{2,3},{4,5},{6,7},{8,9},{10,11},{12,13},{14,15},{16,17},{18,... | collective-permute-start | bytes 2359304 | tf_op jit(solution)/shard_map/ppermute | solution.py:324
  108.1 0.9 copy-start
  111.3 47.3 %all-to-all-start.1 = ((bf16[16,12,16,128]{3,2,1,0:T(8,128)(2,1)}), bf16[16,12,16,128]{3,2,1,0:T(8,128)(2,1)S(1)}, u32[]{:S(2)}, u32[]{:S(2)}) async-start(bf16[16,12,16,128]{3,2,1,0:T(8,128)(2,1)} %assemble_b.1), calls=%async_computation.1 | async-start | bytes 1572864 | tf_op jit(solution)/shard_map/all_to_all | solution.py:327
  121.0 19.3 %collective-permute-start.13 = (bf16[192,16,128]{2,1,0:T(8,128)(2,1)}, bf16[192,16,128]{2,1,0:T(8,128)(2,1)}, u32[]{:S(2)}, u32[]{:S(2)}) collective-permute-start(bf16[192,16,128]{2,1,0:T(8,128)(2,1)} %collective-permute-done.8.h2), channel_id=1, source_target_pairs={{1,0},{3,2},{5,4},{7,6},{9,8},{11,10},{13,12},{15,14},{17,16},{19,... | collective-permute-start | bytes 2359304 | tf_op jit(solution)/shard_map/ppermute | solution.py:326
  122.3 8.2 %collective-permute-start.10 = (bf16[9,16,128]{2,1,0:T(8,128)(2,1)S(1)}, bf16[9,16,128]{2,1,0:T(8,128)(2,1)S(1)}, u32[]{:S(2)}, u32[]{:S(2)}) collective-permute-start(bf16[9,16,128]{2,1,0:T(8,128)(2,1)S(1)} %get-tuple-element.51), channel_id=1, source_target_pairs={{0,8},{8,16},{16,24},{24,0},{1,9},{9,17},{17,25},{25,1},{2,10},{10... | collective-permute-start | bytes 110600 | tf_op jit(solution)/shard_map/ppermute | solution.py:292
  124.3 7.4 %collective-permute-start.11 = (bf16[9,16,128]{2,1,0:T(8,128)(2,1)S(1)}, bf16[9,16,128]{2,1,0:T(8,128)(2,1)S(1)}, u32[]{:S(2)}, u32[]{:S(2)}) collective-permute-start(bf16[9,16,128]{2,1,0:T(8,128)(2,1)S(1)} %get-tuple-element.51), channel_id=1, source_target_pairs={{0,16},{8,24},{16,0},{24,8},{1,17},{9,25},{17,1},{25,9},{2,18},{10... | collective-permute-start | bytes 110600 | tf_op jit(solution)/shard_map/ppermute | solution.py:292
  126.3 7.2 %collective-permute-start.12 = (bf16[9,16,128]{2,1,0:T(8,128)(2,1)S(1)}, bf16[9,16,128]{2,1,0:T(8,128)(2,1)S(1)}, u32[]{:S(2)}, u32[]{:S(2)}) collective-permute-start(bf16[9,16,128]{2,1,0:T(8,128)(2,1)S(1)} %get-tuple-element.51), channel_id=1, source_target_pairs={{0,24},{8,0},{16,8},{24,16},{1,25},{9,1},{17,9},{25,17},{2,26},{10... | collective-permute-start | bytes 110600 | tf_op jit(solution)/shard_map/ppermute | solution.py:292
  133.5 6.8 %collective-permute-start.14 = (bf16[3,16,128]{2,1,0:T(8,128)(2,1)S(1)}, bf16[3,16,128]{2,1,0:T(8,128)(2,1)S(1)}, u32[]{:S(2)}, u32[]{:S(2)}) collective-permute-start(bf16[3,16,128]{2,1,0:T(8,128)(2,1)S(1)} %slice_bitcast_fusion.2.e0), channel_id=1, source_target_pairs={{0,2},{1,3},{2,4},{3,5},{4,6},{5,7},{8,10},{9,11},{10,12},{11,13},... | collective-permute-start | bytes 36872 | tf_op jit(solution)/shard_map/ppermute | solution.py:291
  136.6 5.0 %collective-permute-start.15 = (bf16[3,16,128]{2,1,0:T(8,128)(2,1)S(1)}, bf16[3,16,128]{2,1,0:T(8,128)(2,1)S(1)}, u32[]{:S(2)}, u32[]{:S(2)}) collective-permute-start(bf16[3,16,128]{2,1,0:T(8,128)(2,1)S(1)} %slice_bitcast_fusion.2.e0), channel_id=1, source_target_pairs={{0,1},{1,2},{2,3},{3,4},{4,5},{5,6},{6,7},{8,9},{9,10},{10,11},{11... | collective-permute-start | bytes 36872 | tf_op jit(solution)/shard_map/ppermute | solution.py:291
  139.3 2.4 %copy-start.1 = (bf16[192,16,128]{2,1,0:T(8,128)(2,1)S(1)}, bf16[192,16,128]{2,1,0:T(8,128)(2,1)}, u32[]{:S(2)}) copy-start(bf16[192,16,128]{2,1,0:T(8,128)(2,1)} %copy-done) | copy-start | bytes 2359300
  (1 other events, 0.7 us)

commit v6 on v5

--- a/solution.py
+++ b/solution.py
@@ -119,42 +119,52 @@
     )(tile, q3)
 
 
-def assemble_a_kernel(dz_ref, b0, b1, b2, b3, hop_ref, out_ref):
-    dz = dz_ref[0]
+def assemble_kernel(b0, b1, b2, b3, a_ref, b_ref):
     for z in range(NZ):
         for k, b in enumerate((b0, b1, b2, b3)):
-            out_ref[z, k * PER:(k + 1) * PER] = b[z * PER:(z + 1) * PER, :TILE]
-        out_ref[z, NY * PER] = hop_ref[(z - dz) & (NZ - 1), 0]
-
-
-def assemble_a(dz, blocks, zr1):
-    whole = pl.BlockSpec((NZ * PER, 2 * TILE, HD), lambda i: (0, 0, 0))
-    return pl.pallas_call(
-        assemble_a_kernel,
-        grid=(1,),
-        out_shape=jax.ShapeDtypeStruct((NZ, SLOT, TILE, HD), BF),
-        in_specs=[SM] + [whole] * NY + [pl.BlockSpec((NZ, 1, TILE, HD), lambda i: (0, SLOT - 1, 0, 0))],
-        out_specs=pl.BlockSpec((NZ, SLOT, TILE, HD), lambda i: (0, 0, 0, 0)),
-        compiler_params=params(),
-        name="assemble_a",
-    )(dz, *blocks, zr1)
-
-
-def assemble_b_kernel(b0, b1, b2, b3, out_ref):
+            rows = b[z * PER:(z + 1) * PER]
+            a_ref[z, k * PER:(k + 1) * PER] = rows[:, :TILE]
+            b_ref[z, k * PER:(k + 1) * PER] = rows[:, TILE:]
+        a_ref[z, SLOT - 1] = jnp.zeros((TILE, HD), BF)
+
+
+def assemble(blocks):
+    return pl.pallas_call(
+        assemble_kernel,
+        out_shape=(
+            jax.ShapeDtypeStruct((NZ, SLOT, TILE, HD), BF),
+            jax.ShapeDtypeStruct((NZ, NY * PER, TILE, HD), BF),
+        ),
+        in_specs=[VM] * NY,
+        out_specs=(VM, VM),
+        compiler_params=params(),
+        name="assemble",
+    )(*blocks)
+
+
+def hop_kernel(dz_ref, _, came, out, sem):
+    copies = []
     for z in range(NZ):
-        for k, b in enumerate((b0, b1, b2, b3)):
-            out_ref[z, k * PER:(k + 1) * PER] = b[z * PER:(z + 1) * PER, TILE:]
-
-
-def assemble_b(blocks):
-    return pl.pallas_call(
-        assemble_b_kernel,
-        out_shape=jax.ShapeDtypeStruct((NZ, NY * PER, TILE, HD), BF),
-        in_specs=[VM] * NY,
-        out_specs=VM,
-        compiler_params=params(),
-        name="assemble_b",
-    )(*blocks)
+        cp = pltpu.make_async_copy(
+            came.at[(z - dz_ref[0]) & (NZ - 1), SLOT - 1], out.at[z, SLOT - 1], sem.at[z]
+        )
+        cp.start()
+        copies.append(cp)
+    for cp in copies:
+        cp.wait()
+
+
+def hop(dz, zs, came):
+    return pl.pallas_call(
+        hop_kernel,
+        out_shape=jax.ShapeDtypeStruct(zs.shape, zs.dtype),
+        in_specs=[SM, HB, HB],
+        out_specs=HB,
+        scratch_shapes=[pltpu.SemaphoreType.DMA((NZ,))],
+        input_output_aliases={1: 0},
+        compiler_params=params(),
+        name="hop",
+    )(dz, zs, came)
 
 
 def unpack_kv_kernel(idx_ref, b0, b1, b2, b3, out_ref, held):
@@ -244,25 +254,34 @@
         j = lax.broadcasted_iota(jnp.int32, (rows, span), 1)
         seen = (segq_ref[lo:lo + rows, :] == segk_ref[:, lo:lo + span]) & (j <= i + 2 * ROWS)
         blocks.append((lo, rows, span, seen))
+    units = [(h, b) for h in range(heads) for b in range(len(blocks))]
+
+    def scores(h, b):
+        lo, rows, span, _ = blocks[b]
+        q = q_ref[4 * h:4 * h + 4, lo:lo + rows].reshape(4 * rows, HD)
+        keys = kv_ref[2 * (part * heads + h), lo:lo + span]
+        return lax.dot_general(q, keys, (((1,), (1,)), ((), ())), preferred_element_type=jnp.float32)
+
     copies = []
-    for h in range(heads):
-        k = 2 * (part * heads + h)
-        for lo, rows, span, seen in blocks:
-            q = q_ref[4 * h:4 * h + 4, lo:lo + rows].reshape(4 * rows, HD)
-            s = lax.dot_general(
-                q, kv_ref[k, lo:lo + span], (((1,), (1,)), ((), ())), preferred_element_type=jnp.float32
-            )
-            s = jnp.where(seen[None], s.reshape(4, rows, span), -jnp.inf).reshape(4 * rows, span)
-            w = jnp.exp2((s - jnp.max(s, axis=1, keepdims=True)) * (scale * math.log2(math.e)))
-            total = jnp.sum(w, axis=1, keepdims=True)
-            o = jnp.dot(w.astype(BF), kv_ref[k + 1, lo:lo + span], preferred_element_type=jnp.float32)
-            o = (o / total).astype(BF)
-            for g in range(4):
-                held[h, lo:lo + rows, g * HD:(g + 1) * HD] = o[g * rows:(g + 1) * rows]
-        first = (part * heads + h) * 4 * HD
-        cp = pltpu.make_async_copy(held.at[h], out_hbm.at[:, first:first + 4 * HD], sem.at[h])
-        cp.start()
-        copies.append(cp)
+    later = scores(*units[0])
+    for n, (h, b) in enumerate(units):
+        lo, rows, span, seen = blocks[b]
+        s = later
+        if n + 1 < len(units):
+            later = scores(*units[n + 1])
+        s = jnp.where(seen[None], s.reshape(4, rows, span), -jnp.inf).reshape(4 * rows, span)
+        w = jnp.exp2((s - jnp.max(s, axis=1, keepdims=True)) * (scale * math.log2(math.e)))
+        total = jnp.sum(w, axis=1, keepdims=True)
+        values = kv_ref[2 * (part * heads + h) + 1, lo:lo + span]
+        o = jnp.dot(w.astype(BF), values, preferred_element_type=jnp.float32)
+        o = (o / total).astype(BF)
+        for g in range(4):
+            held[h, lo:lo + rows, g * HD:(g + 1) * HD] = o[g * rows:(g + 1) * rows]
+        if b == len(blocks) - 1:
+            first = (part * heads + h) * 4 * HD
+            cp = pltpu.make_async_copy(held.at[h], out_hbm.at[:, first:first + 4 * HD], sem.at[h])
+            cp.start()
+            copies.append(cp)
     for cp in copies:
         cp.wait()
 
@@ -313,10 +332,9 @@
     qy = pack_q(tile, queries.reshape(ROWS, 2 * TILE, HD))
     n = NZ * PER
     qy = [qy[:n]] + [side(qy[k * n:(k + 1) * n], k) for k in range(1, NY)]
-    qy, note1, note2 = lax.optimization_barrier((qy, note1, note2))
-
-    zr2 = lax.all_to_all(assemble_a(dz, qy, zr1), "z", 0, 0, tiled=True)
-    zs3 = assemble_b(qy)
+    zs2, zs3 = assemble(qy)
+    zs2, zs3, note1, note2, dz = lax.optimization_barrier((zs2, zs3, note1, note2, dz))
+    zr2 = lax.all_to_all(hop(dz, zs2, zr1), "z", 0, 0, tiled=True)
 
     part = [zr1[:, k * PER:(k + 1) * PER].reshape(NZ * PER, TILE, HD) for k in range(NY)]
     own = unpack_kv(idx1, [part[0]] + [side(part[k], k) for k in range(1, NY)])

time: 164 us -> 163 us (level)
    all_to_all x1, waiting for transfers between devices: 13.1 us -> 11.2 us  [on_device(): zr1 = lax.all_to_all(zs1.reshape(NZ, SLOT, TILE, HD), 'z', 0, 0, tiled=True)]
  transfers between devices with their start and end apart: 19 -> 19, of which waited for: 11 -> 10; matrix products, arithmetic and copies ran while one was open for 3% -> 3% of each run, Pallas kernels for 6% -> 6%
where the time goes in v6:
time: 163 us; the launch traced here: 162 us
  starting transfers between devices  78.2 us (48%)
  waiting for transfers between devices  58.3 us (36%)
  Pallas kernels  17.5 us (11%)
  local copies, waits for them, and re-layouts  4.71 us (3%)
  other arithmetic  2.76 us (2%)
    ppermute x9, starting transfers between devices, on_device(): lax.ppermute(a, 'y', [(i, (i + n) % NY) for i in range(NY)])  29.4 us
    ppermute x5, waiting for transfers between devices, on_device(): lax.ppermute(a, 'seq', [(i, i + n) for i in range(NS - n)])  18 us
    ppermute x9, waiting for transfers between devices, on_device(): lax.ppermute(a, 'y', [(i, (i + n) % NY) for i in range(NY)])  15.6 us
    all_to_all x1, starting transfers between devices, on_device(): zr1 = lax.all_to_all(zs1.reshape(NZ, SLOT, TILE, HD), 'z', 0, 0, tiled=True)  15.2 us
    ppermute x5, starting transfers between devices, on_device(): lax.ppermute(a, 'seq', [(i, i + n) for i in range(NS - n)])  13.7 us
    all_to_all x1, waiting for transfers between devices, on_device(): zr3 = lax.all_to_all(zs3, 'z', 0, 0, tiled=True)  11.3 us
    all_to_all x1, waiting for transfers between devices, on_device(): zr1 = lax.all_to_all(zs1.reshape(NZ, SLOT, TILE, HD), 'z', 0, 0, tiled=True)  11.2 us
    all_to_all x1, starting transfers between devices, on_device(): zr3 = lax.all_to_all(zs3, 'z', 0, 0, tiled=True)  9.73 us
  transfers between devices with their start and end apart: 19, of which 10 were waited for; matrix products, arithmetic and copies ran while one was open for 3% of the time, Pallas kernels for 6%

profile of v6, /device:TPU:44, one launch (start us, length us, event | category | flops | bytes accessed | tf_op | source)
XLA Modules:
  0.0 162.5 jit_solution(7060401773793709471)
XLA Ops:
  0.0 3.2 %pack_kv.1 = (bf16[208,16,128]{2,1,0:T(8,128)(2,1)}, s32[192]{0:T(256)}, s32[1]{0:T(128)}) custom-call(s32[1]{0:T(128)} %bitcast.4.me_ref, s32[192]{0:T(256)} %rg_hbm.1, bf16[192,16,128]{2,1,0:T(8,128)(2,1)} %bitcast.60, bf16[192,4096]{1,0:T(8,128)(2,1)} %q_hbm.1), custom_call_target="tpu_custom_call" | custom-call | tf_op jit(solution)/shard_map/pack_kv/pallas_call | solution.py:75
  3.2 15.2 %all-to-all-start = ((bf16[16,13,16,128]{3,2,1,0:T(8,128)(2,1)}), bf16[16,13,16,128]{3,2,1,0:T(8,128)(2,1)S(1)}, u32[]{:S(2)}, u32[]{:S(2)}) async-start(bf16[16,13,16,128]{3,2,1,0:T(8,128)(2,1)} %bitcast.59), calls=%async_computation | async-start | bytes 1703936 | tf_op jit(solution)/shard_map/all_to_all | solution.py:329
  22.0 3.5 %collective-permute-start = (bf16[48,32,128]{2,1,0:T(8,128)(2,1)}, bf16[48,32,128]{2,1,0:T(8,128)(2,1)S(1)}, u32[]{:S(2)}, u32[]{:S(2)}) collective-permute-start(bf16[48,32,128]{2,1,0:T(8,128)(2,1)} %get-tuple-element.51), channel_id=1, source_target_pairs={{0,8},{8,16},{16,24},{24,0},{1,9},{9,17},{17,25},{25,1},{2,10},{10... | collective-permute-start | bytes 1179656 | tf_op jit(solution)/shard_map/ppermute | solution.py:311
  25.5 2.8 %collective-permute-start.1 = (bf16[48,32,128]{2,1,0:T(8,128)(2,1)S(1)}, bf16[48,32,128]{2,1,0:T(8,128)(2,1)S(1)}, u32[]{:S(2)}, u32[]{:S(2)}) collective-permute-start(bf16[48,32,128]{2,1,0:T(8,128)(2,1)S(1)} %get-tuple-element.50), channel_id=1, source_target_pairs={{0,16},{8,24},{16,0},{24,8},{1,17},{9,25},{17,1},{25,9},{2,18},{10... | collective-permute-start | bytes 1179656 | tf_op jit(solution)/shard_map/ppermute | solution.py:311
  28.3 4.3 %collective-permute-start.2 = (bf16[48,32,128]{2,1,0:T(8,128)(2,1)S(1)}, bf16[48,32,128]{2,1,0:T(8,128)(2,1)S(1)}, u32[]{:S(2)}, u32[]{:S(2)}) collective-permute-start(bf16[48,32,128]{2,1,0:T(8,128)(2,1)S(1)} %get-tuple-element.49), channel_id=1, source_target_pairs={{0,24},{8,0},{16,8},{24,16},{1,25},{9,1},{17,9},{25,17},{2,26},{10... | collective-permute-start | bytes 1179656 | tf_op jit(solution)/shard_map/ppermute | solution.py:311
  37.3 3.1 %collective-permute-start.4 = (s32[195]{0:T(256)S(1)}, s32[195]{0:T(256)S(1)}, u32[]{:S(2)}, u32[]{:S(2)}) collective-permute-start(s32[195]{0:T(256)S(1)} %pad_add_fusion.note_ref.n0), channel_id=1, source_target_pairs={{0,2},{1,3},{2,4},{3,5},{4,6},{5,7},{8,10},{9,11},{10,12},{11,13},... | collective-permute-start | bytes 2348 | tf_op jit(solution)/shard_map/ppermute | solution.py:310
  41.1 6.2 %collective-permute-done.2.b3 = bf16[48,32,128]{2,1,0:T(8,128)(2,1)S(1)} collective-permute-done((bf16[48,32,128]{2,1,0:T(8,128)(2,1)S(1)}, bf16[48,32,128]{2,1,0:T(8,128)(2,1)S(1)}, u32[]{:S(2)}, u32[]{:S(2)}) %collective-permute-start.2) | collective-permute-done | bytes 393248 | tf_op jit(solution)/shard_map/ppermute | solution.py:311
  49.3 11.2 %all-to-all-done.came = bf16[16,13,16,128]{3,2,1,0:T(8,128)(2,1)S(1)} async-done(((bf16[16,13,16,128]{3,2,1,0:T(8,128)(2,1)}), bf16[16,13,16,128]{3,2,1,0:T(8,128)(2,1)S(1)}, u32[]{:S(2)}, u32[]{:S(2)}) %all-to-all-start) | async-done | bytes 852000 | tf_op jit(solution)/shard_map/all_to_all | solution.py:329
  61.3 7.4 %all-to-all-start.2 = ((bf16[16,13,16,128]{3,2,1,0:T(8,128)(2,1)}), bf16[16,13,16,128]{3,2,1,0:T(8,128)(2,1)S(1)}, u32[]{:S(2)}, u32[]{:S(2)}) async-start(bf16[16,13,16,128]{3,2,1,0:T(8,128)(2,1)} %hop.1), calls=%async_computation.2 | async-start | bytes 1703936 | tf_op jit(solution)/shard_map/all_to_all | solution.py:337
  68.8 3.5 %collective-permute-start.5 = (bf16[48,16,128]{2,1,0:T(8,128)(2,1)S(1)}, bf16[48,16,128]{2,1,0:T(8,128)(2,1)S(1)}, u32[]{:S(2)}, u32[]{:S(2)}) collective-permute-start(bf16[48,16,128]{2,1,0:T(8,128)(2,1)S(1)} %bitcast.63), channel_id=1, source_target_pairs={{0,8},{8,16},{16,24},{24,0},{1,9},{9,17},{17,25},{25,1},{2,10},{10... | collective-permute-start | bytes 589832 | tf_op jit(solution)/shard_map/ppermute | solution.py:311
  72.3 2.8 %collective-permute-start.6 = (bf16[48,16,128]{2,1,0:T(8,128)(2,1)S(1)}, bf16[48,16,128]{2,1,0:T(8,128)(2,1)S(1)}, u32[]{:S(2)}, u32[]{:S(2)}) collective-permute-start(bf16[48,16,128]{2,1,0:T(8,128)(2,1)S(1)} %bitcast.62), channel_id=1, source_target_pairs={{0,16},{8,24},{16,0},{24,8},{1,17},{9,25},{17,1},{25,9},{2,18},{10... | collective-permute-start | bytes 589832 | tf_op jit(solution)/shard_map/ppermute | solution.py:311
  75.2 4.3 %collective-permute-start.7 = (bf16[48,16,128]{2,1,0:T(8,128)(2,1)S(1)}, bf16[48,16,128]{2,1,0:T(8,128)(2,1)S(1)}, u32[]{:S(2)}, u32[]{:S(2)}) collective-permute-start(bf16[48,16,128]{2,1,0:T(8,128)(2,1)S(1)} %bitcast.61), channel_id=1, source_target_pairs={{0,24},{8,0},{16,8},{24,16},{1,25},{9,1},{17,9},{25,17},{2,26},{10... | collective-permute-start | bytes 589832 | tf_op jit(solution)/shard_map/ppermute | solution.py:311
  79.5 4.0 %collective-permute-done.6.b2 = bf16[48,16,128]{2,1,0:T(8,128)(2,1)S(1)} collective-permute-done((bf16[48,16,128]{2,1,0:T(8,128)(2,1)S(1)}, bf16[48,16,128]{2,1,0:T(8,128)(2,1)S(1)}, u32[]{:S(2)}, u32[]{:S(2)}) %collective-permute-start.6) | collective-permute-done | bytes 196640 | tf_op jit(solution)/shard_map/ppermute | solution.py:311
  83.5 2.4 %collective-permute-done.7.b3 = bf16[48,16,128]{2,1,0:T(8,128)(2,1)S(1)} collective-permute-done((bf16[48,16,128]{2,1,0:T(8,128)(2,1)S(1)}, bf16[48,16,128]{2,1,0:T(8,128)(2,1)S(1)}, u32[]{:S(2)}, u32[]{:S(2)}) %collective-permute-start.7) | collective-permute-done | bytes 196640 | tf_op jit(solution)/shard_map/ppermute | solution.py:311
  86.8 3.1 %collective-permute-start.8 = (bf16[192,16,128]{2,1,0:T(8,128)(2,1)S(1)}, bf16[192,16,128]{2,1,0:T(8,128)(2,1)}, u32[]{:S(2)}, u32[]{:S(2)}) collective-permute-start(bf16[192,16,128]{2,1,0:T(8,128)(2,1)S(1)} %unpack_kv.1.h0), channel_id=1, source_target_pairs={{0,2},{1,3},{2,4},{3,5},{4,6},{5,7},{8,10},{9,11},{10,12},{11,13},... | collective-permute-start | bytes 2359304 | tf_op jit(solution)/shard_map/ppermute | solution.py:310
  91.3 16.6 %collective-permute-done.8.h2 = bf16[192,16,128]{2,1,0:T(8,128)(2,1)} collective-permute-done((bf16[192,16,128]{2,1,0:T(8,128)(2,1)S(1)}, bf16[192,16,128]{2,1,0:T(8,128)(2,1)}, u32[]{:S(2)}, u32[]{:S(2)}) %collective-permute-start.8) | collective-permute-done | bytes 786464 | tf_op jit(solution)/shard_map/ppermute | solution.py:310
  108.8 2.3 %all-to-all-done.2 = bf16[16,13,16,128]{3,2,1,0:T(8,128)(2,1)S(1)} async-done(((bf16[16,13,16,128]{3,2,1,0:T(8,128)(2,1)}), bf16[16,13,16,128]{3,2,1,0:T(8,128)(2,1)S(1)}, u32[]{:S(2)}, u32[]{:S(2)}) %all-to-all-start.2) | async-done | bytes 852000 | tf_op jit(solution)/shard_map/all_to_all | solution.py:337
  111.1 9.7 %all-to-all-start.1 = ((bf16[16,12,16,128]{3,2,1,0:T(8,128)(2,1)}), bf16[16,12,16,128]{3,2,1,0:T(8,128)(2,1)S(1)}, u32[]{:S(2)}, u32[]{:S(2)}) async-start(bf16[16,12,16,128]{3,2,1,0:T(8,128)(2,1)} %copy-done), calls=%async_computation.1 | async-start | bytes 1572864 | tf_op jit(solution)/shard_map/all_to_all | solution.py:345
  126.1 4.2 %collective-permute-start.12 = (bf16[9,16,128]{2,1,0:T(8,128)(2,1)S(1)}, bf16[9,16,128]{2,1,0:T(8,128)(2,1)S(1)}, u32[]{:S(2)}, u32[]{:S(2)}) collective-permute-start(bf16[9,16,128]{2,1,0:T(8,128)(2,1)S(1)} %get-tuple-element.53), channel_id=1, source_target_pairs={{0,24},{8,0},{16,8},{24,16},{1,25},{9,1},{17,9},{25,17},{2,26},{10... | collective-permute-start | bytes 110600 | tf_op jit(solution)/shard_map/ppermute | solution.py:311
  133.4 3.1 %collective-permute-start.14 = (bf16[3,16,128]{2,1,0:T(8,128)(2,1)S(1)}, bf16[3,16,128]{2,1,0:T(8,128)(2,1)S(1)}, u32[]{:S(2)}, u32[]{:S(2)}) collective-permute-start(bf16[3,16,128]{2,1,0:T(8,128)(2,1)S(1)} %slice_bitcast_fusion.2.e0), channel_id=1, source_target_pairs={{0,2},{1,3},{2,4},{3,5},{4,6},{5,7},{8,10},{9,11},{10,12},{11,13},... | collective-permute-start | bytes 36872 | tf_op jit(solution)/shard_map/ppermute | solution.py:310
  136.5 2.5 %collective-permute-start.15 = (bf16[3,16,128]{2,1,0:T(8,128)(2,1)S(1)}, bf16[3,16,128]{2,1,0:T(8,128)(2,1)S(1)}, u32[]{:S(2)}, u32[]{:S(2)}) collective-permute-start(bf16[3,16,128]{2,1,0:T(8,128)(2,1)S(1)} %slice_bitcast_fusion.2.e0), channel_id=1, source_target_pairs={{0,1},{1,2},{2,3},{3,4},{4,5},{5,6},{6,7},{8,9},{9,10},{10,11},{11... | collective-permute-start | bytes 36872 | tf_op jit(solution)/shard_map/ppermute | solution.py:310
  143.9 3.1 %attend.2 = (bf16[192,4096]{1,0:T(8,128)(2,1)}, f32[8,128]{1,0:T(8,128)S(1)}) custom-call(bf16[16,192,128]{2,1,0:T(8,128)(2,1)S(1)} %bitcast.50, bf16[16,576,128]{2,1,0:T(8,128)(2,1)S(1)} %bitcast.44, s32[192,1]{1,0:T(8,128)S(1)} %copy.14.segq_ref, s32[1,576]{1,0:T(1,128)S(1)} %get-tuple-element.40.segk_ref), custom_call_target="tpu_custom_call" | custom-call | flops 905969664 | bytes 4194304 | tf_op jit(solution)/shard_map/attend/pallas_call | solution.py:292
  147.1 11.3 %all-to-all-done.1 = bf16[16,12,16,128]{3,2,1,0:T(8,128)(2,1)S(1)} async-done(((bf16[16,12,16,128]{3,2,1,0:T(8,128)(2,1)}), bf16[16,12,16,128]{3,2,1,0:T(8,128)(2,1)S(1)}, u32[]{:S(2)}, u32[]{:S(2)}) %all-to-all-start.1) | async-done | bytes 786464 | tf_op jit(solution)/shard_map/all_to_all | solution.py:345
  159.4 3.1 %attend.3 = bf16[192,4096]{1,0:T(8,128)(2,1)} custom-call(bf16[16,192,128]{2,1,0:T(8,128)(2,1)S(1)} %bitcast.48, bf16[16,576,128]{2,1,0:T(8,128)(2,1)S(1)} %bitcast.45, s32[192,1]{1,0:T(8,128)S(1)} %copy.14.segq_ref, s32[1,576]{1,0:T(1,128)S(1)} %get-tuple-element.40.segk_ref, ...), custom_call_target="tpu_custom_call", output_to_operand_aliasing={{}: (4, {})} | custom-call | flops 905969664 | bytes 4194304 | tf_op jit(solution)/shard_map/attend/pallas_call | solution.py:292
  (51 shorter events, 28.3 us)
Async XLA Ops:
  0.0 18.5 %copy-start.4 = (bf16[192,4096]{1,0:T(8,128)(2,1)S(1)}, bf16[192,4096]{1,0:T(8,128)(2,1)}, u32[]{:S(2)}) copy-start(bf16[192,4096]{1,0:T(8,128)(2,1)} %q_hbm.1) | copy-start | bytes 4718596
  3.2 57.3 %all-to-all-start = ((bf16[16,13,16,128]{3,2,1,0:T(8,128)(2,1)}), bf16[16,13,16,128]{3,2,1,0:T(8,128)(2,1)S(1)}, u32[]{:S(2)}, u32[]{:S(2)}) async-start(bf16[16,13,16,128]{3,2,1,0:T(8,128)(2,1)} %bitcast.59), calls=%async_computation | async-start | bytes 1703936 | tf_op jit(solution)/shard_map/all_to_all | solution.py:329
  21.0 11.7 %copy-start.6 = (s32[192]{0:T(256)S(1)}, s32[192]{0:T(256)}, u32[]{:S(2)}) copy-start(s32[192]{0:T(256)} %param.8) | copy-start | bytes 2308
  21.0 12.5 %copy-start.5 = (s32[1,192]{1,0:T(1,128)S(1)}, s32[1,192]{1,0:T(1,128)}, u32[]{:S(2)}) copy-start(s32[1,192]{1,0:T(1,128)} %param.9) | copy-start | bytes 2308
  22.0 19.1 %collective-permute-start = (bf16[48,32,128]{2,1,0:T(8,128)(2,1)}, bf16[48,32,128]{2,1,0:T(8,128)(2,1)S(1)}, u32[]{:S(2)}, u32[]{:S(2)}) collective-permute-start(bf16[48,32,128]{2,1,0:T(8,128)(2,1)} %get-tuple-element.51), channel_id=1, source_target_pairs={{0,8},{8,16},{16,24},{24,0},{1,9},{9,17},{17,25},{25,1},{2,10},{10... | collective-permute-start | bytes 1179656 | tf_op jit(solution)/shard_map/ppermute | solution.py:311
  25.5 15.6 %collective-permute-start.1 = (bf16[48,32,128]{2,1,0:T(8,128)(2,1)S(1)}, bf16[48,32,128]{2,1,0:T(8,128)(2,1)S(1)}, u32[]{:S(2)}, u32[]{:S(2)}) collective-permute-start(bf16[48,32,128]{2,1,0:T(8,128)(2,1)S(1)} %get-tuple-element.50), channel_id=1, source_target_pairs={{0,16},{8,24},{16,0},{24,8},{1,17},{9,25},{17,1},{25,9},{2,18},{10... | collective-permute-start | bytes 1179656 | tf_op jit(solution)/shard_map/ppermute | solution.py:311
  28.3 19.0 %collective-permute-start.2 = (bf16[48,32,128]{2,1,0:T(8,128)(2,1)S(1)}, bf16[48,32,128]{2,1,0:T(8,128)(2,1)S(1)}, u32[]{:S(2)}, u32[]{:S(2)}) collective-permute-start(bf16[48,32,128]{2,1,0:T(8,128)(2,1)S(1)} %get-tuple-element.49), channel_id=1, source_target_pairs={{0,24},{8,0},{16,8},{24,16},{1,25},{9,1},{17,9},{25,17},{2,26},{10... | collective-permute-start | bytes 1179656 | tf_op jit(solution)/shard_map/ppermute | solution.py:311
  35.4 13.0 %collective-permute-start.3 = (s32[195]{0:T(256)S(1)}, s32[195]{0:T(256)S(1)}, u32[]{:S(2)}, u32[]{:S(2)}) collective-permute-start(s32[195]{0:T(256)S(1)} %pad_add_fusion.note_ref.n0), channel_id=1, source_target_pairs={{0,1},{1,2},{2,3},{3,4},{4,5},{5,6},{6,7},{8,9},{9,10},{10,11},{11... | collective-permute-start | bytes 2348 | tf_op jit(solution)/shard_map/ppermute | solution.py:310
  37.3 11.0 %collective-permute-start.4 = (s32[195]{0:T(256)S(1)}, s32[195]{0:T(256)S(1)}, u32[]{:S(2)}, u32[]{:S(2)}) collective-permute-start(s32[195]{0:T(256)S(1)} %pad_add_fusion.note_ref.n0), channel_id=1, source_target_pairs={{0,2},{1,3},{2,4},{3,5},{4,6},{5,7},{8,10},{9,11},{10,12},{11,13},... | collective-permute-start | bytes 2348 | tf_op jit(solution)/shard_map/ppermute | solution.py:310
  48.4 0.9 copy-start
  61.3 49.8 %all-to-all-start.2 = ((bf16[16,13,16,128]{3,2,1,0:T(8,128)(2,1)}), bf16[16,13,16,128]{3,2,1,0:T(8,128)(2,1)S(1)}, u32[]{:S(2)}, u32[]{:S(2)}) async-start(bf16[16,13,16,128]{3,2,1,0:T(8,128)(2,1)} %hop.1), calls=%async_computation.2 | async-start | bytes 1703936 | tf_op jit(solution)/shard_map/all_to_all | solution.py:337
  68.8 10.7 %collective-permute-start.5 = (bf16[48,16,128]{2,1,0:T(8,128)(2,1)S(1)}, bf16[48,16,128]{2,1,0:T(8,128)(2,1)S(1)}, u32[]{:S(2)}, u32[]{:S(2)}) collective-permute-start(bf16[48,16,128]{2,1,0:T(8,128)(2,1)S(1)} %bitcast.63), channel_id=1, source_target_pairs={{0,8},{8,16},{16,24},{24,0},{1,9},{9,17},{17,25},{25,1},{2,10},{10... | collective-permute-start | bytes 589832 | tf_op jit(solution)/shard_map/ppermute | solution.py:311
  72.3 11.2 %collective-permute-start.6 = (bf16[48,16,128]{2,1,0:T(8,128)(2,1)S(1)}, bf16[48,16,128]{2,1,0:T(8,128)(2,1)S(1)}, u32[]{:S(2)}, u32[]{:S(2)}) collective-permute-start(bf16[48,16,128]{2,1,0:T(8,128)(2,1)S(1)} %bitcast.62), channel_id=1, source_target_pairs={{0,16},{8,24},{16,0},{24,8},{1,17},{9,25},{17,1},{25,9},{2,18},{10... | collective-permute-start | bytes 589832 | tf_op jit(solution)/shard_map/ppermute | solution.py:311
  75.2 10.7 %collective-permute-start.7 = (bf16[48,16,128]{2,1,0:T(8,128)(2,1)S(1)}, bf16[48,16,128]{2,1,0:T(8,128)(2,1)S(1)}, u32[]{:S(2)}, u32[]{:S(2)}) collective-permute-start(bf16[48,16,128]{2,1,0:T(8,128)(2,1)S(1)} %bitcast.61), channel_id=1, source_target_pairs={{0,24},{8,0},{16,8},{24,16},{1,25},{9,1},{17,9},{25,17},{2,26},{10... | collective-permute-start | bytes 589832 | tf_op jit(solution)/shard_map/ppermute | solution.py:311
  86.8 21.1 %collective-permute-start.8 = (bf16[192,16,128]{2,1,0:T(8,128)(2,1)S(1)}, bf16[192,16,128]{2,1,0:T(8,128)(2,1)}, u32[]{:S(2)}, u32[]{:S(2)}) collective-permute-start(bf16[192,16,128]{2,1,0:T(8,128)(2,1)S(1)} %unpack_kv.1.h0), channel_id=1, source_target_pairs={{0,2},{1,3},{2,4},{3,5},{4,6},{5,7},{8,10},{9,11},{10,12},{11,13},... | collective-permute-start | bytes 2359304 | tf_op jit(solution)/shard_map/ppermute | solution.py:310
  89.9 18.0 %collective-permute-start.9 = (bf16[192,16,128]{2,1,0:T(8,128)(2,1)S(1)}, bf16[192,16,128]{2,1,0:T(8,128)(2,1)S(1)}, u32[]{:S(2)}, u32[]{:S(2)}) collective-permute-start(bf16[192,16,128]{2,1,0:T(8,128)(2,1)S(1)} %unpack_kv.1.h0), channel_id=1, source_target_pairs={{0,1},{2,3},{4,5},{6,7},{8,9},{10,11},{12,13},{14,15},{16,17},{18,... | collective-permute-start | bytes 2359304 | tf_op jit(solution)/shard_map/ppermute | solution.py:342
  111.1 47.2 %all-to-all-start.1 = ((bf16[16,12,16,128]{3,2,1,0:T(8,128)(2,1)}), bf16[16,12,16,128]{3,2,1,0:T(8,128)(2,1)S(1)}, u32[]{:S(2)}, u32[]{:S(2)}) async-start(bf16[16,12,16,128]{3,2,1,0:T(8,128)(2,1)} %copy-done), calls=%async_computation.1 | async-start | bytes 1572864 | tf_op jit(solution)/shard_map/all_to_all | solution.py:345
  120.8 19.3 %collective-permute-start.13 = (bf16[192,16,128]{2,1,0:T(8,128)(2,1)}, bf16[192,16,128]{2,1,0:T(8,128)(2,1)}, u32[]{:S(2)}, u32[]{:S(2)}) collective-permute-start(bf16[192,16,128]{2,1,0:T(8,128)(2,1)} %collective-permute-done.8.h2), channel_id=1, source_target_pairs={{1,0},{3,2},{5,4},{7,6},{9,8},{11,10},{13,12},{15,14},{17,16},{19,... | collective-permute-start | bytes 2359304 | tf_op jit(solution)/shard_map/ppermute | solution.py:344
  122.1 8.2 %collective-permute-start.10 = (bf16[9,16,128]{2,1,0:T(8,128)(2,1)S(1)}, bf16[9,16,128]{2,1,0:T(8,128)(2,1)S(1)}, u32[]{:S(2)}, u32[]{:S(2)}) collective-permute-start(bf16[9,16,128]{2,1,0:T(8,128)(2,1)S(1)} %get-tuple-element.53), channel_id=1, source_target_pairs={{0,8},{8,16},{16,24},{24,0},{1,9},{9,17},{17,25},{25,1},{2,10},{10... | collective-permute-start | bytes 110600 | tf_op jit(solution)/shard_map/ppermute | solution.py:311
  124.1 7.4 %collective-permute-start.11 = (bf16[9,16,128]{2,1,0:T(8,128)(2,1)S(1)}, bf16[9,16,128]{2,1,0:T(8,128)(2,1)S(1)}, u32[]{:S(2)}, u32[]{:S(2)}) collective-permute-start(bf16[9,16,128]{2,1,0:T(8,128)(2,1)S(1)} %get-tuple-element.53), channel_id=1, source_target_pairs={{0,16},{8,24},{16,0},{24,8},{1,17},{9,25},{17,1},{25,9},{2,18},{10... | collective-permute-start | bytes 110600 | tf_op jit(solution)/shard_map/ppermute | solution.py:311
  126.1 7.2 %collective-permute-start.12 = (bf16[9,16,128]{2,1,0:T(8,128)(2,1)S(1)}, bf16[9,16,128]{2,1,0:T(8,128)(2,1)S(1)}, u32[]{:S(2)}, u32[]{:S(2)}) collective-permute-start(bf16[9,16,128]{2,1,0:T(8,128)(2,1)S(1)} %get-tuple-element.53), channel_id=1, source_target_pairs={{0,24},{8,0},{16,8},{24,16},{1,25},{9,1},{17,9},{25,17},{2,26},{10... | collective-permute-start | bytes 110600 | tf_op jit(solution)/shard_map/ppermute | solution.py:311
  133.4 6.8 %collective-permute-start.14 = (bf16[3,16,128]{2,1,0:T(8,128)(2,1)S(1)}, bf16[3,16,128]{2,1,0:T(8,128)(2,1)S(1)}, u32[]{:S(2)}, u32[]{:S(2)}) collective-permute-start(bf16[3,16,128]{2,1,0:T(8,128)(2,1)S(1)} %slice_bitcast_fusion.2.e0), channel_id=1, source_target_pairs={{0,2},{1,3},{2,4},{3,5},{4,6},{5,7},{8,10},{9,11},{10,12},{11,13},... | collective-permute-start | bytes 36872 | tf_op jit(solution)/shard_map/ppermute | solution.py:310
  136.5 5.0 %collective-permute-start.15 = (bf16[3,16,128]{2,1,0:T(8,128)(2,1)S(1)}, bf16[3,16,128]{2,1,0:T(8,128)(2,1)S(1)}, u32[]{:S(2)}, u32[]{:S(2)}) collective-permute-start(bf16[3,16,128]{2,1,0:T(8,128)(2,1)S(1)} %slice_bitcast_fusion.2.e0), channel_id=1, source_target_pairs={{0,1},{1,2},{2,3},{3,4},{4,5},{5,6},{6,7},{8,9},{9,10},{10,11},{11... | collective-permute-start | bytes 36872 | tf_op jit(solution)/shard_map/ppermute | solution.py:310
  139.1 2.4 %copy-start.2 = (bf16[192,16,128]{2,1,0:T(8,128)(2,1)S(1)}, bf16[192,16,128]{2,1,0:T(8,128)(2,1)}, u32[]{:S(2)}) copy-start(bf16[192,16,128]{2,1,0:T(8,128)(2,1)} %copy-done.1) | copy-start | bytes 2359300
  (2 other events, 1.5 us)

commit v7 on v6

v7 whole, which is shorter than its diff:
```python
import functools
import math

import jax
import jax.numpy as jnp
from jax import lax
from jax.experimental import pallas as pl
from jax.experimental.pallas import tpu as pltpu
from jax.sharding import Mesh, PartitionSpec as P

ROWS = 192
NZ, NY, NS = 16, 4, 8
PER = 3
HD = 128
UNIT = 4
KV, QA, QB = 4, 5, 3
BASE = NY * PER
HOP = 3
EXT = 3 * (KV + QA + QB)
SLOT1, SLOT2, SLOT3 = BASE * KV + HOP, BASE * QA + HOP, BASE * QB
BF = jnp.bfloat16
MIB = 1024 * 1024

VM = pl.BlockSpec(memory_space=pltpu.VMEM)
SM = pl.BlockSpec(memory_space=pltpu.SMEM)
HB = pl.BlockSpec(memory_space=pltpu.HBM)


def params(mib=16):
    return pltpu.CompilerParams(vmem_limit_bytes=mib * MIB)


def pack_kv_kernel(me_ref, rg_hbm, kv_hbm, q_hbm, out_hbm, tile_ref, meta_ref, rg, nxt, xrow, kvs, qs, held, sem):
    plan = pltpu.make_async_copy(rg_hbm, rg, sem.at[0])
    plan.start()
    load = pltpu.make_async_copy(kv_hbm, kvs, sem.at[1])
    load.start()
    load_q = pltpu.make_async_copy(q_hbm, qs, sem.at[2])
    load_q.start()
    y = me_ref[0]
    for d in range(NZ * NY):
        nxt[d] = (d // NY * SLOT1 + ((d % NY - y) & (NY - 1)) * PER * KV) * 8
    for e in range(4):
        xrow[e] = 0
    held[...] = jnp.zeros_like(held)
    plan.wait()

    def step(i, far):
        d = rg[i]
        n = nxt[d]
        r = n & 7
        nxt[d] = n + KV * 8 + 1
        over = r >= PER
        tile_ref[i] = jnp.where(over, NZ * SLOT1, n >> 3)
        xrow[jnp.where(over, r - PER, 3)] = i
        return jnp.where(over, d, far)

    meta_ref[0] = lax.fori_loop(0, ROWS, step, 0, unroll=16)
    load.wait()

    def move(i, carry):
        held[pl.ds(tile_ref[i], KV)] = kvs[i]
        return carry

    lax.fori_loop(0, ROWS, move, 0, unroll=16)
    load_q.wait()
    row = lax.broadcasted_iota(jnp.int32, (16, (QA + QB) * UNIT * HD), 0)

    def place(e, u):
        j = e * (KV + QA + QB) + u
        return j // HOP * SLOT1 + BASE * KV + j % HOP

    for e in range(3):
        for u in range(KV):
            held[place(e, u)] = kvs[xrow[e], u]
        first = pl.multiple_of((xrow[e] >> 4) << 4, 16)
        block = qs[pl.ds(first, 16), :].astype(jnp.float32)
        one = jnp.sum(jnp.where(row == (xrow[e] & 15), block, 0.0), axis=0, keepdims=True)
        for u in range(QA + QB):
            parts = [one[:, (u * UNIT + c) * HD:(u * UNIT + c + 1) * HD] for c in range(UNIT)]
            held[place(e, KV + u)] = jnp.concatenate(parts, axis=0).astype(BF)
    store = pltpu.make_async_copy(held.at[pl.ds(0, NZ * SLOT1)], out_hbm, sem.at[3])
    store.start()
    store.wait()


def pack_kv(me, rg, kv, q):
    return pl.pallas_call(
        pack_kv_kernel,
        out_shape=(
            jax.ShapeDtypeStruct((NZ * SLOT1, UNIT, HD), BF),
            jax.ShapeDtypeStruct((ROWS,), jnp.int32),
            jax.ShapeDtypeStruct((1,), jnp.int32),
        ),
        in_specs=[SM, HB, HB, HB],
        out_specs=(HB, SM, SM),
        scratch_shapes=[
            pltpu.SMEM((ROWS,), jnp.int32),
            pltpu.SMEM((NZ * NY,), jnp.int32),
            pltpu.SMEM((4,), jnp.int32),
            pltpu.VMEM((ROWS, KV, UNIT, HD), BF),
            pltpu.VMEM((ROWS, (QA + QB) * UNIT * HD), BF),
            pltpu.VMEM((NZ * SLOT1 + KV, UNIT, HD), BF),
            pltpu.SemaphoreType.DMA((4,)),
        ],
        compiler_params=params(60),
        name="pack_kv",
    )(me, rg, kv, q)


def pack_q_kernel(tile_ref, q_ref, out_ref):
    out_ref[...] = jnp.zeros_like(out_ref)

    def step(i, carry):
        t = tile_ref[i]
        gz = (t * 1286) >> 16
        k = (t - gz * SLOT1) >> 2
        dy = (k * 11) >> 5
        out_ref[jnp.where(gz == NZ, ROWS, (dy * NZ + gz) * PER + k - dy * PER)] = q_ref[i]
        return carry

    lax.fori_loop(0, ROWS, step, 0, unroll=16)


def pack_q(tile, q):
    return pl.pallas_call(
        pack_q_kernel,
        out_shape=jax.ShapeDtypeStruct((ROWS + 1, QA + QB, UNIT, HD), BF),
        in_specs=[SM, VM],
        out_specs=VM,
        compiler_params=params(),
        name="pack_q",
    )(tile, q)


def assemble_kernel(b0, b1, b2, b3, a_ref, b_ref):
    for k, b in enumerate((b0, b1, b2, b3)):

        def step(z, carry, k=k, b=b):
            for r in range(PER):
                a_ref[z, (k * PER + r) * QA:(k * PER + r + 1) * QA] = b[z * PER + r, :QA]
                b_ref[z, (k * PER + r) * QB:(k * PER + r + 1) * QB] = b[z * PER + r, QA:]
            return carry

        lax.fori_loop(0, NZ, step, 0, unroll=4)
    a_ref[:, SLOT2 - HOP:] = jnp.zeros((NZ, HOP, UNIT, HD), BF)


def assemble(blocks):
    return pl.pallas_call(
        assemble_kernel,
        out_shape=(
            jax.ShapeDtypeStruct((NZ, SLOT2, UNIT, HD), BF),
            jax.ShapeDtypeStruct((NZ, SLOT3, UNIT, HD), BF),
        ),
        in_specs=[VM] * NY,
        out_specs=(VM, VM),
        compiler_params=params(),
        name="assemble",
    )(*blocks)


def hop_kernel(dz_ref, _, came, out, sem):
    copies = []
    for z in range(NZ):
        cp = pltpu.make_async_copy(
            came.at[(z - dz_ref[0]) & (NZ - 1), pl.ds(SLOT1 - HOP, HOP)],
            out.at[z, pl.ds(SLOT2 - HOP, HOP)],
            sem.at[z],
        )
        cp.start()
        copies.append(cp)
    for cp in copies:
        cp.wait()


def hop(dz, zs, came):
    return pl.pallas_call(
        hop_kernel,
        out_shape=jax.ShapeDtypeStruct(zs.shape, zs.dtype),
        in_specs=[SM, HB, HB],
        out_specs=HB,
        scratch_shapes=[pltpu.SemaphoreType.DMA((NZ,))],
        input_output_aliases={1: 0},
        compiler_params=params(),
        name="hop",
    )(dz, zs, came)


def unpack_kv_kernel(idx_ref, b0, b1, b2, b3, out_ref, held):
    for k, b in enumerate((b0, b1, b2, b3)):
        held[k * NZ * PER:(k + 1) * NZ * PER] = b[...]

    def step(p, carry):
        out_ref[p] = held[idx_ref[p]]
        return carry

    lax.fori_loop(0, ROWS, step, 0, unroll=8)


def unpack_kv(idx, blocks):
    return pl.pallas_call(
        unpack_kv_kernel,
        out_shape=jax.ShapeDtypeStruct((ROWS, KV, UNIT, HD), BF),
        in_specs=[SM] + [VM] * NY,
        out_specs=VM,
        scratch_shapes=[pltpu.VMEM((ROWS, KV, UNIT, HD), BF)],
        compiler_params=params(),
        name="unpack_kv",
    )(idx, *blocks)


def window_kernel(at_ref, n2, n1, n0, m2, m1, m0, h2, h1a, h1b, h0, e2, e1, e0, out_ref, seg_ref):
    out_ref[:ROWS] = h2[...]
    out_ref[ROWS:2 * ROWS] = h1a[...] + h1b[...]
    out_ref[2 * ROWS:] = h0[...]
    for k, (n, e) in enumerate(((n2, e2), (n1, e1), (n0, e0))):
        for i in range(3):
            out_ref[k * ROWS + n[ROWS + i]] = e[i]
    at = at_ref[0]
    seg_ref[:, :ROWS] = jnp.where(at >= 2, m2[:, :ROWS], -1)
    seg_ref[:, ROWS:2 * ROWS] = jnp.where(at >= 1, m1[:, :ROWS], -1)
    seg_ref[:, 2 * ROWS:] = m0[:, :ROWS]


def window(at, notes, rows, extra):
    wide = lambda a: a.reshape(-1, KV * UNIT, HD)
    return pl.pallas_call(
        window_kernel,
        out_shape=(
            jax.ShapeDtypeStruct((3 * ROWS, KV * UNIT, HD), BF),
            jax.ShapeDtypeStruct((1, 3 * ROWS), jnp.int32),
        ),
        in_specs=[SM] * 4 + [VM] * 10,
        out_specs=(VM, VM),
        compiler_params=params(),
        name="window",
    )(at, *notes, *[n[None] for n in notes], *map(wide, rows), *map(wide, extra))


def unpack_q_kernel(first, units, idx_ref, note_ref, src_ref, ext_ref, *rest):
    out_ref = rest[-1]

    def step(p, carry):
        out_ref[p] = src_ref[pl.ds(idx_ref[p], units)]
        return carry

    lax.fori_loop(0, ROWS, step, 0, unroll=16)
    for e in range(3):
        out_ref[note_ref[ROWS + e]] = ext_ref[e, first:first + units]


def unpack_q(first, units, idx, note, zr, ext, *after):
    rows = pl.pallas_call(
        functools.partial(unpack_q_kernel, first, units),
        out_shape=jax.ShapeDtypeStruct((ROWS, units, UNIT, HD), BF),
        in_specs=[SM, SM, VM, VM] + [VM] * len(after),
        out_specs=VM,
        compiler_params=params(),
        name="unpack_q",
    )(idx, note, zr.reshape(-1, UNIT, HD), ext, *after)
    return rows.reshape(ROWS, units * UNIT, HD).transpose(1, 0, 2)


def attend_kernel(part, heads, scale, q_ref, kv_ref, segq_ref, segk_ref, *rest):
    if part == 0:
        out_hbm, done_ref, held, sem = rest
        done_ref[...] = jnp.zeros_like(done_ref)
    else:
        _, out_hbm, held, sem = rest
    base = part * QA
    blocks = []
    for lo, rows in ((0, 128), (128, 64)):
        span = min(rows + 2 * ROWS, 3 * ROWS - lo)
        i = lax.broadcasted_iota(jnp.int32, (rows, span), 0)
        j = lax.broadcasted_iota(jnp.int32, (rows, span), 1)
        seen = (segq_ref[lo:lo + rows, :] == segk_ref[:, lo:lo + span]) & (j <= i + 2 * ROWS)
        blocks.append((lo, rows, span, seen))
    units = [(h, b) for h in range(heads) for b in range(len(blocks))]

    def scores(h, b):
        lo, rows, span, _ = blocks[b]
        q = q_ref[4 * h:4 * h + 4, lo:lo + rows].reshape(4 * rows, HD)
        keys = kv_ref[2 * (base + h), lo:lo + span]
        return lax.dot_general(q, keys, (((1,), (1,)), ((), ())), preferred_element_type=jnp.float32)

    copies = []
    later = scores(*units[0])
    for n, (h, b) in enumerate(units):
        lo, rows, span, seen = blocks[b]
        s = later
        if n + 1 < len(units):
            later = scores(*units[n + 1])
        s = jnp.where(seen[None], s.reshape(4, rows, span), -jnp.inf).reshape(4 * rows, span)
        w = jnp.exp2((s - jnp.max(s, axis=1, keepdims=True)) * (scale * math.log2(math.e)))
        total = jnp.sum(w, axis=1, keepdims=True)
        values = kv_ref[2 * (base + h) + 1, lo:lo + span]
        o = jnp.dot(w.astype(BF), values, preferred_element_type=jnp.float32)
        o = (o / total).astype(BF)
        for g in range(4):
            held[h, lo:lo + rows, g * HD:(g + 1) * HD] = o[g * rows:(g + 1) * rows]
        if b == len(blocks) - 1:
            first = (base + h) * 4 * HD
            cp = pltpu.make_async_copy(held.at[h], out_hbm.at[:, first:first + 4 * HD], sem.at[h])
            cp.start()
            copies.append(cp)
    for cp in copies:
        cp.wait()


def attend(part, qt, kvt, segq, segk, *prior):
    heads = QB if part else QA
    whole = jax.ShapeDtypeStruct((ROWS, (QA + QB) * UNIT * HD), BF)
    return pl.pallas_call(
        functools.partial(attend_kernel, part, heads, HD ** -0.5),
        out_shape=(whole, jax.ShapeDtypeStruct((8, HD), jnp.float32)) if part == 0 else whole,
        in_specs=[VM] * 4 + [HB] * len(prior),
        out_specs=(HB, VM) if part == 0 else HB,
        scratch_shapes=[pltpu.VMEM((heads, ROWS, 4 * HD), BF), pltpu.SemaphoreType.DMA((heads,))],
        input_output_aliases={4: 0} if prior else {},
        compiler_params=params(32),
        cost_estimate=pl.CostEstimate(
            flops=16 * ROWS * 576 * heads * HD, bytes_accessed=4 << 20, transcendentals=4 * ROWS * 576 * heads
        ),
        name="attend",
    )(qt, kvt, segq, segk, *prior)


def on_device(queries, key_value, route_group, arrive_slot, segment_ids):
    z, y, s = lax.axis_index("z"), lax.axis_index("y"), lax.axis_index("seq")
    kv = key_value.reshape(ROWS, KV, UNIT, HD)
    up = lambda a, n: lax.ppermute(a, "seq", [(i, i + n) for i in range(NS - n)])
    side = lambda a, n: lax.ppermute(a, "y", [(i, (i + n) % NY) for i in range(NY)])

    src, rank = arrive_slot // 6, arrive_slot % 6
    sy, sz = src & (NY - 1), src >> 2
    over = rank >= PER
    dy = (y - sy) & (NY - 1)
    idx1 = jnp.where(over, 0, (dy * NZ + sz) * PER + rank)
    idx2 = jnp.where(over, 0, sz * SLOT2 + (dy * PER + rank) * QA)
    idx3 = jnp.where(over, 0, sz * SLOT3 + (dy * PER + rank) * QB)

    place = jnp.arange(ROWS, dtype=jnp.int32)
    pos = jnp.stack([jnp.sum(jnp.where(rank == PER + e, place, 0)) for e in range(3)])
    note = jnp.concatenate([segment_ids.reshape(ROWS), pos])
    note1, note2 = up(note, 1), up(note, 2)

    zs1, tile, meta = pack_kv(y.reshape(1), route_group, kv, queries)
    k6 = (meta[0] - (z * NY + y)) & (NZ * NY - 1)
    dz = (((y + k6) >> 2) & (NZ - 1)).reshape(1)
    zr1 = lax.all_to_all(zs1.reshape(NZ, SLOT1, UNIT, HD), "z", 0, 0, tiled=True)

    tile, queries = lax.optimization_barrier((tile, queries))
    qy = pack_q(tile, queries.reshape(ROWS, QA + QB, UNIT, HD))
    n = NZ * PER
    qy = [qy[:n]] + [side(qy[k * n:(k + 1) * n], k) for k in range(1, NY)]
    zs2, zs3 = assemble(qy)
    zs2, zs3, note1, note2, dz = lax.optimization_barrier((zs2, zs3, note1, note2, dz))
    zr2 = lax.all_to_all(hop(dz, zs2, zr1), "z", 0, 0, tiled=True)

    run = PER * KV
    part = [zr1[:, k * run:(k + 1) * run].reshape(NZ * PER, KV, UNIT, HD) for k in range(NY)]
    own = unpack_kv(idx1, [part[0]] + [side(part[k], k) for k in range(1, NY)])
    own2 = up(own, 2)
    own1a = lax.ppermute(own, "seq", [(i, i + 1) for i in range(0, NS, 2)])
    zs3, own2, own1a = lax.optimization_barrier((zs3, own2, own1a))
    own1b = lax.ppermute(own2, "seq", [(i + 1, i) for i in range(0, NS, 2)])
    zr3 = lax.all_to_all(zs3, "z", 0, 0, tiled=True)

    came = zr2[:EXT // HOP, SLOT2 - HOP:].reshape(EXT, UNIT, HD)
    ext = jnp.stack([came] + [side(came, k) for k in range(1, NY)])
    ext = lax.dynamic_index_in_dim(ext, k6 & (NY - 1), 0, False).reshape(3, EXT // 3, UNIT, HD)
    ext0 = ext[:, :KV]
    rows, segk = window(
        s.reshape(1), (note2, note1, note), (own2, own1a, own1b, own), (up(ext0, 2), up(ext0, 1), ext0)
    )
    kvt, segq = rows.transpose(1, 0, 2), segment_ids.reshape(ROWS, 1)
    out, done = attend(0, unpack_q(KV, QA, idx2, note, zr2, ext), kvt, segq, segk)
    return attend(1, unpack_q(KV + QA, QB, idx3, note, zr3, ext, done), kvt, segq, segk, out)


def solution(mesh):
    fine = Mesh(mesh.devices.reshape(NZ, NY, NS), ("z", "y", "seq"))
    rows = ("z", "y", "seq")
    return jax.shard_map(
        on_device,
        mesh=fine,
        in_specs=(
            P(rows, None),
            P(rows, None, None, None),
            P(rows),
            P(rows),
            P(("z", "y"), "seq"),
        ),
        out_specs=P(rows, None),
        check_vma=False,
    )
```

time: 163 us -> 162 us (level)
  the two profiles are of different devices: /device:TPU:44 before, /device:TPU:1 now
where the time goes in v7:
time: 162 us; the launch traced here: 161 us
  starting transfers between devices  95.2 us (59%)
  waiting for transfers between devices  36.4 us (22%)
  Pallas kernels  18.9 us (12%)
  local copies, waits for them, and re-layouts  6.37 us (4%)
  other arithmetic  2.86 us (2%)
    ppermute x9, starting transfers between devices, on_device(): lax.ppermute(a, 'y', [(i, (i + n) % NY) for i in range(NY)])  30.9 us
    ppermute x5, starting transfers between devices, on_device(): lax.ppermute(a, 'seq', [(i, i + n) for i in range(NS - n)])  18.2 us
    all_to_all x1, starting transfers between devices, on_device(): lax.all_to_all(zs1.reshape(NZ, SLOT1, UNIT, HD), 'z', 0, 0, tiled=True)  15.8 us
    all_to_all x1, starting transfers between devices, on_device(): zr2 = lax.all_to_all(hop(dz, zs2, zr1), 'z', 0, 0, tiled=True)  12.7 us
    all_to_all x1, starting transfers between devices, on_device(): zr3 = lax.all_to_all(zs3, 'z', 0, 0, tiled=True)  12.7 us
    ppermute x5, waiting for transfers between devices, on_device(): lax.ppermute(a, 'seq', [(i, i + n) for i in range(NS - n)])  12.6 us
    ppermute x9, waiting for transfers between devices, on_device(): lax.ppermute(a, 'y', [(i, (i + n) % NY) for i in range(NY)])  10 us
    all_to_all x1, waiting for transfers between devices, on_device(): zr2 = lax.all_to_all(hop(dz, zs2, zr1), 'z', 0, 0, tiled=True)  9.45 us
  transfers between devices with their start and end apart: 19, of which 9 were waited for; matrix products, arithmetic and copies ran while one was open for 5% of the time, Pallas kernels for 7%

profile of v7, /device:TPU:1, one launch (start us, length us, event | category | flops | bytes accessed | tf_op | source)
XLA Modules:
  0.0 160.7 jit_solution(11715000501118320925)
XLA Ops:
  0.0 3.8 %pack_kv.1 = (bf16[816,4,128]{2,1,0:T(4,128)(2,1)}, s32[192]{0:T(256)}, s32[1]{0:T(128)}) custom-call(s32[1]{0:T(128)} %bitcast.4.me_ref, s32[192]{0:T(256)} %rg_hbm.1, bf16[192,4,4,128]{3,2,1,0:T(4,128)(2,1)} %bitcast.61, bf16[192,4096]{1,0:T(8,128)(2,1)} %q_hbm.1), custom_call_target="tpu_custom_call" | custom-call | tf_op jit(solution)/shard_map/pack_kv/pallas_call | solution.py:88
  3.8 15.8 %all-to-all-start = ((bf16[16,51,4,128]{3,2,1,0:T(4,128)(2,1)}), bf16[16,51,4,128]{3,2,1,0:T(4,128)(2,1)S(1)}, u32[]{:S(2)}, u32[]{:S(2)}) async-start(bf16[16,51,4,128]{3,2,1,0:T(4,128)(2,1)} %bitcast.60), calls=%async_computation | async-start | bytes 1671168 | tf_op jit(solution)/shard_map/all_to_all | solution.py:351
  19.6 2.8 %reshape.79.q_ref = bf16[192,8,4,128]{3,2,1,0:T(4,128)(2,1)S(1)} reshape(bf16[192,4096]{1,0:T(8,128)(2,1)} %q_hbm.1) | data formatting | bytes 3145728 | tf_op jit(solution)/shard_map/reshape | solution.py:354
  25.9 3.2 %collective-permute-start = (bf16[48,8,4,128]{3,2,1,0:T(4,128)(2,1)}, bf16[48,8,4,128]{3,2,1,0:T(4,128)(2,1)S(1)}, u32[]{:S(2)}, u32[]{:S(2)}) collective-permute-start(bf16[48,8,4,128]{3,2,1,0:T(4,128)(2,1)} %get-tuple-element.51), channel_id=1, source_target_pairs={{0,8},{8,16},{16,24},{24,0},{1,9},{9,17},{17,25},{25,1},{2,10},{10... | collective-permute-start | bytes 1179656 | tf_op jit(solution)/shard_map/ppermute | solution.py:333
  29.1 4.5 %collective-permute-start.1 = (bf16[48,8,4,128]{3,2,1,0:T(4,128)(2,1)S(1)}, bf16[48,8,4,128]{3,2,1,0:T(4,128)(2,1)S(1)}, u32[]{:S(2)}, u32[]{:S(2)}) collective-permute-start(bf16[48,8,4,128]{3,2,1,0:T(4,128)(2,1)S(1)} %get-tuple-element.50), channel_id=1, source_target_pairs={{0,16},{8,24},{16,0},{24,8},{1,17},{9,25},{17,1},{25,9},{2,18},{10... | collective-permute-start | bytes 1179656 | tf_op jit(solution)/shard_map/ppermute | solution.py:333
  33.7 3.0 %collective-permute-start.2 = (bf16[48,8,4,128]{3,2,1,0:T(4,128)(2,1)S(1)}, bf16[48,8,4,128]{3,2,1,0:T(4,128)(2,1)S(1)}, u32[]{:S(2)}, u32[]{:S(2)}) collective-permute-start(bf16[48,8,4,128]{3,2,1,0:T(4,128)(2,1)S(1)} %get-tuple-element.49), channel_id=1, source_target_pairs={{0,24},{8,0},{16,8},{24,16},{1,25},{9,1},{17,9},{25,17},{2,26},{10... | collective-permute-start | bytes 1179656 | tf_op jit(solution)/shard_map/ppermute | solution.py:333
  39.4 4.8 %collective-permute-start.3 = (s32[195]{0:T(256)S(1)}, s32[195]{0:T(256)S(1)}, u32[]{:S(2)}, u32[]{:S(2)}) collective-permute-start(s32[195]{0:T(256)S(1)} %pad_add_fusion.note_ref.n0), channel_id=1, source_target_pairs={{0,1},{1,2},{2,3},{3,4},{4,5},{5,6},{6,7},{8,9},{9,10},{10,11},{11... | collective-permute-start | bytes 2348 | tf_op jit(solution)/shard_map/ppermute | solution.py:332
  44.2 3.1 %collective-permute-start.4 = (s32[195]{0:T(256)S(1)}, s32[195]{0:T(256)S(1)}, u32[]{:S(2)}, u32[]{:S(2)}) collective-permute-start(s32[195]{0:T(256)S(1)} %pad_add_fusion.note_ref.n0), channel_id=1, source_target_pairs={{0,2},{1,3},{2,4},{3,5},{4,6},{5,7},{8,10},{9,11},{10,12},{11,13},... | collective-permute-start | bytes 2348 | tf_op jit(solution)/shard_map/ppermute | solution.py:332
  51.5 4.3 %all-to-all-done.came = bf16[16,51,4,128]{3,2,1,0:T(4,128)(2,1)S(1)} async-done(((bf16[16,51,4,128]{3,2,1,0:T(4,128)(2,1)}), bf16[16,51,4,128]{3,2,1,0:T(4,128)(2,1)S(1)}, u32[]{:S(2)}, u32[]{:S(2)}) %all-to-all-start) | async-done | bytes 835616 | tf_op jit(solution)/shard_map/all_to_all | solution.py:351
  56.6 12.7 %all-to-all-start.2 = ((bf16[16,63,4,128]{3,2,1,0:T(4,128)(2,1)}), bf16[16,63,4,128]{3,2,1,0:T(4,128)(2,1)S(1)}, u32[]{:S(2)}, u32[]{:S(2)}) async-start(bf16[16,63,4,128]{3,2,1,0:T(4,128)(2,1)} %hop.1), calls=%async_computation.2 | async-start | bytes 2064384 | tf_op jit(solution)/shard_map/all_to_all | solution.py:359
  69.6 3.2 %collective-permute-start.5 = (bf16[48,4,4,128]{3,2,1,0:T(4,128)(2,1)S(1)}, bf16[48,4,4,128]{3,2,1,0:T(4,128)(2,1)S(1)}, u32[]{:S(2)}, u32[]{:S(2)}) collective-permute-start(bf16[48,4,4,128]{3,2,1,0:T(4,128)(2,1)S(1)} %bitcast.64), channel_id=1, source_target_pairs={{0,8},{8,16},{16,24},{24,0},{1,9},{9,17},{17,25},{25,1},{2,10},{10... | collective-permute-start | bytes 589832 | tf_op jit(solution)/shard_map/ppermute | solution.py:333
  72.8 4.5 %collective-permute-start.6 = (bf16[48,4,4,128]{3,2,1,0:T(4,128)(2,1)S(1)}, bf16[48,4,4,128]{3,2,1,0:T(4,128)(2,1)S(1)}, u32[]{:S(2)}, u32[]{:S(2)}) collective-permute-start(bf16[48,4,4,128]{3,2,1,0:T(4,128)(2,1)S(1)} %bitcast.63), channel_id=1, source_target_pairs={{0,16},{8,24},{16,0},{24,8},{1,17},{9,25},{17,1},{25,9},{2,18},{10... | collective-permute-start | bytes 589832 | tf_op jit(solution)/shard_map/ppermute | solution.py:333
  77.3 3.0 %collective-permute-start.7 = (bf16[48,4,4,128]{3,2,1,0:T(4,128)(2,1)S(1)}, bf16[48,4,4,128]{3,2,1,0:T(4,128)(2,1)S(1)}, u32[]{:S(2)}, u32[]{:S(2)}) collective-permute-start(bf16[48,4,4,128]{3,2,1,0:T(4,128)(2,1)S(1)} %bitcast.62), channel_id=1, source_target_pairs={{0,24},{8,0},{16,8},{24,16},{1,25},{9,1},{17,9},{25,17},{2,26},{10... | collective-permute-start | bytes 589832 | tf_op jit(solution)/shard_map/ppermute | solution.py:333
  80.3 3.5 %collective-permute-done.6.b2 = bf16[48,4,4,128]{3,2,1,0:T(4,128)(2,1)S(1)} collective-permute-done((bf16[48,4,4,128]{3,2,1,0:T(4,128)(2,1)S(1)}, bf16[48,4,4,128]{3,2,1,0:T(4,128)(2,1)S(1)}, u32[]{:S(2)}, u32[]{:S(2)}) %collective-permute-start.6) | collective-permute-done | bytes 196640 | tf_op jit(solution)/shard_map/ppermute | solution.py:333
  85.7 4.0 %collective-permute-start.8 = (bf16[192,4,4,128]{3,2,1,0:T(4,128)(2,1)S(1)}, bf16[192,4,4,128]{3,2,1,0:T(4,128)(2,1)}, u32[]{:S(2)}, u32[]{:S(2)}) collective-permute-start(bf16[192,4,4,128]{3,2,1,0:T(4,128)(2,1)S(1)} %unpack_kv.1), channel_id=1, source_target_pairs={{0,2},{1,3},{2,4},{3,5},{4,6},{5,7},{8,10},{9,11},{10,12},{11,13},... | collective-permute-start | bytes 2359304 | tf_op jit(solution)/shard_map/ppermute | solution.py:332
  91.0 12.6 %collective-permute-done.8 = bf16[192,4,4,128]{3,2,1,0:T(4,128)(2,1)} collective-permute-done((bf16[192,4,4,128]{3,2,1,0:T(4,128)(2,1)S(1)}, bf16[192,4,4,128]{3,2,1,0:T(4,128)(2,1)}, u32[]{:S(2)}, u32[]{:S(2)}) %collective-permute-start.8) | collective-permute-done | bytes 786464 | tf_op jit(solution)/shard_map/ppermute | solution.py:332
  104.5 9.4 %all-to-all-done.2 = bf16[16,63,4,128]{3,2,1,0:T(4,128)(2,1)S(1)} async-done(((bf16[16,63,4,128]{3,2,1,0:T(4,128)(2,1)}), bf16[16,63,4,128]{3,2,1,0:T(4,128)(2,1)S(1)}, u32[]{:S(2)}, u32[]{:S(2)}) %all-to-all-start.2) | async-done | bytes 1032224 | tf_op jit(solution)/shard_map/all_to_all | solution.py:359
  114.0 12.7 %all-to-all-start.1 = ((bf16[16,36,4,128]{3,2,1,0:T(4,128)(2,1)}), bf16[16,36,4,128]{3,2,1,0:T(4,128)(2,1)S(1)}, u32[]{:S(2)}, u32[]{:S(2)}) async-start(bf16[16,36,4,128]{3,2,1,0:T(4,128)(2,1)} %get-tuple-element.32), calls=%async_computation.1 | async-start | bytes 1179648 | tf_op jit(solution)/shard_map/all_to_all | solution.py:368
  126.7 3.6 %collective-permute-start.13 = (bf16[192,4,4,128]{3,2,1,0:T(4,128)(2,1)}, bf16[192,4,4,128]{3,2,1,0:T(4,128)(2,1)}, u32[]{:S(2)}, u32[]{:S(2)}) collective-permute-start(bf16[192,4,4,128]{3,2,1,0:T(4,128)(2,1)} %collective-permute-done.8), channel_id=1, source_target_pairs={{1,0},{3,2},{5,4},{7,6},{9,8},{11,10},{13,12},{15,14},{17,16},{19,... | collective-permute-start | bytes 2359304 | tf_op jit(solution)/shard_map/ppermute | solution.py:367
  130.3 4.6 %collective-permute-start.12 = (bf16[36,4,128]{2,1,0:T(4,128)(2,1)S(1)}, bf16[36,4,128]{2,1,0:T(4,128)(2,1)S(1)}, u32[]{:S(2)}, u32[]{:S(2)}) collective-permute-start(bf16[36,4,128]{2,1,0:T(4,128)(2,1)S(1)} %bitcast.65), channel_id=1, source_target_pairs={{0,24},{8,0},{16,8},{24,16},{1,25},{9,1},{17,9},{25,17},{2,26},{10... | collective-permute-start | bytes 110600 | tf_op jit(solution)/shard_map/ppermute | solution.py:333
  137.2 2.6 %collective-permute-start.10 = (bf16[36,4,128]{2,1,0:T(4,128)(2,1)S(1)}, bf16[36,4,128]{2,1,0:T(4,128)(2,1)S(1)}, u32[]{:S(2)}, u32[]{:S(2)}) collective-permute-start(bf16[36,4,128]{2,1,0:T(4,128)(2,1)S(1)} %bitcast.67), channel_id=1, source_target_pairs={{0,8},{8,16},{16,24},{24,0},{1,9},{9,17},{17,25},{25,1},{2,10},{10... | collective-permute-start | bytes 110600 | tf_op jit(solution)/shard_map/ppermute | solution.py:333
  143.5 3.1 %collective-permute-start.14 = (bf16[3,4,4,128]{3,2,1,0:T(4,128)(2,1)S(1)}, bf16[3,4,4,128]{3,2,1,0:T(4,128)(2,1)S(1)}, u32[]{:S(2)}, u32[]{:S(2)}) collective-permute-start(bf16[3,4,4,128]{3,2,1,0:T(4,128)(2,1)S(1)} %slice.49), channel_id=1, source_target_pairs={{0,2},{1,3},{2,4},{3,5},{4,6},{5,7},{8,10},{9,11},{10,12},{11,13},... | collective-permute-start | bytes 36872 | tf_op jit(solution)/shard_map/ppermute | solution.py:332
  146.7 3.1 %collective-permute-start.15 = (bf16[3,4,4,128]{3,2,1,0:T(4,128)(2,1)S(1)}, bf16[3,4,4,128]{3,2,1,0:T(4,128)(2,1)S(1)}, u32[]{:S(2)}, u32[]{:S(2)}) collective-permute-start(bf16[3,4,4,128]{3,2,1,0:T(4,128)(2,1)S(1)} %slice.49), channel_id=1, source_target_pairs={{0,1},{1,2},{2,3},{3,4},{4,5},{5,6},{6,7},{8,9},{9,10},{10,11},{11... | collective-permute-start | bytes 36872 | tf_op jit(solution)/shard_map/ppermute | solution.py:332
  153.5 3.7 %attend.2 = (bf16[192,4096]{1,0:T(8,128)(2,1)}, f32[8,128]{1,0:T(8,128)S(1)}) custom-call(bf16[20,192,128]{2,1,0:T(8,128)(2,1)S(1)} %bitcast.48, bf16[16,576,128]{2,1,0:T(8,128)(2,1)S(1)} %bitcast.42, s32[192,1]{1,0:T(8,128)S(1)} %copy.13.segq_ref, s32[1,576]{1,0:T(1,128)S(1)} %get-tuple-element.40.segk_ref), custom_call_target="tpu_custom_call" | custom-call | flops 1132462080 | bytes 4194304 | tf_op jit(solution)/shard_map/attend/pallas_call | solution.py:314
  (47 shorter events, 27.9 us)
Async XLA Ops:
  3.8 52.0 %all-to-all-start = ((bf16[16,51,4,128]{3,2,1,0:T(4,128)(2,1)}), bf16[16,51,4,128]{3,2,1,0:T(4,128)(2,1)S(1)}, u32[]{:S(2)}, u32[]{:S(2)}) async-start(bf16[16,51,4,128]{3,2,1,0:T(4,128)(2,1)} %bitcast.60), calls=%async_computation | async-start | bytes 1671168 | tf_op jit(solution)/shard_map/all_to_all | solution.py:351
  19.6 2.8 %copy-start.2 = (s32[192]{0:T(256)S(1)}, s32[192]{0:T(256)}, u32[]{:S(2)}) copy-start(s32[192]{0:T(256)} %get-tuple-element.25.tile_ref) | copy-start | bytes 2308
  24.6 12.0 %copy-start.4 = (s32[192]{0:T(256)S(1)}, s32[192]{0:T(256)}, u32[]{:S(2)}) copy-start(s32[192]{0:T(256)} %param.8) | copy-start | bytes 2308
  24.6 12.8 %copy-start.3 = (s32[1,192]{1,0:T(1,128)S(1)}, s32[1,192]{1,0:T(1,128)}, u32[]{:S(2)}) copy-start(s32[1,192]{1,0:T(1,128)} %param.9) | copy-start | bytes 2308
  25.9 22.1 %collective-permute-start = (bf16[48,8,4,128]{3,2,1,0:T(4,128)(2,1)}, bf16[48,8,4,128]{3,2,1,0:T(4,128)(2,1)S(1)}, u32[]{:S(2)}, u32[]{:S(2)}) collective-permute-start(bf16[48,8,4,128]{3,2,1,0:T(4,128)(2,1)} %get-tuple-element.51), channel_id=1, source_target_pairs={{0,8},{8,16},{16,24},{24,0},{1,9},{9,17},{17,25},{25,1},{2,10},{10... | collective-permute-start | bytes 1179656 | tf_op jit(solution)/shard_map/ppermute | solution.py:333
  29.1 19.4 %collective-permute-start.1 = (bf16[48,8,4,128]{3,2,1,0:T(4,128)(2,1)S(1)}, bf16[48,8,4,128]{3,2,1,0:T(4,128)(2,1)S(1)}, u32[]{:S(2)}, u32[]{:S(2)}) collective-permute-start(bf16[48,8,4,128]{3,2,1,0:T(4,128)(2,1)S(1)} %get-tuple-element.50), channel_id=1, source_target_pairs={{0,16},{8,24},{16,0},{24,8},{1,17},{9,25},{17,1},{25,9},{2,18},{10... | collective-permute-start | bytes 1179656 | tf_op jit(solution)/shard_map/ppermute | solution.py:333
  33.7 16.4 %collective-permute-start.2 = (bf16[48,8,4,128]{3,2,1,0:T(4,128)(2,1)S(1)}, bf16[48,8,4,128]{3,2,1,0:T(4,128)(2,1)S(1)}, u32[]{:S(2)}, u32[]{:S(2)}) collective-permute-start(bf16[48,8,4,128]{3,2,1,0:T(4,128)(2,1)S(1)} %get-tuple-element.49), channel_id=1, source_target_pairs={{0,24},{8,0},{16,8},{24,16},{1,25},{9,1},{17,9},{25,17},{2,26},{10... | collective-permute-start | bytes 1179656 | tf_op jit(solution)/shard_map/ppermute | solution.py:333
  39.4 12.1 %collective-permute-start.3 = (s32[195]{0:T(256)S(1)}, s32[195]{0:T(256)S(1)}, u32[]{:S(2)}, u32[]{:S(2)}) collective-permute-start(s32[195]{0:T(256)S(1)} %pad_add_fusion.note_ref.n0), channel_id=1, source_target_pairs={{0,1},{1,2},{2,3},{3,4},{4,5},{5,6},{6,7},{8,9},{9,10},{10,11},{11... | collective-permute-start | bytes 2348 | tf_op jit(solution)/shard_map/ppermute | solution.py:332
  44.2 7.3 %collective-permute-start.4 = (s32[195]{0:T(256)S(1)}, s32[195]{0:T(256)S(1)}, u32[]{:S(2)}, u32[]{:S(2)}) collective-permute-start(s32[195]{0:T(256)S(1)} %pad_add_fusion.note_ref.n0), channel_id=1, source_target_pairs={{0,2},{1,3},{2,4},{3,5},{4,6},{5,7},{8,10},{9,11},{10,12},{11,13},... | collective-permute-start | bytes 2348 | tf_op jit(solution)/shard_map/ppermute | solution.py:332
  56.6 57.4 %all-to-all-start.2 = ((bf16[16,63,4,128]{3,2,1,0:T(4,128)(2,1)}), bf16[16,63,4,128]{3,2,1,0:T(4,128)(2,1)S(1)}, u32[]{:S(2)}, u32[]{:S(2)}) async-start(bf16[16,63,4,128]{3,2,1,0:T(4,128)(2,1)} %hop.1), calls=%async_computation.2 | async-start | bytes 2064384 | tf_op jit(solution)/shard_map/all_to_all | solution.py:359
  69.6 10.7 %collective-permute-start.5 = (bf16[48,4,4,128]{3,2,1,0:T(4,128)(2,1)S(1)}, bf16[48,4,4,128]{3,2,1,0:T(4,128)(2,1)S(1)}, u32[]{:S(2)}, u32[]{:S(2)}) collective-permute-start(bf16[48,4,4,128]{3,2,1,0:T(4,128)(2,1)S(1)} %bitcast.64), channel_id=1, source_target_pairs={{0,8},{8,16},{16,24},{24,0},{1,9},{9,17},{17,25},{25,1},{2,10},{10... | collective-permute-start | bytes 589832 | tf_op jit(solution)/shard_map/ppermute | solution.py:333
  72.8 11.0 %collective-permute-start.6 = (bf16[48,4,4,128]{3,2,1,0:T(4,128)(2,1)S(1)}, bf16[48,4,4,128]{3,2,1,0:T(4,128)(2,1)S(1)}, u32[]{:S(2)}, u32[]{:S(2)}) collective-permute-start(bf16[48,4,4,128]{3,2,1,0:T(4,128)(2,1)S(1)} %bitcast.63), channel_id=1, source_target_pairs={{0,16},{8,24},{16,0},{24,8},{1,17},{9,25},{17,1},{25,9},{2,18},{10... | collective-permute-start | bytes 589832 | tf_op jit(solution)/shard_map/ppermute | solution.py:333
  77.3 7.4 %collective-permute-start.7 = (bf16[48,4,4,128]{3,2,1,0:T(4,128)(2,1)S(1)}, bf16[48,4,4,128]{3,2,1,0:T(4,128)(2,1)S(1)}, u32[]{:S(2)}, u32[]{:S(2)}) collective-permute-start(bf16[48,4,4,128]{3,2,1,0:T(4,128)(2,1)S(1)} %bitcast.62), channel_id=1, source_target_pairs={{0,24},{8,0},{16,8},{24,16},{1,25},{9,1},{17,9},{25,17},{2,26},{10... | collective-permute-start | bytes 589832 | tf_op jit(solution)/shard_map/ppermute | solution.py:333
  85.7 17.9 %collective-permute-start.8 = (bf16[192,4,4,128]{3,2,1,0:T(4,128)(2,1)S(1)}, bf16[192,4,4,128]{3,2,1,0:T(4,128)(2,1)}, u32[]{:S(2)}, u32[]{:S(2)}) collective-permute-start(bf16[192,4,4,128]{3,2,1,0:T(4,128)(2,1)S(1)} %unpack_kv.1), channel_id=1, source_target_pairs={{0,2},{1,3},{2,4},{3,5},{4,6},{5,7},{8,10},{9,11},{10,12},{11,13},... | collective-permute-start | bytes 2359304 | tf_op jit(solution)/shard_map/ppermute | solution.py:332
  89.7 13.9 %collective-permute-start.9 = (bf16[192,4,4,128]{3,2,1,0:T(4,128)(2,1)S(1)}, bf16[192,4,4,128]{3,2,1,0:T(4,128)(2,1)S(1)}, u32[]{:S(2)}, u32[]{:S(2)}) collective-permute-start(bf16[192,4,4,128]{3,2,1,0:T(4,128)(2,1)S(1)} %unpack_kv.1), channel_id=1, source_target_pairs={{0,1},{2,3},{4,5},{6,7},{8,9},{10,11},{12,13},{14,15},{16,17},{18,... | collective-permute-start | bytes 2359304 | tf_op jit(solution)/shard_map/ppermute | solution.py:365
  103.6 0.9 copy-start
  114.0 43.2 %all-to-all-start.1 = ((bf16[16,36,4,128]{3,2,1,0:T(4,128)(2,1)}), bf16[16,36,4,128]{3,2,1,0:T(4,128)(2,1)S(1)}, u32[]{:S(2)}, u32[]{:S(2)}) async-start(bf16[16,36,4,128]{3,2,1,0:T(4,128)(2,1)} %get-tuple-element.32), calls=%async_computation.1 | async-start | bytes 1179648 | tf_op jit(solution)/shard_map/all_to_all | solution.py:368
  126.7 24.4 %collective-permute-start.13 = (bf16[192,4,4,128]{3,2,1,0:T(4,128)(2,1)}, bf16[192,4,4,128]{3,2,1,0:T(4,128)(2,1)}, u32[]{:S(2)}, u32[]{:S(2)}) collective-permute-start(bf16[192,4,4,128]{3,2,1,0:T(4,128)(2,1)} %collective-permute-done.8), channel_id=1, source_target_pairs={{1,0},{3,2},{5,4},{7,6},{9,8},{11,10},{13,12},{15,14},{17,16},{19,... | collective-permute-start | bytes 2359304 | tf_op jit(solution)/shard_map/ppermute | solution.py:367
  130.3 9.5 %collective-permute-start.12 = (bf16[36,4,128]{2,1,0:T(4,128)(2,1)S(1)}, bf16[36,4,128]{2,1,0:T(4,128)(2,1)S(1)}, u32[]{:S(2)}, u32[]{:S(2)}) collective-permute-start(bf16[36,4,128]{2,1,0:T(4,128)(2,1)S(1)} %bitcast.65), channel_id=1, source_target_pairs={{0,24},{8,0},{16,8},{24,16},{1,25},{9,1},{17,9},{25,17},{2,26},{10... | collective-permute-start | bytes 110600 | tf_op jit(solution)/shard_map/ppermute | solution.py:333
  135.0 6.5 %collective-permute-start.11 = (bf16[36,4,128]{2,1,0:T(4,128)(2,1)S(1)}, bf16[36,4,128]{2,1,0:T(4,128)(2,1)S(1)}, u32[]{:S(2)}, u32[]{:S(2)}) collective-permute-start(bf16[36,4,128]{2,1,0:T(4,128)(2,1)S(1)} %bitcast.66), channel_id=1, source_target_pairs={{0,16},{8,24},{16,0},{24,8},{1,17},{9,25},{17,1},{25,9},{2,18},{10... | collective-permute-start | bytes 110600 | tf_op jit(solution)/shard_map/ppermute | solution.py:333
  137.2 6.2 %collective-permute-start.10 = (bf16[36,4,128]{2,1,0:T(4,128)(2,1)S(1)}, bf16[36,4,128]{2,1,0:T(4,128)(2,1)S(1)}, u32[]{:S(2)}, u32[]{:S(2)}) collective-permute-start(bf16[36,4,128]{2,1,0:T(4,128)(2,1)S(1)} %bitcast.67), channel_id=1, source_target_pairs={{0,8},{8,16},{16,24},{24,0},{1,9},{9,17},{17,25},{25,1},{2,10},{10... | collective-permute-start | bytes 110600 | tf_op jit(solution)/shard_map/ppermute | solution.py:333
  143.5 7.5 %collective-permute-start.14 = (bf16[3,4,4,128]{3,2,1,0:T(4,128)(2,1)S(1)}, bf16[3,4,4,128]{3,2,1,0:T(4,128)(2,1)S(1)}, u32[]{:S(2)}, u32[]{:S(2)}) collective-permute-start(bf16[3,4,4,128]{3,2,1,0:T(4,128)(2,1)S(1)} %slice.49), channel_id=1, source_target_pairs={{0,2},{1,3},{2,4},{3,5},{4,6},{5,7},{8,10},{9,11},{10,12},{11,13},... | collective-permute-start | bytes 36872 | tf_op jit(solution)/shard_map/ppermute | solution.py:332
  146.7 4.4 %collective-permute-start.15 = (bf16[3,4,4,128]{3,2,1,0:T(4,128)(2,1)S(1)}, bf16[3,4,4,128]{3,2,1,0:T(4,128)(2,1)S(1)}, u32[]{:S(2)}, u32[]{:S(2)}) collective-permute-start(bf16[3,4,4,128]{3,2,1,0:T(4,128)(2,1)S(1)} %slice.49), channel_id=1, source_target_pairs={{0,1},{1,2},{2,3},{3,4},{4,5},{5,6},{6,7},{8,9},{9,10},{10,11},{11... | collective-permute-start | bytes 36872 | tf_op jit(solution)/shard_map/ppermute | solution.py:332
  149.9 1.1 copy-start.1

commit v8 on v7

--- a/solution.py
+++ b/solution.py
@@ -42,7 +42,6 @@
         nxt[d] = (d // NY * SLOT1 + ((d % NY - y) & (NY - 1)) * PER * KV) * 8
     for e in range(4):
         xrow[e] = 0
-    held[...] = jnp.zeros_like(held)
     plan.wait()
 
     def step(i, far):
@@ -368,8 +367,9 @@
     zr3 = lax.all_to_all(zs3, "z", 0, 0, tiled=True)
 
     came = zr2[:EXT // HOP, SLOT2 - HOP:].reshape(EXT, UNIT, HD)
-    ext = jnp.stack([came] + [side(came, k) for k in range(1, NY)])
-    ext = lax.dynamic_index_in_dim(ext, k6 & (NY - 1), 0, False).reshape(3, EXT // 3, UNIT, HD)
+    came = jnp.where((k6 & 1) != 0, side(came, 1), came)
+    came = jnp.where((k6 & 2) != 0, side(came, 2), came)
+    ext = came.reshape(3, EXT // 3, UNIT, HD)
     ext0 = ext[:, :KV]
     rows, segk = window(
         s.reshape(1), (note2, note1, note), (own2, own1a, own1b, own), (up(ext0, 2), up(ext0, 1), ext0)

time: 162 us -> 162 us (level)
  waiting for transfers between devices: 36.4 us -> 38.8 us
  starting transfers between devices: 95.2 us -> 93.2 us
    ppermute x9 -> x8, starting transfers between devices: 30.9 us -> 28.4 us  [on_device(): lax.ppermute(a, 'y', [(i, (i + n) % NY) for i in range(NY)])]
    ppermute x9 -> x8, waiting for transfers between devices: 10 us -> 12.4 us  [on_device(): lax.ppermute(a, 'y', [(i, (i + n) % NY) for i in range(NY)])]
  transfers between devices with their start and end apart: 19 -> 18, of which waited for: 9 -> 9; matrix products, arithmetic and copies ran while one was open for 5% -> 5% of each run, Pallas kernels for 7% -> 7%
where the time goes in v8:
time: 162 us; the launch traced here: 161 us
  starting transfers between devices  93.2 us (58%)
  waiting for transfers between devices  38.8 us (24%)
  Pallas kernels  18.9 us (12%)
  local copies, waits for them, and re-layouts  6.37 us (4%)
  other arithmetic  2.79 us (2%)
    ppermute x8, starting transfers between devices, on_device(): lax.ppermute(a, 'y', [(i, (i + n) % NY) for i in range(NY)])  28.4 us
    ppermute x5, starting transfers between devices, on_device(): lax.ppermute(a, 'seq', [(i, i + n) for i in range(NS - n)])  18.7 us
    all_to_all x1, starting transfers between devices, on_device(): lax.all_to_all(zs1.reshape(NZ, SLOT1, UNIT, HD), 'z', 0, 0, tiled=True)  15.8 us
    all_to_all x1, starting transfers between devices, on_device(): zr2 = lax.all_to_all(hop(dz, zs2, zr1), 'z', 0, 0, tiled=True)  12.7 us
    all_to_all x1, starting transfers between devices, on_device(): zr3 = lax.all_to_all(zs3, 'z', 0, 0, tiled=True)  12.7 us
    ppermute x5, waiting for transfers between devices, on_device(): lax.ppermute(a, 'seq', [(i, i + n) for i in range(NS - n)])  12.6 us
    ppermute x8, waiting for transfers between devices, on_device(): lax.ppermute(a, 'y', [(i, (i + n) % NY) for i in range(NY)])  12.4 us
    all_to_all x1, waiting for transfers between devices, on_device(): zr2 = lax.all_to_all(hop(dz, zs2, zr1), 'z', 0, 0, tiled=True)  9.45 us
  transfers between devices with their start and end apart: 18, of which 9 were waited for; matrix products, arithmetic and copies ran while one was open for 5% of the time, Pallas kernels for 7%

profile of v8, /device:TPU:1, one launch (start us, length us, event | category | flops | bytes accessed | tf_op | source)
XLA Modules:
  0.0 160.9 jit_solution(12743038988002129883)
XLA Ops:
  0.0 3.8 %pack_kv.1 = (bf16[816,4,128]{2,1,0:T(4,128)(2,1)}, s32[192]{0:T(256)}, s32[1]{0:T(128)}) custom-call(s32[1]{0:T(128)} %bitcast.4.me_ref, s32[192]{0:T(256)} %rg_hbm.1, bf16[192,4,4,128]{3,2,1,0:T(4,128)(2,1)} %bitcast.61, bf16[192,4096]{1,0:T(8,128)(2,1)} %q_hbm.1), custom_call_target="tpu_custom_call" | custom-call | tf_op jit(solution)/shard_map/pack_kv/pallas_call | solution.py:87
  3.8 15.8 %all-to-all-start = ((bf16[16,51,4,128]{3,2,1,0:T(4,128)(2,1)}), bf16[16,51,4,128]{3,2,1,0:T(4,128)(2,1)S(1)}, u32[]{:S(2)}, u32[]{:S(2)}) async-start(bf16[16,51,4,128]{3,2,1,0:T(4,128)(2,1)} %bitcast.60), calls=%async_computation | async-start | bytes 1671168 | tf_op jit(solution)/shard_map/all_to_all | solution.py:350
  25.9 3.2 %collective-permute-start = (bf16[48,8,4,128]{3,2,1,0:T(4,128)(2,1)}, bf16[48,8,4,128]{3,2,1,0:T(4,128)(2,1)S(1)}, u32[]{:S(2)}, u32[]{:S(2)}) collective-permute-start(bf16[48,8,4,128]{3,2,1,0:T(4,128)(2,1)} %get-tuple-element.51), channel_id=1, source_target_pairs={{0,8},{8,16},{16,24},{24,0},{1,9},{9,17},{17,25},{25,1},{2,10},{10... | collective-permute-start | bytes 1179656 | tf_op jit(solution)/shard_map/ppermute | solution.py:332
  29.1 4.5 %collective-permute-start.1 = (bf16[48,8,4,128]{3,2,1,0:T(4,128)(2,1)S(1)}, bf16[48,8,4,128]{3,2,1,0:T(4,128)(2,1)S(1)}, u32[]{:S(2)}, u32[]{:S(2)}) collective-permute-start(bf16[48,8,4,128]{3,2,1,0:T(4,128)(2,1)S(1)} %get-tuple-element.50), channel_id=1, source_target_pairs={{0,16},{8,24},{16,0},{24,8},{1,17},{9,25},{17,1},{25,9},{2,18},{10... | collective-permute-start | bytes 1179656 | tf_op jit(solution)/shard_map/ppermute | solution.py:332
  33.7 3.0 %collective-permute-start.2 = (bf16[48,8,4,128]{3,2,1,0:T(4,128)(2,1)S(1)}, bf16[48,8,4,128]{3,2,1,0:T(4,128)(2,1)S(1)}, u32[]{:S(2)}, u32[]{:S(2)}) collective-permute-start(bf16[48,8,4,128]{3,2,1,0:T(4,128)(2,1)S(1)} %get-tuple-element.49), channel_id=1, source_target_pairs={{0,24},{8,0},{16,8},{24,16},{1,25},{9,1},{17,9},{25,17},{2,26},{10... | collective-permute-start | bytes 1179656 | tf_op jit(solution)/shard_map/ppermute | solution.py:332
  39.4 4.8 %collective-permute-start.3 = (s32[195]{0:T(256)S(1)}, s32[195]{0:T(256)S(1)}, u32[]{:S(2)}, u32[]{:S(2)}) collective-permute-start(s32[195]{0:T(256)S(1)} %pad_add_fusion.note_ref.n0), channel_id=1, source_target_pairs={{0,1},{1,2},{2,3},{3,4},{4,5},{5,6},{6,7},{8,9},{9,10},{10,11},{11... | collective-permute-start | bytes 2348 | tf_op jit(solution)/shard_map/ppermute | solution.py:331
  44.2 3.1 %collective-permute-start.4 = (s32[195]{0:T(256)S(1)}, s32[195]{0:T(256)S(1)}, u32[]{:S(2)}, u32[]{:S(2)}) collective-permute-start(s32[195]{0:T(256)S(1)} %pad_add_fusion.note_ref.n0), channel_id=1, source_target_pairs={{0,2},{1,3},{2,4},{3,5},{4,6},{5,7},{8,10},{9,11},{10,12},{11,13},... | collective-permute-start | bytes 2348 | tf_op jit(solution)/shard_map/ppermute | solution.py:331
  51.5 4.3 %all-to-all-done.came = bf16[16,51,4,128]{3,2,1,0:T(4,128)(2,1)S(1)} async-done(((bf16[16,51,4,128]{3,2,1,0:T(4,128)(2,1)}), bf16[16,51,4,128]{3,2,1,0:T(4,128)(2,1)S(1)}, u32[]{:S(2)}, u32[]{:S(2)}) %all-to-all-start) | async-done | bytes 835616 | tf_op jit(solution)/shard_map/all_to_all | solution.py:350
  56.6 12.7 %all-to-all-start.2 = ((bf16[16,63,4,128]{3,2,1,0:T(4,128)(2,1)}), bf16[16,63,4,128]{3,2,1,0:T(4,128)(2,1)S(1)}, u32[]{:S(2)}, u32[]{:S(2)}) async-start(bf16[16,63,4,128]{3,2,1,0:T(4,128)(2,1)} %hop.1), calls=%async_computation.2 | async-start | bytes 2064384 | tf_op jit(solution)/shard_map/all_to_all | solution.py:358
  69.6 3.2 %collective-permute-start.5 = (bf16[48,4,4,128]{3,2,1,0:T(4,128)(2,1)S(1)}, bf16[48,4,4,128]{3,2,1,0:T(4,128)(2,1)S(1)}, u32[]{:S(2)}, u32[]{:S(2)}) collective-permute-start(bf16[48,4,4,128]{3,2,1,0:T(4,128)(2,1)S(1)} %bitcast.64), channel_id=1, source_target_pairs={{0,8},{8,16},{16,24},{24,0},{1,9},{9,17},{17,25},{25,1},{2,10},{10... | collective-permute-start | bytes 589832 | tf_op jit(solution)/shard_map/ppermute | solution.py:332
  72.8 4.5 %collective-permute-start.6 = (bf16[48,4,4,128]{3,2,1,0:T(4,128)(2,1)S(1)}, bf16[48,4,4,128]{3,2,1,0:T(4,128)(2,1)S(1)}, u32[]{:S(2)}, u32[]{:S(2)}) collective-permute-start(bf16[48,4,4,128]{3,2,1,0:T(4,128)(2,1)S(1)} %bitcast.63), channel_id=1, source_target_pairs={{0,16},{8,24},{16,0},{24,8},{1,17},{9,25},{17,1},{25,9},{2,18},{10... | collective-permute-start | bytes 589832 | tf_op jit(solution)/shard_map/ppermute | solution.py:332
  77.3 3.0 %collective-permute-start.7 = (bf16[48,4,4,128]{3,2,1,0:T(4,128)(2,1)S(1)}, bf16[48,4,4,128]{3,2,1,0:T(4,128)(2,1)S(1)}, u32[]{:S(2)}, u32[]{:S(2)}) collective-permute-start(bf16[48,4,4,128]{3,2,1,0:T(4,128)(2,1)S(1)} %bitcast.62), channel_id=1, source_target_pairs={{0,24},{8,0},{16,8},{24,16},{1,25},{9,1},{17,9},{25,17},{2,26},{10... | collective-permute-start | bytes 589832 | tf_op jit(solution)/shard_map/ppermute | solution.py:332
  80.3 3.5 %collective-permute-done.6.b2 = bf16[48,4,4,128]{3,2,1,0:T(4,128)(2,1)S(1)} collective-permute-done((bf16[48,4,4,128]{3,2,1,0:T(4,128)(2,1)S(1)}, bf16[48,4,4,128]{3,2,1,0:T(4,128)(2,1)S(1)}, u32[]{:S(2)}, u32[]{:S(2)}) %collective-permute-start.6) | collective-permute-done | bytes 196640 | tf_op jit(solution)/shard_map/ppermute | solution.py:332
  85.7 4.0 %collective-permute-start.8 = (bf16[192,4,4,128]{3,2,1,0:T(4,128)(2,1)S(1)}, bf16[192,4,4,128]{3,2,1,0:T(4,128)(2,1)}, u32[]{:S(2)}, u32[]{:S(2)}) collective-permute-start(bf16[192,4,4,128]{3,2,1,0:T(4,128)(2,1)S(1)} %unpack_kv.1), channel_id=1, source_target_pairs={{0,2},{1,3},{2,4},{3,5},{4,6},{5,7},{8,10},{9,11},{10,12},{11,13},... | collective-permute-start | bytes 2359304 | tf_op jit(solution)/shard_map/ppermute | solution.py:331
  91.0 12.6 %collective-permute-done.8 = bf16[192,4,4,128]{3,2,1,0:T(4,128)(2,1)} collective-permute-done((bf16[192,4,4,128]{3,2,1,0:T(4,128)(2,1)S(1)}, bf16[192,4,4,128]{3,2,1,0:T(4,128)(2,1)}, u32[]{:S(2)}, u32[]{:S(2)}) %collective-permute-start.8) | collective-permute-done | bytes 786464 | tf_op jit(solution)/shard_map/ppermute | solution.py:331
  104.5 9.4 %all-to-all-done.2 = bf16[16,63,4,128]{3,2,1,0:T(4,128)(2,1)S(1)} async-done(((bf16[16,63,4,128]{3,2,1,0:T(4,128)(2,1)}), bf16[16,63,4,128]{3,2,1,0:T(4,128)(2,1)S(1)}, u32[]{:S(2)}, u32[]{:S(2)}) %all-to-all-start.2) | async-done | bytes 1032224 | tf_op jit(solution)/shard_map/all_to_all | solution.py:358
  114.0 12.7 %all-to-all-start.1 = ((bf16[16,36,4,128]{3,2,1,0:T(4,128)(2,1)}), bf16[16,36,4,128]{3,2,1,0:T(4,128)(2,1)S(1)}, u32[]{:S(2)}, u32[]{:S(2)}) async-start(bf16[16,36,4,128]{3,2,1,0:T(4,128)(2,1)} %get-tuple-element.32), calls=%async_computation.1 | async-start | bytes 1179648 | tf_op jit(solution)/shard_map/all_to_all | solution.py:367
  126.7 3.6 %collective-permute-start.12 = (bf16[192,4,4,128]{3,2,1,0:T(4,128)(2,1)}, bf16[192,4,4,128]{3,2,1,0:T(4,128)(2,1)}, u32[]{:S(2)}, u32[]{:S(2)}) collective-permute-start(bf16[192,4,4,128]{3,2,1,0:T(4,128)(2,1)} %collective-permute-done.8), channel_id=1, source_target_pairs={{1,0},{3,2},{5,4},{7,6},{9,8},{11,10},{13,12},{15,14},{17,16},{19,... | collective-permute-start | bytes 2359304 | tf_op jit(solution)/shard_map/ppermute | solution.py:366
  130.3 3.2 %collective-permute-start.10 = (bf16[36,4,128]{2,1,0:T(4,128)(2,1)S(1)}, bf16[36,4,128]{2,1,0:T(4,128)(2,1)S(1)}, u32[]{:S(2)}, u32[]{:S(2)}) collective-permute-start(bf16[36,4,128]{2,1,0:T(4,128)(2,1)S(1)} %bitcast.66), channel_id=1, source_target_pairs={{0,8},{8,16},{16,24},{24,0},{1,9},{9,17},{17,25},{25,1},{2,10},{10... | collective-permute-start | bytes 110600 | tf_op jit(solution)/shard_map/ppermute | solution.py:332
  136.3 3.8 %collective-permute-start.11 = (bf16[36,4,128]{2,1,0:T(4,128)(2,1)S(1)}, bf16[36,4,128]{2,1,0:T(4,128)(2,1)S(1)}, u32[]{:S(2)}, u32[]{:S(2)}) collective-permute-start(bf16[36,4,128]{2,1,0:T(4,128)(2,1)S(1)} %broadcast_select_fusion), channel_id=1, source_target_pairs={{0,16},{8,24},{16,0},{24,8},{1,17},{9,25},{17,1},{25,9},{2,18},{10... | collective-permute-start | bytes 110600 | tf_op jit(solution)/shard_map/ppermute | solution.py:332
  140.2 3.0 %collective-permute-done.11 = bf16[36,4,128]{2,1,0:T(4,128)(2,1)S(1)} collective-permute-done((bf16[36,4,128]{2,1,0:T(4,128)(2,1)S(1)}, bf16[36,4,128]{2,1,0:T(4,128)(2,1)S(1)}, u32[]{:S(2)}, u32[]{:S(2)}) %collective-permute-start.11) | collective-permute-done | bytes 36896 | tf_op jit(solution)/shard_map/ppermute | solution.py:332
  143.2 3.1 %collective-permute-start.13 = (bf16[3,4,4,128]{3,2,1,0:T(4,128)(2,1)S(1)}, bf16[3,4,4,128]{3,2,1,0:T(4,128)(2,1)S(1)}, u32[]{:S(2)}, u32[]{:S(2)}) collective-permute-start(bf16[3,4,4,128]{3,2,1,0:T(4,128)(2,1)S(1)} %slice.49), channel_id=1, source_target_pairs={{0,2},{1,3},{2,4},{3,5},{4,6},{5,7},{8,10},{9,11},{10,12},{11,13},... | collective-permute-start | bytes 36872 | tf_op jit(solution)/shard_map/ppermute | solution.py:331
  146.4 3.7 %collective-permute-start.14 = (bf16[3,4,4,128]{3,2,1,0:T(4,128)(2,1)S(1)}, bf16[3,4,4,128]{3,2,1,0:T(4,128)(2,1)S(1)}, u32[]{:S(2)}, u32[]{:S(2)}) collective-permute-start(bf16[3,4,4,128]{3,2,1,0:T(4,128)(2,1)S(1)} %slice.49), channel_id=1, source_target_pairs={{0,1},{1,2},{2,3},{3,4},{4,5},{5,6},{6,7},{8,9},{9,10},{10,11},{11... | collective-permute-start | bytes 36872 | tf_op jit(solution)/shard_map/ppermute | solution.py:331
  153.7 3.6 %attend.2 = (bf16[192,4096]{1,0:T(8,128)(2,1)}, f32[8,128]{1,0:T(8,128)S(1)}) custom-call(bf16[20,192,128]{2,1,0:T(8,128)(2,1)S(1)} %bitcast.48, bf16[16,576,128]{2,1,0:T(8,128)(2,1)S(1)} %bitcast.42, s32[192,1]{1,0:T(8,128)S(1)} %copy.13.segq_ref, s32[1,576]{1,0:T(1,128)S(1)} %get-tuple-element.40.segk_ref), custom_call_target="tpu_custom_call" | custom-call | flops 1132462080 | bytes 4194304 | tf_op jit(solution)/shard_map/attend/pallas_call | solution.py:313
  (46 shorter events, 27.7 us)
Async XLA Ops:
  3.8 52.0 %all-to-all-start = ((bf16[16,51,4,128]{3,2,1,0:T(4,128)(2,1)}), bf16[16,51,4,128]{3,2,1,0:T(4,128)(2,1)S(1)}, u32[]{:S(2)}, u32[]{:S(2)}) async-start(bf16[16,51,4,128]{3,2,1,0:T(4,128)(2,1)} %bitcast.60), calls=%async_computation | async-start | bytes 1671168 | tf_op jit(solution)/shard_map/all_to_all | solution.py:350
  19.6 2.8 %copy-start.2 = (s32[192]{0:T(256)S(1)}, s32[192]{0:T(256)}, u32[]{:S(2)}) copy-start(s32[192]{0:T(256)} %get-tuple-element.25.tile_ref) | copy-start | bytes 2308
  24.6 12.0 %copy-start.4 = (s32[192]{0:T(256)S(1)}, s32[192]{0:T(256)}, u32[]{:S(2)}) copy-start(s32[192]{0:T(256)} %param.8) | copy-start | bytes 2308
  24.6 12.8 %copy-start.3 = (s32[1,192]{1,0:T(1,128)S(1)}, s32[1,192]{1,0:T(1,128)}, u32[]{:S(2)}) copy-start(s32[1,192]{1,0:T(1,128)} %param.9) | copy-start | bytes 2308
  25.9 22.0 %collective-permute-start = (bf16[48,8,4,128]{3,2,1,0:T(4,128)(2,1)}, bf16[48,8,4,128]{3,2,1,0:T(4,128)(2,1)S(1)}, u32[]{:S(2)}, u32[]{:S(2)}) collective-permute-start(bf16[48,8,4,128]{3,2,1,0:T(4,128)(2,1)} %get-tuple-element.51), channel_id=1, source_target_pairs={{0,8},{8,16},{16,24},{24,0},{1,9},{9,17},{17,25},{25,1},{2,10},{10... | collective-permute-start | bytes 1179656 | tf_op jit(solution)/shard_map/ppermute | solution.py:332
  29.1 19.4 %collective-permute-start.1 = (bf16[48,8,4,128]{3,2,1,0:T(4,128)(2,1)S(1)}, bf16[48,8,4,128]{3,2,1,0:T(4,128)(2,1)S(1)}, u32[]{:S(2)}, u32[]{:S(2)}) collective-permute-start(bf16[48,8,4,128]{3,2,1,0:T(4,128)(2,1)S(1)} %get-tuple-element.50), channel_id=1, source_target_pairs={{0,16},{8,24},{16,0},{24,8},{1,17},{9,25},{17,1},{25,9},{2,18},{10... | collective-permute-start | bytes 1179656 | tf_op jit(solution)/shard_map/ppermute | solution.py:332
  33.7 16.4 %collective-permute-start.2 = (bf16[48,8,4,128]{3,2,1,0:T(4,128)(2,1)S(1)}, bf16[48,8,4,128]{3,2,1,0:T(4,128)(2,1)S(1)}, u32[]{:S(2)}, u32[]{:S(2)}) collective-permute-start(bf16[48,8,4,128]{3,2,1,0:T(4,128)(2,1)S(1)} %get-tuple-element.49), channel_id=1, source_target_pairs={{0,24},{8,0},{16,8},{24,16},{1,25},{9,1},{17,9},{25,17},{2,26},{10... | collective-permute-start | bytes 1179656 | tf_op jit(solution)/shard_map/ppermute | solution.py:332
  39.4 12.1 %collective-permute-start.3 = (s32[195]{0:T(256)S(1)}, s32[195]{0:T(256)S(1)}, u32[]{:S(2)}, u32[]{:S(2)}) collective-permute-start(s32[195]{0:T(256)S(1)} %pad_add_fusion.note_ref.n0), channel_id=1, source_target_pairs={{0,1},{1,2},{2,3},{3,4},{4,5},{5,6},{6,7},{8,9},{9,10},{10,11},{11... | collective-permute-start | bytes 2348 | tf_op jit(solution)/shard_map/ppermute | solution.py:331
  44.2 7.3 %collective-permute-start.4 = (s32[195]{0:T(256)S(1)}, s32[195]{0:T(256)S(1)}, u32[]{:S(2)}, u32[]{:S(2)}) collective-permute-start(s32[195]{0:T(256)S(1)} %pad_add_fusion.note_ref.n0), channel_id=1, source_target_pairs={{0,2},{1,3},{2,4},{3,5},{4,6},{5,7},{8,10},{9,11},{10,12},{11,13},... | collective-permute-start | bytes 2348 | tf_op jit(solution)/shard_map/ppermute | solution.py:331
  56.6 57.4 %all-to-all-start.2 = ((bf16[16,63,4,128]{3,2,1,0:T(4,128)(2,1)}), bf16[16,63,4,128]{3,2,1,0:T(4,128)(2,1)S(1)}, u32[]{:S(2)}, u32[]{:S(2)}) async-start(bf16[16,63,4,128]{3,2,1,0:T(4,128)(2,1)} %hop.1), calls=%async_computation.2 | async-start | bytes 2064384 | tf_op jit(solution)/shard_map/all_to_all | solution.py:358
  69.6 10.7 %collective-permute-start.5 = (bf16[48,4,4,128]{3,2,1,0:T(4,128)(2,1)S(1)}, bf16[48,4,4,128]{3,2,1,0:T(4,128)(2,1)S(1)}, u32[]{:S(2)}, u32[]{:S(2)}) collective-permute-start(bf16[48,4,4,128]{3,2,1,0:T(4,128)(2,1)S(1)} %bitcast.64), channel_id=1, source_target_pairs={{0,8},{8,16},{16,24},{24,0},{1,9},{9,17},{17,25},{25,1},{2,10},{10... | collective-permute-start | bytes 589832 | tf_op jit(solution)/shard_map/ppermute | solution.py:332
  72.8 11.0 %collective-permute-start.6 = (bf16[48,4,4,128]{3,2,1,0:T(4,128)(2,1)S(1)}, bf16[48,4,4,128]{3,2,1,0:T(4,128)(2,1)S(1)}, u32[]{:S(2)}, u32[]{:S(2)}) collective-permute-start(bf16[48,4,4,128]{3,2,1,0:T(4,128)(2,1)S(1)} %bitcast.63), channel_id=1, source_target_pairs={{0,16},{8,24},{16,0},{24,8},{1,17},{9,25},{17,1},{25,9},{2,18},{10... | collective-permute-start | bytes 589832 | tf_op jit(solution)/shard_map/ppermute | solution.py:332
  77.3 7.4 %collective-permute-start.7 = (bf16[48,4,4,128]{3,2,1,0:T(4,128)(2,1)S(1)}, bf16[48,4,4,128]{3,2,1,0:T(4,128)(2,1)S(1)}, u32[]{:S(2)}, u32[]{:S(2)}) collective-permute-start(bf16[48,4,4,128]{3,2,1,0:T(4,128)(2,1)S(1)} %bitcast.62), channel_id=1, source_target_pairs={{0,24},{8,0},{16,8},{24,16},{1,25},{9,1},{17,9},{25,17},{2,26},{10... | collective-permute-start | bytes 589832 | tf_op jit(solution)/shard_map/ppermute | solution.py:332
  85.7 17.9 %collective-permute-start.8 = (bf16[192,4,4,128]{3,2,1,0:T(4,128)(2,1)S(1)}, bf16[192,4,4,128]{3,2,1,0:T(4,128)(2,1)}, u32[]{:S(2)}, u32[]{:S(2)}) collective-permute-start(bf16[192,4,4,128]{3,2,1,0:T(4,128)(2,1)S(1)} %unpack_kv.1), channel_id=1, source_target_pairs={{0,2},{1,3},{2,4},{3,5},{4,6},{5,7},{8,10},{9,11},{10,12},{11,13},... | collective-permute-start | bytes 2359304 | tf_op jit(solution)/shard_map/ppermute | solution.py:331
  89.7 13.9 %collective-permute-start.9 = (bf16[192,4,4,128]{3,2,1,0:T(4,128)(2,1)S(1)}, bf16[192,4,4,128]{3,2,1,0:T(4,128)(2,1)S(1)}, u32[]{:S(2)}, u32[]{:S(2)}) collective-permute-start(bf16[192,4,4,128]{3,2,1,0:T(4,128)(2,1)S(1)} %unpack_kv.1), channel_id=1, source_target_pairs={{0,1},{2,3},{4,5},{6,7},{8,9},{10,11},{12,13},{14,15},{16,17},{18,... | collective-permute-start | bytes 2359304 | tf_op jit(solution)/shard_map/ppermute | solution.py:364
  103.6 0.9 copy-start
  114.0 43.4 %all-to-all-start.1 = ((bf16[16,36,4,128]{3,2,1,0:T(4,128)(2,1)}), bf16[16,36,4,128]{3,2,1,0:T(4,128)(2,1)S(1)}, u32[]{:S(2)}, u32[]{:S(2)}) async-start(bf16[16,36,4,128]{3,2,1,0:T(4,128)(2,1)} %get-tuple-element.32), calls=%async_computation.1 | async-start | bytes 1179648 | tf_op jit(solution)/shard_map/all_to_all | solution.py:367
  126.7 24.6 %collective-permute-start.12 = (bf16[192,4,4,128]{3,2,1,0:T(4,128)(2,1)}, bf16[192,4,4,128]{3,2,1,0:T(4,128)(2,1)}, u32[]{:S(2)}, u32[]{:S(2)}) collective-permute-start(bf16[192,4,4,128]{3,2,1,0:T(4,128)(2,1)} %collective-permute-done.8), channel_id=1, source_target_pairs={{1,0},{3,2},{5,4},{7,6},{9,8},{11,10},{13,12},{15,14},{17,16},{19,... | collective-permute-start | bytes 2359304 | tf_op jit(solution)/shard_map/ppermute | solution.py:366
  130.3 6.0 %collective-permute-start.10 = (bf16[36,4,128]{2,1,0:T(4,128)(2,1)S(1)}, bf16[36,4,128]{2,1,0:T(4,128)(2,1)S(1)}, u32[]{:S(2)}, u32[]{:S(2)}) collective-permute-start(bf16[36,4,128]{2,1,0:T(4,128)(2,1)S(1)} %bitcast.66), channel_id=1, source_target_pairs={{0,8},{8,16},{16,24},{24,0},{1,9},{9,17},{17,25},{25,1},{2,10},{10... | collective-permute-start | bytes 110600 | tf_op jit(solution)/shard_map/ppermute | solution.py:332
  136.3 6.9 %collective-permute-start.11 = (bf16[36,4,128]{2,1,0:T(4,128)(2,1)S(1)}, bf16[36,4,128]{2,1,0:T(4,128)(2,1)S(1)}, u32[]{:S(2)}, u32[]{:S(2)}) collective-permute-start(bf16[36,4,128]{2,1,0:T(4,128)(2,1)S(1)} %broadcast_select_fusion), channel_id=1, source_target_pairs={{0,16},{8,24},{16,0},{24,8},{1,17},{9,25},{17,1},{25,9},{2,18},{10... | collective-permute-start | bytes 110600 | tf_op jit(solution)/shard_map/ppermute | solution.py:332
  143.2 8.0 %collective-permute-start.13 = (bf16[3,4,4,128]{3,2,1,0:T(4,128)(2,1)S(1)}, bf16[3,4,4,128]{3,2,1,0:T(4,128)(2,1)S(1)}, u32[]{:S(2)}, u32[]{:S(2)}) collective-permute-start(bf16[3,4,4,128]{3,2,1,0:T(4,128)(2,1)S(1)} %slice.49), channel_id=1, source_target_pairs={{0,2},{1,3},{2,4},{3,5},{4,6},{5,7},{8,10},{9,11},{10,12},{11,13},... | collective-permute-start | bytes 36872 | tf_op jit(solution)/shard_map/ppermute | solution.py:331
  146.4 4.9 %collective-permute-start.14 = (bf16[3,4,4,128]{3,2,1,0:T(4,128)(2,1)S(1)}, bf16[3,4,4,128]{3,2,1,0:T(4,128)(2,1)S(1)}, u32[]{:S(2)}, u32[]{:S(2)}) collective-permute-start(bf16[3,4,4,128]{3,2,1,0:T(4,128)(2,1)S(1)} %slice.49), channel_id=1, source_target_pairs={{0,1},{1,2},{2,3},{3,4},{4,5},{5,6},{6,7},{8,9},{9,10},{10,11},{11... | collective-permute-start | bytes 36872 | tf_op jit(solution)/shard_map/ppermute | solution.py:331
  150.2 1.1 copy-start.1

commit v9 on v8

--- a/solution.py
+++ b/solution.py
@@ -39,7 +39,7 @@
     load_q.start()
     y = me_ref[0]
     for d in range(NZ * NY):
-        nxt[d] = (d // NY * SLOT1 + ((d % NY - y) & (NY - 1)) * PER * KV) * 8
+        nxt[d] = (d // NY * 64 + ((d % NY - y) & (NY - 1)) * PER * KV) * 8
     for e in range(4):
         xrow[e] = 0
     plan.wait()
@@ -50,7 +50,7 @@
         r = n & 7
         nxt[d] = n + KV * 8 + 1
         over = r >= PER
-        tile_ref[i] = jnp.where(over, NZ * SLOT1, n >> 3)
+        tile_ref[i] = jnp.where(over, NZ * 64, n >> 3)
         xrow[jnp.where(over, r - PER, 3)] = i
         return jnp.where(over, d, far)
 
@@ -58,16 +58,21 @@
     load.wait()
 
     def move(i, carry):
-        held[pl.ds(tile_ref[i], KV)] = kvs[i]
+        t = tile_ref[i]
+        held[t >> 6, pl.ds(t & 63, KV)] = kvs[i]
         return carry
 
     lax.fori_loop(0, ROWS, move, 0, unroll=16)
+    base = pltpu.make_async_copy(
+        held.at[pl.ds(0, NZ), pl.ds(0, BASE * KV)], out_hbm.at[:, pl.ds(0, BASE * KV)], sem.at[3]
+    )
+    base.start()
     load_q.wait()
     row = lax.broadcasted_iota(jnp.int32, (16, (QA + QB) * UNIT * HD), 0)
 
     def place(e, u):
         j = e * (KV + QA + QB) + u
-        return j // HOP * SLOT1 + BASE * KV + j % HOP
+        return j // HOP, BASE * KV + j % HOP
 
     for e in range(3):
         for u in range(KV):
@@ -78,16 +83,19 @@
         for u in range(QA + QB):
             parts = [one[:, (u * UNIT + c) * HD:(u * UNIT + c + 1) * HD] for c in range(UNIT)]
             held[place(e, KV + u)] = jnp.concatenate(parts, axis=0).astype(BF)
-    store = pltpu.make_async_copy(held.at[pl.ds(0, NZ * SLOT1)], out_hbm, sem.at[3])
-    store.start()
-    store.wait()
+    more = pltpu.make_async_copy(
+        held.at[pl.ds(0, NZ), pl.ds(BASE * KV, HOP)], out_hbm.at[:, pl.ds(BASE * KV, HOP)], sem.at[4]
+    )
+    more.start()
+    base.wait()
+    more.wait()
 
 
 def pack_kv(me, rg, kv, q):
     return pl.pallas_call(
         pack_kv_kernel,
         out_shape=(
-            jax.ShapeDtypeStruct((NZ * SLOT1, UNIT, HD), BF),
+            jax.ShapeDtypeStruct((NZ, SLOT1, UNIT, HD), BF),
             jax.ShapeDtypeStruct((ROWS,), jnp.int32),
             jax.ShapeDtypeStruct((1,), jnp.int32),
         ),
@@ -99,8 +107,8 @@
             pltpu.SMEM((4,), jnp.int32),
             pltpu.VMEM((ROWS, KV, UNIT, HD), BF),
             pltpu.VMEM((ROWS, (QA + QB) * UNIT * HD), BF),
-            pltpu.VMEM((NZ * SLOT1 + KV, UNIT, HD), BF),
-            pltpu.SemaphoreType.DMA((4,)),
+            pltpu.VMEM((NZ + 1, SLOT1, UNIT, HD), BF),
+            pltpu.SemaphoreType.DMA((5,)),
         ],
         compiler_params=params(60),
         name="pack_kv",
@@ -112,8 +120,8 @@
 
     def step(i, carry):
         t = tile_ref[i]
-        gz = (t * 1286) >> 16
-        k = (t - gz * SLOT1) >> 2
+        gz = t >> 6
+        k = (t & 63) >> 2
         dy = (k * 11) >> 5
         out_ref[jnp.where(gz == NZ, ROWS, (dy * NZ + gz) * PER + k - dy * PER)] = q_ref[i]
         return carry
@@ -347,7 +355,7 @@
     zs1, tile, meta = pack_kv(y.reshape(1), route_group, kv, queries)
     k6 = (meta[0] - (z * NY + y)) & (NZ * NY - 1)
     dz = (((y + k6) >> 2) & (NZ - 1)).reshape(1)
-    zr1 = lax.all_to_all(zs1.reshape(NZ, SLOT1, UNIT, HD), "z", 0, 0, tiled=True)
+    zr1 = lax.all_to_all(zs1, "z", 0, 0, tiled=True)
 
     tile, queries = lax.optimization_barrier((tile, queries))
     qy = pack_q(tile, queries.reshape(ROWS, QA + QB, UNIT, HD))
@@ -362,8 +370,8 @@
     own = unpack_kv(idx1, [part[0]] + [side(part[k], k) for k in range(1, NY)])
     own2 = up(own, 2)
     own1a = lax.ppermute(own, "seq", [(i, i + 1) for i in range(0, NS, 2)])
-    zs3, own2, own1a = lax.optimization_barrier((zs3, own2, own1a))
     own1b = lax.ppermute(own2, "seq", [(i + 1, i) for i in range(0, NS, 2)])
+    zs3, own2, own1a, own1b = lax.optimization_barrier((zs3, own2, own1a, own1b))
     zr3 = lax.all_to_all(zs3, "z", 0, 0, tiled=True)
 
     came = zr2[:EXT // HOP, SLOT2 - HOP:].reshape(EXT, UNIT, HD)

time: 162 us -> 162 us (level); the launches traced: 161 us -> 159 us
  waiting for transfers between devices: 38.8 us -> 32.8 us
  starting transfers between devices: 93.2 us -> 95.7 us
  local copies, waits for them, and re-layouts: 6.37 us -> 8.68 us
    all_to_all x1, waiting for transfers between devices: 9.45 us -> 2.7 us  [on_device(): zr2 = lax.all_to_all(hop(dz, zs2, zr1), 'z', 0, 0, tiled=True)]
    unnamed x10 -> x18, local copies, waits for them, and re-layouts: 0.95 us -> 3.26 us
  transfers between devices with their start and end apart: 18 -> 18, of which waited for: 9 -> 9; matrix products, arithmetic and copies ran while one was open for 5% -> 5% of each run, Pallas kernels for 7% -> 6%
where the time goes in v9:
time: 162 us; the launch traced here: 159 us
  starting transfers between devices  95.7 us (59%)
  waiting for transfers between devices  32.8 us (20%)
  Pallas kernels  18.1 us (11%)
  local copies, waits for them, and re-layouts  8.68 us (5%)
  other arithmetic  2.71 us (2%)
    ppermute x8, starting transfers between devices, on_device(): lax.ppermute(a, 'y', [(i, (i + n) % NY) for i in range(NY)])  28.2 us
    ppermute x5, starting transfers between devices, on_device(): lax.ppermute(a, 'seq', [(i, i + n) for i in range(NS - n)])  20.2 us
    all_to_all x1, starting transfers between devices, on_device(): zr1 = lax.all_to_all(zs1, 'z', 0, 0, tiled=True)  15.8 us
    ppermute x5, waiting for transfers between devices, on_device(): lax.ppermute(a, 'seq', [(i, i + n) for i in range(NS - n)])  13.5 us
    all_to_all x1, starting transfers between devices, on_device(): zr2 = lax.all_to_all(hop(dz, zs2, zr1), 'z', 0, 0, tiled=True)  12.7 us
    all_to_all x1, starting transfers between devices, on_device(): zr3 = lax.all_to_all(zs3, 'z', 0, 0, tiled=True)  12.7 us
    ppermute x8, waiting for transfers between devices, on_device(): lax.ppermute(a, 'y', [(i, (i + n) % NY) for i in range(NY)])  12.2 us
    pallas_call x2, Pallas kernels, attend(): pl.pallas_call(functools.partial(attend_kernel, part, heads, HD ** (-0.5)...  6.21 us
  transfers between devices with their start and end apart: 18, of which 9 were waited for; matrix products, arithmetic and copies ran while one was open for 5% of the time, Pallas kernels for 6%

profile of v9, /device:TPU:1, one launch (start us, length us, event | category | flops | bytes accessed | tf_op | source)
XLA Modules:
  0.0 159.1 jit_solution(2346777992979895212)
XLA Ops:
  0.0 3.9 %pack_kv.1 = (bf16[16,51,4,128]{3,2,1,0:T(4,128)(2,1)}, s32[192]{0:T(256)}, s32[1]{0:T(128)}) custom-call(s32[1]{0:T(128)} %bitcast.4.me_ref, s32[192]{0:T(256)} %rg_hbm.1, bf16[192,4,4,128]{3,2,1,0:T(4,128)(2,1)} %bitcast.61, bf16[192,4096]{1,0:T(8,128)(2,1)} %q_hbm.1), custom_call_target="tpu_custom_call" | custom-call | tf_op jit(solution)/shard_map/pack_kv/pallas_call | solution.py:95
  3.9 15.8 %all-to-all-start = ((bf16[16,51,4,128]{3,2,1,0:T(4,128)(2,1)}), bf16[16,51,4,128]{3,2,1,0:T(4,128)(2,1)S(1)}, u32[]{:S(2)}, u32[]{:S(2)}) async-start(bf16[16,51,4,128]{3,2,1,0:T(4,128)(2,1)} %get-tuple-element.32), calls=%async_computation | async-start | bytes 1671168 | tf_op jit(solution)/shard_map/all_to_all | solution.py:358
  19.7 2.8 %reshape.75.q_ref = bf16[192,8,4,128]{3,2,1,0:T(4,128)(2,1)S(1)} reshape(bf16[192,4096]{1,0:T(8,128)(2,1)} %q_hbm.1) | data formatting | bytes 3145728 | tf_op jit(solution)/shard_map/reshape | solution.py:361
  25.9 3.2 %collective-permute-start = (bf16[48,8,4,128]{3,2,1,0:T(4,128)(2,1)}, bf16[48,8,4,128]{3,2,1,0:T(4,128)(2,1)S(1)}, u32[]{:S(2)}, u32[]{:S(2)}) collective-permute-start(bf16[48,8,4,128]{3,2,1,0:T(4,128)(2,1)} %get-tuple-element.53), channel_id=1, source_target_pairs={{0,8},{8,16},{16,24},{24,0},{1,9},{9,17},{17,25},{25,1},{2,10},{10... | collective-permute-start | bytes 1179656 | tf_op jit(solution)/shard_map/ppermute | solution.py:340
  29.1 4.5 %collective-permute-start.1 = (bf16[48,8,4,128]{3,2,1,0:T(4,128)(2,1)S(1)}, bf16[48,8,4,128]{3,2,1,0:T(4,128)(2,1)S(1)}, u32[]{:S(2)}, u32[]{:S(2)}) collective-permute-start(bf16[48,8,4,128]{3,2,1,0:T(4,128)(2,1)S(1)} %get-tuple-element.52), channel_id=1, source_target_pairs={{0,16},{8,24},{16,0},{24,8},{1,17},{9,25},{17,1},{25,9},{2,18},{10... | collective-permute-start | bytes 1179656 | tf_op jit(solution)/shard_map/ppermute | solution.py:340
  33.7 3.0 %collective-permute-start.2 = (bf16[48,8,4,128]{3,2,1,0:T(4,128)(2,1)S(1)}, bf16[48,8,4,128]{3,2,1,0:T(4,128)(2,1)S(1)}, u32[]{:S(2)}, u32[]{:S(2)}) collective-permute-start(bf16[48,8,4,128]{3,2,1,0:T(4,128)(2,1)S(1)} %get-tuple-element.51), channel_id=1, source_target_pairs={{0,24},{8,0},{16,8},{24,16},{1,25},{9,1},{17,9},{25,17},{2,26},{10... | collective-permute-start | bytes 1179656 | tf_op jit(solution)/shard_map/ppermute | solution.py:340
  39.3 4.8 %collective-permute-start.3 = (s32[195]{0:T(256)S(1)}, s32[195]{0:T(256)S(1)}, u32[]{:S(2)}, u32[]{:S(2)}) collective-permute-start(s32[195]{0:T(256)S(1)} %pad_add_fusion.note_ref.n0), channel_id=1, source_target_pairs={{0,1},{1,2},{2,3},{3,4},{4,5},{5,6},{6,7},{8,9},{9,10},{10,11},{11... | collective-permute-start | bytes 2348 | tf_op jit(solution)/shard_map/ppermute | solution.py:339
  44.1 3.1 %collective-permute-start.4 = (s32[195]{0:T(256)S(1)}, s32[195]{0:T(256)S(1)}, u32[]{:S(2)}, u32[]{:S(2)}) collective-permute-start(s32[195]{0:T(256)S(1)} %pad_add_fusion.note_ref.n0), channel_id=1, source_target_pairs={{0,2},{1,3},{2,4},{3,5},{4,6},{5,7},{8,10},{9,11},{10,12},{11,13},... | collective-permute-start | bytes 2348 | tf_op jit(solution)/shard_map/ppermute | solution.py:339
  51.5 4.4 %all-to-all-done.came = bf16[16,51,4,128]{3,2,1,0:T(4,128)(2,1)S(1)} async-done(((bf16[16,51,4,128]{3,2,1,0:T(4,128)(2,1)}), bf16[16,51,4,128]{3,2,1,0:T(4,128)(2,1)S(1)}, u32[]{:S(2)}, u32[]{:S(2)}) %all-to-all-start) | async-done | bytes 835616 | tf_op jit(solution)/shard_map/all_to_all | solution.py:358
  56.7 12.7 %all-to-all-start.2 = ((bf16[16,63,4,128]{3,2,1,0:T(4,128)(2,1)}), bf16[16,63,4,128]{3,2,1,0:T(4,128)(2,1)S(1)}, u32[]{:S(2)}, u32[]{:S(2)}) async-start(bf16[16,63,4,128]{3,2,1,0:T(4,128)(2,1)} %hop.1), calls=%async_computation.2 | async-start | bytes 2064384 | tf_op jit(solution)/shard_map/all_to_all | solution.py:366
  69.7 3.2 %collective-permute-start.5 = (bf16[48,4,4,128]{3,2,1,0:T(4,128)(2,1)S(1)}, bf16[48,4,4,128]{3,2,1,0:T(4,128)(2,1)S(1)}, u32[]{:S(2)}, u32[]{:S(2)}) collective-permute-start(bf16[48,4,4,128]{3,2,1,0:T(4,128)(2,1)S(1)} %bitcast.64), channel_id=1, source_target_pairs={{0,8},{8,16},{16,24},{24,0},{1,9},{9,17},{17,25},{25,1},{2,10},{10... | collective-permute-start | bytes 589832 | tf_op jit(solution)/shard_map/ppermute | solution.py:340
  72.9 4.5 %collective-permute-start.6 = (bf16[48,4,4,128]{3,2,1,0:T(4,128)(2,1)S(1)}, bf16[48,4,4,128]{3,2,1,0:T(4,128)(2,1)S(1)}, u32[]{:S(2)}, u32[]{:S(2)}) collective-permute-start(bf16[48,4,4,128]{3,2,1,0:T(4,128)(2,1)S(1)} %bitcast.63), channel_id=1, source_target_pairs={{0,16},{8,24},{16,0},{24,8},{1,17},{9,25},{17,1},{25,9},{2,18},{10... | collective-permute-start | bytes 589832 | tf_op jit(solution)/shard_map/ppermute | solution.py:340
  77.4 3.0 %collective-permute-start.7 = (bf16[48,4,4,128]{3,2,1,0:T(4,128)(2,1)S(1)}, bf16[48,4,4,128]{3,2,1,0:T(4,128)(2,1)S(1)}, u32[]{:S(2)}, u32[]{:S(2)}) collective-permute-start(bf16[48,4,4,128]{3,2,1,0:T(4,128)(2,1)S(1)} %bitcast.62), channel_id=1, source_target_pairs={{0,24},{8,0},{16,8},{24,16},{1,25},{9,1},{17,9},{25,17},{2,26},{10... | collective-permute-start | bytes 589832 | tf_op jit(solution)/shard_map/ppermute | solution.py:340
  80.4 3.5 %collective-permute-done.6.b2 = bf16[48,4,4,128]{3,2,1,0:T(4,128)(2,1)S(1)} collective-permute-done((bf16[48,4,4,128]{3,2,1,0:T(4,128)(2,1)S(1)}, bf16[48,4,4,128]{3,2,1,0:T(4,128)(2,1)S(1)}, u32[]{:S(2)}, u32[]{:S(2)}) %collective-permute-start.6) | collective-permute-done | bytes 196640 | tf_op jit(solution)/shard_map/ppermute | solution.py:340
  85.8 3.2 %collective-permute-start.8 = (bf16[192,4,4,128]{3,2,1,0:T(4,128)(2,1)S(1)}, bf16[192,4,4,128]{3,2,1,0:T(4,128)(2,1)S(1)}, u32[]{:S(2)}, u32[]{:S(2)}) collective-permute-start(bf16[192,4,4,128]{3,2,1,0:T(4,128)(2,1)S(1)} %unpack_kv.1), channel_id=1, source_target_pairs={{0,2},{1,3},{2,4},{3,5},{4,6},{5,7},{8,10},{9,11},{10,12},{11,13},... | collective-permute-start | bytes 2359304 | tf_op jit(solution)/shard_map/ppermute | solution.py:339
  90.3 13.4 %collective-permute-done.8 = bf16[192,4,4,128]{3,2,1,0:T(4,128)(2,1)S(1)} collective-permute-done((bf16[192,4,4,128]{3,2,1,0:T(4,128)(2,1)S(1)}, bf16[192,4,4,128]{3,2,1,0:T(4,128)(2,1)S(1)}, u32[]{:S(2)}, u32[]{:S(2)}) %collective-permute-start.8) | collective-permute-done | bytes 786464 | tf_op jit(solution)/shard_map/ppermute | solution.py:339
  103.7 4.9 %collective-permute-start.10 = (bf16[192,4,4,128]{3,2,1,0:T(4,128)(2,1)S(1)}, bf16[192,4,4,128]{3,2,1,0:T(4,128)(2,1)S(1)}, u32[]{:S(2)}, u32[]{:S(2)}) collective-permute-start(bf16[192,4,4,128]{3,2,1,0:T(4,128)(2,1)S(1)} %collective-permute-done.8), channel_id=1, source_target_pairs={{1,0},{3,2},{5,4},{7,6},{9,8},{11,10},{13,12},{15,14},{17,16},{19,... | collective-permute-start | bytes 2359304 | tf_op jit(solution)/shard_map/ppermute | solution.py:373
  114.1 12.7 %all-to-all-start.1 = ((bf16[16,36,4,128]{3,2,1,0:T(4,128)(2,1)}), bf16[16,36,4,128]{3,2,1,0:T(4,128)(2,1)S(1)}, u32[]{:S(2)}, u32[]{:S(2)}) async-start(bf16[16,36,4,128]{3,2,1,0:T(4,128)(2,1)} %get-tuple-element.33), calls=%async_computation.1 | async-start | bytes 1179648 | tf_op jit(solution)/shard_map/all_to_all | solution.py:375
  126.8 3.2 %collective-permute-start.11 = (bf16[36,4,128]{2,1,0:T(4,128)(2,1)S(1)}, bf16[36,4,128]{2,1,0:T(4,128)(2,1)S(1)}, u32[]{:S(2)}, u32[]{:S(2)}) collective-permute-start(bf16[36,4,128]{2,1,0:T(4,128)(2,1)S(1)} %bitcast.66), channel_id=1, source_target_pairs={{0,8},{8,16},{16,24},{24,0},{1,9},{9,17},{17,25},{25,1},{2,10},{10... | collective-permute-start | bytes 110600 | tf_op jit(solution)/shard_map/ppermute | solution.py:340
  132.8 3.5 %collective-permute-start.12 = (bf16[36,4,128]{2,1,0:T(4,128)(2,1)S(1)}, bf16[36,4,128]{2,1,0:T(4,128)(2,1)S(1)}, u32[]{:S(2)}, u32[]{:S(2)}) collective-permute-start(bf16[36,4,128]{2,1,0:T(4,128)(2,1)S(1)} %broadcast_select_fusion), channel_id=1, source_target_pairs={{0,16},{8,24},{16,0},{24,8},{1,17},{9,25},{17,1},{25,9},{2,18},{10... | collective-permute-start | bytes 110600 | tf_op jit(solution)/shard_map/ppermute | solution.py:340
  136.3 2.9 %collective-permute-done.12 = bf16[36,4,128]{2,1,0:T(4,128)(2,1)S(1)} collective-permute-done((bf16[36,4,128]{2,1,0:T(4,128)(2,1)S(1)}, bf16[36,4,128]{2,1,0:T(4,128)(2,1)S(1)}, u32[]{:S(2)}, u32[]{:S(2)}) %collective-permute-start.12) | collective-permute-done | bytes 36896 | tf_op jit(solution)/shard_map/ppermute | solution.py:340
  139.3 3.1 %collective-permute-start.13 = (bf16[3,4,4,128]{3,2,1,0:T(4,128)(2,1)S(1)}, bf16[3,4,4,128]{3,2,1,0:T(4,128)(2,1)S(1)}, u32[]{:S(2)}, u32[]{:S(2)}) collective-permute-start(bf16[3,4,4,128]{3,2,1,0:T(4,128)(2,1)S(1)} %slice.49), channel_id=1, source_target_pairs={{0,2},{1,3},{2,4},{3,5},{4,6},{5,7},{8,10},{9,11},{10,12},{11,13},... | collective-permute-start | bytes 36872 | tf_op jit(solution)/shard_map/ppermute | solution.py:339
  142.4 6.0 %collective-permute-start.14 = (bf16[3,4,4,128]{3,2,1,0:T(4,128)(2,1)S(1)}, bf16[3,4,4,128]{3,2,1,0:T(4,128)(2,1)S(1)}, u32[]{:S(2)}, u32[]{:S(2)}) collective-permute-start(bf16[3,4,4,128]{3,2,1,0:T(4,128)(2,1)S(1)} %slice.49), channel_id=1, source_target_pairs={{0,1},{1,2},{2,3},{3,4},{4,5},{5,6},{6,7},{8,9},{9,10},{10,11},{11... | collective-permute-start | bytes 36872 | tf_op jit(solution)/shard_map/ppermute | solution.py:339
  151.9 3.6 %attend.2 = (bf16[192,4096]{1,0:T(8,128)(2,1)}, f32[8,128]{1,0:T(8,128)S(1)}) custom-call(bf16[20,192,128]{2,1,0:T(8,128)(2,1)S(1)} %bitcast.47, bf16[16,576,128]{2,1,0:T(8,128)(2,1)S(1)} %bitcast.41, s32[192,1]{1,0:T(8,128)S(1)} %copy.13.segq_ref, s32[1,576]{1,0:T(1,128)S(1)} %get-tuple-element.42.segk_ref), custom_call_target="tpu_custom_call" | custom-call | flops 1132462080 | bytes 4194304 | tf_op jit(solution)/shard_map/attend/pallas_call | solution.py:321
  (54 shorter events, 28.9 us)
Async XLA Ops:
  3.9 52.0 %all-to-all-start = ((bf16[16,51,4,128]{3,2,1,0:T(4,128)(2,1)}), bf16[16,51,4,128]{3,2,1,0:T(4,128)(2,1)S(1)}, u32[]{:S(2)}, u32[]{:S(2)}) async-start(bf16[16,51,4,128]{3,2,1,0:T(4,128)(2,1)} %get-tuple-element.32), calls=%async_computation | async-start | bytes 1671168 | tf_op jit(solution)/shard_map/all_to_all | solution.py:358
  19.7 2.8 %copy-start.6 = (s32[192]{0:T(256)S(1)}, s32[192]{0:T(256)}, u32[]{:S(2)}) copy-start(s32[192]{0:T(256)} %get-tuple-element.26.tile_ref) | copy-start | bytes 2308
  24.6 12.0 %copy-start.8 = (s32[192]{0:T(256)S(1)}, s32[192]{0:T(256)}, u32[]{:S(2)}) copy-start(s32[192]{0:T(256)} %param.8) | copy-start | bytes 2308
  24.6 12.8 %copy-start.7 = (s32[1,192]{1,0:T(1,128)S(1)}, s32[1,192]{1,0:T(1,128)}, u32[]{:S(2)}) copy-start(s32[1,192]{1,0:T(1,128)} %param.9) | copy-start | bytes 2308
  25.9 22.0 %collective-permute-start = (bf16[48,8,4,128]{3,2,1,0:T(4,128)(2,1)}, bf16[48,8,4,128]{3,2,1,0:T(4,128)(2,1)S(1)}, u32[]{:S(2)}, u32[]{:S(2)}) collective-permute-start(bf16[48,8,4,128]{3,2,1,0:T(4,128)(2,1)} %get-tuple-element.53), channel_id=1, source_target_pairs={{0,8},{8,16},{16,24},{24,0},{1,9},{9,17},{17,25},{25,1},{2,10},{10... | collective-permute-start | bytes 1179656 | tf_op jit(solution)/shard_map/ppermute | solution.py:340
  29.1 19.4 %collective-permute-start.1 = (bf16[48,8,4,128]{3,2,1,0:T(4,128)(2,1)S(1)}, bf16[48,8,4,128]{3,2,1,0:T(4,128)(2,1)S(1)}, u32[]{:S(2)}, u32[]{:S(2)}) collective-permute-start(bf16[48,8,4,128]{3,2,1,0:T(4,128)(2,1)S(1)} %get-tuple-element.52), channel_id=1, source_target_pairs={{0,16},{8,24},{16,0},{24,8},{1,17},{9,25},{17,1},{25,9},{2,18},{10... | collective-permute-start | bytes 1179656 | tf_op jit(solution)/shard_map/ppermute | solution.py:340
  33.7 16.4 %collective-permute-start.2 = (bf16[48,8,4,128]{3,2,1,0:T(4,128)(2,1)S(1)}, bf16[48,8,4,128]{3,2,1,0:T(4,128)(2,1)S(1)}, u32[]{:S(2)}, u32[]{:S(2)}) collective-permute-start(bf16[48,8,4,128]{3,2,1,0:T(4,128)(2,1)S(1)} %get-tuple-element.51), channel_id=1, source_target_pairs={{0,24},{8,0},{16,8},{24,16},{1,25},{9,1},{17,9},{25,17},{2,26},{10... | collective-permute-start | bytes 1179656 | tf_op jit(solution)/shard_map/ppermute | solution.py:340
  39.3 12.2 %collective-permute-start.3 = (s32[195]{0:T(256)S(1)}, s32[195]{0:T(256)S(1)}, u32[]{:S(2)}, u32[]{:S(2)}) collective-permute-start(s32[195]{0:T(256)S(1)} %pad_add_fusion.note_ref.n0), channel_id=1, source_target_pairs={{0,1},{1,2},{2,3},{3,4},{4,5},{5,6},{6,7},{8,9},{9,10},{10,11},{11... | collective-permute-start | bytes 2348 | tf_op jit(solution)/shard_map/ppermute | solution.py:339
  44.1 7.4 %collective-permute-start.4 = (s32[195]{0:T(256)S(1)}, s32[195]{0:T(256)S(1)}, u32[]{:S(2)}, u32[]{:S(2)}) collective-permute-start(s32[195]{0:T(256)S(1)} %pad_add_fusion.note_ref.n0), channel_id=1, source_target_pairs={{0,2},{1,3},{2,4},{3,5},{4,6},{5,7},{8,10},{9,11},{10,12},{11,13},... | collective-permute-start | bytes 2348 | tf_op jit(solution)/shard_map/ppermute | solution.py:339
  56.7 57.4 %all-to-all-start.2 = ((bf16[16,63,4,128]{3,2,1,0:T(4,128)(2,1)}), bf16[16,63,4,128]{3,2,1,0:T(4,128)(2,1)S(1)}, u32[]{:S(2)}, u32[]{:S(2)}) async-start(bf16[16,63,4,128]{3,2,1,0:T(4,128)(2,1)} %hop.1), calls=%async_computation.2 | async-start | bytes 2064384 | tf_op jit(solution)/shard_map/all_to_all | solution.py:366
  69.7 10.7 %collective-permute-start.5 = (bf16[48,4,4,128]{3,2,1,0:T(4,128)(2,1)S(1)}, bf16[48,4,4,128]{3,2,1,0:T(4,128)(2,1)S(1)}, u32[]{:S(2)}, u32[]{:S(2)}) collective-permute-start(bf16[48,4,4,128]{3,2,1,0:T(4,128)(2,1)S(1)} %bitcast.64), channel_id=1, source_target_pairs={{0,8},{8,16},{16,24},{24,0},{1,9},{9,17},{17,25},{25,1},{2,10},{10... | collective-permute-start | bytes 589832 | tf_op jit(solution)/shard_map/ppermute | solution.py:340
  72.9 11.0 %collective-permute-start.6 = (bf16[48,4,4,128]{3,2,1,0:T(4,128)(2,1)S(1)}, bf16[48,4,4,128]{3,2,1,0:T(4,128)(2,1)S(1)}, u32[]{:S(2)}, u32[]{:S(2)}) collective-permute-start(bf16[48,4,4,128]{3,2,1,0:T(4,128)(2,1)S(1)} %bitcast.63), channel_id=1, source_target_pairs={{0,16},{8,24},{16,0},{24,8},{1,17},{9,25},{17,1},{25,9},{2,18},{10... | collective-permute-start | bytes 589832 | tf_op jit(solution)/shard_map/ppermute | solution.py:340
  77.4 7.4 %collective-permute-start.7 = (bf16[48,4,4,128]{3,2,1,0:T(4,128)(2,1)S(1)}, bf16[48,4,4,128]{3,2,1,0:T(4,128)(2,1)S(1)}, u32[]{:S(2)}, u32[]{:S(2)}) collective-permute-start(bf16[48,4,4,128]{3,2,1,0:T(4,128)(2,1)S(1)} %bitcast.62), channel_id=1, source_target_pairs={{0,24},{8,0},{16,8},{24,16},{1,25},{9,1},{17,9},{25,17},{2,26},{10... | collective-permute-start | bytes 589832 | tf_op jit(solution)/shard_map/ppermute | solution.py:340
  85.8 17.9 %collective-permute-start.8 = (bf16[192,4,4,128]{3,2,1,0:T(4,128)(2,1)S(1)}, bf16[192,4,4,128]{3,2,1,0:T(4,128)(2,1)S(1)}, u32[]{:S(2)}, u32[]{:S(2)}) collective-permute-start(bf16[192,4,4,128]{3,2,1,0:T(4,128)(2,1)S(1)} %unpack_kv.1), channel_id=1, source_target_pairs={{0,2},{1,3},{2,4},{3,5},{4,6},{5,7},{8,10},{9,11},{10,12},{11,13},... | collective-permute-start | bytes 2359304 | tf_op jit(solution)/shard_map/ppermute | solution.py:339
  89.0 20.5 %collective-permute-start.9 = (bf16[192,4,4,128]{3,2,1,0:T(4,128)(2,1)S(1)}, bf16[192,4,4,128]{3,2,1,0:T(4,128)(2,1)S(1)}, u32[]{:S(2)}, u32[]{:S(2)}) collective-permute-start(bf16[192,4,4,128]{3,2,1,0:T(4,128)(2,1)S(1)} %unpack_kv.1), channel_id=1, source_target_pairs={{0,1},{2,3},{4,5},{6,7},{8,9},{10,11},{12,13},{14,15},{16,17},{18,... | collective-permute-start | bytes 2359304 | tf_op jit(solution)/shard_map/ppermute | solution.py:372
  103.7 6.7 %collective-permute-start.10 = (bf16[192,4,4,128]{3,2,1,0:T(4,128)(2,1)S(1)}, bf16[192,4,4,128]{3,2,1,0:T(4,128)(2,1)S(1)}, u32[]{:S(2)}, u32[]{:S(2)}) collective-permute-start(bf16[192,4,4,128]{3,2,1,0:T(4,128)(2,1)S(1)} %collective-permute-done.8), channel_id=1, source_target_pairs={{1,0},{3,2},{5,4},{7,6},{9,8},{11,10},{13,12},{15,14},{17,16},{19,... | collective-permute-start | bytes 2359304 | tf_op jit(solution)/shard_map/ppermute | solution.py:373
  114.1 41.5 %all-to-all-start.1 = ((bf16[16,36,4,128]{3,2,1,0:T(4,128)(2,1)}), bf16[16,36,4,128]{3,2,1,0:T(4,128)(2,1)S(1)}, u32[]{:S(2)}, u32[]{:S(2)}) async-start(bf16[16,36,4,128]{3,2,1,0:T(4,128)(2,1)} %get-tuple-element.33), calls=%async_computation.1 | async-start | bytes 1179648 | tf_op jit(solution)/shard_map/all_to_all | solution.py:375
  126.8 6.0 %collective-permute-start.11 = (bf16[36,4,128]{2,1,0:T(4,128)(2,1)S(1)}, bf16[36,4,128]{2,1,0:T(4,128)(2,1)S(1)}, u32[]{:S(2)}, u32[]{:S(2)}) collective-permute-start(bf16[36,4,128]{2,1,0:T(4,128)(2,1)S(1)} %bitcast.66), channel_id=1, source_target_pairs={{0,8},{8,16},{16,24},{24,0},{1,9},{9,17},{17,25},{25,1},{2,10},{10... | collective-permute-start | bytes 110600 | tf_op jit(solution)/shard_map/ppermute | solution.py:340
  132.8 6.5 %collective-permute-start.12 = (bf16[36,4,128]{2,1,0:T(4,128)(2,1)S(1)}, bf16[36,4,128]{2,1,0:T(4,128)(2,1)S(1)}, u32[]{:S(2)}, u32[]{:S(2)}) collective-permute-start(bf16[36,4,128]{2,1,0:T(4,128)(2,1)S(1)} %broadcast_select_fusion), channel_id=1, source_target_pairs={{0,16},{8,24},{16,0},{24,8},{1,17},{9,25},{17,1},{25,9},{2,18},{10... | collective-permute-start | bytes 110600 | tf_op jit(solution)/shard_map/ppermute | solution.py:340
  139.3 10.3 %collective-permute-start.13 = (bf16[3,4,4,128]{3,2,1,0:T(4,128)(2,1)S(1)}, bf16[3,4,4,128]{3,2,1,0:T(4,128)(2,1)S(1)}, u32[]{:S(2)}, u32[]{:S(2)}) collective-permute-start(bf16[3,4,4,128]{3,2,1,0:T(4,128)(2,1)S(1)} %slice.49), channel_id=1, source_target_pairs={{0,2},{1,3},{2,4},{3,5},{4,6},{5,7},{8,10},{9,11},{10,12},{11,13},... | collective-permute-start | bytes 36872 | tf_op jit(solution)/shard_map/ppermute | solution.py:339
  142.4 7.2 %collective-permute-start.14 = (bf16[3,4,4,128]{3,2,1,0:T(4,128)(2,1)S(1)}, bf16[3,4,4,128]{3,2,1,0:T(4,128)(2,1)S(1)}, u32[]{:S(2)}, u32[]{:S(2)}) collective-permute-start(bf16[3,4,4,128]{3,2,1,0:T(4,128)(2,1)S(1)} %slice.49), channel_id=1, source_target_pairs={{0,1},{1,2},{2,3},{3,4},{4,5},{5,6},{6,7},{8,9},{9,10},{10,11},{11... | collective-permute-start | bytes 36872 | tf_op jit(solution)/shard_map/ppermute | solution.py:339
  148.6 1.1 copy-start.1
  148.6 1.4 copy-start.3
  148.6 1.6 %copy-start.5 = (bf16[192,4,4,128]{3,2,1,0:T(4,128)(2,1)S(1)}, bf16[192,4,4,128]{3,2,1,0:T(4,128)(2,1)}, u32[]{:S(2)}) copy-start(bf16[192,4,4,128]{3,2,1,0:T(4,128)(2,1)} %copy-done.4) | copy-start | bytes 2359300
  (3 other events, 2.7 us)

commit v10 on v9

--- a/solution.py
+++ b/solution.py
@@ -50,19 +50,14 @@
         r = n & 7
         nxt[d] = n + KV * 8 + 1
         over = r >= PER
-        tile_ref[i] = jnp.where(over, NZ * 64, n >> 3)
+        t = jnp.where(over, NZ * 64, n >> 3)
+        tile_ref[i] = t
+        held[t >> 6, pl.ds(t & 63, KV)] = kvs[i]
         xrow[jnp.where(over, r - PER, 3)] = i
         return jnp.where(over, d, far)
 
+    load.wait()
     meta_ref[0] = lax.fori_loop(0, ROWS, step, 0, unroll=16)
-    load.wait()
-
-    def move(i, carry):
-        t = tile_ref[i]
-        held[t >> 6, pl.ds(t & 63, KV)] = kvs[i]
-        return carry
-
-    lax.fori_loop(0, ROWS, move, 0, unroll=16)
     base = pltpu.make_async_copy(
         held.at[pl.ds(0, NZ), pl.ds(0, BASE * KV)], out_hbm.at[:, pl.ds(0, BASE * KV)], sem.at[3]
     )
@@ -306,11 +301,12 @@
         o = (o / total).astype(BF)
         for g in range(4):
             held[h, lo:lo + rows, g * HD:(g + 1) * HD] = o[g * rows:(g + 1) * rows]
-        if b == len(blocks) - 1:
-            first = (base + h) * 4 * HD
-            cp = pltpu.make_async_copy(held.at[h], out_hbm.at[:, first:first + 4 * HD], sem.at[h])
-            cp.start()
-            copies.append(cp)
+        first = (base + h) * 4 * HD
+        cp = pltpu.make_async_copy(
+            held.at[h, lo:lo + rows], out_hbm.at[lo:lo + rows, first:first + 4 * HD], sem.at[n]
+        )
+        cp.start()
+        copies.append(cp)
     for cp in copies:
         cp.wait()
 
@@ -323,7 +319,7 @@
         out_shape=(whole, jax.ShapeDtypeStruct((8, HD), jnp.float32)) if part == 0 else whole,
         in_specs=[VM] * 4 + [HB] * len(prior),
         out_specs=(HB, VM) if part == 0 else HB,
-        scratch_shapes=[pltpu.VMEM((heads, ROWS, 4 * HD), BF), pltpu.SemaphoreType.DMA((heads,))],
+        scratch_shapes=[pltpu.VMEM((heads, ROWS, 4 * HD), BF), pltpu.SemaphoreType.DMA((2 * heads,))],
         input_output_aliases={4: 0} if prior else {},
         compiler_params=params(32),
         cost_estimate=pl.CostEstimate(

time: 162 us -> 162 us (level)
  no operation moved by 1% of the time
where the time goes in v10:
time: 162 us; the launch traced here: 159 us
  starting transfers between devices  95.7 us (59%)
  waiting for transfers between devices  32.8 us (20%)
  Pallas kernels  18.1 us (11%)
  local copies, waits for them, and re-layouts  8.68 us (5%)
  other arithmetic  2.71 us (2%)
    ppermute x8, starting transfers between devices, on_device(): lax.ppermute(a, 'y', [(i, (i + n) % NY) for i in range(NY)])  28.2 us
    ppermute x5, starting transfers between devices, on_device(): lax.ppermute(a, 'seq', [(i, i + n) for i in range(NS - n)])  20.2 us
    all_to_all x1, starting transfers between devices, on_device(): zr1 = lax.all_to_all(zs1, 'z', 0, 0, tiled=True)  15.8 us
    ppermute x5, waiting for transfers between devices, on_device(): lax.ppermute(a, 'seq', [(i, i + n) for i in range(NS - n)])  13.5 us
    all_to_all x1, starting transfers between devices, on_device(): zr2 = lax.all_to_all(hop(dz, zs2, zr1), 'z', 0, 0, tiled=True)  12.7 us
    all_to_all x1, starting transfers between devices, on_device(): zr3 = lax.all_to_all(zs3, 'z', 0, 0, tiled=True)  12.7 us
    ppermute x8, waiting for transfers between devices, on_device(): lax.ppermute(a, 'y', [(i, (i + n) % NY) for i in range(NY)])  12.2 us
    pallas_call x2, Pallas kernels, attend(): pl.pallas_call(functools.partial(attend_kernel, part, heads, HD ** (-0.5)...  6.26 us
  transfers between devices with their start and end apart: 18, of which 9 were waited for; matrix products, arithmetic and copies ran while one was open for 5% of the time, Pallas kernels for 6%

profile of v10, /device:TPU:1, one launch (start us, length us, event | category | flops | bytes accessed | tf_op | source)
XLA Modules:
  0.0 159.1 jit_solution(15296715776135176017)
XLA Ops:
  0.0 3.9 %pack_kv.1 = (bf16[16,51,4,128]{3,2,1,0:T(4,128)(2,1)}, s32[192]{0:T(256)}, s32[1]{0:T(128)}) custom-call(s32[1]{0:T(128)} %bitcast.4.me_ref, s32[192]{0:T(256)} %rg_hbm.1, bf16[192,4,4,128]{3,2,1,0:T(4,128)(2,1)} %bitcast.61, bf16[192,4096]{1,0:T(8,128)(2,1)} %q_hbm.1), custom_call_target="tpu_custom_call" | custom-call | tf_op jit(solution)/shard_map/pack_kv/pallas_call | solution.py:90
  3.9 15.8 %all-to-all-start = ((bf16[16,51,4,128]{3,2,1,0:T(4,128)(2,1)}), bf16[16,51,4,128]{3,2,1,0:T(4,128)(2,1)S(1)}, u32[]{:S(2)}, u32[]{:S(2)}) async-start(bf16[16,51,4,128]{3,2,1,0:T(4,128)(2,1)} %get-tuple-element.32), calls=%async_computation | async-start | bytes 1671168 | tf_op jit(solution)/shard_map/all_to_all | solution.py:354
  19.7 2.8 %reshape.75.q_ref = bf16[192,8,4,128]{3,2,1,0:T(4,128)(2,1)S(1)} reshape(bf16[192,4096]{1,0:T(8,128)(2,1)} %q_hbm.1) | data formatting | bytes 3145728 | tf_op jit(solution)/shard_map/reshape | solution.py:357
  25.9 3.2 %collective-permute-start = (bf16[48,8,4,128]{3,2,1,0:T(4,128)(2,1)}, bf16[48,8,4,128]{3,2,1,0:T(4,128)(2,1)S(1)}, u32[]{:S(2)}, u32[]{:S(2)}) collective-permute-start(bf16[48,8,4,128]{3,2,1,0:T(4,128)(2,1)} %get-tuple-element.53), channel_id=1, source_target_pairs={{0,8},{8,16},{16,24},{24,0},{1,9},{9,17},{17,25},{25,1},{2,10},{10... | collective-permute-start | bytes 1179656 | tf_op jit(solution)/shard_map/ppermute | solution.py:336
  29.1 4.5 %collective-permute-start.1 = (bf16[48,8,4,128]{3,2,1,0:T(4,128)(2,1)S(1)}, bf16[48,8,4,128]{3,2,1,0:T(4,128)(2,1)S(1)}, u32[]{:S(2)}, u32[]{:S(2)}) collective-permute-start(bf16[48,8,4,128]{3,2,1,0:T(4,128)(2,1)S(1)} %get-tuple-element.52), channel_id=1, source_target_pairs={{0,16},{8,24},{16,0},{24,8},{1,17},{9,25},{17,1},{25,9},{2,18},{10... | collective-permute-start | bytes 1179656 | tf_op jit(solution)/shard_map/ppermute | solution.py:336
  33.6 3.0 %collective-permute-start.2 = (bf16[48,8,4,128]{3,2,1,0:T(4,128)(2,1)S(1)}, bf16[48,8,4,128]{3,2,1,0:T(4,128)(2,1)S(1)}, u32[]{:S(2)}, u32[]{:S(2)}) collective-permute-start(bf16[48,8,4,128]{3,2,1,0:T(4,128)(2,1)S(1)} %get-tuple-element.51), channel_id=1, source_target_pairs={{0,24},{8,0},{16,8},{24,16},{1,25},{9,1},{17,9},{25,17},{2,26},{10... | collective-permute-start | bytes 1179656 | tf_op jit(solution)/shard_map/ppermute | solution.py:336
  39.3 4.8 %collective-permute-start.3 = (s32[195]{0:T(256)S(1)}, s32[195]{0:T(256)S(1)}, u32[]{:S(2)}, u32[]{:S(2)}) collective-permute-start(s32[195]{0:T(256)S(1)} %pad_add_fusion.note_ref.n0), channel_id=1, source_target_pairs={{0,1},{1,2},{2,3},{3,4},{4,5},{5,6},{6,7},{8,9},{9,10},{10,11},{11... | collective-permute-start | bytes 2348 | tf_op jit(solution)/shard_map/ppermute | solution.py:335
  44.1 3.1 %collective-permute-start.4 = (s32[195]{0:T(256)S(1)}, s32[195]{0:T(256)S(1)}, u32[]{:S(2)}, u32[]{:S(2)}) collective-permute-start(s32[195]{0:T(256)S(1)} %pad_add_fusion.note_ref.n0), channel_id=1, source_target_pairs={{0,2},{1,3},{2,4},{3,5},{4,6},{5,7},{8,10},{9,11},{10,12},{11,13},... | collective-permute-start | bytes 2348 | tf_op jit(solution)/shard_map/ppermute | solution.py:335
  51.5 4.4 %all-to-all-done.came = bf16[16,51,4,128]{3,2,1,0:T(4,128)(2,1)S(1)} async-done(((bf16[16,51,4,128]{3,2,1,0:T(4,128)(2,1)}), bf16[16,51,4,128]{3,2,1,0:T(4,128)(2,1)S(1)}, u32[]{:S(2)}, u32[]{:S(2)}) %all-to-all-start) | async-done | bytes 835616 | tf_op jit(solution)/shard_map/all_to_all | solution.py:354
  56.7 12.7 %all-to-all-start.2 = ((bf16[16,63,4,128]{3,2,1,0:T(4,128)(2,1)}), bf16[16,63,4,128]{3,2,1,0:T(4,128)(2,1)S(1)}, u32[]{:S(2)}, u32[]{:S(2)}) async-start(bf16[16,63,4,128]{3,2,1,0:T(4,128)(2,1)} %hop.1), calls=%async_computation.2 | async-start | bytes 2064384 | tf_op jit(solution)/shard_map/all_to_all | solution.py:362
  69.7 3.2 %collective-permute-start.5 = (bf16[48,4,4,128]{3,2,1,0:T(4,128)(2,1)S(1)}, bf16[48,4,4,128]{3,2,1,0:T(4,128)(2,1)S(1)}, u32[]{:S(2)}, u32[]{:S(2)}) collective-permute-start(bf16[48,4,4,128]{3,2,1,0:T(4,128)(2,1)S(1)} %bitcast.64), channel_id=1, source_target_pairs={{0,8},{8,16},{16,24},{24,0},{1,9},{9,17},{17,25},{25,1},{2,10},{10... | collective-permute-start | bytes 589832 | tf_op jit(solution)/shard_map/ppermute | solution.py:336
  72.9 4.5 %collective-permute-start.6 = (bf16[48,4,4,128]{3,2,1,0:T(4,128)(2,1)S(1)}, bf16[48,4,4,128]{3,2,1,0:T(4,128)(2,1)S(1)}, u32[]{:S(2)}, u32[]{:S(2)}) collective-permute-start(bf16[48,4,4,128]{3,2,1,0:T(4,128)(2,1)S(1)} %bitcast.63), channel_id=1, source_target_pairs={{0,16},{8,24},{16,0},{24,8},{1,17},{9,25},{17,1},{25,9},{2,18},{10... | collective-permute-start | bytes 589832 | tf_op jit(solution)/shard_map/ppermute | solution.py:336
  77.4 3.0 %collective-permute-start.7 = (bf16[48,4,4,128]{3,2,1,0:T(4,128)(2,1)S(1)}, bf16[48,4,4,128]{3,2,1,0:T(4,128)(2,1)S(1)}, u32[]{:S(2)}, u32[]{:S(2)}) collective-permute-start(bf16[48,4,4,128]{3,2,1,0:T(4,128)(2,1)S(1)} %bitcast.62), channel_id=1, source_target_pairs={{0,24},{8,0},{16,8},{24,16},{1,25},{9,1},{17,9},{25,17},{2,26},{10... | collective-permute-start | bytes 589832 | tf_op jit(solution)/shard_map/ppermute | solution.py:336
  80.4 3.5 %collective-permute-done.6.b2 = bf16[48,4,4,128]{3,2,1,0:T(4,128)(2,1)S(1)} collective-permute-done((bf16[48,4,4,128]{3,2,1,0:T(4,128)(2,1)S(1)}, bf16[48,4,4,128]{3,2,1,0:T(4,128)(2,1)S(1)}, u32[]{:S(2)}, u32[]{:S(2)}) %collective-permute-start.6) | collective-permute-done | bytes 196640 | tf_op jit(solution)/shard_map/ppermute | solution.py:336
  85.8 3.2 %collective-permute-start.8 = (bf16[192,4,4,128]{3,2,1,0:T(4,128)(2,1)S(1)}, bf16[192,4,4,128]{3,2,1,0:T(4,128)(2,1)S(1)}, u32[]{:S(2)}, u32[]{:S(2)}) collective-permute-start(bf16[192,4,4,128]{3,2,1,0:T(4,128)(2,1)S(1)} %unpack_kv.1), channel_id=1, source_target_pairs={{0,2},{1,3},{2,4},{3,5},{4,6},{5,7},{8,10},{9,11},{10,12},{11,13},... | collective-permute-start | bytes 2359304 | tf_op jit(solution)/shard_map/ppermute | solution.py:335
  90.2 13.4 %collective-permute-done.8 = bf16[192,4,4,128]{3,2,1,0:T(4,128)(2,1)S(1)} collective-permute-done((bf16[192,4,4,128]{3,2,1,0:T(4,128)(2,1)S(1)}, bf16[192,4,4,128]{3,2,1,0:T(4,128)(2,1)S(1)}, u32[]{:S(2)}, u32[]{:S(2)}) %collective-permute-start.8) | collective-permute-done | bytes 786464 | tf_op jit(solution)/shard_map/ppermute | solution.py:335
  103.7 4.9 %collective-permute-start.10 = (bf16[192,4,4,128]{3,2,1,0:T(4,128)(2,1)S(1)}, bf16[192,4,4,128]{3,2,1,0:T(4,128)(2,1)S(1)}, u32[]{:S(2)}, u32[]{:S(2)}) collective-permute-start(bf16[192,4,4,128]{3,2,1,0:T(4,128)(2,1)S(1)} %collective-permute-done.8), channel_id=1, source_target_pairs={{1,0},{3,2},{5,4},{7,6},{9,8},{11,10},{13,12},{15,14},{17,16},{19,... | collective-permute-start | bytes 2359304 | tf_op jit(solution)/shard_map/ppermute | solution.py:369
  114.0 12.7 %all-to-all-start.1 = ((bf16[16,36,4,128]{3,2,1,0:T(4,128)(2,1)}), bf16[16,36,4,128]{3,2,1,0:T(4,128)(2,1)S(1)}, u32[]{:S(2)}, u32[]{:S(2)}) async-start(bf16[16,36,4,128]{3,2,1,0:T(4,128)(2,1)} %get-tuple-element.33), calls=%async_computation.1 | async-start | bytes 1179648 | tf_op jit(solution)/shard_map/all_to_all | solution.py:371
  126.8 3.2 %collective-permute-start.11 = (bf16[36,4,128]{2,1,0:T(4,128)(2,1)S(1)}, bf16[36,4,128]{2,1,0:T(4,128)(2,1)S(1)}, u32[]{:S(2)}, u32[]{:S(2)}) collective-permute-start(bf16[36,4,128]{2,1,0:T(4,128)(2,1)S(1)} %bitcast.66), channel_id=1, source_target_pairs={{0,8},{8,16},{16,24},{24,0},{1,9},{9,17},{17,25},{25,1},{2,10},{10... | collective-permute-start | bytes 110600 | tf_op jit(solution)/shard_map/ppermute | solution.py:336
  132.8 3.5 %collective-permute-start.12 = (bf16[36,4,128]{2,1,0:T(4,128)(2,1)S(1)}, bf16[36,4,128]{2,1,0:T(4,128)(2,1)S(1)}, u32[]{:S(2)}, u32[]{:S(2)}) collective-permute-start(bf16[36,4,128]{2,1,0:T(4,128)(2,1)S(1)} %broadcast_select_fusion), channel_id=1, source_target_pairs={{0,16},{8,24},{16,0},{24,8},{1,17},{9,25},{17,1},{25,9},{2,18},{10... | collective-permute-start | bytes 110600 | tf_op jit(solution)/shard_map/ppermute | solution.py:336
  136.3 2.9 %collective-permute-done.12 = bf16[36,4,128]{2,1,0:T(4,128)(2,1)S(1)} collective-permute-done((bf16[36,4,128]{2,1,0:T(4,128)(2,1)S(1)}, bf16[36,4,128]{2,1,0:T(4,128)(2,1)S(1)}, u32[]{:S(2)}, u32[]{:S(2)}) %collective-permute-start.12) | collective-permute-done | bytes 36896 | tf_op jit(solution)/shard_map/ppermute | solution.py:336
  139.3 3.1 %collective-permute-start.13 = (bf16[3,4,4,128]{3,2,1,0:T(4,128)(2,1)S(1)}, bf16[3,4,4,128]{3,2,1,0:T(4,128)(2,1)S(1)}, u32[]{:S(2)}, u32[]{:S(2)}) collective-permute-start(bf16[3,4,4,128]{3,2,1,0:T(4,128)(2,1)S(1)} %slice.49), channel_id=1, source_target_pairs={{0,2},{1,3},{2,4},{3,5},{4,6},{5,7},{8,10},{9,11},{10,12},{11,13},... | collective-permute-start | bytes 36872 | tf_op jit(solution)/shard_map/ppermute | solution.py:335
  142.4 6.0 %collective-permute-start.14 = (bf16[3,4,4,128]{3,2,1,0:T(4,128)(2,1)S(1)}, bf16[3,4,4,128]{3,2,1,0:T(4,128)(2,1)S(1)}, u32[]{:S(2)}, u32[]{:S(2)}) collective-permute-start(bf16[3,4,4,128]{3,2,1,0:T(4,128)(2,1)S(1)} %slice.49), channel_id=1, source_target_pairs={{0,1},{1,2},{2,3},{3,4},{4,5},{5,6},{6,7},{8,9},{9,10},{10,11},{11... | collective-permute-start | bytes 36872 | tf_op jit(solution)/shard_map/ppermute | solution.py:335
  151.8 3.7 %attend.2 = (bf16[192,4096]{1,0:T(8,128)(2,1)}, f32[8,128]{1,0:T(8,128)S(1)}) custom-call(bf16[20,192,128]{2,1,0:T(8,128)(2,1)S(1)} %bitcast.47, bf16[16,576,128]{2,1,0:T(8,128)(2,1)S(1)} %bitcast.41, s32[192,1]{1,0:T(8,128)S(1)} %copy.13.segq_ref, s32[1,576]{1,0:T(1,128)S(1)} %get-tuple-element.42.segk_ref), custom_call_target="tpu_custom_call" | custom-call | flops 1132462080 | bytes 4194304 | tf_op jit(solution)/shard_map/attend/pallas_call | solution.py:317
  (54 shorter events, 28.9 us)
Async XLA Ops:
  3.9 52.0 %all-to-all-start = ((bf16[16,51,4,128]{3,2,1,0:T(4,128)(2,1)}), bf16[16,51,4,128]{3,2,1,0:T(4,128)(2,1)S(1)}, u32[]{:S(2)}, u32[]{:S(2)}) async-start(bf16[16,51,4,128]{3,2,1,0:T(4,128)(2,1)} %get-tuple-element.32), calls=%async_computation | async-start | bytes 1671168 | tf_op jit(solution)/shard_map/all_to_all | solution.py:354
  19.7 2.8 %copy-start.6 = (s32[192]{0:T(256)S(1)}, s32[192]{0:T(256)}, u32[]{:S(2)}) copy-start(s32[192]{0:T(256)} %get-tuple-element.26.tile_ref) | copy-start | bytes 2308
  24.6 12.0 %copy-start.8 = (s32[192]{0:T(256)S(1)}, s32[192]{0:T(256)}, u32[]{:S(2)}) copy-start(s32[192]{0:T(256)} %param.8) | copy-start | bytes 2308
  24.6 12.8 %copy-start.7 = (s32[1,192]{1,0:T(1,128)S(1)}, s32[1,192]{1,0:T(1,128)}, u32[]{:S(2)}) copy-start(s32[1,192]{1,0:T(1,128)} %param.9) | copy-start | bytes 2308
  25.9 22.0 %collective-permute-start = (bf16[48,8,4,128]{3,2,1,0:T(4,128)(2,1)}, bf16[48,8,4,128]{3,2,1,0:T(4,128)(2,1)S(1)}, u32[]{:S(2)}, u32[]{:S(2)}) collective-permute-start(bf16[48,8,4,128]{3,2,1,0:T(4,128)(2,1)} %get-tuple-element.53), channel_id=1, source_target_pairs={{0,8},{8,16},{16,24},{24,0},{1,9},{9,17},{17,25},{25,1},{2,10},{10... | collective-permute-start | bytes 1179656 | tf_op jit(solution)/shard_map/ppermute | solution.py:336
  29.1 19.4 %collective-permute-start.1 = (bf16[48,8,4,128]{3,2,1,0:T(4,128)(2,1)S(1)}, bf16[48,8,4,128]{3,2,1,0:T(4,128)(2,1)S(1)}, u32[]{:S(2)}, u32[]{:S(2)}) collective-permute-start(bf16[48,8,4,128]{3,2,1,0:T(4,128)(2,1)S(1)} %get-tuple-element.52), channel_id=1, source_target_pairs={{0,16},{8,24},{16,0},{24,8},{1,17},{9,25},{17,1},{25,9},{2,18},{10... | collective-permute-start | bytes 1179656 | tf_op jit(solution)/shard_map/ppermute | solution.py:336
  33.6 16.4 %collective-permute-start.2 = (bf16[48,8,4,128]{3,2,1,0:T(4,128)(2,1)S(1)}, bf16[48,8,4,128]{3,2,1,0:T(4,128)(2,1)S(1)}, u32[]{:S(2)}, u32[]{:S(2)}) collective-permute-start(bf16[48,8,4,128]{3,2,1,0:T(4,128)(2,1)S(1)} %get-tuple-element.51), channel_id=1, source_target_pairs={{0,24},{8,0},{16,8},{24,16},{1,25},{9,1},{17,9},{25,17},{2,26},{10... | collective-permute-start | bytes 1179656 | tf_op jit(solution)/shard_map/ppermute | solution.py:336
  39.3 12.2 %collective-permute-start.3 = (s32[195]{0:T(256)S(1)}, s32[195]{0:T(256)S(1)}, u32[]{:S(2)}, u32[]{:S(2)}) collective-permute-start(s32[195]{0:T(256)S(1)} %pad_add_fusion.note_ref.n0), channel_id=1, source_target_pairs={{0,1},{1,2},{2,3},{3,4},{4,5},{5,6},{6,7},{8,9},{9,10},{10,11},{11... | collective-permute-start | bytes 2348 | tf_op jit(solution)/shard_map/ppermute | solution.py:335
  44.1 7.4 %collective-permute-start.4 = (s32[195]{0:T(256)S(1)}, s32[195]{0:T(256)S(1)}, u32[]{:S(2)}, u32[]{:S(2)}) collective-permute-start(s32[195]{0:T(256)S(1)} %pad_add_fusion.note_ref.n0), channel_id=1, source_target_pairs={{0,2},{1,3},{2,4},{3,5},{4,6},{5,7},{8,10},{9,11},{10,12},{11,13},... | collective-permute-start | bytes 2348 | tf_op jit(solution)/shard_map/ppermute | solution.py:335
  56.7 57.4 %all-to-all-start.2 = ((bf16[16,63,4,128]{3,2,1,0:T(4,128)(2,1)}), bf16[16,63,4,128]{3,2,1,0:T(4,128)(2,1)S(1)}, u32[]{:S(2)}, u32[]{:S(2)}) async-start(bf16[16,63,4,128]{3,2,1,0:T(4,128)(2,1)} %hop.1), calls=%async_computation.2 | async-start | bytes 2064384 | tf_op jit(solution)/shard_map/all_to_all | solution.py:362
  69.7 10.7 %collective-permute-start.5 = (bf16[48,4,4,128]{3,2,1,0:T(4,128)(2,1)S(1)}, bf16[48,4,4,128]{3,2,1,0:T(4,128)(2,1)S(1)}, u32[]{:S(2)}, u32[]{:S(2)}) collective-permute-start(bf16[48,4,4,128]{3,2,1,0:T(4,128)(2,1)S(1)} %bitcast.64), channel_id=1, source_target_pairs={{0,8},{8,16},{16,24},{24,0},{1,9},{9,17},{17,25},{25,1},{2,10},{10... | collective-permute-start | bytes 589832 | tf_op jit(solution)/shard_map/ppermute | solution.py:336
  72.9 11.0 %collective-permute-start.6 = (bf16[48,4,4,128]{3,2,1,0:T(4,128)(2,1)S(1)}, bf16[48,4,4,128]{3,2,1,0:T(4,128)(2,1)S(1)}, u32[]{:S(2)}, u32[]{:S(2)}) collective-permute-start(bf16[48,4,4,128]{3,2,1,0:T(4,128)(2,1)S(1)} %bitcast.63), channel_id=1, source_target_pairs={{0,16},{8,24},{16,0},{24,8},{1,17},{9,25},{17,1},{25,9},{2,18},{10... | collective-permute-start | bytes 589832 | tf_op jit(solution)/shard_map/ppermute | solution.py:336
  77.4 7.4 %collective-permute-start.7 = (bf16[48,4,4,128]{3,2,1,0:T(4,128)(2,1)S(1)}, bf16[48,4,4,128]{3,2,1,0:T(4,128)(2,1)S(1)}, u32[]{:S(2)}, u32[]{:S(2)}) collective-permute-start(bf16[48,4,4,128]{3,2,1,0:T(4,128)(2,1)S(1)} %bitcast.62), channel_id=1, source_target_pairs={{0,24},{8,0},{16,8},{24,16},{1,25},{9,1},{17,9},{25,17},{2,26},{10... | collective-permute-start | bytes 589832 | tf_op jit(solution)/shard_map/ppermute | solution.py:336
  85.8 17.9 %collective-permute-start.8 = (bf16[192,4,4,128]{3,2,1,0:T(4,128)(2,1)S(1)}, bf16[192,4,4,128]{3,2,1,0:T(4,128)(2,1)S(1)}, u32[]{:S(2)}, u32[]{:S(2)}) collective-permute-start(bf16[192,4,4,128]{3,2,1,0:T(4,128)(2,1)S(1)} %unpack_kv.1), channel_id=1, source_target_pairs={{0,2},{1,3},{2,4},{3,5},{4,6},{5,7},{8,10},{9,11},{10,12},{11,13},... | collective-permute-start | bytes 2359304 | tf_op jit(solution)/shard_map/ppermute | solution.py:335
  88.9 20.5 %collective-permute-start.9 = (bf16[192,4,4,128]{3,2,1,0:T(4,128)(2,1)S(1)}, bf16[192,4,4,128]{3,2,1,0:T(4,128)(2,1)S(1)}, u32[]{:S(2)}, u32[]{:S(2)}) collective-permute-start(bf16[192,4,4,128]{3,2,1,0:T(4,128)(2,1)S(1)} %unpack_kv.1), channel_id=1, source_target_pairs={{0,1},{2,3},{4,5},{6,7},{8,9},{10,11},{12,13},{14,15},{16,17},{18,... | collective-permute-start | bytes 2359304 | tf_op jit(solution)/shard_map/ppermute | solution.py:368
  103.7 6.7 %collective-permute-start.10 = (bf16[192,4,4,128]{3,2,1,0:T(4,128)(2,1)S(1)}, bf16[192,4,4,128]{3,2,1,0:T(4,128)(2,1)S(1)}, u32[]{:S(2)}, u32[]{:S(2)}) collective-permute-start(bf16[192,4,4,128]{3,2,1,0:T(4,128)(2,1)S(1)} %collective-permute-done.8), channel_id=1, source_target_pairs={{1,0},{3,2},{5,4},{7,6},{9,8},{11,10},{13,12},{15,14},{17,16},{19,... | collective-permute-start | bytes 2359304 | tf_op jit(solution)/shard_map/ppermute | solution.py:369
  114.0 41.5 %all-to-all-start.1 = ((bf16[16,36,4,128]{3,2,1,0:T(4,128)(2,1)}), bf16[16,36,4,128]{3,2,1,0:T(4,128)(2,1)S(1)}, u32[]{:S(2)}, u32[]{:S(2)}) async-start(bf16[16,36,4,128]{3,2,1,0:T(4,128)(2,1)} %get-tuple-element.33), calls=%async_computation.1 | async-start | bytes 1179648 | tf_op jit(solution)/shard_map/all_to_all | solution.py:371
  126.8 6.0 %collective-permute-start.11 = (bf16[36,4,128]{2,1,0:T(4,128)(2,1)S(1)}, bf16[36,4,128]{2,1,0:T(4,128)(2,1)S(1)}, u32[]{:S(2)}, u32[]{:S(2)}) collective-permute-start(bf16[36,4,128]{2,1,0:T(4,128)(2,1)S(1)} %bitcast.66), channel_id=1, source_target_pairs={{0,8},{8,16},{16,24},{24,0},{1,9},{9,17},{17,25},{25,1},{2,10},{10... | collective-permute-start | bytes 110600 | tf_op jit(solution)/shard_map/ppermute | solution.py:336
  132.8 6.5 %collective-permute-start.12 = (bf16[36,4,128]{2,1,0:T(4,128)(2,1)S(1)}, bf16[36,4,128]{2,1,0:T(4,128)(2,1)S(1)}, u32[]{:S(2)}, u32[]{:S(2)}) collective-permute-start(bf16[36,4,128]{2,1,0:T(4,128)(2,1)S(1)} %broadcast_select_fusion), channel_id=1, source_target_pairs={{0,16},{8,24},{16,0},{24,8},{1,17},{9,25},{17,1},{25,9},{2,18},{10... | collective-permute-start | bytes 110600 | tf_op jit(solution)/shard_map/ppermute | solution.py:336
  139.3 10.3 %collective-permute-start.13 = (bf16[3,4,4,128]{3,2,1,0:T(4,128)(2,1)S(1)}, bf16[3,4,4,128]{3,2,1,0:T(4,128)(2,1)S(1)}, u32[]{:S(2)}, u32[]{:S(2)}) collective-permute-start(bf16[3,4,4,128]{3,2,1,0:T(4,128)(2,1)S(1)} %slice.49), channel_id=1, source_target_pairs={{0,2},{1,3},{2,4},{3,5},{4,6},{5,7},{8,10},{9,11},{10,12},{11,13},... | collective-permute-start | bytes 36872 | tf_op jit(solution)/shard_map/ppermute | solution.py:335
  142.4 7.2 %collective-permute-start.14 = (bf16[3,4,4,128]{3,2,1,0:T(4,128)(2,1)S(1)}, bf16[3,4,4,128]{3,2,1,0:T(4,128)(2,1)S(1)}, u32[]{:S(2)}, u32[]{:S(2)}) collective-permute-start(bf16[3,4,4,128]{3,2,1,0:T(4,128)(2,1)S(1)} %slice.49), channel_id=1, source_target_pairs={{0,1},{1,2},{2,3},{3,4},{4,5},{5,6},{6,7},{8,9},{9,10},{10,11},{11... | collective-permute-start | bytes 36872 | tf_op jit(solution)/shard_map/ppermute | solution.py:335
  148.5 1.1 copy-start.1
  148.6 1.4 copy-start.3
  148.6 1.6 %copy-start.5 = (bf16[192,4,4,128]{3,2,1,0:T(4,128)(2,1)S(1)}, bf16[192,4,4,128]{3,2,1,0:T(4,128)(2,1)}, u32[]{:S(2)}) copy-start(bf16[192,4,4,128]{3,2,1,0:T(4,128)(2,1)} %copy-done.4) | copy-start | bytes 2359300
  (3 other events, 2.7 us)
